TPU v7x, 32 devices: a whole 2x2x4 slice. The times are simulated.
32 devices in a mesh: lat: 8 (over z, y), mp: 4 (over x, core).
Axes of the slice: x: 2, y: 2, z: 4, core: 2. Of those that a mesh axis runs over, the one named last changes fastest.
Arguments:
- tokens: bfloat16 [16384, 1024], P(('lat', 'mp')), may hold values from -20 to 20
- gain: float32 [1024], replicated, may hold values from 0.1 to 1.9
- qkv_weight: bfloat16 [16, 192, 1024], P('mp'), may hold values from -2 to 2
- out_weight: bfloat16 [16, 64, 1024], P('mp'), may hold values from -1 to 1
- row_cells: int32 [64], replicated, may hold values from 32 to 256, as said below
- upstream: bfloat16 [16384, 1024], P(('lat', 'mp')), may hold values from -6 to 6
Outputs:
- update: bfloat16 [16384, 1024], P(('lat', 'mp'))
- grad_input: bfloat16 [16384, 1024], P(('lat', 'mp'))
- grad_qkv: float32 [16, 192, 1024], P('mp')
- grad_out: float32 [16, 64, 1024], P('mp')
Inputs may be any that keep to these rules, and one draw needn't show every extreme that they name: `row_cells`: A row's live cells are its first ones; rows at the equator hold all 256, rows at the poles 256 // 8.
All inputs are finite; a program needn't handle non-finite values.
Results may differ from a plain program's by a relative error of at most 0.0085.
The roundings to bfloat16 on the way count: a program that leaves them out, or rounds other values in their place, can miss the bound.
Values may be sent and summed in bfloat16 or wider, within the bound.
No kernel may reach another device: no remote copies, remote signals or barrier semaphores. Data moves between devices by JAX's collectives and lax.ppermute only.
A program may use at most 192 MiB of HBM per device.

v0:
```python
import functools
import math
import jax
import jax.numpy as jnp
from jax import lax
from jax.experimental import pallas as pl
from jax.experimental.pallas import tpu as pltpu

HEAD_WIDTH = 64
LONGITUDES = 256
BAND_ROWS = 8
HALO = 6
EXT_ROWS = BAND_ROWS + 2 * HALO
LANES = 256
QUERY_ROWS = 4
KEY_ROWS = QUERY_ROWS + 2 * HALO
BLOCK = 8
BLOCKS = LONGITUDES // BLOCK
KEYS = KEY_ROWS * BLOCK
MASKED = -1e30


def nn(a, b):
    return lax.dot_general(a, b, (((1,), (0,)), ((), ())), preferred_element_type=jnp.float32)


def nt(a, b):
    return lax.dot_general(a, b, (((1,), (1,)), ((), ())), preferred_element_type=jnp.float32)


def attention_kernel(
    heads,
    cells,
    q, go, k_top, k_own, k_bot, v_top, v_own, v_bot,
    out, dq, dk_own, dv_own, dk_top, dv_top, dk_bot, dv_bot,
    k_s, v_s, kt_s, vt_s, dk_s, dv_s, live_s, near_s,
):
    feats = heads * HEAD_WIDTH
    tile_cols = LANES // heads // QUERY_ROWS
    tile_queries = QUERY_ROWS * tile_cols
    window = tile_cols // BLOCK + 2

    def load_pair(p, carry):
        cols = pl.ds(pl.multiple_of(p * 16, 16), 16)
        for parts, rows_s, turned_s in (((k_top, k_own, k_bot), k_s, kt_s), ((v_top, v_own, v_bot), v_s, vt_s)):
            both = jnp.concatenate([part[:, cols, :].astype(jnp.float32) for part in parts], axis=0)
            for half in range(2):
                block = both[:, 8 * half:8 * half + 8, :].reshape(EXT_ROWS * BLOCK, feats)
                rows_s[2 * p + half] = block.astype(jnp.bfloat16)
                for upper in range(2):
                    first = upper * QUERY_ROWS * BLOCK
                    turned_s[upper, 2 * p + half] = block[first:first + KEYS].T.astype(jnp.bfloat16)
        for half in range(2):
            col = (2 * p + half) * BLOCK + lax.broadcasted_iota(jnp.int32, (BLOCK, 128), 0)
            for row in range(EXT_ROWS):
                live_s[2 * p + half, row * BLOCK:(row + 1) * BLOCK, :] = jnp.where(col < cells[row], 0.0, MASKED)
        return carry

    lax.fori_loop(0, BLOCKS // 2, load_pair, 0)
    dk_s[...] = jnp.zeros_like(dk_s)
    dv_s[...] = jnp.zeros_like(dv_s)

    lane = lax.broadcasted_iota(jnp.int32, (KEYS, LANES), 1) % tile_queries
    query_row = lane // tile_cols
    query_col = lane % tile_cols
    key = lax.broadcasted_iota(jnp.int32, (KEYS, LANES), 0)
    row_gap = key // BLOCK - query_row
    for j in range(window):
        col_gap = (j - 1) * BLOCK + key % BLOCK - query_col
        near = (row_gap >= 0) & (row_gap <= 2 * HALO) & (col_gap >= -HALO) & (col_gap <= HALO)
        near_s[j] = jnp.where(near, 0.0, MASKED)

    own_head = (
        lax.broadcasted_iota(jnp.int32, (LANES, feats), 0) // tile_queries
        == lax.broadcasted_iota(jnp.int32, (LANES, feats), 1) // HEAD_WIDTH
    )
    own_head_turned = (
        lax.broadcasted_iota(jnp.int32, (feats, LANES), 1) // tile_queries
        == lax.broadcasted_iota(jnp.int32, (feats, LANES), 0) // HEAD_WIDTH
    )
    query_lane = lax.broadcasted_iota(jnp.int32, (1, LANES), 1) % tile_queries

    def spread(ref, upper, cols):
        tile = ref[upper * QUERY_ROWS:(upper + 1) * QUERY_ROWS, cols, :].reshape(tile_queries, feats)
        if heads == 1:
            return tile
        stacked = jnp.concatenate([tile] * heads, axis=0)
        return jnp.where(own_head, stacked, jnp.zeros_like(stacked))

    def gather(turned):
        if heads == 1:
            tile = turned.T
        else:
            tall = jnp.where(own_head_turned, turned, 0.0).T
            tile = sum(tall[h * tile_queries:(h + 1) * tile_queries] for h in range(heads))
        return tile.astype(jnp.bfloat16).reshape(QUERY_ROWS, tile_cols, feats)

    def one_tile(upper, tile):
        start = pl.multiple_of(tile * tile_cols, 16)
        cols = pl.ds(start, tile_cols)
        rows = slice(upper * QUERY_ROWS, (upper + 1) * QUERY_ROWS)
        keys = pl.ds(upper * QUERY_ROWS * BLOCK, KEYS)
        index = [(tile * (tile_cols // BLOCK) + j + BLOCKS - 1) % BLOCKS for j in range(window)]
        queries = spread(q, upper, cols)
        grads = spread(go, upper, cols)
        scores = [
            nt(k_s[index[j], keys, :], queries)
            + near_s[j]
            + jnp.concatenate([live_s[index[j], keys, :]] * (LANES // 128), axis=1)
            for j in range(window)
        ]
        highest = jnp.max(functools.reduce(jnp.maximum, scores), axis=0, keepdims=True)
        terms = [jnp.exp(score - highest) for score in scores]
        total = jnp.sum(sum(terms), axis=0, keepdims=True)
        query_cells = jnp.zeros((1, LANES), jnp.int32)
        for row in range(QUERY_ROWS):
            cell = cells[HALO + upper * QUERY_ROWS + row]
            query_cells = jnp.where(query_lane // tile_cols == row, cell, query_cells)
        live = start + query_lane % tile_cols < query_cells
        inverse = jnp.where(live, 1.0 / total, 0.0)
        probs = [term * inverse for term in terms]
        grad_probs = [nt(v_s[index[j], keys, :], grads) for j in range(window)]
        delta = jnp.sum(sum(p * g for p, g in zip(probs, grad_probs)), axis=0, keepdims=True)
        weights = [p.astype(jnp.bfloat16) for p in probs]
        grad_scores = [(p * (g - delta)).astype(jnp.bfloat16) for p, g in zip(probs, grad_probs)]
        for j in range(window):
            dv_s[index[j], keys, :] += nn(weights[j], grads)
            dk_s[index[j], keys, :] += nn(grad_scores[j], queries)
        values_turned = jnp.concatenate([vt_s[upper, index[j]] for j in range(window)], axis=1)
        keys_turned = jnp.concatenate([kt_s[upper, index[j]] for j in range(window)], axis=1)
        out[rows, cols, :] = gather(nn(values_turned, jnp.concatenate(weights, axis=0)))
        dq[rows, cols, :] = gather(nn(keys_turned, jnp.concatenate(grad_scores, axis=0)) * (HEAD_WIDTH ** -0.5))

    def tile_pair(tile, carry):
        for upper in range(2):
            one_tile(upper, tile)
        return carry

    lax.fori_loop(0, LONGITUDES // tile_cols, tile_pair, 0)

    def store_pair(p, carry):
        cols = pl.ds(pl.multiple_of(p * 16, 16), 16)
        for sums, top, own, bot in ((dk_s, dk_top, dk_own, dk_bot), (dv_s, dv_top, dv_own, dv_bot)):
            both = jnp.concatenate(
                [sums[2 * p + half].reshape(EXT_ROWS, BLOCK, feats) for half in range(2)], axis=1
            )
            top[:, cols, :] = both[:HALO].astype(jnp.bfloat16)
            own[:, cols, :] = both[HALO:HALO + BAND_ROWS]
            bot[:, cols, :] = both[HALO + BAND_ROWS:].astype(jnp.bfloat16)
        return carry

    lax.fori_loop(0, BLOCKS // 2, store_pair, 0)


def attention(cells, q, go, k_parts, v_parts):
    feats = q.shape[-1]
    heads = feats // HEAD_WIDTH
    window = LANES // heads // QUERY_ROWS // BLOCK + 2
    vmem = pl.BlockSpec(memory_space=pltpu.VMEM)
    grid = lambda rows, kind: jax.ShapeDtypeStruct((rows, LONGITUDES, feats), kind)
    bf16, f32 = jnp.bfloat16, jnp.float32
    pairs = BAND_ROWS * LONGITUDES * heads * KEYS * window
    return pl.pallas_call(
        functools.partial(attention_kernel, heads),
        out_shape=(
            grid(BAND_ROWS, bf16), grid(BAND_ROWS, bf16),
            grid(BAND_ROWS, f32), grid(BAND_ROWS, f32),
            grid(HALO, bf16), grid(HALO, bf16), grid(HALO, bf16), grid(HALO, bf16),
        ),
        in_specs=[pl.BlockSpec(memory_space=pltpu.SMEM)] + [vmem] * 8,
        out_specs=(vmem,) * 8,
        scratch_shapes=[
            pltpu.VMEM((BLOCKS, EXT_ROWS * BLOCK, feats), bf16),
            pltpu.VMEM((BLOCKS, EXT_ROWS * BLOCK, feats), bf16),
            pltpu.VMEM((2, BLOCKS, feats, KEYS), bf16),
            pltpu.VMEM((2, BLOCKS, feats, KEYS), bf16),
            pltpu.VMEM((BLOCKS, EXT_ROWS * BLOCK, feats), f32),
            pltpu.VMEM((BLOCKS, EXT_ROWS * BLOCK, feats), f32),
            pltpu.VMEM((BLOCKS, EXT_ROWS * BLOCK, 128), f32),
            pltpu.VMEM((window, KEYS, LANES), f32),
        ],
        compiler_params=pltpu.CompilerParams(vmem_limit_bytes=60 * 2**20),
        cost_estimate=pl.CostEstimate(
            flops=12 * pairs * HEAD_WIDTH, transcendentals=pairs, bytes_accessed=20 * 2**20
        ),
    )(cells, q, go, *k_parts, *v_parts)


from jax.sharding import PartitionSpec as P

WIDTH = 1024


def passed_along(x, axis, by):
    length = lax.axis_size(axis)
    pairs = [(i, i + by) for i in range(length) if 0 <= i + by < length]
    return lax.ppermute(x, axis, pairs)


def halo_parts(x):
    before = passed_along(x[BAND_ROWS - HALO:], "lat", 1)
    after = passed_along(x[:HALO], "lat", -1)
    return before, x, after


def on_device(tokens, gain, qkv_weight, out_weight, row_cells, upstream):
    heads = qkv_weight.shape[0]
    feats = heads * HEAD_WIDTH
    band_tokens = BAND_ROWS * LONGITUDES
    grad_scale = 4.0 / math.sqrt(band_tokens * lax.axis_size("lat"))
    band_start = lax.axis_index("lat") * BAND_ROWS
    cells = lax.dynamic_slice_in_dim(jnp.pad(row_cells, (HALO, HALO)), band_start, EXT_ROWS)

    features = tokens.astype(jnp.float32)
    inverse = lax.rsqrt(jnp.mean(features * features, axis=1, keepdims=True) + 1e-06)
    normed = (features * inverse * gain[None, :]).astype(jnp.bfloat16)
    normed_band = lax.all_gather(normed, "mp", axis=0, tiled=True)
    band_upstream = lax.all_gather(upstream, "mp", axis=0, tiled=True)

    split_weight = qkv_weight.reshape(heads, 3, HEAD_WIDTH, WIDTH).transpose(1, 0, 2, 3)
    split_weight = split_weight.reshape(3 * feats, WIDTH)
    out_flat = out_weight.reshape(feats, WIDTH)
    qkv = nt(normed_band, split_weight)
    q = (qkv[:, :feats].astype(jnp.bfloat16) * HEAD_WIDTH ** -0.5).astype(jnp.bfloat16)
    k = qkv[:, feats:2 * feats].astype(jnp.bfloat16)
    v = qkv[:, 2 * feats:].astype(jnp.bfloat16)
    grid = lambda x: x.reshape(BAND_ROWS, LONGITUDES, feats)
    grad_heads = nt(band_upstream, out_flat).astype(jnp.bfloat16)
    k_parts, v_parts = halo_parts(grid(k)), halo_parts(grid(v))
    out, dq, dk, dv, dk_top, dv_top, dk_bot, dv_bot = attention(
        cells, grid(q), grid(grad_heads), k_parts, v_parts
    )
    flat = lambda x: x.reshape(band_tokens, feats)

    def joined(own, top, bot):
        from_above = passed_along(top, "lat", -1).astype(jnp.float32)
        from_below = passed_along(bot, "lat", 1).astype(jnp.float32)
        own = own + jnp.pad(from_below, ((0, BAND_ROWS - HALO), (0, 0), (0, 0)))
        own = own + jnp.pad(from_above, ((BAND_ROWS - HALO, 0), (0, 0), (0, 0)))
        return flat(own.astype(jnp.bfloat16))

    dk, dv = joined(dk, dk_top, dk_bot), joined(dv, dv_top, dv_bot)
    grad_proj = jnp.concatenate([flat(dq), dk, dv], axis=1)

    update = lax.psum_scatter(
        nn(flat(out), out_flat).astype(jnp.bfloat16), "mp", scatter_dimension=0, tiled=True
    )
    tn = lambda a, b: lax.dot_general(a, b, (((0,), (0,)), ((), ())), preferred_element_type=jnp.float32)
    grad_out = lax.psum(tn(flat(out), band_upstream).astype(jnp.bfloat16), "lat").astype(jnp.float32)
    grad_qkv = lax.psum(tn(grad_proj, normed_band).astype(jnp.bfloat16), "lat").astype(jnp.float32)
    grad_qkv = grad_qkv.reshape(3, heads, HEAD_WIDTH, WIDTH).transpose(1, 0, 2, 3)
    grad_normed = lax.psum_scatter(
        nn(grad_proj, split_weight).astype(jnp.bfloat16), "mp", scatter_dimension=0, tiled=True
    ).astype(jnp.float32)
    centred = features * inverse
    scaled = gain[None, :] * grad_normed
    grad_input = inverse * (scaled - centred * jnp.mean(scaled * centred, axis=1, keepdims=True))
    return (
        update,
        grad_input.astype(jnp.bfloat16),
        grad_qkv.reshape(heads, 3 * HEAD_WIDTH, WIDTH) * grad_scale,
        (grad_out * grad_scale).reshape(heads, HEAD_WIDTH, WIDTH),
    )


def solution(mesh):
    return jax.shard_map(
        on_device,
        mesh=mesh,
        in_specs=(
            P(("lat", "mp"), None),
            P(),
            P("mp", None, None),
            P("mp", None, None),
            P(),
            P(("lat", "mp"), None),
        ),
        out_specs=(
            P(("lat", "mp"), None),
            P(("lat", "mp"), None),
            P("mp", None, None),
            P("mp", None, None),
        ),
        check_vma=False,
    )
```

profile of v0, /device:TPU:0, one launch (start us, length us, event | category | flops | bytes accessed | tf_op | source)
XLA Modules:
  0.0 453.6 jit_solution(5360788263794587124)
XLA Ops:
  7.2 0.0 all-gather.3.cloned.1.call-start
  7.2 1.6 fusion.8
  8.9 2.5 fusion.3
  11.4 0.0 all-gather.3.cloned.1.call-update
  11.4 0.0 all-gather.5.cloned.1.call-start
  11.5 0.7 all-gather.5.cloned.1.call-update
  12.2 0.0 all-reduce.8.cloned.1.call-start
  12.2 1.3 copy.12
  13.6 0.6 pad_dynamic-slice_fusion.cells
  14.2 34.6 %all-gather.3.cloned.1.call-done = bf16[2048,1024]{1,0:T(8,128)(2,1)} async-done(((bf16[512,1024]{1,0:T(8,128)(2,1)}), bf16[2048,1024]{1,0:T(8,128)(2,1)}) %all-gather.3.cloned.1.call-update) | async-done | bytes 4194320 | tf_op jit(solution)/shard_map/all_gather | solution.py:217
  48.8 6.2 %convolution_convert_fusion.2 = bf16[2048,768]{1,0:T(8,128)(2,1)S(1)} fusion(bf16[2048,1024]{1,0:T(8,128)(2,1)} %all-gather.3.cloned.1.call-done, bf16[768,1024]{1,0:T(8,128)(2,1)} %bitcast.39), kind=kOutput, calls=%fused_computation.2 | convolution fusion | flops 3222798336 | bytes 8912896 | tf_op jit(solution)/shard_map/dot_general | solution.py:28
  54.9 1.5 fusion.11
  56.4 0.4 copy-done.2
  56.9 4.3 collective-permute-start.2
  61.1 1.3 collective-permute-start.3
  62.4 1.3 collective-permute-start.1
  63.7 6.1 %collective-permute-start = (bf16[6,256,256]{2,1,0:T(8,128)(2,1)S(1)}, bf16[6,256,256]{2,1,0:T(8,128)(2,1)}, u32[]{:S(2)}, u32[]{:S(2)}) collective-permute-start(bf16[6,256,256]{2,1,0:T(8,128)(2,1)S(1)} %bitcast.49), channel_id=1, source_target_pairs={{0,4},{4,8},{8,12},{12,16},{16,20},{20,24},{24,28},{1,5},{5,9},{9,... | collective-permute-start | bytes 2359304 | tf_op jit(solution)/shard_map/ppermute | solution.py:197
  69.8 15.0 %all-gather.5.cloned.1.call-done = bf16[2048,1024]{1,0:T(8,128)(2,1)} async-done(((bf16[512,1024]{1,0:T(8,128)(2,1)}), bf16[2048,1024]{1,0:T(8,128)(2,1)}) %all-gather.5.cloned.1.call-update) | async-done | bytes 4194320 | tf_op jit(solution)/shard_map/all_gather | solution.py:218
  84.8 4.6 %convolution_convert_fusion.3 = bf16[2048,256]{1,0:T(8,128)(2,1)} fusion(bf16[2048,1024]{1,0:T(8,128)(2,1)} %all-gather.5.cloned.1.call-done, bf16[256,1024]{1,0:T(8,128)(2,1)S(1)} %bitcast.32), kind=kOutput, calls=%fused_computation.10 | convolution fusion | flops 1074266112 | bytes 5767168 | tf_op jit(solution)/shard_map/dot_general | solution.py:28
  89.4 1.7 fusion.12
  91.2 20.9 %collective-permute-done.2.v_top = bf16[6,256,256]{2,1,0:T(8,128)(2,1)} collective-permute-done((bf16[6,256,256]{2,1,0:T(8,128)(2,1)}, bf16[6,256,256]{2,1,0:T(8,128)(2,1)}, u32[]{:S(2)}, u32[]{:S(2)}) %collective-permute-start.2) | collective-permute-done | bytes 786464 | tf_op jit(solution)/shard_map/ppermute | solution.py:197
  112.1 16.1 %collective-permute-done.k_top = bf16[6,256,256]{2,1,0:T(8,128)(2,1)} collective-permute-done((bf16[6,256,256]{2,1,0:T(8,128)(2,1)S(1)}, bf16[6,256,256]{2,1,0:T(8,128)(2,1)}, u32[]{:S(2)}, u32[]{:S(2)}) %collective-permute-start) | collective-permute-done | bytes 786464 | tf_op jit(solution)/shard_map/ppermute | solution.py:197
  128.2 41.8 %shard_map.93 = (bf16[8,256,256]{2,1,0:T(8,128)(2,1)}, bf16[8,256,256]{2,1,0:T(8,128)(2,1)}, f32[8,256,256]{2,1,0:T(8,128)}, f32[8,256,256]{2,1,0:T(8,128)}, bf1...) custom-call(s32[20]{0:T(128)} %pad_dynamic-slice_fusion.cells, ...), custom_call_target="tpu_custom_call" | custom-call | flops 3221225472 | bytes 20971520 | tf_op jit(solution)/shard_map/pallas_call | solution.py:163
  170.0 4.5 %collective-permute-start.4 = (bf16[6,256,256]{2,1,0:T(8,128)(2,1)}, bf16[6,256,256]{2,1,0:T(8,128)(2,1)S(1)}, u32[]{:S(2)}, u32[]{:S(2)}) collective-permute-start(bf16[6,256,256]{2,1,0:T(8,128)(2,1)} %get-tuple-element.15), channel_id=1, source_target_pairs={{0,4},{4,8},{8,12},{12,16},{16,20},{20,24},{24,28},{1,5},{5,9},{9,... | collective-permute-start | bytes 2359304 | tf_op jit(solution)/shard_map/ppermute | solution.py:197
  174.6 1.3 collective-permute-start.5
  175.9 4.9 %collective-permute-start.6 = (bf16[6,256,256]{2,1,0:T(8,128)(2,1)}, bf16[6,256,256]{2,1,0:T(8,128)(2,1)S(1)}, u32[]{:S(2)}, u32[]{:S(2)}) collective-permute-start(bf16[6,256,256]{2,1,0:T(8,128)(2,1)} %get-tuple-element.18), channel_id=1, source_target_pairs={{0,4},{4,8},{8,12},{12,16},{16,20},{20,24},{24,28},{1,5},{5,9},{9,... | collective-permute-start | bytes 2359304 | tf_op jit(solution)/shard_map/ppermute | solution.py:197
  180.8 1.5 collective-permute-start.7
  182.3 4.7 %convolution_convert_fusion.5 = bf16[256,1024]{1,0:T(8,128)(2,1)} fusion(bf16[2048,256]{1,0:T(8,128)(2,1)} %bitcast.36, bf16[2048,1024]{1,0:T(8,128)(2,1)} %all-gather.5.cloned.1.call-done), kind=kOutput, calls=%fused_computation.21 | convolution fusion | flops 1074003968 | bytes 5767168 | tf_op jit(solution)/shard_map/dot_general | solution.py:248
  187.0 39.5 %collective-permute-done.4 = bf16[6,256,256]{2,1,0:T(8,128)(2,1)S(1)} collective-permute-done((bf16[6,256,256]{2,1,0:T(8,128)(2,1)}, bf16[6,256,256]{2,1,0:T(8,128)(2,1)S(1)}, u32[]{:S(2)}, u32[]{:S(2)}) %collective-permute-start.4) | collective-permute-done | bytes 786464 | tf_op jit(solution)/shard_map/ppermute | solution.py:197
  226.5 0.4 add_convert_fusion.1
  226.9 14.9 %collective-permute-done.6 = bf16[6,256,256]{2,1,0:T(8,128)(2,1)S(1)} collective-permute-done((bf16[6,256,256]{2,1,0:T(8,128)(2,1)}, bf16[6,256,256]{2,1,0:T(8,128)(2,1)S(1)}, u32[]{:S(2)}, u32[]{:S(2)}) %collective-permute-start.6) | collective-permute-done | bytes 786464 | tf_op jit(solution)/shard_map/ppermute | solution.py:197
  241.8 0.4 add_convert_fusion
  242.2 1.0 copy-done.9
  243.1 4.8 %convolution_convert_fusion.4 = bf16[768,1024]{1,0:T(8,128)(2,1)} fusion(bf16[2048,1024]{1,0:T(8,128)(2,1)S(1)} %copy-done.12, bf16[2048,256]{1,0:T(8,128)(2,1)S(1)} %bitcast.47, bf16[2048,256]{1,0:T(8,128)(2,1)S(1)} %bitcast.45, bf16[2048,256]{1,0:T(8,128)(2,1)S(1)} %bitcast.53), kind=kOutput, calls=%fused_computation.20 | convolution fusion | flops 3231449088 | bytes 8912896 | tf_op jit(solution)/shard_map/dot_general | solution.py:248
  247.9 0.0 reduce-scatter.5.cloned.1.call-start
  248.0 6.6 %convolution_convert_fusion.1 = bf16[2048,1024]{1,0:T(8,128)(2,1)} fusion(bf16[768,1024]{1,0:T(8,128)(2,1)S(1)} %bitcast.40, bf16[2048,256]{1,0:T(8,128)(2,1)} %bitcast.48, bf16[2048,256]{1,0:T(8,128)(2,1)S(1)} %bitcast.46, bf16[2048,256]{1,0:T(8,128)(2,1)} %bitcast.52), kind=kOutput, calls=%fused_computation.1 | convolution fusion | flops 3232759808 | bytes 8912896 | tf_op jit(solution)/shard_map/dot_general | solution.py:24
  254.6 0.0 reduce-scatter.5.cloned.1.call-update
  254.7 0.0 reduce-scatter.3.cloned.1.call-start
  254.7 1.2 copy-done.4
  255.9 3.3 convolution_convert_fusion
  259.2 93.5 %all-reduce.8.cloned.1.call-done = (bf16[768,1024]{1,0:T(8,128)(2,1)}, bf16[256,1024]{1,0:T(8,128)(2,1)}) async-done(((bf16[768,1024]{1,0:T(8,128)(2,1)}, bf16[256,1024]{1,0:T(8,128)(2,1)}), (bf16[768,1024]{1,0:T(8,128)(2,1)}, bf16[256,1024]{1,0:T(8,128)(2,1)})) %all-reduce.8.cloned.1.call-update) | async-done | bytes 2097168 | tf_op jit(solution)/shard_map/psum | solution.py:250
  352.7 1.8 convert_multiply_fusion
  354.5 1.9 copy.13
  356.4 1.1 convert_multiply_fusion.4
  357.5 41.9 %reduce-scatter.5.cloned.1.call-done = bf16[512,1024]{1,0:T(8,128)(2,1)} async-done(((bf16[2048,1024]{1,0:T(8,128)(2,1)}), bf16[512,1024]{1,0:T(8,128)(2,1)}) %reduce-scatter.5.cloned.1.call-update) | async-done | bytes 1048592 | tf_op jit(solution)/shard_map/reduce_scatter | solution.py:252
  399.4 1.8 fusion.4
  401.1 2.8 fusion.7
  403.9 43.1 %reduce-scatter.3.cloned.1.call-done = bf16[512,1024]{1,0:T(8,128)(2,1)} async-done(((bf16[2048,1024]{1,0:T(8,128)(2,1)}), bf16[512,1024]{1,0:T(8,128)(2,1)}) %reduce-scatter.3.cloned.1.call-update) | async-done | bytes 1048592 | tf_op jit(solution)/shard_map/reduce_scatter | solution.py:245
  (35 shorter events, 0.1 us)
Async XLA Ops:
  7.2 77.7 %copy-start = (bf16[4,64,1024]{2,1,0:T(8,128)(2,1)S(1)}, bf16[4,64,1024]{2,1,0:T(8,128)(2,1)}, u32[]{:S(2)}) copy-start(bf16[4,64,1024]{2,1,0:T(8,128)(2,1)} %param.9) | copy-start | bytes 1572868
  7.2 5.0 %copy-start.7 = (bf16[4,192,1024]{2,1,0:T(8,128)(2,1)S(1)}, bf16[4,192,1024]{2,1,0:T(8,128)(2,1)}, u32[]{:S(2)}) copy-start(bf16[4,192,1024]{2,1,0:T(8,128)(2,1)} %param.8) | copy-start | bytes 4718596
  7.2 41.6 %all-gather.3.cloned.1.call-start = ((), (), s32[]{:S(2)}) async-start(), calls=%async_computation.2 | async-start | bytes 5242880 | tf_op jit(solution)/shard_map/all_gather | solution.py:217
  11.4 2.2 copy-start.13
  11.4 73.4 %all-gather.5.cloned.1.call-start = ((), (), s32[]{:S(2)}) async-start(), calls=%async_computation.3 | async-start | bytes 5242880 | tf_op jit(solution)/shard_map/all_gather | solution.py:218
  12.2 340.5 %all-reduce.8.cloned.1.call-start = ((), (), s32[]{:S(2)}) async-start(), calls=%async_computation.6 | async-start | bytes 4194304 | tf_op jit(solution)/shard_map/psum | solution.py:250
  54.9 1.9 copy-start.2
  56.9 55.3 %collective-permute-start.2 = (bf16[6,256,256]{2,1,0:T(8,128)(2,1)}, bf16[6,256,256]{2,1,0:T(8,128)(2,1)}, u32[]{:S(2)}, u32[]{:S(2)}) collective-permute-start(bf16[6,256,256]{2,1,0:T(8,128)(2,1)} %bitcast.9), channel_id=1, source_target_pairs={{0,4},{4,8},{8,12},{12,16},{16,20},{20,24},{24,28},{1,5},{5,9},{9,... | collective-permute-start | bytes 2359304 | tf_op jit(solution)/shard_map/ppermute | solution.py:197
  61.1 51.0 %collective-permute-start.3 = (bf16[6,256,256]{2,1,0:T(8,128)(2,1)S(1)}, bf16[6,256,256]{2,1,0:T(8,128)(2,1)}, u32[]{:S(2)}, u32[]{:S(2)}) collective-permute-start(bf16[6,256,256]{2,1,0:T(8,128)(2,1)S(1)} %bitcast.51), channel_id=1, source_target_pairs={{4,0},{8,4},{12,8},{16,12},{20,16},{24,20},{28,24},{5,1},{9,5},{13... | collective-permute-start | bytes 2359304 | tf_op jit(solution)/shard_map/ppermute | solution.py:197
  62.4 49.7 %collective-permute-start.1 = (bf16[6,256,256]{2,1,0:T(8,128)(2,1)S(1)}, bf16[6,256,256]{2,1,0:T(8,128)(2,1)}, u32[]{:S(2)}, u32[]{:S(2)}) collective-permute-start(bf16[6,256,256]{2,1,0:T(8,128)(2,1)S(1)} %bitcast.50), channel_id=1, source_target_pairs={{4,0},{8,4},{12,8},{16,12},{20,16},{24,20},{28,24},{5,1},{9,5},{13... | collective-permute-start | bytes 2359304 | tf_op jit(solution)/shard_map/ppermute | solution.py:197
  63.7 64.5 %collective-permute-start = (bf16[6,256,256]{2,1,0:T(8,128)(2,1)S(1)}, bf16[6,256,256]{2,1,0:T(8,128)(2,1)}, u32[]{:S(2)}, u32[]{:S(2)}) collective-permute-start(bf16[6,256,256]{2,1,0:T(8,128)(2,1)S(1)} %bitcast.49), channel_id=1, source_target_pairs={{0,4},{4,8},{8,12},{12,16},{16,20},{20,24},{24,28},{1,5},{5,9},{9,... | collective-permute-start | bytes 2359304 | tf_op jit(solution)/shard_map/ppermute | solution.py:197
  84.8 4.6 %copy-start.3 = (bf16[2048,768]{1,0:T(8,128)(2,1)S(1)}, bf16[2048,768]{1,0:T(8,128)(2,1)}, u32[]{:S(2)}) copy-start(bf16[2048,768]{1,0:T(8,128)(2,1)} %copy-done.2) | copy-start | bytes 9437188
  170.0 56.5 %collective-permute-start.4 = (bf16[6,256,256]{2,1,0:T(8,128)(2,1)}, bf16[6,256,256]{2,1,0:T(8,128)(2,1)S(1)}, u32[]{:S(2)}, u32[]{:S(2)}) collective-permute-start(bf16[6,256,256]{2,1,0:T(8,128)(2,1)} %get-tuple-element.15), channel_id=1, source_target_pairs={{0,4},{4,8},{8,12},{12,16},{16,20},{20,24},{24,28},{1,5},{5,9},{9,... | collective-permute-start | bytes 2359304 | tf_op jit(solution)/shard_map/ppermute | solution.py:197
  174.6 52.0 %collective-permute-start.5 = (bf16[6,256,256]{2,1,0:T(8,128)(2,1)}, bf16[6,256,256]{2,1,0:T(8,128)(2,1)S(1)}, u32[]{:S(2)}, u32[]{:S(2)}) collective-permute-start(bf16[6,256,256]{2,1,0:T(8,128)(2,1)} %get-tuple-element.16), channel_id=1, source_target_pairs={{4,0},{8,4},{12,8},{16,12},{20,16},{24,20},{28,24},{5,1},{9,5},{13... | collective-permute-start | bytes 2359304 | tf_op jit(solution)/shard_map/ppermute | solution.py:197
  175.9 65.9 %collective-permute-start.6 = (bf16[6,256,256]{2,1,0:T(8,128)(2,1)}, bf16[6,256,256]{2,1,0:T(8,128)(2,1)S(1)}, u32[]{:S(2)}, u32[]{:S(2)}) collective-permute-start(bf16[6,256,256]{2,1,0:T(8,128)(2,1)} %get-tuple-element.18), channel_id=1, source_target_pairs={{0,4},{4,8},{8,12},{12,16},{16,20},{20,24},{24,28},{1,5},{5,9},{9,... | collective-permute-start | bytes 2359304 | tf_op jit(solution)/shard_map/ppermute | solution.py:197
  180.8 61.0 %collective-permute-start.7 = (bf16[6,256,256]{2,1,0:T(8,128)(2,1)}, bf16[6,256,256]{2,1,0:T(8,128)(2,1)S(1)}, u32[]{:S(2)}, u32[]{:S(2)}) collective-permute-start(bf16[6,256,256]{2,1,0:T(8,128)(2,1)} %get-tuple-element.19), channel_id=1, source_target_pairs={{4,0},{8,4},{12,8},{16,12},{20,16},{24,20},{28,24},{5,1},{9,5},{13... | collective-permute-start | bytes 2359304 | tf_op jit(solution)/shard_map/ppermute | solution.py:197
  182.3 44.3 %copy-start.6 = (f32[8,256,256]{2,1,0:T(8,128)S(1)}, f32[8,256,256]{2,1,0:T(8,128)}, u32[]{:S(2)}) copy-start(f32[8,256,256]{2,1,0:T(8,128)} %get-tuple-element.14) | copy-start | bytes 6291460
  187.0 54.8 %copy-start.5 = (f32[8,256,256]{2,1,0:T(8,128)S(1)}, f32[8,256,256]{2,1,0:T(8,128)}, u32[]{:S(2)}) copy-start(f32[8,256,256]{2,1,0:T(8,128)} %get-tuple-element.17) | copy-start | bytes 6291460
  226.5 16.6 %copy-start.14 = (bf16[8,256,256]{2,1,0:T(8,128)(2,1)S(1)}, bf16[8,256,256]{2,1,0:T(8,128)(2,1)}, u32[]{:S(2)}) copy-start(bf16[8,256,256]{2,1,0:T(8,128)(2,1)} %get-tuple-element.13) | copy-start | bytes 3145732
  226.9 16.2 %copy-start.12 = (bf16[2048,1024]{1,0:T(8,128)(2,1)S(1)}, bf16[2048,1024]{1,0:T(8,128)(2,1)}, u32[]{:S(2)}) copy-start(bf16[2048,1024]{1,0:T(8,128)(2,1)} %all-gather.3.cloned.1.call-done) | copy-start | bytes 12582916
  242.2 1.0 copy-start.9
  243.1 4.8 %copy-start.8 = (bf16[3,4,64,1024]{3,2,1,0:T(8,128)(2,1)S(1)}, bf16[3,4,64,1024]{3,2,1,0:T(8,128)(2,1)}, u32[]{:S(2)}) copy-start(bf16[3,4,64,1024]{3,2,1,0:T(8,128)(2,1)} %copy.12) | copy-start | bytes 4718596
  247.9 151.4 %reduce-scatter.5.cloned.1.call-start = ((), (), s32[]{:S(2)}) async-start(), calls=%async_computation.5 | async-start | bytes 5242880 | tf_op jit(solution)/shard_map/reduce_scatter | solution.py:252
  254.6 1.3 copy-start.4
  254.7 192.4 %reduce-scatter.3.cloned.1.call-start = ((), (), s32[]{:S(2)}) async-start(), calls=%async_computation.4 | async-start | bytes 5242880 | tf_op jit(solution)/shard_map/reduce_scatter | solution.py:245
  354.5 1.9 copy-start.10
  354.5 44.9 %copy-start.1 = (bf16[512,1024]{1,0:T(8,128)(2,1)S(1)}, bf16[512,1024]{1,0:T(8,128)(2,1)}, u32[]{:S(2)}) copy-start(bf16[512,1024]{1,0:T(8,128)(2,1)} %param.6) | copy-start | bytes 3145732
  354.5 44.9 %copy-start.11 = (f32[1024]{0:T(1024)S(1)}, f32[1024]{0:T(1024)}, u32[]{:S(2)}) copy-start(f32[1024]{0:T(1024)} %param.7) | copy-start | bytes 12292
Sparse Core Ops, SparseCore 0:
  11.5 37.1 all-gather.2
  50.3 34.4 all-gather.4
  248.1 104.5 all-reduce.7
  355.0 44.2 reduce-scatter.4
  402.5 44.5 reduce-scatter.2
where the time goes:
time: 454 us
  waiting for transfers between devices  320 us (70%)
  Pallas kernels  41.8 us (9%)
  matrix products  30.2 us (7%)
  starting transfers between devices  25.4 us (6%)
  other arithmetic  14.1 us (3%)
  between operations  14 us (3%)
  local copies, waits for them, and re-layouts  7.95 us (2%)
    psum x1, waiting for transfers between devices, on_device(): lax.psum(tn(grad_proj, normed_band).astype(jnp.bfloat16), 'lat')  93.5 us
    ppermute x8, waiting for transfers between devices, passed_along(): return lax.ppermute(x, axis, pairs)  91.4 us
    reduce_scatter x1, waiting for transfers between devices, on_device(): lax.psum_scatter(nn(flat(out), out_flat).astype(jnp.bfloat16), 'mp', scat...  43.1 us
    reduce_scatter x1, waiting for transfers between devices, on_device(): lax.psum_scatter(nn(grad_proj, split_weight).astype(jnp.bfloat16), 'mp',...  41.9 us
    pallas_call x1, Pallas kernels, attention(): pl.pallas_call(functools.partial(attention_kernel, heads), out_shape=(gri...  41.8 us
    all_gather x1, waiting for transfers between devices, on_device(): normed_band = lax.all_gather(normed, 'mp', axis=0, tiled=True)  34.6 us
    ppermute x8, starting transfers between devices, passed_along(): return lax.ppermute(x, axis, pairs)  25.2 us
    all_gather x1, waiting for transfers between devices, on_device(): band_upstream = lax.all_gather(upstream, 'mp', axis=0, tiled=True)  15 us
  transfers between devices with their start and end apart: 13, of which 9 were waited for; matrix products, arithmetic and copies ran while one was open for 9% of the time, Pallas kernels for 0%

commit v1 on v0

--- a/solution.py
+++ b/solution.py
@@ -186,20 +186,34 @@
     )(cells, q, go, *k_parts, *v_parts)
 
 
-from jax.sharding import PartitionSpec as P
+from jax.sharding import Mesh, PartitionSpec as P
 
 WIDTH = 1024
-
-
-def passed_along(x, axis, by):
-    length = lax.axis_size(axis)
+GROUP = ("y", "m", "c")
+
+
+def tn(a, b):
+    return lax.dot_general(a, b, (((0,), (0,)), ((), ())), preferred_element_type=jnp.float32)
+
+
+def to_bands(halves, step):
+    dm, dc = step
+    place = lambda y, m, c: (y * halves + m) * 2 + c
+    return [
+        (place(y, m, c), place((c + dc) % 2, (m + dm) % halves, y))
+        for y in range(2) for m in range(halves) for c in range(2)
+    ]
+
+
+def passed_along(x, by):
+    length = lax.axis_size("z") * 2
     pairs = [(i, i + by) for i in range(length) if 0 <= i + by < length]
-    return lax.ppermute(x, axis, pairs)
+    return lax.ppermute(x, ("z", "c"), pairs)
 
 
 def halo_parts(x):
-    before = passed_along(x[BAND_ROWS - HALO:], "lat", 1)
-    after = passed_along(x[:HALO], "lat", -1)
+    before = passed_along(x[BAND_ROWS - HALO:], 1)
+    after = passed_along(x[:HALO], -1)
     return before, x, after
 
 
@@ -207,34 +221,68 @@
     heads = qkv_weight.shape[0]
     feats = heads * HEAD_WIDTH
     band_tokens = BAND_ROWS * LONGITUDES
-    grad_scale = 4.0 / math.sqrt(band_tokens * lax.axis_size("lat"))
-    band_start = lax.axis_index("lat") * BAND_ROWS
+    chunk = tokens.shape[0]
+    halves = lax.axis_size("m")
+    y, m, c = (lax.axis_index(axis) for axis in GROUP)
+    steps = [(dm, dc) for dm in range(halves) for dc in range(2)]
+    arrives = [((m - dm) % halves) * 2 + (y - dc) % 2 for dm, dc in steps]
+    leads = [((m + dm) % halves) * 2 + (c + dc) % 2 for dm, dc in steps]
+    grad_scale = 4.0 / math.sqrt(band_tokens * lax.axis_size("z") * 2)
+    band_start = (lax.axis_index("z") * 2 + c) * BAND_ROWS
     cells = lax.dynamic_slice_in_dim(jnp.pad(row_cells, (HALO, HALO)), band_start, EXT_ROWS)
+
+    def send(x, step):
+        return lax.ppermute(x, GROUP, to_bands(halves, step))
+
+    def send_back(x, step):
+        return lax.ppermute(x, GROUP, [(b, a) for a, b in to_bands(halves, step)])
+
+    def in_order(parts):
+        whole = jnp.zeros((band_tokens,) + parts[0].shape[1:], parts[0].dtype)
+        for part, at in zip(parts, arrives):
+            whole = lax.dynamic_update_slice_in_dim(whole, part, at * chunk, 0)
+        return whole
+
+    def group_weight(weight):
+        pairs = [((y * halves + m) * 2 + y, (y * halves + m) * 2 + 1 - y) for y in range(2) for m in range(halves)]
+        return jnp.where(c == y, weight, lax.ppermute(weight, GROUP, pairs))
 
     features = tokens.astype(jnp.float32)
     inverse = lax.rsqrt(jnp.mean(features * features, axis=1, keepdims=True) + 1e-06)
     normed = (features * inverse * gain[None, :]).astype(jnp.bfloat16)
-    normed_band = lax.all_gather(normed, "mp", axis=0, tiled=True)
-    band_upstream = lax.all_gather(upstream, "mp", axis=0, tiled=True)
-
+    normed_band = in_order([send(normed, step) for step in steps])
+
+    out_full = lax.all_gather(out_weight.reshape(feats, WIDTH), ("m", "c"), axis=0, tiled=True)
+    grad_heads_own = nt(upstream, out_full).astype(jnp.bfloat16)
     split_weight = qkv_weight.reshape(heads, 3, HEAD_WIDTH, WIDTH).transpose(1, 0, 2, 3)
-    split_weight = split_weight.reshape(3 * feats, WIDTH)
-    out_flat = out_weight.reshape(feats, WIDTH)
+    split_weight = group_weight(split_weight.reshape(3 * feats, WIDTH))
     qkv = nt(normed_band, split_weight)
     q = (qkv[:, :feats].astype(jnp.bfloat16) * HEAD_WIDTH ** -0.5).astype(jnp.bfloat16)
     k = qkv[:, feats:2 * feats].astype(jnp.bfloat16)
     v = qkv[:, 2 * feats:].astype(jnp.bfloat16)
     grid = lambda x: x.reshape(BAND_ROWS, LONGITUDES, feats)
-    grad_heads = nt(band_upstream, out_flat).astype(jnp.bfloat16)
+    flat = lambda x: x.reshape(band_tokens, feats)
     k_parts, v_parts = halo_parts(grid(k)), halo_parts(grid(v))
+    grad_heads = in_order([
+        send(lax.dynamic_slice_in_dim(grad_heads_own, lead * feats, feats, 1), step)
+        for step, lead in zip(steps, leads)
+    ])
+    held, k_parts = lax.optimization_barrier((upstream, k_parts))
+    band_upstream = in_order([send(held, step) for step in steps])
+
     out, dq, dk, dv, dk_top, dv_top, dk_bot, dv_bot = attention(
         cells, grid(q), grid(grad_heads), k_parts, v_parts
     )
-    flat = lambda x: x.reshape(band_tokens, feats)
+    out = flat(out)
+
+    update = 0.0
+    for step, lead, arrive in zip(steps, leads, arrives):
+        part = send_back(lax.dynamic_slice_in_dim(out, arrive * chunk, chunk, 0), step)
+        update += nn(part, lax.dynamic_slice_in_dim(out_full, lead * feats, feats, 0))
 
     def joined(own, top, bot):
-        from_above = passed_along(top, "lat", -1).astype(jnp.float32)
-        from_below = passed_along(bot, "lat", 1).astype(jnp.float32)
+        from_above = passed_along(top, -1).astype(jnp.float32)
+        from_below = passed_along(bot, 1).astype(jnp.float32)
         own = own + jnp.pad(from_below, ((0, BAND_ROWS - HALO), (0, 0), (0, 0)))
         own = own + jnp.pad(from_above, ((BAND_ROWS - HALO, 0), (0, 0), (0, 0)))
         return flat(own.astype(jnp.bfloat16))
@@ -242,44 +290,39 @@
     dk, dv = joined(dk, dk_top, dk_bot), joined(dv, dv_top, dv_bot)
     grad_proj = jnp.concatenate([flat(dq), dk, dv], axis=1)
 
-    update = lax.psum_scatter(
-        nn(flat(out), out_flat).astype(jnp.bfloat16), "mp", scatter_dimension=0, tiled=True
-    )
-    tn = lambda a, b: lax.dot_general(a, b, (((0,), (0,)), ((), ())), preferred_element_type=jnp.float32)
-    grad_out = lax.psum(tn(flat(out), band_upstream).astype(jnp.bfloat16), "lat").astype(jnp.float32)
-    grad_qkv = lax.psum(tn(grad_proj, normed_band).astype(jnp.bfloat16), "lat").astype(jnp.float32)
-    grad_qkv = grad_qkv.reshape(3, heads, HEAD_WIDTH, WIDTH).transpose(1, 0, 2, 3)
-    grad_normed = lax.psum_scatter(
-        nn(grad_proj, split_weight).astype(jnp.bfloat16), "mp", scatter_dimension=0, tiled=True
-    ).astype(jnp.float32)
+    part = nn(grad_proj, split_weight).astype(jnp.bfloat16)
+    grad_normed = 0.0
+    for step, arrive in zip(steps, arrives):
+        grad_normed += send_back(
+            lax.dynamic_slice_in_dim(part, arrive * chunk, chunk, 0), step
+        ).astype(jnp.float32)
     centred = features * inverse
     scaled = gain[None, :] * grad_normed
     grad_input = inverse * (scaled - centred * jnp.mean(scaled * centred, axis=1, keepdims=True))
+
+    grads = jnp.concatenate([tn(grad_proj, normed_band), tn(out, band_upstream)], axis=0)
+    grads = lax.psum(grads.astype(jnp.bfloat16), ("z", "c"))
+    pairs = [
+        ((1 - y) * halves * 2 + m * 2 + 1 - y, y * halves * 2 + m * 2 + 1 - y)
+        for y in range(2) for m in range(halves)
+    ]
+    grads = jnp.where(c == y, grads, lax.ppermute(grads, GROUP, pairs)).astype(jnp.float32) * grad_scale
+    grad_qkv = grads[:3 * feats].reshape(3, heads, HEAD_WIDTH, WIDTH).transpose(1, 0, 2, 3)
     return (
-        update,
+        update.astype(jnp.bfloat16),
         grad_input.astype(jnp.bfloat16),
-        grad_qkv.reshape(heads, 3 * HEAD_WIDTH, WIDTH) * grad_scale,
-        (grad_out * grad_scale).reshape(heads, HEAD_WIDTH, WIDTH),
+        grad_qkv.reshape(heads, 3 * HEAD_WIDTH, WIDTH),
+        grads[3 * feats:].reshape(heads, HEAD_WIDTH, WIDTH),
     )
 
 
 def solution(mesh):
+    devices = mesh.devices.reshape(mesh.shape["lat"] // 2, 2, mesh.shape["mp"] // 2, 2)
+    tokens, weights = P(("z", "y", "m", "c"), None), P(("m", "c"), None, None)
     return jax.shard_map(
         on_device,
-        mesh=mesh,
-        in_specs=(
-            P(("lat", "mp"), None),
-            P(),
-            P("mp", None, None),
-            P("mp", None, None),
-            P(),
-            P(("lat", "mp"), None),
-        ),
-        out_specs=(
-            P(("lat", "mp"), None),
-            P(("lat", "mp"), None),
-            P("mp", None, None),
-            P("mp", None, None),
-        ),
+        mesh=Mesh(devices, ("z", "y", "m", "c")),
+        in_specs=(tokens, P(), weights, weights, P(), tokens),
+        out_specs=(tokens, tokens, weights, weights),
         check_vma=False,
     )

time: 454 us -> 317 us (0.70)
  waiting for transfers between devices: 320 us -> 118 us
  starting transfers between devices: 25.4 us -> 75.3 us
  local copies, waits for them, and re-layouts: 7.95 us -> 29.3 us
  matrix products: 30.2 us -> 22.4 us
    reduce_scatter x2 -> x0, waiting for transfers between devices: 85 us -> none  [the longest x1 43.1 us: on_device(): lax.psum_scatter(nn(flat(out), out_flat).astype(jnp.bfloat16), 'mp', scat...]
    ppermute x8 -> x30, starting transfers between devices: 25.2 us -> 75.2 us  [the longest x12 26.3 us: send(): return lax.ppermute(x, GROUP, to_bands(halves, step))]
    all_gather x2 -> x1, waiting for transfers between devices: 49.6 us -> 0.02 us  [on_device(): lax.all_gather(out_weight.reshape(feats, WIDTH), ('m', 'c'), axis=0, tile...]
    psum x1, waiting for transfers between devices: 93.5 us -> 46 us  [on_device(): grads = lax.psum(grads.astype(jnp.bfloat16), ('z', 'c'))]
    ppermute x8 -> x30, waiting for transfers between devices: 91.4 us -> 72.2 us  [the longest x12 59.8 us: send(): return lax.ppermute(x, GROUP, to_bands(halves, step))]
    dynamic_update_slice x0 -> x12, local copies, waits for them, and re-layouts: none -> 12.4 us  [in_order(): whole = lax.dynamic_update_slice_in_dim(whole, part, at * chunk, 0)]
    dot_general x2, matrix products: 9.48 us -> 4.79 us  [tn(): lax.dot_general(a, b, (((0,), (0,)), ((), ())), preferred_element_type=jn...]
    dot_general x2 -> x5, matrix products: 9.92 us -> 10.6 us  [nn(): lax.dot_general(a, b, (((1,), (0,)), ((), ())), preferred_element_type=jn...]
  transfers between devices with their start and end apart: 13 -> 32, of which waited for: 9 -> 8; matrix products, arithmetic and copies ran while one was open for 9% -> 15% of each run, Pallas kernels for 0% -> 13%
where the time goes in v1:
time: 317 us; the launch traced here: 315 us
  waiting for transfers between devices  118 us (37%)
  starting transfers between devices  75.3 us (24%)
  Pallas kernels  40.9 us (13%)
  local copies, waits for them, and re-layouts  29.3 us (9%)
  matrix products  22.4 us (7%)
  between operations  14.7 us (5%)
  other arithmetic  14.6 us (5%)
    ppermute x12, waiting for transfers between devices, send(): return lax.ppermute(x, GROUP, to_bands(halves, step))  59.8 us
    psum x1, waiting for transfers between devices, on_device(): grads = lax.psum(grads.astype(jnp.bfloat16), ('z', 'c'))  46 us
    pallas_call x1, Pallas kernels, attention(): pl.pallas_call(functools.partial(attention_kernel, heads), out_shape=(gri...  40.9 us
    ppermute x12, starting transfers between devices, send(): return lax.ppermute(x, GROUP, to_bands(halves, step))  26.3 us
    ppermute x8, starting transfers between devices, passed_along(): return lax.ppermute(x, ('z', 'c'), pairs)  22.5 us
    ppermute x8, starting transfers between devices, send_back(): return lax.ppermute(x, GROUP, [(b, a) for a, b in to_bands(halves, step)])  20.2 us
    dynamic_update_slice x12, local copies, waits for them, and re-layouts, in_order(): whole = lax.dynamic_update_slice_in_dim(whole, part, at * chunk, 0)  12.4 us
    ppermute x1, waiting for transfers between devices, on_device(): lax.ppermute(grads, GROUP, pairs)  12 us
  transfers between devices with their start and end apart: 32, of which 8 were waited for; matrix products, arithmetic and copies ran while one was open for 15% of the time, Pallas kernels for 13%

profile of v1, /device:TPU:0, one launch (start us, length us, event | category | flops | bytes accessed | tf_op | source)
XLA Modules:
  0.0 315.4 jit_solution(17598093976826250443)
XLA Ops:
  7.2 1.6 fusion.8
  8.8 2.5 fusion.3
  11.4 9.5 %collective-permute-start = (bf16[512,1024]{1,0:T(8,128)(2,1)}, bf16[512,1024]{1,0:T(8,128)(2,1)}, u32[]{:S(2)}, u32[]{:S(2)}) collective-permute-start(bf16[512,1024]{1,0:T(8,128)(2,1)} %fusion.3), channel_id=1, source_target_pairs={{0,0},{1,4},{2,2},{3,6},{4,1},{5,5},{6,3},{7,7},{8,8},{9,12},{10,1... | collective-permute-start | bytes 3145736 | tf_op jit(solution)/shard_map/ppermute | solution.py:235
  21.0 2.4 collective-permute-start.4
  23.5 3.0 collective-permute-start.2
  27.9 1.3 constant_dynamic-update-slice_fusion.11
  29.2 16.4 %collective-permute-done.1 = bf16[512,1024]{1,0:T(8,128)(2,1)S(1)} collective-permute-done((bf16[512,1024]{1,0:T(8,128)(2,1)}, bf16[512,1024]{1,0:T(8,128)(2,1)S(1)}, u32[]{:S(2)}, u32[]{:S(2)}) %collective-permute-start.1) | collective-permute-done | bytes 1048608 | tf_op jit(solution)/shard_map/ppermute | solution.py:235
  45.8 15.6 %collective-permute-done.2 = bf16[512,1024]{1,0:T(8,128)(2,1)} collective-permute-done((bf16[512,1024]{1,0:T(8,128)(2,1)}, bf16[512,1024]{1,0:T(8,128)(2,1)}, u32[]{:S(2)}, u32[]{:S(2)}) %collective-permute-start.2) | collective-permute-done | bytes 1048608 | tf_op jit(solution)/shard_map/ppermute | solution.py:235
  62.7 21.8 %collective-permute-done.3 = bf16[512,1024]{1,0:T(8,128)(2,1)} collective-permute-done((bf16[512,1024]{1,0:T(8,128)(2,1)}, bf16[512,1024]{1,0:T(8,128)(2,1)}, u32[]{:S(2)}, u32[]{:S(2)}) %collective-permute-start.3) | collective-permute-done | bytes 1048608 | tf_op jit(solution)/shard_map/ppermute | solution.py:235
  85.9 3.8 %convolution_convert_fusion.1 = bf16[2048,768]{1,0:T(8,128)(2,1)S(1)} fusion(bf16[2048,1024]{1,0:T(8,128)(2,1)S(1)} %constant_dynamic-update-slice_fusion.8, bf16[768,1024]{1,0:T(8,128)(2,1)S(1)} %bitcast.36, bf16[768,1024]{1,0:T(8,128)(2,1)} %collective-permute-done.4, pred[]{:T(512)S(6)} %eq.21), kind=kOutput, calls=%fused_computation.2 | convolution fusion | flops 3223584768 | bytes 10485761 | tf_op jit(solution)/shard_map/dot_general | solution.py:28
  89.7 1.7 fusion.25
  92.7 5.8 %collective-permute-start.9 = (bf16[6,256,256]{2,1,0:T(8,128)(2,1)}, bf16[6,256,256]{2,1,0:T(8,128)(2,1)}, u32[]{:S(2)}, u32[]{:S(2)}) collective-permute-start(bf16[6,256,256]{2,1,0:T(8,128)(2,1)} %bitcast.50), channel_id=1, source_target_pairs={{0,1},{1,8},{8,9},{9,16},{16,17},{17,24},{24,25},{2,3},{3,10},{10,... | collective-permute-start | bytes 2359304 | tf_op jit(solution)/shard_map/ppermute | solution.py:211
  98.5 3.7 %collective-permute-start.11 = (bf16[6,256,256]{2,1,0:T(8,128)(2,1)}, bf16[6,256,256]{2,1,0:T(8,128)(2,1)}, u32[]{:S(2)}, u32[]{:S(2)}) collective-permute-start(bf16[6,256,256]{2,1,0:T(8,128)(2,1)} %bitcast.49), channel_id=1, source_target_pairs={{0,1},{1,8},{8,9},{9,16},{16,17},{17,24},{24,25},{2,3},{3,10},{10,... | collective-permute-start | bytes 2359304 | tf_op jit(solution)/shard_map/ppermute | solution.py:211
  103.5 3.2 %convolution_convert_fusion.3 = bf16[512,1024]{1,0:T(8,128)(2,1)S(1)} fusion(bf16[512,1024]{1,0:T(8,128)(2,1)} %param.11, bf16[1024,1024]{1,0:T(8,128)(2,1)} %all-gather.2.cloned.1.call-done), kind=kOutput, calls=%fused_computation.22 | convolution fusion | flops 1074266112 | bytes 4194304 | tf_op jit(solution)/shard_map/dot_general | solution.py:28
  108.3 4.0 %collective-permute-start.6 = (bf16[512,256]{1,0:T(8,128)(2,1)S(1)}, bf16[512,256]{1,0:T(8,128)(2,1)S(1)}, u32[]{:S(2)}, u32[]{:S(2)}) collective-permute-start(bf16[512,256]{1,0:T(8,128)(2,1)S(1)} %get-tuple-element.45), channel_id=1, source_target_pairs={{0,4},{1,0},{2,6},{3,2},{4,5},{5,1},{6,7},{7,3},{8,12},{9,8},{10,1... | collective-permute-start | bytes 786440 | tf_op jit(solution)/shard_map/ppermute | solution.py:235
  112.3 1.7 fusion.26
  114.0 1.9 collective-permute-start.25
  116.6 3.8 %collective-permute-start.8 = (bf16[512,256]{1,0:T(8,128)(2,1)S(1)}, bf16[512,256]{1,0:T(8,128)(2,1)}, u32[]{:S(2)}, u32[]{:S(2)}) collective-permute-start(bf16[512,256]{1,0:T(8,128)(2,1)S(1)} %get-tuple-element.43), channel_id=1, source_target_pairs={{0,6},{1,2},{2,4},{3,0},{4,7},{5,3},{6,5},{7,1},{8,14},{9,10},{10,... | collective-permute-start | bytes 786440 | tf_op jit(solution)/shard_map/ppermute | solution.py:235
  122.1 3.3 %collective-permute-done.7 = bf16[512,256]{1,0:T(8,128)(2,1)} collective-permute-done((bf16[512,256]{1,0:T(8,128)(2,1)}, bf16[512,256]{1,0:T(8,128)(2,1)}, u32[]{:S(2)}, u32[]{:S(2)}) %collective-permute-start.7) | collective-permute-done | bytes 262176 | tf_op jit(solution)/shard_map/ppermute | solution.py:235
  126.5 1.7 constant_dynamic-update-slice_fusion.7
  128.1 2.7 collective-permute-done.8
  130.8 1.4 collective-permute-start.28
  132.2 1.7 constant_dynamic-update-slice_fusion.6
  133.9 1.7 constant_dynamic-update-slice_fusion.5
  135.6 1.7 constant_dynamic-update-slice_fusion.4
  137.3 40.9 %shard_map.93 = (bf16[8,256,256]{2,1,0:T(8,128)(2,1)}, bf16[8,256,256]{2,1,0:T(8,128)(2,1)}, f32[8,256,256]{2,1,0:T(8,128)}, f32[8,256,256]{2,1,0:T(8,128)}, bf1...) custom-call(s32[20]{0:T(128)} %pad_dynamic-slice_fusion.cells, ...), custom_call_target="tpu_custom_call" | custom-call | flops 3221225472 | bytes 20971520 | tf_op jit(solution)/shard_map/pallas_call | solution.py:163
  178.2 2.1 collective-permute-start.17
  183.4 5.5 %collective-permute-start.19 = (bf16[6,256,256]{2,1,0:T(8,128)(2,1)S(1)}, bf16[6,256,256]{2,1,0:T(8,128)(2,1)S(1)}, u32[]{:S(2)}, u32[]{:S(2)}) collective-permute-start(bf16[6,256,256]{2,1,0:T(8,128)(2,1)S(1)} %copy-done.22), channel_id=1, source_target_pairs={{0,1},{1,8},{8,9},{9,16},{16,17},{17,24},{24,25},{2,3},{3,10},{10,... | collective-permute-start | bytes 2359304 | tf_op jit(solution)/shard_map/ppermute | solution.py:211
  189.0 1.6 collective-permute-start.20
  196.1 2.2 copy-done.2
  198.3 3.5 %convolution_convert_fusion.2 = bf16[768,1024]{1,0:T(8,128)(2,1)S(1)} fusion(bf16[2048,1024]{1,0:T(8,128)(2,1)S(1)} %copy-done.2, bf16[2048,256]{1,0:T(8,128)(2,1)S(1)} %bitcast.46, bf16[2048,256]{1,0:T(8,128)(2,1)S(1)} %bitcast.44, bf16[2048,256]{1,0:T(8,128)(2,1)S(1)} %bitcast.53), kind=kOutput, calls=%fused_computation.20 | convolution fusion | flops 3231449088 | bytes 8912896 | tf_op jit(solution)/shard_map/dot_general | solution.py:196
  201.8 1.5 pad_maximum_fusion.1
  203.5 9.6 %collective-permute-start.14 = (bf16[512,256]{1,0:T(8,128)(2,1)S(1)}, bf16[512,256]{1,0:T(8,128)(2,1)S(1)}, u32[]{:S(2)}, u32[]{:S(2)}) collective-permute-start(bf16[512,256]{1,0:T(8,128)(2,1)S(1)} %get-tuple-element.41), channel_id=1, source_target_pairs={{4,0},{0,1},{6,2},{2,3},{5,4},{1,5},{7,6},{3,7},{12,8},{8,9},{14,1... | collective-permute-start | bytes 786440 | tf_op jit(solution)/shard_map/ppermute | solution.py:238
  213.7 1.7 collective-permute-start.15
  215.3 3.0 collective-permute-start.16
  218.4 4.7 %convolution_convert_fusion = bf16[2048,1024]{1,0:T(8,128)(2,1)S(1)} fusion(bf16[2048,256]{1,0:T(8,128)(2,1)S(1)} %bitcast.47, bf16[2048,256]{1,0:T(8,128)(2,1)S(1)} %bitcast.45, bf16[2048,256]{1,0:T(8,128)(2,1)} %bitcast.52, bf16[768,1024]{1,0:T(8,128)(2,1)S(1)} %bitcast.37, bf16[768,1024]{1,0:T(8,128)(2,1)} %collective-permute-done.4, pred[]{:T(512)S(6)} %eq.21), kind=kOutput, calls=%fused_computation.1 | convolution fusion | flops 3233546240 | bytes 10485761 | tf_op jit(solution)/shard_map/dot_general | solution.py:24
  223.1 2.1 constant_dynamic-slice_fusion.3
  225.2 1.9 collective-permute-start.21
  229.4 1.8 collective-permute-start.24
  231.2 46.0 %all-reduce.7.cloned.1.call-done = bf16[1024,1024]{1,0:T(8,128)(2,1)} async-done(((bf16[1024,1024]{1,0:T(8,128)(2,1)}), bf16[1024,1024]{1,0:T(8,128)(2,1)}) %all-reduce.7.cloned.1.call-update) | async-done | bytes 2097168 | tf_op jit(solution)/shard_map/psum | solution.py:304
  277.1 3.8 %collective-permute-start.29 = (bf16[1024,1024]{1,0:T(8,128)(2,1)}, bf16[1024,1024]{1,0:T(8,128)(2,1)S(1)}, u32[]{:S(2)}, u32[]{:S(2)}) collective-permute-start(bf16[1024,1024]{1,0:T(8,128)(2,1)} %all-reduce.7.cloned.1.call-done), channel_id=1, source_target_pairs={{5,1},{7,3},{0,4},{2,6},{13,9},{15,11},{8,12},{10,14},{21,17},{23,... | collective-permute-start | bytes 6291464 | tf_op jit(solution)/shard_map/ppermute | solution.py:309
  281.0 1.5 fusion.15
  283.0 1.4 fusion.13
  284.4 2.6 add_convert_fusion.2
  287.0 2.2 fusion.4
  289.2 3.3 %fusion.7 = bf16[512,1024]{1,0:T(8,128)(2,1)} fusion(bf16[512,1024]{1,0:T(8,128)(2,1)S(1)} %copy-done, f32[512]{0:T(512)S(1)} %broadcast_multiply_fusion, f32[512]{0:T(512)S(1)} %add_rsqrt_fusion, bf16[512,1024]{1,0:T(8,128)(2,1)} %collective-permute-done.24, bf16[512,1024]{1,0:T(8,128)(2,1)S(1)} %collective-permute-done.23, ...), kind=kLoop, calls=%fused_computation.13 | loop fusion | flops 7340032 | bytes 6299648 | tf_op jit(solution)/shard_map/convert_element_type | solution.py:313
  292.5 12.0 %collective-permute-done.29 = bf16[1024,1024]{1,0:T(8,128)(2,1)S(1)} collective-permute-done((bf16[1024,1024]{1,0:T(8,128)(2,1)}, bf16[1024,1024]{1,0:T(8,128)(2,1)S(1)}, u32[]{:S(2)}, u32[]{:S(2)}) %collective-permute-start.29) | collective-permute-done | bytes 2097184 | tf_op jit(solution)/shard_map/ppermute | solution.py:309
  306.7 1.9 copy.13
  (113 shorter events, 26.3 us)
Async XLA Ops:
  7.2 13.7 %copy-start.7 = (bf16[4,192,1024]{2,1,0:T(8,128)(2,1)S(1)}, bf16[4,192,1024]{2,1,0:T(8,128)(2,1)}, u32[]{:S(2)}) copy-start(bf16[4,192,1024]{2,1,0:T(8,128)(2,1)} %param.8) | copy-start | bytes 4718596
  7.2 96.3 %all-gather.2.cloned.1.call-start = ((), (), s32[]{:S(2)}) async-start(), calls=%async_computation | async-start | bytes 2621440 | tf_op jit(solution)/shard_map/all_gather | solution.py:255
  11.4 16.0 %collective-permute-start = (bf16[512,1024]{1,0:T(8,128)(2,1)}, bf16[512,1024]{1,0:T(8,128)(2,1)}, u32[]{:S(2)}, u32[]{:S(2)}) collective-permute-start(bf16[512,1024]{1,0:T(8,128)(2,1)} %fusion.3), channel_id=1, source_target_pairs={{0,0},{1,4},{2,2},{3,6},{4,1},{5,5},{6,3},{7,7},{8,8},{9,12},{10,1... | collective-permute-start | bytes 3145736 | tf_op jit(solution)/shard_map/ppermute | solution.py:235
  21.0 6.9 %copy-start.8 = (bf16[3,4,64,1024]{3,2,1,0:T(8,128)(2,1)}, bf16[3,4,64,1024]{3,2,1,0:T(8,128)(2,1)S(1)}, u32[]{:S(2)}) copy-start(bf16[3,4,64,1024]{3,2,1,0:T(8,128)(2,1)S(1)} %copy.12) | copy-start | bytes 4718596
  21.0 64.9 %collective-permute-start.4 = (bf16[768,1024]{1,0:T(8,128)(2,1)S(1)}, bf16[768,1024]{1,0:T(8,128)(2,1)}, u32[]{:S(2)}, u32[]{:S(2)}) collective-permute-start(bf16[768,1024]{1,0:T(8,128)(2,1)S(1)} %bitcast.35), channel_id=1, source_target_pairs={{0,1},{2,3},{5,4},{7,6},{8,9},{10,11},{13,12},{15,14},{16,17},{18,... | collective-permute-start | bytes 4718600 | tf_op jit(solution)/shard_map/ppermute | solution.py:248
  23.4 22.3 %collective-permute-start.1 = (bf16[512,1024]{1,0:T(8,128)(2,1)}, bf16[512,1024]{1,0:T(8,128)(2,1)S(1)}, u32[]{:S(2)}, u32[]{:S(2)}) collective-permute-start(bf16[512,1024]{1,0:T(8,128)(2,1)} %fusion.3), channel_id=1, source_target_pairs={{0,4},{1,0},{2,6},{3,2},{4,5},{5,1},{6,7},{7,3},{8,12},{9,8},{10,1... | collective-permute-start | bytes 3145736 | tf_op jit(solution)/shard_map/ppermute | solution.py:235
  23.4 253.7 %all-reduce.7.cloned.1.call-start = ((), (), s32[]{:S(2)}) async-start(), calls=%async_computation.1 | async-start | bytes 4194304 | tf_op jit(solution)/shard_map/psum | solution.py:304
  23.5 37.9 %collective-permute-start.2 = (bf16[512,1024]{1,0:T(8,128)(2,1)}, bf16[512,1024]{1,0:T(8,128)(2,1)}, u32[]{:S(2)}, u32[]{:S(2)}) collective-permute-start(bf16[512,1024]{1,0:T(8,128)(2,1)} %fusion.3), channel_id=1, source_target_pairs={{0,2},{1,6},{2,0},{3,4},{4,3},{5,7},{6,1},{7,5},{8,10},{9,14},{10,... | collective-permute-start | bytes 3145736 | tf_op jit(solution)/shard_map/ppermute | solution.py:235
  26.5 58.0 %collective-permute-start.3 = (bf16[512,1024]{1,0:T(8,128)(2,1)}, bf16[512,1024]{1,0:T(8,128)(2,1)}, u32[]{:S(2)}, u32[]{:S(2)}) collective-permute-start(bf16[512,1024]{1,0:T(8,128)(2,1)} %fusion.3), channel_id=1, source_target_pairs={{0,6},{1,2},{2,4},{3,0},{4,7},{5,3},{6,5},{7,1},{8,14},{9,10},{10,... | collective-permute-start | bytes 3145736 | tf_op jit(solution)/shard_map/ppermute | solution.py:235
  45.8 40.1 %copy-start.9 = (bf16[3,4,64,1024]{3,2,1,0:T(8,128)(2,1)S(1)}, bf16[3,4,64,1024]{3,2,1,0:T(8,128)(2,1)}, u32[]{:S(2)}) copy-start(bf16[3,4,64,1024]{3,2,1,0:T(8,128)(2,1)} %copy-done.8) | copy-start | bytes 4718596
  85.8 3.8 %copy-start.1 = (bf16[2048,1024]{1,0:T(8,128)(2,1)}, bf16[2048,1024]{1,0:T(8,128)(2,1)S(1)}, u32[]{:S(2)}) copy-start(bf16[2048,1024]{1,0:T(8,128)(2,1)S(1)} %constant_dynamic-update-slice_fusion.8) | copy-start | bytes 12582916
  91.4 16.9 %collective-permute-start.10 = (bf16[6,256,256]{2,1,0:T(8,128)(2,1)}, bf16[6,256,256]{2,1,0:T(8,128)(2,1)}, u32[]{:S(2)}, u32[]{:S(2)}) collective-permute-start(bf16[6,256,256]{2,1,0:T(8,128)(2,1)} %bitcast.8), channel_id=1, source_target_pairs={{1,0},{8,1},{9,8},{16,9},{17,16},{24,17},{25,24},{3,2},{10,3},{11,... | collective-permute-start | bytes 2359304 | tf_op jit(solution)/shard_map/ppermute | solution.py:211
  92.7 21.3 %collective-permute-start.9 = (bf16[6,256,256]{2,1,0:T(8,128)(2,1)}, bf16[6,256,256]{2,1,0:T(8,128)(2,1)}, u32[]{:S(2)}, u32[]{:S(2)}) collective-permute-start(bf16[6,256,256]{2,1,0:T(8,128)(2,1)} %bitcast.50), channel_id=1, source_target_pairs={{0,1},{1,8},{8,9},{9,16},{16,17},{17,24},{24,25},{2,3},{3,10},{10,... | collective-permute-start | bytes 2359304 | tf_op jit(solution)/shard_map/ppermute | solution.py:211
  98.5 17.4 %collective-permute-start.11 = (bf16[6,256,256]{2,1,0:T(8,128)(2,1)}, bf16[6,256,256]{2,1,0:T(8,128)(2,1)}, u32[]{:S(2)}, u32[]{:S(2)}) collective-permute-start(bf16[6,256,256]{2,1,0:T(8,128)(2,1)} %bitcast.49), channel_id=1, source_target_pairs={{0,1},{1,8},{8,9},{9,16},{16,17},{17,24},{24,25},{2,3},{3,10},{10,... | collective-permute-start | bytes 2359304 | tf_op jit(solution)/shard_map/ppermute | solution.py:211
  102.2 35.1 %collective-permute-start.12 = (bf16[6,256,256]{2,1,0:T(8,128)(2,1)}, bf16[6,256,256]{2,1,0:T(8,128)(2,1)}, u32[]{:S(2)}, u32[]{:S(2)}) collective-permute-start(bf16[6,256,256]{2,1,0:T(8,128)(2,1)} %bitcast.48), channel_id=1, source_target_pairs={{1,0},{8,1},{9,8},{16,9},{17,16},{24,17},{25,24},{3,2},{10,3},{11,... | collective-permute-start | bytes 2359304 | tf_op jit(solution)/shard_map/ppermute | solution.py:211
  107.6 9.0 %collective-permute-start.5 = (bf16[512,256]{1,0:T(8,128)(2,1)S(1)}, bf16[512,256]{1,0:T(8,128)(2,1)S(1)}, u32[]{:S(2)}, u32[]{:S(2)}) collective-permute-start(bf16[512,256]{1,0:T(8,128)(2,1)S(1)} %get-tuple-element.46), channel_id=1, source_target_pairs={{0,0},{1,4},{2,2},{3,6},{4,1},{5,5},{6,3},{7,7},{8,8},{9,12},{10,1... | collective-permute-start | bytes 786440 | tf_op jit(solution)/shard_map/ppermute | solution.py:235
  108.3 13.3 %copy-start.23 = (s32[64]{0:T(128)S(1)}, s32[64]{0:T(128)}, u32[]{:S(2)}) copy-start(s32[64]{0:T(128)} %param.10) | copy-start | bytes 772
  108.3 12.0 %collective-permute-start.6 = (bf16[512,256]{1,0:T(8,128)(2,1)S(1)}, bf16[512,256]{1,0:T(8,128)(2,1)S(1)}, u32[]{:S(2)}, u32[]{:S(2)}) collective-permute-start(bf16[512,256]{1,0:T(8,128)(2,1)S(1)} %get-tuple-element.45), channel_id=1, source_target_pairs={{0,4},{1,0},{2,6},{3,2},{4,5},{5,1},{6,7},{7,3},{8,12},{9,8},{10,1... | collective-permute-start | bytes 786440 | tf_op jit(solution)/shard_map/ppermute | solution.py:235
  114.0 66.4 %collective-permute-start.25 = (bf16[512,1024]{1,0:T(8,128)(2,1)}, bf16[512,1024]{1,0:T(8,128)(2,1)S(1)}, u32[]{:S(2)}, u32[]{:S(2)}) collective-permute-start(bf16[512,1024]{1,0:T(8,128)(2,1)} %param.11), channel_id=1, source_target_pairs={{0,0},{1,4},{2,2},{3,6},{4,1},{5,5},{6,3},{7,7},{8,8},{9,12},{10,1... | collective-permute-start | bytes 3145736 | tf_op jit(solution)/shard_map/ppermute | solution.py:235
  115.9 9.5 %collective-permute-start.7 = (bf16[512,256]{1,0:T(8,128)(2,1)}, bf16[512,256]{1,0:T(8,128)(2,1)}, u32[]{:S(2)}, u32[]{:S(2)}) collective-permute-start(bf16[512,256]{1,0:T(8,128)(2,1)} %get-tuple-element.44), channel_id=1, source_target_pairs={{0,2},{1,6},{2,0},{3,4},{4,3},{5,7},{6,1},{7,5},{8,10},{9,14},{10,... | collective-permute-start | bytes 786440 | tf_op jit(solution)/shard_map/ppermute | solution.py:235
  116.6 3.8 %copy-start.19 = (bf16[512,256]{1,0:T(8,128)(2,1)}, bf16[512,256]{1,0:T(8,128)(2,1)S(1)}, u32[]{:S(2)}) copy-start(bf16[512,256]{1,0:T(8,128)(2,1)S(1)} %collective-permute-done.5) | copy-start | bytes 786436
  116.6 14.3 %collective-permute-start.8 = (bf16[512,256]{1,0:T(8,128)(2,1)S(1)}, bf16[512,256]{1,0:T(8,128)(2,1)}, u32[]{:S(2)}, u32[]{:S(2)}) collective-permute-start(bf16[512,256]{1,0:T(8,128)(2,1)S(1)} %get-tuple-element.43), channel_id=1, source_target_pairs={{0,6},{1,2},{2,4},{3,0},{4,7},{5,3},{6,5},{7,1},{8,14},{9,10},{10,... | collective-permute-start | bytes 786440 | tf_op jit(solution)/shard_map/ppermute | solution.py:235
  121.0 61.3 %collective-permute-start.26 = (bf16[512,1024]{1,0:T(8,128)(2,1)}, bf16[512,1024]{1,0:T(8,128)(2,1)S(1)}, u32[]{:S(2)}, u32[]{:S(2)}) collective-permute-start(bf16[512,1024]{1,0:T(8,128)(2,1)} %param.11), channel_id=1, source_target_pairs={{0,4},{1,0},{2,6},{3,2},{4,5},{5,1},{6,7},{7,3},{8,12},{9,8},{10,1... | collective-permute-start | bytes 3145736 | tf_op jit(solution)/shard_map/ppermute | solution.py:235
  125.4 63.6 %collective-permute-start.27 = (bf16[512,1024]{1,0:T(8,128)(2,1)}, bf16[512,1024]{1,0:T(8,128)(2,1)S(1)}, u32[]{:S(2)}, u32[]{:S(2)}) collective-permute-start(bf16[512,1024]{1,0:T(8,128)(2,1)} %param.11), channel_id=1, source_target_pairs={{0,2},{1,6},{2,0},{3,4},{4,3},{5,7},{6,1},{7,5},{8,10},{9,14},{10,... | collective-permute-start | bytes 3145736 | tf_op jit(solution)/shard_map/ppermute | solution.py:235
  130.8 59.9 %collective-permute-start.28 = (bf16[512,1024]{1,0:T(8,128)(2,1)}, bf16[512,1024]{1,0:T(8,128)(2,1)}, u32[]{:S(2)}, u32[]{:S(2)}) collective-permute-start(bf16[512,1024]{1,0:T(8,128)(2,1)} %param.11), channel_id=1, source_target_pairs={{0,6},{1,2},{2,4},{3,0},{4,7},{5,3},{6,5},{7,1},{8,14},{9,10},{10,... | collective-permute-start | bytes 3145736 | tf_op jit(solution)/shard_map/ppermute | solution.py:235
  178.2 15.1 %collective-permute-start.17 = (bf16[6,256,256]{2,1,0:T(8,128)(2,1)}, bf16[6,256,256]{2,1,0:T(8,128)(2,1)S(1)}, u32[]{:S(2)}, u32[]{:S(2)}) collective-permute-start(bf16[6,256,256]{2,1,0:T(8,128)(2,1)} %get-tuple-element.22), channel_id=1, source_target_pairs={{0,1},{1,8},{8,9},{9,16},{16,17},{17,24},{24,25},{2,3},{3,10},{10,... | collective-permute-start | bytes 2359304 | tf_op jit(solution)/shard_map/ppermute | solution.py:211
  180.4 13.0 %collective-permute-start.18 = (bf16[6,256,256]{2,1,0:T(8,128)(2,1)}, bf16[6,256,256]{2,1,0:T(8,128)(2,1)S(1)}, u32[]{:S(2)}, u32[]{:S(2)}) collective-permute-start(bf16[6,256,256]{2,1,0:T(8,128)(2,1)} %get-tuple-element.23), channel_id=1, source_target_pairs={{1,0},{8,1},{9,8},{16,9},{17,16},{24,17},{25,24},{3,2},{10,3},{11,... | collective-permute-start | bytes 2359304 | tf_op jit(solution)/shard_map/ppermute | solution.py:211
  182.2 6.8 %copy-start.21 = (bf16[6,256,256]{2,1,0:T(8,128)(2,1)S(1)}, bf16[6,256,256]{2,1,0:T(8,128)(2,1)}, u32[]{:S(2)}) copy-start(bf16[6,256,256]{2,1,0:T(8,128)(2,1)} %get-tuple-element.26) | copy-start | bytes 2359300
  183.4 10.7 %collective-permute-start.19 = (bf16[6,256,256]{2,1,0:T(8,128)(2,1)S(1)}, bf16[6,256,256]{2,1,0:T(8,128)(2,1)S(1)}, u32[]{:S(2)}, u32[]{:S(2)}) collective-permute-start(bf16[6,256,256]{2,1,0:T(8,128)(2,1)S(1)} %copy-done.22), channel_id=1, source_target_pairs={{0,1},{1,8},{8,9},{9,16},{16,17},{17,24},{24,25},{2,3},{3,10},{10,... | collective-permute-start | bytes 2359304 | tf_op jit(solution)/shard_map/ppermute | solution.py:211
  189.0 3.1 copy-start.11
  189.0 5.5 %collective-permute-start.20 = (bf16[6,256,256]{2,1,0:T(8,128)(2,1)S(1)}, bf16[6,256,256]{2,1,0:T(8,128)(2,1)S(1)}, u32[]{:S(2)}, u32[]{:S(2)}) collective-permute-start(bf16[6,256,256]{2,1,0:T(8,128)(2,1)S(1)} %copy-done.21), channel_id=1, source_target_pairs={{1,0},{8,1},{9,8},{16,9},{17,16},{24,17},{25,24},{3,2},{10,3},{11,... | collective-permute-start | bytes 2359304 | tf_op jit(solution)/shard_map/ppermute | solution.py:211
  196.1 5.7 %copy-start.14 = (bf16[8,256,256]{2,1,0:T(8,128)(2,1)}, bf16[8,256,256]{2,1,0:T(8,128)(2,1)S(1)}, u32[]{:S(2)}) copy-start(bf16[8,256,256]{2,1,0:T(8,128)(2,1)S(1)} %add_convert_fusion) | copy-start | bytes 3145732
  203.3 15.1 %copy-start.10 = (bf16[3,4,64,1024]{3,2,1,0:T(8,128)(2,1)S(1)}, bf16[3,4,64,1024]{3,2,1,0:T(8,128)(2,1)}, u32[]{:S(2)}) copy-start(bf16[3,4,64,1024]{3,2,1,0:T(8,128)(2,1)} %copy-done.8) | copy-start | bytes 4718596
  203.3 15.1 %copy-start.13 = (bf16[8,256,256]{2,1,0:T(8,128)(2,1)S(1)}, bf16[8,256,256]{2,1,0:T(8,128)(2,1)}, u32[]{:S(2)}) copy-start(bf16[8,256,256]{2,1,0:T(8,128)(2,1)} %copy-done.12) | copy-start | bytes 3145732
  203.4 15.1 %copy-start.15 = (bf16[8,256,256]{2,1,0:T(8,128)(2,1)S(1)}, bf16[8,256,256]{2,1,0:T(8,128)(2,1)}, u32[]{:S(2)}) copy-start(bf16[8,256,256]{2,1,0:T(8,128)(2,1)} %copy-done.14) | copy-start | bytes 3145732
  203.5 23.7 %collective-permute-start.14 = (bf16[512,256]{1,0:T(8,128)(2,1)S(1)}, bf16[512,256]{1,0:T(8,128)(2,1)S(1)}, u32[]{:S(2)}, u32[]{:S(2)}) collective-permute-start(bf16[512,256]{1,0:T(8,128)(2,1)S(1)} %get-tuple-element.41), channel_id=1, source_target_pairs={{4,0},{0,1},{6,2},{2,3},{5,4},{1,5},{7,6},{3,7},{12,8},{8,9},{14,1... | collective-permute-start | bytes 786440 | tf_op jit(solution)/shard_map/ppermute | solution.py:238
  213.0 14.8 %collective-permute-start.13 = (bf16[512,256]{1,0:T(8,128)(2,1)S(1)}, bf16[512,256]{1,0:T(8,128)(2,1)S(1)}, u32[]{:S(2)}, u32[]{:S(2)}) collective-permute-start(bf16[512,256]{1,0:T(8,128)(2,1)S(1)} %get-tuple-element.42), channel_id=1, source_target_pairs={{0,0},{4,1},{2,2},{6,3},{1,4},{5,5},{3,6},{7,7},{8,8},{12,9},{10,1... | collective-permute-start | bytes 786440 | tf_op jit(solution)/shard_map/ppermute | solution.py:238
  213.7 15.7 %collective-permute-start.15 = (bf16[512,256]{1,0:T(8,128)(2,1)S(1)}, bf16[512,256]{1,0:T(8,128)(2,1)}, u32[]{:S(2)}, u32[]{:S(2)}) collective-permute-start(bf16[512,256]{1,0:T(8,128)(2,1)S(1)} %get-tuple-element.40), channel_id=1, source_target_pairs={{2,0},{6,1},{0,2},{4,3},{3,4},{7,5},{1,6},{5,7},{10,8},{14,9},{8,1... | collective-permute-start | bytes 786440 | tf_op jit(solution)/shard_map/ppermute | solution.py:238
  215.3 15.8 %collective-permute-start.16 = (bf16[512,256]{1,0:T(8,128)(2,1)S(1)}, bf16[512,256]{1,0:T(8,128)(2,1)}, u32[]{:S(2)}, u32[]{:S(2)}) collective-permute-start(bf16[512,256]{1,0:T(8,128)(2,1)S(1)} %get-tuple-element.39), channel_id=1, source_target_pairs={{6,0},{2,1},{4,2},{0,3},{7,4},{3,5},{5,6},{1,7},{14,8},{10,9},{12,... | collective-permute-start | bytes 786440 | tf_op jit(solution)/shard_map/ppermute | solution.py:238
  225.2 61.8 %collective-permute-start.21 = (bf16[512,1024]{1,0:T(8,128)(2,1)}, bf16[512,1024]{1,0:T(8,128)(2,1)S(1)}, u32[]{:S(2)}, u32[]{:S(2)}) collective-permute-start(bf16[512,1024]{1,0:T(8,128)(2,1)} %get-tuple-element.28), channel_id=1, source_target_pairs={{0,0},{4,1},{2,2},{6,3},{1,4},{5,5},{3,6},{7,7},{8,8},{12,9},{10,1... | collective-permute-start | bytes 3145736 | tf_op jit(solution)/shard_map/ppermute | solution.py:238
  227.1 59.9 %collective-permute-start.22 = (bf16[512,1024]{1,0:T(8,128)(2,1)}, bf16[512,1024]{1,0:T(8,128)(2,1)S(1)}, u32[]{:S(2)}, u32[]{:S(2)}) collective-permute-start(bf16[512,1024]{1,0:T(8,128)(2,1)} %get-tuple-element.31), channel_id=1, source_target_pairs={{4,0},{0,1},{6,2},{2,3},{5,4},{1,5},{7,6},{3,7},{12,8},{8,9},{14,1... | collective-permute-start | bytes 3145736 | tf_op jit(solution)/shard_map/ppermute | solution.py:238
  228.5 58.5 %collective-permute-start.23 = (bf16[512,1024]{1,0:T(8,128)(2,1)}, bf16[512,1024]{1,0:T(8,128)(2,1)S(1)}, u32[]{:S(2)}, u32[]{:S(2)}) collective-permute-start(bf16[512,1024]{1,0:T(8,128)(2,1)} %get-tuple-element.30), channel_id=1, source_target_pairs={{2,0},{6,1},{0,2},{4,3},{3,4},{7,5},{1,6},{5,7},{10,8},{14,9},{8,1... | collective-permute-start | bytes 3145736 | tf_op jit(solution)/shard_map/ppermute | solution.py:238
  229.4 57.6 %collective-permute-start.24 = (bf16[512,1024]{1,0:T(8,128)(2,1)}, bf16[512,1024]{1,0:T(8,128)(2,1)}, u32[]{:S(2)}, u32[]{:S(2)}) collective-permute-start(bf16[512,1024]{1,0:T(8,128)(2,1)} %get-tuple-element.29), channel_id=1, source_target_pairs={{6,0},{2,1},{4,2},{0,3},{7,4},{3,5},{5,6},{1,7},{14,8},{10,9},{12,... | collective-permute-start | bytes 3145736 | tf_op jit(solution)/shard_map/ppermute | solution.py:238
  277.1 5.3 %copy-start.5 = (bf16[1024,1024]{1,0:T(8,128)(2,1)S(1)}, bf16[1024,1024]{1,0:T(8,128)(2,1)}, u32[]{:S(2)}) copy-start(bf16[1024,1024]{1,0:T(8,128)(2,1)} %all-gather.2.cloned.1.call-done) | copy-start | bytes 6291460
  277.1 5.4 %copy-start.17 = (bf16[512,256]{1,0:T(8,128)(2,1)S(1)}, bf16[512,256]{1,0:T(8,128)(2,1)}, u32[]{:S(2)}) copy-start(bf16[512,256]{1,0:T(8,128)(2,1)} %copy-done.16) | copy-start | bytes 786436
  277.1 27.4 %collective-permute-start.29 = (bf16[1024,1024]{1,0:T(8,128)(2,1)}, bf16[1024,1024]{1,0:T(8,128)(2,1)S(1)}, u32[]{:S(2)}, u32[]{:S(2)}) collective-permute-start(bf16[1024,1024]{1,0:T(8,128)(2,1)} %all-reduce.7.cloned.1.call-done), channel_id=1, source_target_pairs={{5,1},{7,3},{0,4},{2,6},{13,9},{15,11},{8,12},{10,14},{21,17},{23,... | collective-permute-start | bytes 6291464 | tf_op jit(solution)/shard_map/ppermute | solution.py:309
  284.4 2.6 copy-start
  289.2 15.3 %copy-start.6 = (bf16[1024,1024]{1,0:T(8,128)(2,1)S(1)}, bf16[1024,1024]{1,0:T(8,128)(2,1)}, u32[]{:S(2)}) copy-start(bf16[1024,1024]{1,0:T(8,128)(2,1)} %all-reduce.7.cloned.1.call-done) | copy-start | bytes 6291460
  (9 other events, 15.8 us)
Sparse Core Ops, SparseCore 0:
  23.5 36.4 all-gather.1
  203.5 73.6 all-reduce.6

commit v2 on v1

v2 whole, which is shorter than its diff:
```python
import functools
import math
import jax
import jax.numpy as jnp
from jax import lax
from jax.experimental import pallas as pl
from jax.experimental.pallas import tpu as pltpu

HEAD_WIDTH = 64
LONGITUDES = 256
BAND_ROWS = 8
HALO = 6
EXT_ROWS = BAND_ROWS + 2 * HALO
LANES = 256
QUERY_ROWS = 4
KEY_ROWS = QUERY_ROWS + 2 * HALO
BLOCK = 8
BLOCKS = LONGITUDES // BLOCK
KEYS = KEY_ROWS * BLOCK
MASKED = -1e30


def nn(a, b):
    return lax.dot_general(a, b, (((1,), (0,)), ((), ())), preferred_element_type=jnp.float32)


def nt(a, b):
    return lax.dot_general(a, b, (((1,), (1,)), ((), ())), preferred_element_type=jnp.float32)


def attention_kernel(
    heads,
    cells,
    qkv, go, kv_top, kv_bot,
    outq, dkv_own, dkv_top, dkv_bot,
    k_s, v_s, kt_s, vt_s, dk_s, dv_s, live_s, near_s,
):
    feats = heads * HEAD_WIDTH
    tile_cols = LANES // heads // QUERY_ROWS
    tile_queries = QUERY_ROWS * tile_cols
    window = tile_cols // BLOCK + 2

    def load_pair(p, carry):
        cols = pl.ds(pl.multiple_of(p * 16, 16), 16)
        for first, rows_s, turned_s in ((0, k_s, kt_s), (feats, v_s, vt_s)):
            both = jnp.concatenate([
                kv_top[:, cols, first:first + feats].astype(jnp.float32),
                qkv[:, cols, feats + first:2 * feats + first].astype(jnp.float32),
                kv_bot[:, cols, first:first + feats].astype(jnp.float32),
            ], axis=0)
            for half in range(2):
                block = both[:, 8 * half:8 * half + 8, :].reshape(EXT_ROWS * BLOCK, feats)
                rows_s[2 * p + half] = block.astype(jnp.bfloat16)
                for upper in range(2):
                    low = upper * QUERY_ROWS * BLOCK
                    turned_s[upper, 2 * p + half] = block[low:low + KEYS].T.astype(jnp.bfloat16)
        for half in range(2):
            col = (2 * p + half) * BLOCK + lax.broadcasted_iota(jnp.int32, (BLOCK, 128), 0)
            for row in range(EXT_ROWS):
                live_s[2 * p + half, row * BLOCK:(row + 1) * BLOCK, :] = jnp.where(col < cells[row], 0.0, MASKED)
        return carry

    lax.fori_loop(0, BLOCKS // 2, load_pair, 0)
    dk_s[...] = jnp.zeros_like(dk_s)
    dv_s[...] = jnp.zeros_like(dv_s)

    lane = lax.broadcasted_iota(jnp.int32, (KEYS, LANES), 1) % tile_queries
    query_row = lane // tile_cols
    query_col = lane % tile_cols
    key = lax.broadcasted_iota(jnp.int32, (KEYS, LANES), 0)
    row_gap = key // BLOCK - query_row
    for j in range(window):
        col_gap = (j - 1) * BLOCK + key % BLOCK - query_col
        near = (row_gap >= 0) & (row_gap <= 2 * HALO) & (col_gap >= -HALO) & (col_gap <= HALO)
        near_s[j] = jnp.where(near, 0.0, MASKED)

    own_head = (
        lax.broadcasted_iota(jnp.int32, (LANES, feats), 0) // tile_queries
        == lax.broadcasted_iota(jnp.int32, (LANES, feats), 1) // HEAD_WIDTH
    )
    own_head_turned = (
        lax.broadcasted_iota(jnp.int32, (feats, LANES), 1) // tile_queries
        == lax.broadcasted_iota(jnp.int32, (feats, LANES), 0) // HEAD_WIDTH
    )
    query_lane = lax.broadcasted_iota(jnp.int32, (1, LANES), 1) % tile_queries

    def spread(ref, upper, cols):
        tile = ref[upper * QUERY_ROWS:(upper + 1) * QUERY_ROWS, cols, :feats].reshape(tile_queries, feats)
        if heads == 1:
            return tile
        stacked = jnp.concatenate([tile] * heads, axis=0)
        return jnp.where(own_head, stacked, jnp.zeros_like(stacked))

    def gather(turned):
        if heads == 1:
            tile = turned.T
        else:
            tall = jnp.where(own_head_turned, turned, 0.0).T
            tile = sum(tall[h * tile_queries:(h + 1) * tile_queries] for h in range(heads))
        return tile.astype(jnp.bfloat16).reshape(QUERY_ROWS, tile_cols, feats)

    def one_tile(upper, tile):
        start = pl.multiple_of(tile * tile_cols, 16)
        cols = pl.ds(start, tile_cols)
        rows = slice(upper * QUERY_ROWS, (upper + 1) * QUERY_ROWS)
        keys = pl.ds(upper * QUERY_ROWS * BLOCK, KEYS)
        index = [(tile * (tile_cols // BLOCK) + j + BLOCKS - 1) % BLOCKS for j in range(window)]
        queries = spread(qkv, upper, cols)
        grads = spread(go, upper, cols)
        scores = [
            nt(k_s[index[j], keys, :], queries)
            + near_s[j]
            + jnp.concatenate([live_s[index[j], keys, :]] * (LANES // 128), axis=1)
            for j in range(window)
        ]
        highest = jnp.max(functools.reduce(jnp.maximum, scores), axis=0, keepdims=True)
        terms = [jnp.exp(score - highest) for score in scores]
        total = jnp.sum(sum(terms), axis=0, keepdims=True)
        query_cells = jnp.zeros((1, LANES), jnp.int32)
        for row in range(QUERY_ROWS):
            cell = cells[HALO + upper * QUERY_ROWS + row]
            query_cells = jnp.where(query_lane // tile_cols == row, cell, query_cells)
        live = start + query_lane % tile_cols < query_cells
        inverse = jnp.where(live, 1.0 / total, 0.0)
        probs = [term * inverse for term in terms]
        grad_probs = [nt(v_s[index[j], keys, :], grads) for j in range(window)]
        delta = jnp.sum(sum(p * g for p, g in zip(probs, grad_probs)), axis=0, keepdims=True)
        weights = [p.astype(jnp.bfloat16) for p in probs]
        grad_scores = [(p * (g - delta)).astype(jnp.bfloat16) for p, g in zip(probs, grad_probs)]
        for j in range(window):
            dv_s[index[j], keys, :] += nn(weights[j], grads)
            dk_s[index[j], keys, :] += nn(grad_scores[j], queries)
        values_turned = jnp.concatenate([vt_s[upper, index[j]] for j in range(window)], axis=1)
        keys_turned = jnp.concatenate([kt_s[upper, index[j]] for j in range(window)], axis=1)
        outq[rows, cols, :feats] = gather(nn(values_turned, jnp.concatenate(weights, axis=0)))
        outq[rows, cols, feats:] = gather(nn(keys_turned, jnp.concatenate(grad_scores, axis=0)))

    def tile_pair(tile, carry):
        for upper in range(2):
            one_tile(upper, tile)
        return carry

    lax.fori_loop(0, LONGITUDES // tile_cols, tile_pair, 0)

    def store_pair(p, carry):
        cols = pl.ds(pl.multiple_of(p * 16, 16), 16)
        for first, sums in ((0, dk_s), (feats, dv_s)):
            both = jnp.concatenate(
                [sums[2 * p + half].reshape(EXT_ROWS, BLOCK, feats) for half in range(2)], axis=1
            )
            dkv_top[:, cols, first:first + feats] = both[:HALO].astype(jnp.bfloat16)
            dkv_own[:, cols, first:first + feats] = both[HALO:HALO + BAND_ROWS]
            dkv_bot[:, cols, first:first + feats] = both[HALO + BAND_ROWS:].astype(jnp.bfloat16)
        return carry

    lax.fori_loop(0, BLOCKS // 2, store_pair, 0)


def attention(cells, qkv, go, kv_top, kv_bot):
    feats = go.shape[-1]
    heads = feats // HEAD_WIDTH
    window = LANES // heads // QUERY_ROWS // BLOCK + 2
    vmem = pl.BlockSpec(memory_space=pltpu.VMEM)
    grid = lambda rows, kind: jax.ShapeDtypeStruct((rows, LONGITUDES, 2 * feats), kind)
    bf16, f32 = jnp.bfloat16, jnp.float32
    pairs = BAND_ROWS * LONGITUDES * heads * KEYS * window
    return pl.pallas_call(
        functools.partial(attention_kernel, heads),
        out_shape=(grid(BAND_ROWS, bf16), grid(BAND_ROWS, f32), grid(HALO, bf16), grid(HALO, bf16)),
        in_specs=[pl.BlockSpec(memory_space=pltpu.SMEM)] + [vmem] * 4,
        out_specs=(vmem,) * 4,
        scratch_shapes=[
            pltpu.VMEM((BLOCKS, EXT_ROWS * BLOCK, feats), bf16),
            pltpu.VMEM((BLOCKS, EXT_ROWS * BLOCK, feats), bf16),
            pltpu.VMEM((2, BLOCKS, feats, KEYS), bf16),
            pltpu.VMEM((2, BLOCKS, feats, KEYS), bf16),
            pltpu.VMEM((BLOCKS, EXT_ROWS * BLOCK, feats), f32),
            pltpu.VMEM((BLOCKS, EXT_ROWS * BLOCK, feats), f32),
            pltpu.VMEM((BLOCKS, EXT_ROWS * BLOCK, 128), f32),
            pltpu.VMEM((window, KEYS, LANES), f32),
        ],
        compiler_params=pltpu.CompilerParams(vmem_limit_bytes=60 * 2**20),
        cost_estimate=pl.CostEstimate(
            flops=12 * pairs * HEAD_WIDTH, transcendentals=pairs, bytes_accessed=20 * 2**20
        ),
    )(cells, qkv, go, kv_top, kv_bot)


from jax.sharding import Mesh, PartitionSpec as P

WIDTH = 1024
GROUP = ("y", "m", "c")


def tn(a, b):
    return lax.dot_general(a, b, (((0,), (0,)), ((), ())), preferred_element_type=jnp.float32)


def to_bands(halves, step):
    dm, dc = step
    place = lambda y, m, c: (y * halves + m) * 2 + c
    return [
        (place(y, m, c), place((c + dc) % 2, (m + dm) % halves, y))
        for y in range(2) for m in range(halves) for c in range(2)
    ]


def passed_along(x, by):
    length = lax.axis_size("z") * 2
    pairs = [(i, i + by) for i in range(length) if 0 <= i + by < length]
    return lax.ppermute(x, ("z", "c"), pairs)


def after(x, *others):
    return lax.optimization_barrier((x, *others))[0]


def on_device(tokens, gain, qkv_weight, out_weight, row_cells, upstream):
    heads = qkv_weight.shape[0]
    feats = heads * HEAD_WIDTH
    band_tokens = BAND_ROWS * LONGITUDES
    chunk = tokens.shape[0]
    halves, layers = lax.axis_size("m"), lax.axis_size("z")
    z, y, m, c = (lax.axis_index(axis) for axis in ("z",) + GROUP)
    steps = [(dm, dc) for dc in range(2) for dm in range(halves)]
    arrives = [((m - dm) % halves) * 2 + (y - dc) % 2 for dm, dc in steps]
    grad_scale = 4.0 / math.sqrt(band_tokens * layers * 2)
    band_start = (z * 2 + c) * BAND_ROWS
    cells = lax.dynamic_slice_in_dim(jnp.pad(row_cells, (HALO, HALO)), band_start, EXT_ROWS)

    def send(x, step):
        return lax.ppermute(x, GROUP, to_bands(halves, step))

    def send_back(x, step):
        return lax.ppermute(x, GROUP, [(b, a) for a, b in to_bands(halves, step)])

    def in_order(parts):
        whole = jnp.zeros((band_tokens,) + parts[0].shape[1:], parts[0].dtype)
        for part, at in zip(parts, arrives):
            whole = lax.dynamic_update_slice_in_dim(whole, part, at * chunk, 0)
        return whole

    def in_steps(whole):
        return [lax.dynamic_slice_in_dim(whole, at * chunk, chunk, 0) for at in arrives]

    def from_ahead(x, dm):
        return lax.ppermute(x, "m", [((i + dm) % halves, i) for i in range(halves)])

    def from_sibling(x):
        return lax.ppermute(x, "c", [(0, 1), (1, 0)])

    out_flat = out_weight.reshape(feats, WIDTH)
    out_mine = jnp.concatenate([out_flat] + [from_ahead(out_flat, dm) for dm in range(1, halves)], axis=0)

    features = tokens.astype(jnp.float32)
    inverse = lax.rsqrt(jnp.mean(features * features, axis=1, keepdims=True) + 1e-06)
    normed = (features * inverse * gain[None, :]).astype(jnp.bfloat16)
    normed_parts = [send(normed, step) for step in steps]

    split = qkv_weight.reshape(heads, 3, HEAD_WIDTH, WIDTH).transpose(1, 0, 2, 3).reshape(3 * feats, WIDTH)
    eighth = jnp.where(jnp.arange(3 * feats) < feats, HEAD_WIDTH ** -0.5, 1.0)[:, None].astype(jnp.bfloat16)
    split = split * eighth
    pairs = [((y * halves + m) * 2 + y, (y * halves + m) * 2 + 1 - y) for y in range(2) for m in range(halves)]
    group_split = jnp.where(c == y, split, lax.ppermute(split, GROUP, pairs))

    out_blocks = jnp.concatenate([out_mine, from_sibling(out_mine)], axis=0)
    grad_heads_own = nt(upstream, out_blocks).astype(jnp.bfloat16)

    qkv = in_order([nt(part, group_split).astype(jnp.bfloat16) for part in normed_parts])
    qkv = qkv.reshape(BAND_ROWS, LONGITUDES, 3 * feats)
    kv_top = passed_along(qkv[BAND_ROWS - HALO:, :, feats:], 1)
    kv_bot = passed_along(qkv[:HALO, :, feats:], -1)
    grad_heads = in_order([
        send(after(grad_heads_own[:, i * feats:(i + 1) * feats], qkv), step) for i, step in enumerate(steps)
    ]).reshape(BAND_ROWS, LONGITUDES, feats)

    held = after(upstream, grad_heads)
    upstream_parts = [send(held, step) for step in steps]
    share = 3 * feats // layers
    held = after(lax.dynamic_slice_in_dim(split, z * share, share, 0), kv_top, kv_bot)
    others = [lax.all_gather(from_ahead(held, dm), "z", axis=0, tiled=True) for dm in range(1, halves)]
    split_mine = jnp.concatenate([split] + others, axis=0)
    split_blocks = jnp.concatenate([split_mine, from_sibling(split_mine)], axis=0)

    outq, dkv, dkv_top, dkv_bot = attention(cells, qkv, grad_heads, kv_top, kv_bot)

    from_above = passed_along(dkv_top, -1)
    from_below = passed_along(dkv_bot, 1)
    outq_parts = in_steps(outq.reshape(band_tokens, 2 * feats))
    outq_own = jnp.concatenate([send_back(part, step) for part, step in zip(outq_parts, steps)], axis=1)
    outq_own = outq_own.reshape(chunk, len(steps), 2, feats)
    out_own = outq_own[:, :, 0].reshape(chunk, len(steps) * feats)
    update = nn(out_own, out_blocks).astype(jnp.bfloat16)

    def reduced(grads):
        pairs = [
            ((1 - y) * halves * 2 + m * 2 + 1 - y, y * halves * 2 + m * 2 + 1 - y)
            for y in range(2) for m in range(halves)
        ]
        return jnp.where(c == y, grads, lax.ppermute(grads, GROUP, pairs)).astype(jnp.float32)

    outq_steps = jnp.concatenate(outq_parts, axis=0)
    normed_steps = jnp.concatenate(normed_parts, axis=0)
    upstream_steps = jnp.concatenate(upstream_parts, axis=0)
    early = jnp.concatenate([tn(outq_steps[:, :feats], upstream_steps), tn(outq_steps[:, feats:], normed_steps)])
    early_sum = lax.psum(early.astype(jnp.bfloat16), ("z", "c"))
    early = reduced(early_sum)
    grad_out = early[:feats] * grad_scale
    grad_query = early[feats:] * (grad_scale * HEAD_WIDTH ** -0.5)

    wide = lambda x, low, high: jnp.pad(x.astype(jnp.float32), ((low, high), (0, 0), (0, 0)))
    dkv = dkv + wide(from_below, 0, BAND_ROWS - HALO) + wide(from_above, BAND_ROWS - HALO, 0)
    dkv_parts = in_steps(dkv.astype(jnp.bfloat16).reshape(band_tokens, 2 * feats))
    dkv_own = [send_back(part, step) for part, step in zip(dkv_parts, steps)]
    grad_normed = 0.0
    for i, part in enumerate(dkv_own):
        block = split_blocks[i * 3 * feats:(i + 1) * 3 * feats]
        grad_normed += nn(outq_own[:, i, 1], block[:feats]) + nn(part, block[feats:])
    centred = features * inverse
    scaled = gain[None, :] * grad_normed
    grad_input = inverse * (scaled - centred * jnp.mean(scaled * centred, axis=1, keepdims=True))

    late = tn(jnp.concatenate(dkv_parts, axis=0), normed_steps).astype(jnp.bfloat16)
    late = reduced(lax.psum(after(late, early_sum), ("z", "c"))) * grad_scale
    by_head = lambda x: x.reshape(heads, HEAD_WIDTH, WIDTH)
    grad_qkv = jnp.concatenate([by_head(grad_query), by_head(late[:feats]), by_head(late[feats:])], axis=1)
    return update, grad_input.astype(jnp.bfloat16), grad_qkv, by_head(grad_out)


def solution(mesh):
    devices = mesh.devices.reshape(mesh.shape["lat"] // 2, 2, mesh.shape["mp"] // 2, 2)
    tokens, weights = P(("z", "y", "m", "c"), None), P(("m", "c"), None, None)
    return jax.shard_map(
        on_device,
        mesh=Mesh(devices, ("z", "y", "m", "c")),
        in_specs=(tokens, P(), weights, weights, P(), tokens),
        out_specs=(tokens, tokens, weights, weights),
        check_vma=False,
    )
```

time: 317 us -> 395 us (1.25)
  waiting for transfers between devices: 118 us -> 169 us
  matrix products: 22.4 us -> 43.5 us
  other arithmetic: 14.6 us -> 20.6 us
  starting transfers between devices: 75.3 us -> 69.4 us
    psum x1 -> x2, waiting for transfers between devices: 46 us -> 84.4 us  [the longest x1 46 us: on_device(): late = reduced(lax.psum(after(late, early_sum), ('z', 'c'))) * grad_scale]
    ppermute x12, waiting for transfers between devices: 59.8 us -> 30.8 us  [send(): return lax.ppermute(x, GROUP, to_bands(halves, step))]
    ppermute x8, waiting for transfers between devices: 0.02 us -> 22 us  [send_back(): return lax.ppermute(x, GROUP, [(b, a) for a, b in to_bands(halves, step)])]
    ppermute x2 -> x7, waiting for transfers between devices: 12 us -> 31.5 us  [the longest x2 21.5 us: from_ahead(): return lax.ppermute(x, 'm', [((i + dm) % halves, i) for i in range(halves)])]
    dynamic_update_slice x12 -> x4, local copies, waits for them, and re-layouts: 12.4 us -> 0.1 us  [in_order(): whole = lax.dynamic_update_slice_in_dim(whole, part, at * chunk, 0)]
    unnamed x50 -> x51, local copies, waits for them, and re-layouts: 6.12 us -> 17.7 us
    ppermute x2 -> x7, starting transfers between devices: 6.27 us -> 17.8 us  [the longest x2 8.23 us: reduced(): lax.ppermute(grads, GROUP, pairs)]
    ppermute x8 -> x4, starting transfers between devices: 22.5 us -> 11.6 us  [passed_along(): return lax.ppermute(x, ('z', 'c'), pairs)]
  transfers between devices with their start and end apart: 32 -> 34, of which waited for: 8 -> 11; matrix products, arithmetic and copies ran while one was open for 15% -> 20% of each run, Pallas kernels for 13% -> 10%
where the time goes in v2:
time: 395 us; the launch traced here: 392 us
  waiting for transfers between devices  169 us (43%)
  starting transfers between devices  69.4 us (18%)
  matrix products  43.5 us (11%)
  Pallas kernels  40.9 us (10%)
  local copies, waits for them, and re-layouts  32.6 us (8%)
  other arithmetic  20.6 us (5%)
  between operations  16.1 us (4%)
    psum x1, waiting for transfers between devices, on_device(): late = reduced(lax.psum(after(late, early_sum), ('z', 'c'))) * grad_scale  46 us
    pallas_call x1, Pallas kernels, attention(): pl.pallas_call(functools.partial(attention_kernel, heads), out_shape=(gri...  40.9 us
    psum x1, waiting for transfers between devices, on_device(): early_sum = lax.psum(early.astype(jnp.bfloat16), ('z', 'c'))  38.5 us
    ppermute x12, waiting for transfers between devices, send(): return lax.ppermute(x, GROUP, to_bands(halves, step))  30.8 us
    ppermute x12, starting transfers between devices, send(): return lax.ppermute(x, GROUP, to_bands(halves, step))  27.4 us
    ppermute x8, waiting for transfers between devices, send_back(): return lax.ppermute(x, GROUP, [(b, a) for a, b in to_bands(halves, step)])  22 us
    ppermute x2, waiting for transfers between devices, from_ahead(): return lax.ppermute(x, 'm', [((i + dm) % halves, i) for i in range(halves)])  21.5 us
    dot_general x9, matrix products, nn(): lax.dot_general(a, b, (((1,), (0,)), ((), ())), preferred_element_type=jn...  20.1 us
  transfers between devices with their start and end apart: 34, of which 11 were waited for; matrix products, arithmetic and copies ran while one was open for 20% of the time, Pallas kernels for 10%

profile of v2, /device:TPU:0, one launch (start us, length us, event | category | flops | bytes accessed | tf_op | source)
XLA Modules:
  0.0 391.8 jit_solution(6739271948478743018)
XLA Ops:
  9.9 3.7 collective-permute-start.1
  15.2 9.5 %collective-permute-start = (bf16[512,1024]{1,0:T(8,128)(2,1)}, bf16[512,1024]{1,0:T(8,128)(2,1)}, u32[]{:S(2)}, u32[]{:S(2)}) collective-permute-start(bf16[512,1024]{1,0:T(8,128)(2,1)} %fusion.11), channel_id=1, source_target_pairs={{0,0},{1,4},{2,2},{3,6},{4,1},{5,5},{6,3},{7,7},{8,8},{9,12},{10,1... | collective-permute-start | bytes 3145736 | tf_op jit(solution)/shard_map/ppermute | solution.py:232
  24.7 2.3 collective-permute-start.5
  27.6 12.3 %collective-permute-done.5 = bf16[256,1024]{1,0:T(8,128)(2,1)} collective-permute-done((bf16[256,1024]{1,0:T(8,128)(2,1)S(1)}, bf16[256,1024]{1,0:T(8,128)(2,1)}, u32[]{:S(2)}, u32[]{:S(2)}) %collective-permute-start.5) | collective-permute-done | bytes 524320 | tf_op jit(solution)/shard_map/ppermute | solution.py:247
  41.1 2.2 collective-permute-start.6
  43.8 2.3 fusion.28
  46.1 16.3 %collective-permute-done.2 = bf16[512,1024]{1,0:T(8,128)(2,1)} collective-permute-done((bf16[512,1024]{1,0:T(8,128)(2,1)}, bf16[512,1024]{1,0:T(8,128)(2,1)}, u32[]{:S(2)}, u32[]{:S(2)}) %collective-permute-start.2) | collective-permute-done | bytes 1048608 | tf_op jit(solution)/shard_map/ppermute | solution.py:232
  62.4 2.3 fusion.29
  64.7 2.3 fusion.30
  67.0 9.0 %collective-permute-done.4 = bf16[512,1024]{1,0:T(8,128)(2,1)S(1)} collective-permute-done((bf16[512,1024]{1,0:T(8,128)(2,1)}, bf16[512,1024]{1,0:T(8,128)(2,1)S(1)}, u32[]{:S(2)}, u32[]{:S(2)}) %collective-permute-start.4) | collective-permute-done | bytes 1048608 | tf_op jit(solution)/shard_map/ppermute | solution.py:232
  77.0 2.2 fusion.57
  79.7 4.1 %collective-permute-start.11 = (bf16[6,256,512]{2,1,0:T(8,128)(2,1)}, bf16[6,256,512]{2,1,0:T(8,128)(2,1)}, u32[]{:S(2)}, u32[]{:S(2)}) collective-permute-start(bf16[6,256,512]{2,1,0:T(8,128)(2,1)} %get-tuple-element.27), channel_id=1, source_target_pairs={{0,1},{1,8},{8,9},{9,16},{16,17},{17,24},{24,25},{2,3},{3,10},{10,... | collective-permute-start | bytes 4718600 | tf_op jit(solution)/shard_map/ppermute | solution.py:211
  85.1 3.0 fusion.32
  89.7 2.3 constant_dynamic-update-slice_fusion.3
  92.0 2.3 constant_dynamic-update-slice_fusion.2
  95.8 3.4 collective-permute-start.9
  99.3 2.3 constant_dynamic-update-slice_fusion.1
  102.9 5.5 %collective-permute-done.9 = bf16[512,256]{0,1:T(8,128)(2,1)} collective-permute-done((bf16[512,256]{0,1:T(8,128)(2,1)}, bf16[512,256]{0,1:T(8,128)(2,1)}, u32[]{:S(2)}, u32[]{:S(2)}) %collective-permute-start.9) | collective-permute-done | bytes 262176 | tf_op jit(solution)/shard_map/ppermute | solution.py:232
  113.2 9.5 %collective-permute-start.25 = (bf16[512,1024]{1,0:T(8,128)(2,1)}, bf16[512,1024]{1,0:T(8,128)(2,1)}, u32[]{:S(2)}, u32[]{:S(2)}) collective-permute-start(bf16[512,1024]{1,0:T(8,128)(2,1)} %param.11), channel_id=1, source_target_pairs={{0,0},{1,4},{2,2},{3,6},{4,1},{5,5},{6,3},{7,7},{8,8},{9,12},{10,1... | collective-permute-start | bytes 3145736 | tf_op jit(solution)/shard_map/ppermute | solution.py:232
  125.4 40.9 %shard_map.93 = (bf16[8,256,512]{2,1,0:T(8,128)(2,1)}, f32[8,256,512]{2,1,0:T(8,128)}, bf16[6,256,512]{2,1,0:T(8,128)(2,1)}, bf16[6,256,512]{2,1,0:T(8,128)(2,1)}) custom-call(s32[20]{0:T(128)} %pad_dynamic-slice_fusion.cells, bf16[8,256,768]{2,1,0:T(8,128)(2,1)} %bitcast.55, bf16[8,256,256]{2,1,0:T(8,128)(2,1)} %bitcast.68, ...), custom_call_target="tpu_custom_call" | custom-call | flops 3221225472 | bytes 20971520 | tf_op jit(solution)/shard_map/pallas_call | solution.py:167
  166.3 2.7 constant_dynamic-slice_fusion.8
  169.0 2.1 copy.35
  171.1 2.1 copy.36
  177.0 3.4 convolution_convert_fusion.6
  180.5 3.4 fusion.33
  186.5 9.2 %collective-permute-done.20 = bf16[192,1024]{1,0:T(8,128)(2,1)S(1)} collective-permute-done((bf16[192,1024]{1,0:T(8,128)(2,1)S(1)}, bf16[192,1024]{1,0:T(8,128)(2,1)S(1)}, u32[]{:S(2)}, u32[]{:S(2)}) %collective-permute-start.20) | collective-permute-done | bytes 393248 | tf_op jit(solution)/shard_map/ppermute | solution.py:247
  198.2 4.9 %collective-permute-start.17 = (bf16[6,256,512]{2,1,0:T(8,128)(2,1)}, bf16[6,256,512]{2,1,0:T(8,128)(2,1)}, u32[]{:S(2)}, u32[]{:S(2)}) collective-permute-start(bf16[6,256,512]{2,1,0:T(8,128)(2,1)} %get-tuple-element.21), channel_id=1, source_target_pairs={{0,1},{1,8},{8,9},{9,16},{16,17},{17,24},{24,25},{2,3},{3,10},{10,... | collective-permute-start | bytes 4718600 | tf_op jit(solution)/shard_map/ppermute | solution.py:211
  205.8 2.7 collective-permute-start.16
  208.5 11.0 %collective-permute-done.14 = bf16[512,512]{0,1:T(8,128)(2,1)S(1)} collective-permute-done((bf16[512,512]{0,1:T(8,128)(2,1)}, bf16[512,512]{0,1:T(8,128)(2,1)S(1)}, u32[]{:S(2)}, u32[]{:S(2)}) %collective-permute-start.14) | collective-permute-done | bytes 524320 | tf_op jit(solution)/shard_map/ppermute | solution.py:235
  220.7 9.7 %collective-permute-done.16 = bf16[512,512]{0,1:T(8,128)(2,1)S(1)} collective-permute-done((bf16[512,512]{0,1:T(8,128)(2,1)S(1)}, bf16[512,512]{0,1:T(8,128)(2,1)S(1)}, u32[]{:S(2)}, u32[]{:S(2)}) %collective-permute-start.16) | collective-permute-done | bytes 524320 | tf_op jit(solution)/shard_map/ppermute | solution.py:235
  233.0 38.5 %all-reduce.6.cloned.1.call-done = bf16[512,1024]{1,0:T(8,128)(2,1)} async-done(((bf16[512,1024]{1,0:T(8,128)(2,1)}), bf16[512,1024]{1,0:T(8,128)(2,1)}) %all-reduce.6.cloned.1.call-update) | async-done | bytes 1048592 | tf_op jit(solution)/shard_map/psum | solution.py:306
  271.5 4.5 %collective-permute-start.29 = (bf16[512,1024]{1,0:T(8,128)(2,1)}, bf16[512,1024]{1,0:T(8,128)(2,1)}, u32[]{:S(2)}, u32[]{:S(2)}) collective-permute-start(bf16[512,1024]{1,0:T(8,128)(2,1)} %all-reduce.6.cloned.1.call-done), channel_id=1, source_target_pairs={{5,1},{7,3},{0,4},{2,6},{13,9},{15,11},{8,12},{10,14},{21,17},{23,... | collective-permute-start | bytes 3145736 | tf_op jit(solution)/shard_map/ppermute | solution.py:300
  275.9 4.1 %convolution_convert_fusion = bf16[512,1024]{1,0:T(8,128)(2,1)} fusion(bf16[512,1024]{0,1:T(8,128)(2,1)} %bitcast.67, bf16[512,1024]{1,0:T(8,128)(2,1)} %copy-done.20, bf16[256,1024]{1,0:T(8,128)(2,1)} %collective-permute-done.5, bf16[256,1024]{1,0:T(8,128)(2,1)S(1)} %bitcast.73), kind=kOutput, calls=%fused_computation.38 | convolution fusion | flops 1080557568 | bytes 4194304 | tf_op jit(solution)/shard_map/dot_general | solution.py:24
  280.0 2.7 add_convert_fusion
  283.9 3.5 pad_maximum_fusion
  287.5 5.7 %fusion.25 = bf16[512,1024]{1,0:T(8,128)(2,1)} fusion(bf16[2048,1024]{1,0:T(8,128)(2,1)} %constant_dynamic-update-slice_fusion, bf16[512,512]{1,0:T(8,128)(2,1)S(1)} %get-tuple-element.33, bf16[512,512]{1,0:T(8,128)(2,1)S(1)} %copy-done.16, bf16[512,512]{1,0:T(8,128)(2,1)} %get-tuple-element.35, bf16[512,512]{1,0:T(8,128)(2,1)S(1)} %copy-done.17), kind=kOutput, calls=%fused_computation.37 | convolution fusion | flops 2156396544 | bytes 7340032 | tf_op jit(solution)/shard_map/dot_general | solution.py:196
  293.2 2.8 fusion.51
  297.5 5.4 %collective-permute-start.19 = (bf16[512,512]{1,0:T(8,128)(2,1)}, bf16[512,512]{1,0:T(8,128)(2,1)}, u32[]{:S(2)}, u32[]{:S(2)}) collective-permute-start(bf16[512,512]{1,0:T(8,128)(2,1)} %get-tuple-element.32), channel_id=1, source_target_pairs={{0,0},{4,1},{2,2},{6,3},{1,4},{5,5},{3,6},{7,7},{8,8},{12,9},{10,1... | collective-permute-start | bytes 1572872 | tf_op jit(solution)/shard_map/ppermute | solution.py:235
  304.5 46.0 %all-reduce.8.cloned.1.call-done = bf16[512,1024]{1,0:T(8,128)(2,1)} async-done(((bf16[512,1024]{1,0:T(8,128)(2,1)}), bf16[512,1024]{1,0:T(8,128)(2,1)}) %all-reduce.8.cloned.1.call-update) | async-done | bytes 1048592 | tf_op jit(solution)/shard_map/psum | solution.py:324
  350.4 3.8 collective-permute-start.30
  354.2 2.8 slice_multiply_fusion
  357.1 1.9 fusion.44
  360.4 1.8 fusion.42
  362.2 9.9 %collective-permute-done.30 = bf16[512,1024]{1,0:T(8,128)(2,1)S(1)} collective-permute-done((bf16[512,1024]{1,0:T(8,128)(2,1)}, bf16[512,1024]{1,0:T(8,128)(2,1)S(1)}, u32[]{:S(2)}, u32[]{:S(2)}) %collective-permute-start.30) | collective-permute-done | bytes 1048608 | tf_op jit(solution)/shard_map/ppermute | solution.py:300
  372.7 2.1 pad_maximum_fusion.1
  376.4 1.9 fusion.40
  378.3 2.1 fusion.38
  380.4 2.5 fusion.12
  (130 shorter events, 45.1 us)
Async XLA Ops:
  8.0 263.5 %all-reduce.6.cloned.1.call-start = ((), (), s32[]{:S(2)}) async-start(), calls=%async_computation.1 | async-start | bytes 2097152 | tf_op jit(solution)/shard_map/psum | solution.py:306
  9.6 4.3 %copy-start.1 = (bf16[3,4,64,1024]{3,2,1,0:T(8,128)(2,1)}, bf16[3,4,64,1024]{3,2,1,0:T(8,128)(2,1)S(1)}, u32[]{:S(2)}) copy-start(bf16[3,4,64,1024]{3,2,1,0:T(8,128)(2,1)S(1)} %copy.22) | copy-start | bytes 4718596
  9.6 4.0 %copy-start = (bf16[512,1024]{1,0:T(8,128)(2,1)S(1)}, bf16[512,1024]{1,0:T(8,128)(2,1)}, u32[]{:S(2)}) copy-start(bf16[512,1024]{1,0:T(8,128)(2,1)} %param.6) | copy-start | bytes 3145732
  9.6 4.3 %copy-start.19 = (f32[1024]{0:T(1024)S(1)}, f32[1024]{0:T(1024)}, u32[]{:S(2)}) copy-start(f32[1024]{0:T(1024)} %param.7) | copy-start | bytes 12292
  9.9 14.8 %copy-start.12 = (bf16[4,64,1024]{2,1,0:T(8,128)(2,1)S(1)}, bf16[4,64,1024]{2,1,0:T(8,128)(2,1)}, u32[]{:S(2)}) copy-start(bf16[4,64,1024]{2,1,0:T(8,128)(2,1)} %param.9) | copy-start | bytes 1572868
  9.9 17.1 %copy-start.21 = (s32[64]{0:T(128)S(1)}, s32[64]{0:T(128)}, u32[]{:S(2)}) copy-start(s32[64]{0:T(128)} %param.10) | copy-start | bytes 772
  9.9 31.1 %collective-permute-start.1 = (bf16[768,1024]{1,0:T(8,128)(2,1)S(1)}, bf16[768,1024]{1,0:T(8,128)(2,1)}, u32[]{:S(2)}, u32[]{:S(2)}) collective-permute-start(bf16[768,1024]{1,0:T(8,128)(2,1)S(1)} %bitcast_multiply_fusion), channel_id=1, source_target_pairs={{0,1},{2,3},{5,4},{7,6},{8,9},{10,11},{13,12},{15,14},{16,17},{18,... | collective-permute-start | bytes 4718600 | tf_op jit(solution)/shard_map/ppermute | solution.py:264
  15.2 28.4 %collective-permute-start = (bf16[512,1024]{1,0:T(8,128)(2,1)}, bf16[512,1024]{1,0:T(8,128)(2,1)}, u32[]{:S(2)}, u32[]{:S(2)}) collective-permute-start(bf16[512,1024]{1,0:T(8,128)(2,1)} %fusion.11), channel_id=1, source_target_pairs={{0,0},{1,4},{2,2},{3,6},{4,1},{5,5},{6,3},{7,7},{8,8},{9,12},{10,1... | collective-permute-start | bytes 3145736 | tf_op jit(solution)/shard_map/ppermute | solution.py:232
  24.7 15.3 %collective-permute-start.5 = (bf16[256,1024]{1,0:T(8,128)(2,1)S(1)}, bf16[256,1024]{1,0:T(8,128)(2,1)}, u32[]{:S(2)}, u32[]{:S(2)}) collective-permute-start(bf16[256,1024]{1,0:T(8,128)(2,1)S(1)} %bitcast.70), channel_id=1, source_target_pairs={{2,0},{0,2},{3,1},{1,3},{6,4},{4,6},{7,5},{5,7},{10,8},{8,10},{11,... | collective-permute-start | bytes 1572872 | tf_op jit(solution)/shard_map/ppermute | solution.py:247
  27.0 35.4 %collective-permute-start.2 = (bf16[512,1024]{1,0:T(8,128)(2,1)}, bf16[512,1024]{1,0:T(8,128)(2,1)}, u32[]{:S(2)}, u32[]{:S(2)}) collective-permute-start(bf16[512,1024]{1,0:T(8,128)(2,1)} %fusion.11), channel_id=1, source_target_pairs={{0,2},{1,6},{2,0},{3,4},{4,3},{5,7},{6,1},{7,5},{8,10},{9,14},{10,... | collective-permute-start | bytes 3145736 | tf_op jit(solution)/shard_map/ppermute | solution.py:232
  27.0 37.7 %collective-permute-start.3 = (bf16[512,1024]{1,0:T(8,128)(2,1)}, bf16[512,1024]{1,0:T(8,128)(2,1)}, u32[]{:S(2)}, u32[]{:S(2)}) collective-permute-start(bf16[512,1024]{1,0:T(8,128)(2,1)} %fusion.11), channel_id=1, source_target_pairs={{0,4},{1,0},{2,6},{3,2},{4,5},{5,1},{6,7},{7,3},{8,12},{9,8},{10,1... | collective-permute-start | bytes 3145736 | tf_op jit(solution)/shard_map/ppermute | solution.py:232
  27.1 16.2 %copy-start.2 = (bf16[3,4,64,1024]{3,2,1,0:T(8,128)(2,1)S(1)}, bf16[3,4,64,1024]{3,2,1,0:T(8,128)(2,1)}, u32[]{:S(2)}) copy-start(bf16[3,4,64,1024]{3,2,1,0:T(8,128)(2,1)} %copy-done.1) | copy-start | bytes 4718596
  40.0 36.0 %collective-permute-start.4 = (bf16[512,1024]{1,0:T(8,128)(2,1)}, bf16[512,1024]{1,0:T(8,128)(2,1)S(1)}, u32[]{:S(2)}, u32[]{:S(2)}) collective-permute-start(bf16[512,1024]{1,0:T(8,128)(2,1)} %fusion.11), channel_id=1, source_target_pairs={{0,6},{1,2},{2,4},{3,0},{4,7},{5,3},{6,5},{7,1},{8,14},{9,10},{10,... | collective-permute-start | bytes 3145736 | tf_op jit(solution)/shard_map/ppermute | solution.py:232
  41.1 44.0 %collective-permute-start.6 = (bf16[512,1024]{1,0:T(8,128)(2,1)S(1)}, bf16[512,1024]{1,0:T(8,128)(2,1)S(1)}, u32[]{:S(2)}, u32[]{:S(2)}) collective-permute-start(bf16[512,1024]{1,0:T(8,128)(2,1)S(1)} %pad_maximum_fusion.5), channel_id=1, source_target_pairs={{0,1},{1,0},{2,3},{3,2},{4,5},{5,4},{6,7},{7,6},{8,9},{9,8},{10,11... | collective-permute-start | bytes 3145736 | tf_op jit(solution)/shard_map/ppermute | solution.py:250
  79.7 44.5 %collective-permute-start.11 = (bf16[6,256,512]{2,1,0:T(8,128)(2,1)}, bf16[6,256,512]{2,1,0:T(8,128)(2,1)}, u32[]{:S(2)}, u32[]{:S(2)}) collective-permute-start(bf16[6,256,512]{2,1,0:T(8,128)(2,1)} %get-tuple-element.27), channel_id=1, source_target_pairs={{0,1},{1,8},{8,9},{9,16},{16,17},{17,24},{24,25},{2,3},{3,10},{10,... | collective-permute-start | bytes 4718600 | tf_op jit(solution)/shard_map/ppermute | solution.py:211
  83.8 41.7 %collective-permute-start.12 = (bf16[6,256,512]{2,1,0:T(8,128)(2,1)}, bf16[6,256,512]{2,1,0:T(8,128)(2,1)}, u32[]{:S(2)}, u32[]{:S(2)}) collective-permute-start(bf16[6,256,512]{2,1,0:T(8,128)(2,1)} %get-tuple-element.26), channel_id=1, source_target_pairs={{1,0},{8,1},{9,8},{16,9},{17,16},{24,17},{25,24},{3,2},{10,3},{11,... | collective-permute-start | bytes 4718600 | tf_op jit(solution)/shard_map/ppermute | solution.py:211
  89.0 10.2 %collective-permute-start.7 = (bf16[512,256]{0,1:T(8,128)(2,1)S(1)}, bf16[512,256]{0,1:T(8,128)(2,1)S(1)}, u32[]{:S(2)}, u32[]{:S(2)}) collective-permute-start(bf16[512,256]{0,1:T(8,128)(2,1)S(1)} %get-tuple-element.15), channel_id=1, source_target_pairs={{0,0},{1,4},{2,2},{3,6},{4,1},{5,5},{6,3},{7,7},{8,8},{9,12},{10,1... | collective-permute-start | bytes 786440 | tf_op jit(solution)/shard_map/ppermute | solution.py:232
  94.3 8.5 %collective-permute-start.8 = (bf16[512,256]{0,1:T(8,128)(2,1)}, bf16[512,256]{0,1:T(8,128)(2,1)S(1)}, u32[]{:S(2)}, u32[]{:S(2)}) collective-permute-start(bf16[512,256]{0,1:T(8,128)(2,1)} %get-tuple-element.16), channel_id=1, source_target_pairs={{0,2},{1,6},{2,0},{3,4},{4,3},{5,7},{6,1},{7,5},{8,10},{9,14},{10,... | collective-permute-start | bytes 786440 | tf_op jit(solution)/shard_map/ppermute | solution.py:232
  95.8 12.6 %collective-permute-start.9 = (bf16[512,256]{0,1:T(8,128)(2,1)}, bf16[512,256]{0,1:T(8,128)(2,1)}, u32[]{:S(2)}, u32[]{:S(2)}) collective-permute-start(bf16[512,256]{0,1:T(8,128)(2,1)} %get-tuple-element.17), channel_id=1, source_target_pairs={{0,4},{1,0},{2,6},{3,2},{4,5},{5,1},{6,7},{7,3},{8,12},{9,8},{10,1... | collective-permute-start | bytes 786440 | tf_op jit(solution)/shard_map/ppermute | solution.py:232
  99.2 10.3 %collective-permute-start.10 = (bf16[512,256]{0,1:T(8,128)(2,1)}, bf16[512,256]{0,1:T(8,128)(2,1)}, u32[]{:S(2)}, u32[]{:S(2)}) collective-permute-start(bf16[512,256]{0,1:T(8,128)(2,1)} %get-tuple-element.18), channel_id=1, source_target_pairs={{0,6},{1,2},{2,4},{3,0},{4,7},{5,3},{6,5},{7,1},{8,14},{9,10},{10,... | collective-permute-start | bytes 786440 | tf_op jit(solution)/shard_map/ppermute | solution.py:232
  113.2 67.2 %collective-permute-start.25 = (bf16[512,1024]{1,0:T(8,128)(2,1)}, bf16[512,1024]{1,0:T(8,128)(2,1)}, u32[]{:S(2)}, u32[]{:S(2)}) collective-permute-start(bf16[512,1024]{1,0:T(8,128)(2,1)} %param.11), channel_id=1, source_target_pairs={{0,0},{1,4},{2,2},{3,6},{4,1},{5,5},{6,3},{7,7},{8,8},{9,12},{10,1... | collective-permute-start | bytes 3145736 | tf_op jit(solution)/shard_map/ppermute | solution.py:232
  122.7 57.7 %collective-permute-start.26 = (bf16[512,1024]{1,0:T(8,128)(2,1)}, bf16[512,1024]{1,0:T(8,128)(2,1)}, u32[]{:S(2)}, u32[]{:S(2)}) collective-permute-start(bf16[512,1024]{1,0:T(8,128)(2,1)} %param.11), channel_id=1, source_target_pairs={{0,2},{1,6},{2,0},{3,4},{4,3},{5,7},{6,1},{7,5},{8,10},{9,14},{10,... | collective-permute-start | bytes 3145736 | tf_op jit(solution)/shard_map/ppermute | solution.py:232
  124.2 56.3 %collective-permute-start.27 = (bf16[512,1024]{1,0:T(8,128)(2,1)}, bf16[512,1024]{1,0:T(8,128)(2,1)}, u32[]{:S(2)}, u32[]{:S(2)}) collective-permute-start(bf16[512,1024]{1,0:T(8,128)(2,1)} %param.11), channel_id=1, source_target_pairs={{0,4},{1,0},{2,6},{3,2},{4,5},{5,1},{6,7},{7,3},{8,12},{9,8},{10,1... | collective-permute-start | bytes 3145736 | tf_op jit(solution)/shard_map/ppermute | solution.py:232
  124.2 56.3 %collective-permute-start.28 = (bf16[512,1024]{1,0:T(8,128)(2,1)}, bf16[512,1024]{1,0:T(8,128)(2,1)}, u32[]{:S(2)}, u32[]{:S(2)}) collective-permute-start(bf16[512,1024]{1,0:T(8,128)(2,1)} %param.11), channel_id=1, source_target_pairs={{0,6},{1,2},{2,4},{3,0},{4,7},{5,3},{6,5},{7,1},{8,14},{9,10},{10,... | collective-permute-start | bytes 3145736 | tf_op jit(solution)/shard_map/ppermute | solution.py:232
  185.0 98.9 %all-gather.2.cloned.1.call-start = ((), (), s32[]{:S(2)}) async-start(), calls=%async_computation | async-start | bytes 1966080 | tf_op jit(solution)/shard_map/all_gather | solution.py:281
  185.1 10.6 %collective-permute-start.20 = (bf16[192,1024]{1,0:T(8,128)(2,1)S(1)}, bf16[192,1024]{1,0:T(8,128)(2,1)S(1)}, u32[]{:S(2)}, u32[]{:S(2)}) collective-permute-start(bf16[192,1024]{1,0:T(8,128)(2,1)S(1)} %constant_dynamic-slice_fusion.3), channel_id=1, source_target_pairs={{2,0},{0,2},{3,1},{1,3},{6,4},{4,6},{7,5},{5,7},{10,8},{8,10},{11,... | collective-permute-start | bytes 1179656 | tf_op jit(solution)/shard_map/ppermute | solution.py:247
  196.4 154.0 %all-reduce.8.cloned.1.call-start = ((), (), s32[]{:S(2)}) async-start(), calls=%async_computation.2 | async-start | bytes 2097152 | tf_op jit(solution)/shard_map/psum | solution.py:324
  196.5 9.3 %collective-permute-start.13 = (bf16[512,512]{0,1:T(8,128)(2,1)}, bf16[512,512]{0,1:T(8,128)(2,1)S(1)}, u32[]{:S(2)}, u32[]{:S(2)}) collective-permute-start(bf16[512,512]{0,1:T(8,128)(2,1)} %copy.35), channel_id=1, source_target_pairs={{0,0},{4,1},{2,2},{6,3},{1,4},{5,5},{3,6},{7,7},{8,8},{12,9},{10,1... | collective-permute-start | bytes 1572872 | tf_op jit(solution)/shard_map/ppermute | solution.py:235
  198.2 81.8 %collective-permute-start.17 = (bf16[6,256,512]{2,1,0:T(8,128)(2,1)}, bf16[6,256,512]{2,1,0:T(8,128)(2,1)}, u32[]{:S(2)}, u32[]{:S(2)}) collective-permute-start(bf16[6,256,512]{2,1,0:T(8,128)(2,1)} %get-tuple-element.21), channel_id=1, source_target_pairs={{0,1},{1,8},{8,9},{9,16},{16,17},{17,24},{24,25},{2,3},{3,10},{10,... | collective-permute-start | bytes 4718600 | tf_op jit(solution)/shard_map/ppermute | solution.py:211
  203.1 76.9 %collective-permute-start.18 = (bf16[6,256,512]{2,1,0:T(8,128)(2,1)}, bf16[6,256,512]{2,1,0:T(8,128)(2,1)}, u32[]{:S(2)}, u32[]{:S(2)}) collective-permute-start(bf16[6,256,512]{2,1,0:T(8,128)(2,1)} %get-tuple-element.22), channel_id=1, source_target_pairs={{1,0},{8,1},{9,8},{16,9},{17,16},{24,17},{25,24},{3,2},{10,3},{11,... | collective-permute-start | bytes 4718600 | tf_op jit(solution)/shard_map/ppermute | solution.py:211
  204.4 15.1 %collective-permute-start.14 = (bf16[512,512]{0,1:T(8,128)(2,1)}, bf16[512,512]{0,1:T(8,128)(2,1)S(1)}, u32[]{:S(2)}, u32[]{:S(2)}) collective-permute-start(bf16[512,512]{0,1:T(8,128)(2,1)} %copy.36), channel_id=1, source_target_pairs={{2,0},{6,1},{0,2},{4,3},{3,4},{7,5},{1,6},{5,7},{10,8},{14,9},{8,1... | collective-permute-start | bytes 1572872 | tf_op jit(solution)/shard_map/ppermute | solution.py:235
  205.8 14.9 %collective-permute-start.15 = (bf16[512,512]{0,1:T(8,128)(2,1)}, bf16[512,512]{0,1:T(8,128)(2,1)S(1)}, u32[]{:S(2)}, u32[]{:S(2)}) collective-permute-start(bf16[512,512]{0,1:T(8,128)(2,1)} %copy.37), channel_id=1, source_target_pairs={{4,0},{0,1},{6,2},{2,3},{5,4},{1,5},{7,6},{3,7},{12,8},{8,9},{14,1... | collective-permute-start | bytes 1572872 | tf_op jit(solution)/shard_map/ppermute | solution.py:235
  205.8 24.6 %collective-permute-start.16 = (bf16[512,512]{0,1:T(8,128)(2,1)S(1)}, bf16[512,512]{0,1:T(8,128)(2,1)S(1)}, u32[]{:S(2)}, u32[]{:S(2)}) collective-permute-start(bf16[512,512]{0,1:T(8,128)(2,1)S(1)} %copy.38), channel_id=1, source_target_pairs={{6,0},{2,1},{4,2},{0,3},{7,4},{3,5},{5,6},{1,7},{14,8},{10,9},{12,... | collective-permute-start | bytes 1572872 | tf_op jit(solution)/shard_map/ppermute | solution.py:235
  230.6 45.4 %copy-start.13 = (bf16[4,64,1024]{2,1,0:T(8,128)(2,1)S(1)}, bf16[4,64,1024]{2,1,0:T(8,128)(2,1)}, u32[]{:S(2)}) copy-start(bf16[4,64,1024]{2,1,0:T(8,128)(2,1)} %param.9) | copy-start | bytes 1572868
  271.5 31.4 %collective-permute-start.29 = (bf16[512,1024]{1,0:T(8,128)(2,1)}, bf16[512,1024]{1,0:T(8,128)(2,1)}, u32[]{:S(2)}, u32[]{:S(2)}) collective-permute-start(bf16[512,1024]{1,0:T(8,128)(2,1)} %all-reduce.6.cloned.1.call-done), channel_id=1, source_target_pairs={{5,1},{7,3},{0,4},{2,6},{13,9},{15,11},{8,12},{10,14},{21,17},{23,... | collective-permute-start | bytes 3145736 | tf_op jit(solution)/shard_map/ppermute | solution.py:300
  275.9 4.1 %copy-start.7 = (f32[8,256,512]{2,1,0:T(8,128)S(1)}, f32[8,256,512]{2,1,0:T(8,128)}, u32[]{:S(2)}) copy-start(f32[8,256,512]{2,1,0:T(8,128)} %get-tuple-element.20) | copy-start | bytes 12582916
  283.9 3.6 copy-start.14
  283.9 3.6 copy-start.16
  283.9 3.6 copy-start.17
  287.5 87.3 %collective-permute-start.22 = (bf16[1536,1024]{1,0:T(8,128)(2,1)}, bf16[1536,1024]{1,0:T(8,128)(2,1)}, u32[]{:S(2)}, u32[]{:S(2)}) collective-permute-start(bf16[1536,1024]{1,0:T(8,128)(2,1)} %pad_maximum_fusion), channel_id=1, source_target_pairs={{0,1},{1,0},{2,3},{3,2},{4,5},{5,4},{6,7},{7,6},{8,9},{9,8},{10,11... | collective-permute-start | bytes 9437192 | tf_op jit(solution)/shard_map/ppermute | solution.py:250
  293.2 9.6 %copy-start.8 = (bf16[512,1024]{1,0:T(8,128)(2,1)S(1)}, bf16[512,1024]{1,0:T(8,128)(2,1)}, u32[]{:S(2)}) copy-start(bf16[512,1024]{1,0:T(8,128)(2,1)} %all-reduce.6.cloned.1.call-done) | copy-start | bytes 3145732
  296.1 64.3 %collective-permute-start.21 = (bf16[512,512]{1,0:T(8,128)(2,1)}, bf16[512,512]{1,0:T(8,128)(2,1)}, u32[]{:S(2)}, u32[]{:S(2)}) collective-permute-start(bf16[512,512]{1,0:T(8,128)(2,1)} %get-tuple-element.35), channel_id=1, source_target_pairs={{2,0},{6,1},{0,2},{4,3},{3,4},{7,5},{1,6},{5,7},{10,8},{14,9},{8,1... | collective-permute-start | bytes 1572872 | tf_op jit(solution)/shard_map/ppermute | solution.py:235
  297.5 78.9 %collective-permute-start.23 = (bf16[512,512]{1,0:T(8,128)(2,1)}, bf16[512,512]{1,0:T(8,128)(2,1)S(1)}, u32[]{:S(2)}, u32[]{:S(2)}) collective-permute-start(bf16[512,512]{1,0:T(8,128)(2,1)} %get-tuple-element.34), channel_id=1, source_target_pairs={{4,0},{0,1},{6,2},{2,3},{5,4},{1,5},{7,6},{3,7},{12,8},{8,9},{14,1... | collective-permute-start | bytes 1572872 | tf_op jit(solution)/shard_map/ppermute | solution.py:235
  297.5 59.5 %collective-permute-start.19 = (bf16[512,512]{1,0:T(8,128)(2,1)}, bf16[512,512]{1,0:T(8,128)(2,1)}, u32[]{:S(2)}, u32[]{:S(2)}) collective-permute-start(bf16[512,512]{1,0:T(8,128)(2,1)} %get-tuple-element.32), channel_id=1, source_target_pairs={{0,0},{4,1},{2,2},{6,3},{1,4},{5,5},{3,6},{7,7},{8,8},{12,9},{10,1... | collective-permute-start | bytes 1572872 | tf_op jit(solution)/shard_map/ppermute | solution.py:235
  350.4 6.6 %copy-start.15 = (bf16[512,512]{1,0:T(8,128)(2,1)S(1)}, bf16[512,512]{1,0:T(8,128)(2,1)}, u32[]{:S(2)}) copy-start(bf16[512,512]{1,0:T(8,128)(2,1)} %copy-done.14) | copy-start | bytes 1572868
  350.4 21.7 %collective-permute-start.30 = (bf16[512,1024]{1,0:T(8,128)(2,1)}, bf16[512,1024]{1,0:T(8,128)(2,1)S(1)}, u32[]{:S(2)}, u32[]{:S(2)}) collective-permute-start(bf16[512,1024]{1,0:T(8,128)(2,1)} %all-reduce.8.cloned.1.call-done), channel_id=1, source_target_pairs={{5,1},{7,3},{0,4},{2,6},{13,9},{15,11},{8,12},{10,14},{21,17},{23,... | collective-permute-start | bytes 3145736 | tf_op jit(solution)/shard_map/ppermute | solution.py:300
  357.0 21.3 %collective-permute-start.24 = (bf16[512,512]{1,0:T(8,128)(2,1)S(1)}, bf16[512,512]{1,0:T(8,128)(2,1)S(1)}, u32[]{:S(2)}, u32[]{:S(2)}) collective-permute-start(bf16[512,512]{1,0:T(8,128)(2,1)S(1)} %copy-done.15), channel_id=1, source_target_pairs={{6,0},{2,1},{4,2},{0,3},{7,4},{3,5},{5,6},{1,7},{14,8},{10,9},{12,... | collective-permute-start | bytes 1572872 | tf_op jit(solution)/shard_map/ppermute | solution.py:235
  360.4 11.8 %copy-start.9 = (bf16[512,1024]{1,0:T(8,128)(2,1)S(1)}, bf16[512,1024]{1,0:T(8,128)(2,1)}, u32[]{:S(2)}) copy-start(bf16[512,1024]{1,0:T(8,128)(2,1)} %all-reduce.8.cloned.1.call-done) | copy-start | bytes 3145732
  (8 other events, 13.8 us)
Sparse Core Ops, SparseCore 0:
  185.1 86.2 all-reduce.5
  293.4 57.0 all-reduce.7
Sparse Core Ops, SparseCore 1:
  196.5 51.6 all-gather.1

commit v3 on v2

v3 whole, which is shorter than its diff:
```python
import functools
import math
import jax
import jax.numpy as jnp
from jax import lax
from jax.experimental import pallas as pl
from jax.experimental.pallas import tpu as pltpu

HEAD_WIDTH = 64
LONGITUDES = 256
BAND_ROWS = 8
HALO = 6
EXT_ROWS = BAND_ROWS + 2 * HALO
LANES = 256
QUERY_ROWS = 4
KEY_ROWS = QUERY_ROWS + 2 * HALO
BLOCK = 8
BLOCKS = LONGITUDES // BLOCK
KEYS = KEY_ROWS * BLOCK
MASKED = -1e30


def nn(a, b):
    return lax.dot_general(a, b, (((1,), (0,)), ((), ())), preferred_element_type=jnp.float32)


def nt(a, b):
    return lax.dot_general(a, b, (((1,), (1,)), ((), ())), preferred_element_type=jnp.float32)


def row_cols(row, start, size):
    return pl.ds(pl.multiple_of(row * LONGITUDES + start, 16), size)


def attention_kernel(
    heads, steps,
    cells, order, qkv, kv_top, kv_bot, *refs,
):
    go_parts, refs = refs[:steps], refs[steps:]
    outq_parts, refs = refs[:steps], refs[steps:]
    dkv_own, dkv_top, dkv_bot, outq, go, k_s, v_s, kt_s, vt_s, dk_s, dv_s, live_s, near_s, sems = refs
    feats = heads * HEAD_WIDTH
    chunk = BAND_ROWS * LONGITUDES // steps
    moves = [
        pltpu.make_async_copy(part, go.at[pl.ds(pl.multiple_of(order[i], 16), chunk)], sems.at[i])
        for i, part in enumerate(go_parts)
    ]
    for move in moves:
        move.start()
    tile_cols = LANES // heads // QUERY_ROWS
    tile_queries = QUERY_ROWS * tile_cols
    window = tile_cols // BLOCK + 2

    def load_pair(p, carry):
        for first, rows_s, turned_s in ((0, k_s, kt_s), (feats, v_s, vt_s)):
            both = jnp.stack(
                [kv_top[row_cols(row, p * 16, 16), first:first + feats] for row in range(HALO)]
                + [qkv[row_cols(row, p * 16, 16), feats + first:2 * feats + first] for row in range(BAND_ROWS)]
                + [kv_bot[row_cols(row, p * 16, 16), first:first + feats] for row in range(HALO)]
            ).astype(jnp.float32)
            for half in range(2):
                block = both[:, 8 * half:8 * half + 8, :].reshape(EXT_ROWS * BLOCK, feats)
                rows_s[2 * p + half] = block.astype(jnp.bfloat16)
                for upper in range(2):
                    low = upper * QUERY_ROWS * BLOCK
                    turned_s[upper, 2 * p + half] = block[low:low + KEYS].T.astype(jnp.bfloat16)
        for half in range(2):
            col = (2 * p + half) * BLOCK + lax.broadcasted_iota(jnp.int32, (BLOCK, 128), 0)
            for row in range(EXT_ROWS):
                live_s[2 * p + half, row * BLOCK:(row + 1) * BLOCK, :] = jnp.where(col < cells[row], 0.0, MASKED)
        return carry

    lax.fori_loop(0, BLOCKS // 2, load_pair, 0)
    dk_s[...] = jnp.zeros_like(dk_s)
    dv_s[...] = jnp.zeros_like(dv_s)

    lane = lax.broadcasted_iota(jnp.int32, (KEYS, LANES), 1) % tile_queries
    query_row = lane // tile_cols
    query_col = lane % tile_cols
    key = lax.broadcasted_iota(jnp.int32, (KEYS, LANES), 0)
    row_gap = key // BLOCK - query_row
    for j in range(window):
        col_gap = (j - 1) * BLOCK + key % BLOCK - query_col
        near = (row_gap >= 0) & (row_gap <= 2 * HALO) & (col_gap >= -HALO) & (col_gap <= HALO)
        near_s[j] = jnp.where(near, 0.0, MASKED)

    own_head = (
        lax.broadcasted_iota(jnp.int32, (LANES, feats), 0) // tile_queries
        == lax.broadcasted_iota(jnp.int32, (LANES, feats), 1) // HEAD_WIDTH
    )
    own_head_turned = (
        lax.broadcasted_iota(jnp.int32, (feats, LANES), 1) // tile_queries
        == lax.broadcasted_iota(jnp.int32, (feats, LANES), 0) // HEAD_WIDTH
    )
    query_lane = lax.broadcasted_iota(jnp.int32, (1, LANES), 1) % tile_queries

    def spread(ref, upper, start):
        tile = jnp.concatenate([
            ref[row_cols(upper * QUERY_ROWS + row, start, tile_cols), :feats] for row in range(QUERY_ROWS)
        ], axis=0)
        if heads == 1:
            return tile
        stacked = jnp.concatenate([tile] * heads, axis=0)
        return jnp.where(own_head, stacked, jnp.zeros_like(stacked))

    def gather(turned):
        if heads == 1:
            tile = turned.T
        else:
            tall = jnp.where(own_head_turned, turned, 0.0).T
            tile = sum(tall[h * tile_queries:(h + 1) * tile_queries] for h in range(heads))
        return tile.astype(jnp.bfloat16)

    def one_tile(upper, tile):
        start = pl.multiple_of(tile * tile_cols, 16)
        keys = pl.ds(upper * QUERY_ROWS * BLOCK, KEYS)
        index = [(tile * (tile_cols // BLOCK) + j + BLOCKS - 1) % BLOCKS for j in range(window)]
        queries = spread(qkv, upper, start)
        grads = spread(go, upper, start)
        scores = [
            nt(k_s[index[j], keys, :], queries)
            + near_s[j]
            + jnp.concatenate([live_s[index[j], keys, :]] * (LANES // 128), axis=1)
            for j in range(window)
        ]
        highest = jnp.max(functools.reduce(jnp.maximum, scores), axis=0, keepdims=True)
        terms = [jnp.exp(score - highest) for score in scores]
        total = jnp.sum(sum(terms), axis=0, keepdims=True)
        query_cells = jnp.zeros((1, LANES), jnp.int32)
        for row in range(QUERY_ROWS):
            cell = cells[HALO + upper * QUERY_ROWS + row]
            query_cells = jnp.where(query_lane // tile_cols == row, cell, query_cells)
        live = start + query_lane % tile_cols < query_cells
        inverse = jnp.where(live, 1.0 / total, 0.0)
        probs = [term * inverse for term in terms]
        grad_probs = [nt(v_s[index[j], keys, :], grads) for j in range(window)]
        delta = jnp.sum(sum(p * g for p, g in zip(probs, grad_probs)), axis=0, keepdims=True)
        weights = [p.astype(jnp.bfloat16) for p in probs]
        grad_scores = [(p * (g - delta)).astype(jnp.bfloat16) for p, g in zip(probs, grad_probs)]
        for j in range(window):
            dv_s[index[j], keys, :] += nn(weights[j], grads)
            dk_s[index[j], keys, :] += nn(grad_scores[j], queries)
        values_turned = jnp.concatenate([vt_s[upper, index[j]] for j in range(window)], axis=1)
        keys_turned = jnp.concatenate([kt_s[upper, index[j]] for j in range(window)], axis=1)
        heads_out = gather(nn(values_turned, jnp.concatenate(weights, axis=0)))
        grad_query = gather(nn(keys_turned, jnp.concatenate(grad_scores, axis=0)))
        for row in range(QUERY_ROWS):
            at = row_cols(upper * QUERY_ROWS + row, start, tile_cols)
            outq[at, :feats] = heads_out[row * tile_cols:(row + 1) * tile_cols]
            outq[at, feats:] = grad_query[row * tile_cols:(row + 1) * tile_cols]

    def tile_pair(tile, carry):
        for upper in range(2):
            one_tile(upper, tile)
        return carry

    for move in moves:
        move.wait()
    lax.fori_loop(0, LONGITUDES // tile_cols, tile_pair, 0)
    moves = [
        pltpu.make_async_copy(outq.at[pl.ds(pl.multiple_of(order[i], 16), chunk)], part, sems.at[i])
        for i, part in enumerate(outq_parts)
    ]
    for move in moves:
        move.start()

    def store_pair(p, carry):
        for first, sums in ((0, dk_s), (feats, dv_s)):
            both = jnp.concatenate(
                [sums[2 * p + half].reshape(EXT_ROWS, BLOCK, feats) for half in range(2)], axis=1
            )
            for row in range(HALO):
                dkv_top[row_cols(row, p * 16, 16), first:first + feats] = both[row].astype(jnp.bfloat16)
                dkv_bot[row_cols(row, p * 16, 16), first:first + feats] = (
                    both[HALO + BAND_ROWS + row].astype(jnp.bfloat16)
                )
            for row in range(BAND_ROWS):
                dkv_own[row_cols(row, p * 16, 16), first:first + feats] = both[HALO + row]
        return carry

    lax.fori_loop(0, BLOCKS // 2, store_pair, 0)
    for move in moves:
        move.wait()


VMEM = pl.BlockSpec(memory_space=pltpu.VMEM)
SMEM = pl.BlockSpec(memory_space=pltpu.SMEM)
HBM = pl.BlockSpec(memory_space=pl.ANY)
BF16, F32 = jnp.bfloat16, jnp.float32


def shape(rows, cols, kind=BF16):
    return jax.ShapeDtypeStruct((rows, cols), kind)


def call(kernel, out_shape, in_specs, out_specs, args, flops, scratch=(), transcendentals=0):
    moved = sum(x.size * x.dtype.itemsize for x in (*args, *out_shape))
    return pl.pallas_call(
        kernel,
        out_shape=tuple(out_shape),
        in_specs=list(in_specs),
        out_specs=tuple(out_specs),
        scratch_shapes=list(scratch),
        compiler_params=pltpu.CompilerParams(vmem_limit_bytes=60 * 2**20),
        cost_estimate=pl.CostEstimate(
            flops=flops, transcendentals=transcendentals, bytes_accessed=moved
        ),
    )(*args)


def attention(cells, order, qkv, kv_top, kv_bot, go_parts):
    steps, feats = len(go_parts), go_parts[0].shape[-1]
    heads = feats // HEAD_WIDTH
    window = LANES // heads // QUERY_ROWS // BLOCK + 2
    band, halo, chunk = BAND_ROWS * LONGITUDES, HALO * LONGITUDES, go_parts[0].shape[0]
    pairs = band * heads * KEYS * window
    results = call(
        functools.partial(attention_kernel, heads, steps),
        [shape(chunk, 2 * feats)] * steps
        + [shape(band, 2 * feats, F32), shape(halo, 2 * feats), shape(halo, 2 * feats)],
        [SMEM, SMEM, VMEM, VMEM, VMEM] + [HBM] * steps,
        [HBM] * steps + [VMEM] * 3,
        (cells, order, qkv, kv_top, kv_bot, *go_parts),
        flops=12 * pairs * HEAD_WIDTH * heads,
        transcendentals=pairs,
        scratch=[
            pltpu.VMEM((band, 2 * feats), BF16),
            pltpu.VMEM((band, feats), BF16),
            pltpu.VMEM((BLOCKS, EXT_ROWS * BLOCK, feats), BF16),
            pltpu.VMEM((BLOCKS, EXT_ROWS * BLOCK, feats), BF16),
            pltpu.VMEM((2, BLOCKS, feats, KEYS), BF16),
            pltpu.VMEM((2, BLOCKS, feats, KEYS), BF16),
            pltpu.VMEM((BLOCKS, EXT_ROWS * BLOCK, feats), F32),
            pltpu.VMEM((BLOCKS, EXT_ROWS * BLOCK, feats), F32),
            pltpu.VMEM((BLOCKS, EXT_ROWS * BLOCK, 128), F32),
            pltpu.VMEM((window, KEYS, LANES), F32),
            pltpu.SemaphoreType.DMA((steps,)),
        ],
    )
    return (results[:steps], *results[steps:])


def norm_kernel(tokens, gain, normed):
    features = tokens[...].astype(F32)
    inverse = lax.rsqrt(jnp.mean(features * features, axis=1, keepdims=True) + 1e-06)
    normed[...] = (features * inverse * gain[...]).astype(BF16)


def norm(tokens, gain):
    return call(
        norm_kernel, [shape(*tokens.shape)], [VMEM] * 2, [VMEM], (tokens, gain[None, :]), flops=4 * tokens.size
    )[0]


def grad_heads_kernel(steps, upstream, *refs):
    for block, out in zip(refs[:steps], refs[steps:]):
        out[...] = nt(upstream[...], block[...]).astype(BF16)


def grad_heads_parts(upstream, blocks):
    steps, feats = len(blocks), blocks[0].shape[0]
    return call(
        functools.partial(grad_heads_kernel, steps),
        [shape(upstream.shape[0], feats)] * steps,
        [VMEM] * (1 + steps), [VMEM] * steps, (upstream, *blocks),
        flops=2 * steps * feats * upstream.size,
    )


def projection_kernel(steps, feats, order, weight, *refs):
    parts, (qkv, kv_up, kv_down, held, sems) = refs[:steps], refs[steps:]
    chunk = held.shape[1]
    moves = [pltpu.make_async_copy(part, held.at[i], sems.at[i]) for i, part in enumerate(parts)]
    for move in moves:
        move.start()
    for i, move in enumerate(moves):
        move.wait()
        at = pl.ds(pl.multiple_of(order[i], 16), chunk)
        for first in range(0, 3 * feats, feats):
            qkv[at, first:first + feats] = nt(held[i], weight[first:first + feats, :]).astype(BF16)
    kv_up[...] = qkv[(BAND_ROWS - HALO) * LONGITUDES:, feats:]
    kv_down[...] = qkv[:HALO * LONGITUDES, feats:]


def projections(order, weight, parts):
    steps, feats = len(parts), weight.shape[0] // 3
    chunk, width = parts[0].shape
    band, halo = BAND_ROWS * LONGITUDES, HALO * LONGITUDES
    return call(
        functools.partial(projection_kernel, steps, feats),
        [shape(band, 3 * feats), shape(halo, 2 * feats), shape(halo, 2 * feats)],
        [SMEM, VMEM] + [HBM] * steps, [VMEM] * 3, (order, weight, *parts),
        flops=2 * band * weight.size,
        scratch=[pltpu.VMEM((steps, chunk, width), BF16), pltpu.SemaphoreType.DMA((steps,))],
    )


def join_kernel(steps, order, own, above, below, *refs):
    parts, (whole, sems) = refs[:steps], refs[steps:]
    chunk = parts[0].shape[0]
    low, high = (BAND_ROWS - HALO) * LONGITUDES, HALO * LONGITUDES
    whole[:low] = (own[:low] + below[:low].astype(F32)).astype(BF16)
    whole[low:high] = (own[low:high] + below[low:].astype(F32) + above[:high - low].astype(F32)).astype(BF16)
    whole[high:] = (own[high:] + above[high - low:].astype(F32)).astype(BF16)
    moves = [
        pltpu.make_async_copy(whole.at[pl.ds(pl.multiple_of(order[i], 16), chunk)], part, sems.at[i])
        for i, part in enumerate(parts)
    ]
    for move in moves:
        move.start()
    for move in moves:
        move.wait()


def joined(order, own, above, below, steps):
    band, feats = own.shape
    return call(
        functools.partial(join_kernel, steps),
        [shape(band // steps, feats)] * steps,
        [SMEM] + [VMEM] * 3, [HBM] * steps, (order, own, above, below), flops=2 * own.size,
        scratch=[pltpu.VMEM((band, feats), BF16), pltpu.SemaphoreType.DMA((steps,))],
    )


def weight_grad_kernel(steps, sides, core, *refs):
    lefts, refs = refs[:steps], refs[steps:]
    rights, (keep, give, sums) = [refs[i * steps:(i + 1) * steps] for i in range(sides)], refs[sides * steps:]
    feats = sums.shape[0] // sides
    for side, parts in enumerate(rights):
        at = slice(side * feats, (side + 1) * feats)
        for i, (left, right) in enumerate(zip(lefts, parts)):
            product = lax.dot_general(
                left[:, at], right[...], (((0,), (0,)), ((), ())), preferred_element_type=F32
            )
            sums[at, :] = product if i == 0 else sums[at, :] + product
    half = sums.shape[0] // 2
    mine, other = (pl.ds(pl.multiple_of(at * half, 16), half) for at in (core[0], 1 - core[0]))
    keep[...] = sums[mine, :]
    give[...] = sums[other, :].astype(BF16)


def weight_grad(core, lefts, *rights):
    steps, width = len(lefts), rights[0][0].shape[1]
    rows = lefts[0].shape[1]
    args = (core, *lefts, *(part for parts in rights for part in parts))
    return call(
        functools.partial(weight_grad_kernel, steps, len(rights)),
        [shape(rows // 2, width, F32), shape(rows // 2, width)],
        [SMEM] + [VMEM] * (len(args) - 1), [VMEM] * 2, args,
        flops=2 * steps * lefts[0].size * width,
        scratch=[pltpu.VMEM((rows, width), F32)],
    )


def update_kernel(steps, *refs):
    out = refs[-1]
    feats = refs[steps].shape[0]
    out[...] = sum(nn(part[:, :feats], block[...]) for part, block in zip(refs[:steps], refs[steps:])).astype(BF16)


def updates(outq_own, blocks):
    steps, (feats, width) = len(blocks), blocks[0].shape
    chunk = outq_own[0].shape[0]
    return call(
        functools.partial(update_kernel, steps), [shape(chunk, width)], [VMEM] * (2 * steps), [VMEM],
        (*outq_own, *blocks), flops=2 * steps * chunk * feats * width,
    )[0]


def grad_input_kernel(steps, tokens, gain, *refs):
    outq, dkv, blocks, grad = refs[:steps], refs[steps:2 * steps], refs[2 * steps:3 * steps], refs[-1]
    feats = blocks[0].shape[0] // 3
    grad_normed = sum(
        nn(outq[i][:, feats:], blocks[i][:feats, :]) + nn(dkv[i][...], blocks[i][feats:, :]) for i in range(steps)
    )
    features = tokens[...].astype(F32)
    inverse = lax.rsqrt(jnp.mean(features * features, axis=1, keepdims=True) + 1e-06)
    centred = features * inverse
    scaled = gain[...] * grad_normed
    grad[...] = (inverse * (scaled - centred * jnp.mean(scaled * centred, axis=1, keepdims=True))).astype(BF16)


def grad_inputs(tokens, gain, outq_own, dkv_own, blocks):
    steps = len(blocks)
    return call(
        functools.partial(grad_input_kernel, steps), [shape(*tokens.shape)], [VMEM] * (2 + 3 * steps), [VMEM],
        (tokens, gain[None, :], *outq_own, *dkv_own, *blocks),
        flops=2 * steps * tokens.shape[0] * blocks[0].size,
    )[0]


from jax.sharding import Mesh, PartitionSpec as P

WIDTH = 1024
GROUP = ("y", "m", "c")


def to_bands(halves, step):
    dm, dc = step
    place = lambda y, m, c: (y * halves + m) * 2 + c
    return [
        (place(y, m, c), place((c + dc) % 2, (m + dm) % halves, y))
        for y in range(2) for m in range(halves) for c in range(2)
    ]


def passed_along(x, by):
    length = lax.axis_size("z") * 2
    pairs = [(i, i + by) for i in range(length) if 0 <= i + by < length]
    return lax.ppermute(x, ("z", "c"), pairs)


def after(x, *others):
    return lax.optimization_barrier((x, *others))[0]


def on_device(tokens, gain, qkv_weight, out_weight, row_cells, upstream):
    heads = qkv_weight.shape[0]
    feats = heads * HEAD_WIDTH
    band_tokens = BAND_ROWS * LONGITUDES
    chunk = tokens.shape[0]
    halves, layers = lax.axis_size("m"), lax.axis_size("z")
    z, y, m, c = (lax.axis_index(axis) for axis in ("z",) + GROUP)
    core = jnp.reshape(c, (1,))
    steps = [(dm, dc) for dc in range(2) for dm in range(halves)]
    order = jnp.stack([((m - dm) % halves) * 2 + (y - dc) % 2 for dm, dc in steps]) * chunk
    grad_scale = 4.0 / math.sqrt(band_tokens * layers * 2)
    band_start = (z * 2 + c) * BAND_ROWS
    cells = lax.dynamic_slice_in_dim(jnp.pad(row_cells, (HALO, HALO)), band_start, EXT_ROWS)

    def send(parts):
        return [lax.ppermute(x, GROUP, to_bands(halves, step)) for x, step in zip(parts, steps)]

    def send_back(parts):
        return [
            lax.ppermute(x, GROUP, [(b, a) for a, b in to_bands(halves, step)]) for x, step in zip(parts, steps)
        ]

    def from_ahead(x, dm):
        return lax.ppermute(x, "m", [((i + dm) % halves, i) for i in range(halves)])

    def from_sibling(x):
        return lax.ppermute(x, "c", [(0, 1), (1, 0)])

    out_blocks = [out_weight.reshape(feats, WIDTH)]
    out_blocks += [from_ahead(out_blocks[0], dm) for dm in range(1, halves)]
    normed_parts = send([norm(tokens, gain)] * len(steps))
    out_blocks += [from_sibling(block) for block in out_blocks]

    split = qkv_weight.reshape(heads, 3, HEAD_WIDTH, WIDTH).transpose(1, 0, 2, 3).reshape(3 * feats, WIDTH)
    eighth = jnp.where(jnp.arange(3 * feats) < feats, HEAD_WIDTH ** -0.5, 1.0)[:, None].astype(BF16)
    split = split * eighth
    sibling_split = from_sibling(split)
    grad_heads_own = grad_heads_parts(upstream, out_blocks)

    qkv, kv_up, kv_down = projections(order, jnp.where(c == y, split, sibling_split), normed_parts)
    kv_top, kv_bot = passed_along(kv_up, 1), passed_along(kv_down, -1)
    grad_heads = send([after(part, qkv) for part in grad_heads_own])

    upstream_parts = send([after(upstream, *grad_heads)] * len(steps))
    share = 3 * feats // layers
    held = after(lax.dynamic_slice_in_dim(split, z * share, share, 0), kv_top, kv_bot)
    split_blocks = [split]
    split_blocks += [lax.all_gather(from_ahead(held, dm), "z", axis=0, tiled=True) for dm in range(1, halves)]
    split_blocks += [sibling_split] + [from_sibling(block) for block in split_blocks[1:]]

    outq_parts, dkv, dkv_top, dkv_bot = attention(cells, order, qkv, kv_top, kv_bot, grad_heads)

    from_above, from_below = passed_along(dkv_top, -1), passed_along(dkv_bot, 1)
    outq_own = send_back(outq_parts)
    early = weight_grad(core, outq_parts, upstream_parts, normed_parts)
    dkv_parts = joined(order, dkv, from_above, from_below, len(steps))
    dkv_own = send_back(dkv_parts)
    late = weight_grad(core, dkv_parts, normed_parts)

    update = updates(outq_own, out_blocks)
    grad_input = grad_inputs(tokens, gain, outq_own, dkv_own, split_blocks)

    def reduced(keep, give):
        both = (keep + from_sibling(give).astype(F32)).astype(BF16)
        return lax.psum(both, "z")

    def spread(half):
        other = from_sibling(half)
        whole = jnp.concatenate([jnp.where(c == 0, half, other), jnp.where(c == 0, other, half)], axis=0)
        pairs = [
            ((1 - y) * halves * 2 + m * 2 + 1 - y, y * halves * 2 + m * 2 + 1 - y)
            for y in range(2) for m in range(halves)
        ]
        return jnp.where(c == y, whole, lax.ppermute(whole, GROUP, pairs)).astype(F32)

    early_half = reduced(*early)
    late_half = reduced(after(late[0], early_half), late[1])
    early, late = spread(early_half), spread(late_half) * grad_scale
    by_head = lambda x: x.reshape(heads, HEAD_WIDTH, WIDTH)
    grad_out = by_head(early[:feats] * grad_scale)
    grad_query = early[feats:] * (grad_scale * HEAD_WIDTH ** -0.5)
    grad_qkv = jnp.concatenate([by_head(grad_query), by_head(late[:feats]), by_head(late[feats:])], axis=1)
    return update, grad_input, grad_qkv, grad_out


def solution(mesh):
    devices = mesh.devices.reshape(mesh.shape["lat"] // 2, 2, mesh.shape["mp"] // 2, 2)
    tokens, weights = P(("z", "y", "m", "c"), None), P(("m", "c"), None, None)
    return jax.shard_map(
        on_device,
        mesh=Mesh(devices, ("z", "y", "m", "c")),
        in_specs=(tokens, P(), weights, weights, P(), tokens),
        out_specs=(tokens, tokens, weights, weights),
        check_vma=False,
    )
```

time: 395 us -> 357 us (0.904)
  Pallas kernels: 40.9 us -> 90.3 us
  matrix products: 43.5 us -> 0 us
  waiting for transfers between devices: 169 us -> 132 us
  starting transfers between devices: 69.4 us -> 100 us
  local copies, waits for them, and re-layouts: 32.6 us -> 5.82 us
  other arithmetic: 20.6 us -> 13.1 us
    pallas_call x1 -> x9, Pallas kernels: 40.9 us -> 90.3 us  [call(): pl.pallas_call(kernel, out_shape=tuple(out_shape), in_specs=list(in_specs...]
    dot_general x17 -> x0, matrix products: 43.5 us -> none  [the longest x9 20.1 us: nn(): lax.dot_general(a, b, (((1,), (0,)), ((), ())), preferred_element_type=jn...]
    psum x2, waiting for transfers between devices: 84.4 us -> 42.8 us  [reduced(): return lax.psum(both, 'z')]
    ppermute x23 -> x22, starting transfers between devices: 51.8 us -> 72.8 us  [the longest x12 37.6 us: send(): lax.ppermute(x, GROUP, to_bands(halves, step))]
    unnamed x51 -> x40, local copies, waits for them, and re-layouts: 17.7 us -> 3.42 us
    ppermute x2, waiting for transfers between devices: 21.5 us -> 8.42 us  [from_ahead(): return lax.ppermute(x, 'm', [((i + dm) % halves, i) for i in range(halves)])]
    ppermute x2 -> x8, starting transfers between devices: 2.2 us -> 11.6 us  [from_sibling(): return lax.ppermute(x, 'c', [(0, 1), (1, 0)])]
    ppermute x23 -> x22, waiting for transfers between devices: 62.7 us -> 70.2 us  [the longest x12 46.9 us: send(): lax.ppermute(x, GROUP, to_bands(halves, step))]
  transfers between devices with their start and end apart: 34 -> 39, of which waited for: 11 -> 16; matrix products, arithmetic and copies ran while one was open for 20% -> 3% of each run, Pallas kernels for 10% -> 23%
where the time goes in v3:
time: 357 us; the launch traced here: 355 us
  waiting for transfers between devices  132 us (37%)
  starting transfers between devices  100 us (28%)
  Pallas kernels  90.3 us (25%)
  between operations  14 us (4%)
  other arithmetic  13.1 us (4%)
  local copies, waits for them, and re-layouts  5.82 us (2%)
    pallas_call x9, Pallas kernels, call(): pl.pallas_call(kernel, out_shape=tuple(out_shape), in_specs=list(in_specs...  90.3 us
    ppermute x12, waiting for transfers between devices, send(): lax.ppermute(x, GROUP, to_bands(halves, step))  46.9 us
    psum x2, waiting for transfers between devices, reduced(): return lax.psum(both, 'z')  42.8 us
    ppermute x12, starting transfers between devices, send(): lax.ppermute(x, GROUP, to_bands(halves, step))  37.6 us
    ppermute x2, starting transfers between devices, spread(): lax.ppermute(whole, GROUP, pairs)  28.6 us
    ppermute x8, waiting for transfers between devices, send_back(): lax.ppermute(x, GROUP, [(b, a) for a, b in to_bands(halves, step)])  18.4 us
    ppermute x4, starting transfers between devices, passed_along(): return lax.ppermute(x, ('z', 'c'), pairs)  12.5 us
    ppermute x8, starting transfers between devices, from_sibling(): return lax.ppermute(x, 'c', [(0, 1), (1, 0)])  11.6 us
  transfers between devices with their start and end apart: 39, of which 16 were waited for; matrix products, arithmetic and copies ran while one was open for 3% of the time, Pallas kernels for 23%

profile of v3, /device:TPU:0, one launch (start us, length us, event | category | flops | bytes accessed | tf_op | source)
XLA Modules:
  0.0 355.3 jit_solution(1998767154710011757)
XLA Ops:
  7.2 1.6 copy.10
  9.7 2.6 shard_map.93
  12.3 9.4 %collective-permute-start.1 = (bf16[512,1024]{1,0:T(8,128)(2,1)}, bf16[512,1024]{1,0:T(8,128)(2,1)}, u32[]{:S(2)}, u32[]{:S(2)}) collective-permute-start(bf16[512,1024]{1,0:T(8,128)(2,1)} %shard_map.93), channel_id=1, source_target_pairs={{0,0},{1,4},{2,2},{3,6},{4,1},{5,5},{6,3},{7,7},{8,8},{9,12},{10,1... | collective-permute-start | bytes 3145736 | tf_op jit(solution)/shard_map/ppermute | solution.py:432
  21.7 3.0 collective-permute-start.2
  26.5 1.5 collective-permute-start.7
  28.0 1.5 broadcast_select_fusion.weight
  29.6 19.5 %collective-permute-done.2.refs_1_.refs_9_.refs_5_ = bf16[512,1024]{1,0:T(8,128)(2,1)} collective-permute-done((bf16[512,1024]{1,0:T(8,128)(2,1)}, bf16[512,1024]{1,0:T(8,128)(2,1)}, u32[]{:S(2)}, u32[]{:S(2)}) %collective-permute-start.2) | collective-permute-done | bytes 1048608 | tf_op jit(solution)/shard_map/ppermute | solution.py:432
  49.1 6.1 %collective-permute-done.3.refs_2_.refs_10_.refs_6_ = bf16[512,1024]{1,0:T(8,128)(2,1)} collective-permute-done((bf16[512,1024]{1,0:T(8,128)(2,1)}, bf16[512,1024]{1,0:T(8,128)(2,1)}, u32[]{:S(2)}, u32[]{:S(2)}) %collective-permute-start.3) | collective-permute-done | bytes 1048608 | tf_op jit(solution)/shard_map/ppermute | solution.py:432
  55.2 14.5 %collective-permute-done.4.refs_3_.refs_11_.refs_7_ = bf16[512,1024]{1,0:T(8,128)(2,1)} collective-permute-done((bf16[512,1024]{1,0:T(8,128)(2,1)}, bf16[512,1024]{1,0:T(8,128)(2,1)}, u32[]{:S(2)}, u32[]{:S(2)}) %collective-permute-start.4) | collective-permute-done | bytes 1048608 | tf_op jit(solution)/shard_map/ppermute | solution.py:432
  69.7 10.5 %shard_map.94 = (bf16[2048,768]{1,0:T(8,128)(2,1)}, bf16[1536,512]{1,0:T(8,128)(2,1)}, bf16[1536,512]{1,0:T(8,128)(2,1)}) custom-call(s32[4]{0:T(128)} %add_multiply_fusion.order, bf16[768,1024]{1,0:T(8,128)(2,1)} %broadcast_select_fusion.weight, bf16[512,1024]{1,0:T(8,128)(2,1)} %collective-permute-done.1.refs_0_.refs_8_.refs_4_, ...), custom_call_target="tpu_custom_call" | custom-call | flops 3221225472 | bytes 12058640 | tf_op jit(solution)/shard_map/pallas_call | solution.py:198
  80.2 5.3 %collective-permute-start.5 = (bf16[1536,512]{1,0:T(8,128)(2,1)}, bf16[1536,512]{1,0:T(8,128)(2,1)}, u32[]{:S(2)}, u32[]{:S(2)}) collective-permute-start(bf16[1536,512]{1,0:T(8,128)(2,1)} %get-tuple-element.34), channel_id=1, source_target_pairs={{0,1},{1,8},{8,9},{9,16},{16,17},{17,24},{24,25},{2,3},{3,10},{10,... | collective-permute-start | bytes 4718600 | tf_op jit(solution)/shard_map/ppermute | solution.py:410
  88.1 3.0 collective-permute-done.8.refs_2_.refs_6_
  91.1 1.4 collective-permute-done.9.refs_3_.refs_7_
  93.3 3.9 %shard_map.95 = (bf16[512,256]{1,0:T(8,128)(2,1)}, bf16[512,256]{1,0:T(8,128)(2,1)}, bf16[512,256]{1,0:T(8,128)(2,1)}, bf16[512,256]{1,0:T(8,128)(2,1)}) custom-call(bf16[512,1024]{1,0:T(8,128)(2,1)} %upstream.1, bf16[256,1024]{1,0:T(8,128)(2,1)} %bitcast.24, bf16[256,1024]{1,0:T(8,128)(2,1)} %collective-permute-done.7.refs_1_.refs_5_, ...), custom_call_target="tpu_custom_call" | custom-call | flops 1073741824 | bytes 4194304 | tf_op jit(solution)/shard_map/pallas_call | solution.py:198
  97.2 1.6 collective-permute-start.10
  98.8 1.5 collective-permute-start.11
  100.3 1.8 collective-permute-start.12
  102.1 8.2 %collective-permute-start.13 = (bf16[512,256]{1,0:T(8,128)(2,1)}, bf16[512,256]{1,0:T(8,128)(2,1)S(1)}, u32[]{:S(2)}, u32[]{:S(2)}) collective-permute-start(bf16[512,256]{1,0:T(8,128)(2,1)} %get-tuple-element.43), channel_id=1, source_target_pairs={{0,6},{1,2},{2,4},{3,0},{4,7},{5,3},{6,5},{7,1},{8,14},{9,10},{10,... | collective-permute-start | bytes 786440 | tf_op jit(solution)/shard_map/ppermute | solution.py:432
  111.0 6.7 %collective-permute-done.13.refs_3_ = bf16[512,256]{1,0:T(8,128)(2,1)S(1)} collective-permute-done((bf16[512,256]{1,0:T(8,128)(2,1)}, bf16[512,256]{1,0:T(8,128)(2,1)S(1)}, u32[]{:S(2)}, u32[]{:S(2)}) %collective-permute-start.13) | collective-permute-done | bytes 262176 | tf_op jit(solution)/shard_map/ppermute | solution.py:432
  117.7 9.5 %collective-permute-start.26 = (bf16[512,1024]{1,0:T(8,128)(2,1)}, bf16[512,1024]{1,0:T(8,128)(2,1)}, u32[]{:S(2)}, u32[]{:S(2)}) collective-permute-start(bf16[512,1024]{1,0:T(8,128)(2,1)} %upstream.1), channel_id=1, source_target_pairs={{0,0},{1,4},{2,2},{3,6},{4,1},{5,5},{6,3},{7,7},{8,8},{9,12},{10,1... | collective-permute-start | bytes 3145736 | tf_op jit(solution)/shard_map/ppermute | solution.py:432
  127.2 1.3 collective-permute-start.29
  128.5 40.7 %shard_map.96 = (bf16[512,512]{1,0:T(8,128)(2,1)}, bf16[512,512]{1,0:T(8,128)(2,1)}, bf16[512,512]{1,0:T(8,128)(2,1)}, bf16[512,512]{1,0:T(8,128)(2,1)}, f32[204...) custom-call(s32[20]{0:T(128)} %pad_dynamic-slice_fusion.cells, s32[4]{0:T(128)} %add_multiply_fusion.order, ...), custom_call_target="tpu_custom_call" | custom-call | flops 12884901888 | bytes 16777312 | tf_op jit(solution)/shard_map/pallas_call | solution.py:198
  170.5 4.6 %collective-permute-start.19 = (bf16[1536,512]{1,0:T(8,128)(2,1)}, bf16[1536,512]{1,0:T(8,128)(2,1)}, u32[]{:S(2)}, u32[]{:S(2)}) collective-permute-start(bf16[1536,512]{1,0:T(8,128)(2,1)} %get-tuple-element.50), channel_id=1, source_target_pairs={{0,1},{1,8},{8,9},{9,16},{16,17},{17,24},{24,25},{2,3},{3,10},{10,... | collective-permute-start | bytes 4718600 | tf_op jit(solution)/shard_map/ppermute | solution.py:410
  175.1 7.6 %shard_map.100 = (f32[256,1024]{1,0:T(8,128)}, bf16[256,1024]{1,0:T(8,128)(2,1)}) custom-call(s32[1]{0:T(128)} %bitcast.9.core, bf16[512,512]{1,0:T(8,128)(2,1)} %get-tuple-element.44.refs_0_, bf16[512,512]{1,0:T(8,128)(2,1)} %get-tuple-element.45.refs_1_, bf16[512,512]{1,0:T(8,128)(2,1)} %get-tuple-element.46.refs_2_, ...), custom_call_target="tpu_custom_call" | custom-call | flops 2147483648 | bytes 12058628 | tf_op jit(solution)/shard_map/pallas_call | solution.py:198
  183.4 1.7 collective-permute-done.30
  185.2 2.2 add_convert_fusion.1
  188.6 5.1 %shard_map.98 = (bf16[512,512]{1,0:T(8,128)(2,1)}, bf16[512,512]{1,0:T(8,128)(2,1)}, bf16[512,512]{1,0:T(8,128)(2,1)}, bf16[512,512]{1,0:T(8,128)(2,1)}) custom-call(s32[4]{0:T(128)} %add_multiply_fusion.order, f32[2048,512]{1,0:T(8,128)} %get-tuple-element.48.own, bf16[1536,512]{1,0:T(8,128)(2,1)} %copy-done.3, bf16[1536,512]{1,0:T(8,128)(2,1)} %collective-permute-done.19.below), custom_call_target="tpu_custom_call" | custom-call | flops 2097152 | bytes 9437200 | tf_op jit(solution)/shard_map/pallas_call | solution.py:198
  193.7 6.4 %shard_map.101 = (f32[256,1024]{1,0:T(8,128)}, bf16[256,1024]{1,0:T(8,128)(2,1)}) custom-call(s32[1]{0:T(128)} %bitcast.9.core, bf16[512,512]{1,0:T(8,128)(2,1)} %get-tuple-element.51.refs_0_, bf16[512,512]{1,0:T(8,128)(2,1)} %get-tuple-element.52.refs_1_, bf16[512,512]{1,0:T(8,128)(2,1)} %get-tuple-element.53.refs_2_, ...), custom_call_target="tpu_custom_call" | custom-call | flops 2147483648 | bytes 7864324 | tf_op jit(solution)/shard_map/pallas_call | solution.py:198
  200.1 9.0 %collective-permute-start.33 = (bf16[256,1024]{1,0:T(8,128)(2,1)}, bf16[256,1024]{1,0:T(8,128)(2,1)S(1)}, u32[]{:S(2)}, u32[]{:S(2)}) collective-permute-start(bf16[256,1024]{1,0:T(8,128)(2,1)} %get-tuple-element.61), channel_id=1, source_target_pairs={{0,1},{1,0},{2,3},{3,2},{4,5},{5,4},{6,7},{7,6},{8,9},{9,8},{10,11... | collective-permute-start | bytes 1572872 | tf_op jit(solution)/shard_map/ppermute | solution.py:443
  209.0 14.8 %all-reduce.4.cloned.1.call-done = bf16[256,1024]{1,0:T(8,128)(2,1)} async-done(((bf16[256,1024]{1,0:T(8,128)(2,1)}), bf16[256,1024]{1,0:T(8,128)(2,1)}) %all-reduce.4.cloned.1.call-update) | async-done | bytes 524304 | tf_op jit(solution)/shard_map/psum | solution.py:481
  223.8 2.2 add_convert_fusion
  226.2 1.5 collective-permute-start.24
  227.7 8.4 %collective-permute-done.24 = bf16[192,1024]{1,0:T(8,128)(2,1)S(1)} collective-permute-done((bf16[192,1024]{1,0:T(8,128)(2,1)S(1)}, bf16[192,1024]{1,0:T(8,128)(2,1)S(1)}, u32[]{:S(2)}, u32[]{:S(2)}) %collective-permute-start.24) | collective-permute-done | bytes 393248 | tf_op jit(solution)/shard_map/ppermute | solution.py:440
  237.0 28.0 %all-reduce.6.cloned.1.call-done = bf16[256,1024]{1,0:T(8,128)(2,1)} async-done(((bf16[256,1024]{1,0:T(8,128)(2,1)}), bf16[256,1024]{1,0:T(8,128)(2,1)}) %all-reduce.6.cloned.1.call-update) | async-done | bytes 524304 | tf_op jit(solution)/shard_map/psum | solution.py:481
  266.2 4.4 %collective-permute-start.32 = (bf16[512,1024]{1,0:T(8,128)(2,1)}, bf16[512,1024]{1,0:T(8,128)(2,1)}, u32[]{:S(2)}, u32[]{:S(2)}) collective-permute-start(bf16[512,1024]{1,0:T(8,128)(2,1)} %pad_maximum_fusion.1), channel_id=1, source_target_pairs={{5,1},{7,3},{0,4},{2,6},{13,9},{15,11},{8,12},{10,14},{21,17},{23,... | collective-permute-start | bytes 3145736 | tf_op jit(solution)/shard_map/ppermute | solution.py:490
  270.5 1.7 collective-permute-start.14
  272.2 1.5 collective-permute-start.15
  275.2 24.2 %collective-permute-start.35 = (bf16[512,1024]{1,0:T(8,128)(2,1)}, bf16[512,1024]{1,0:T(8,128)(2,1)}, u32[]{:S(2)}, u32[]{:S(2)}) collective-permute-start(bf16[512,1024]{1,0:T(8,128)(2,1)} %pad_maximum_fusion.2), channel_id=1, source_target_pairs={{5,1},{7,3},{0,4},{2,6},{13,9},{15,11},{8,12},{10,14},{21,17},{23,... | collective-permute-start | bytes 3145736 | tf_op jit(solution)/shard_map/ppermute | solution.py:490
  299.4 4.3 %all-gather.2.cloned.1.call-done.refs_9_ = bf16[768,1024]{1,0:T(8,128)(2,1)} async-done(((bf16[192,1024]{1,0:T(8,128)(2,1)}), bf16[768,1024]{1,0:T(8,128)(2,1)}) %all-gather.2.cloned.1.call-update) | async-done | bytes 1572880 | tf_op jit(solution)/shard_map/all_gather | solution.py:464
  303.7 3.4 collective-permute-done.16.refs_2_
  307.1 4.4 %shard_map.97 = bf16[512,1024]{1,0:T(8,128)(2,1)} custom-call(bf16[512,512]{1,0:T(8,128)(2,1)} %copy-done.1, bf16[512,512]{1,0:T(8,128)(2,1)} %copy-done.2, bf16[512,512]{1,0:T(8,128)(2,1)} %collective-permute-done.16.refs_2_, bf16[512,512]{1,0:T(8,128)(2,1)} %collective-permute-done.17.refs_3_, bf16[256,1024]{1,0:T(8,128)(2,1)} %bitcast.25, ...), custom_call_target="tpu_custom_call" | custom-call | flops 1073741824 | bytes 5242880 | tf_op jit(solution)/shard_map/pallas_call | solution.py:198
  311.5 1.7 collective-permute-start.20
  313.2 1.5 collective-permute-start.21
  316.2 4.9 %collective-permute-done.35 = bf16[512,1024]{1,0:T(8,128)(2,1)} collective-permute-done((bf16[512,1024]{1,0:T(8,128)(2,1)}, bf16[512,1024]{1,0:T(8,128)(2,1)}, u32[]{:S(2)}, u32[]{:S(2)}) %collective-permute-start.35) | collective-permute-done | bytes 1048608 | tf_op jit(solution)/shard_map/ppermute | solution.py:490
  321.7 2.1 pad_maximum_fusion
  323.8 4.4 %collective-permute-done.21.refs_5_ = bf16[512,512]{1,0:T(8,128)(2,1)S(1)} collective-permute-done((bf16[512,512]{1,0:T(8,128)(2,1)}, bf16[512,512]{1,0:T(8,128)(2,1)S(1)}, u32[]{:S(2)}, u32[]{:S(2)}) %collective-permute-start.21) | collective-permute-done | bytes 524320 | tf_op jit(solution)/shard_map/ppermute | solution.py:436
  328.2 10.6 %collective-permute-done.22.refs_6_ = bf16[512,512]{1,0:T(8,128)(2,1)S(1)} collective-permute-done((bf16[512,512]{1,0:T(8,128)(2,1)}, bf16[512,512]{1,0:T(8,128)(2,1)S(1)}, u32[]{:S(2)}, u32[]{:S(2)}) %collective-permute-start.22) | collective-permute-done | bytes 524320 | tf_op jit(solution)/shard_map/ppermute | solution.py:436
  339.6 9.2 %shard_map.99 = bf16[512,1024]{1,0:T(8,128)(2,1)} custom-call(bf16[512,1024]{1,0:T(8,128)(2,1)} %tokens.3, f32[1,1024]{1,0:T(1,128)} %bitcast.28, bf16[512,512]{1,0:T(8,128)(2,1)} %copy-done.1, bf16[512,512]{1,0:T(8,128)(2,1)} %copy-done.2, bf16[512,512]{1,0:T(8,128)(2,1)} %collective-permute-done.16.refs_2_, ...), custom_call_target="tpu_custom_call" | custom-call | flops 3221225472 | bytes 12587008 | tf_op jit(solution)/shard_map/pallas_call | solution.py:198
  (100 shorter events, 16.4 us)
Async XLA Ops:
  7.2 216.6 %all-reduce.4.cloned.1.call-start = ((), (), s32[]{:S(2)}) async-start(), calls=%async_computation.1 | async-start | bytes 1048576 | tf_op jit(solution)/shard_map/psum | solution.py:481
  9.1 217.0 %copy-start = (bf16[768,1024]{1,0:T(8,128)(2,1)}, bf16[768,1024]{1,0:T(8,128)(2,1)S(1)}, u32[]{:S(2)}) copy-start(bf16[768,1024]{1,0:T(8,128)(2,1)S(1)} %bitcast_multiply_fusion.refs_8_) | copy-start | bytes 4718596
  9.1 17.4 %collective-permute-start = (bf16[768,1024]{1,0:T(8,128)(2,1)S(1)}, bf16[768,1024]{1,0:T(8,128)(2,1)}, u32[]{:S(2)}, u32[]{:S(2)}) collective-permute-start(bf16[768,1024]{1,0:T(8,128)(2,1)S(1)} %bitcast_multiply_fusion.refs_8_), channel_id=1, source_target_pairs={{0,1},{1,0},{2,3},{3,2},{4,5},{5,4},{6,7},{7,6},{8,9},{9,8},{10,11... | collective-permute-start | bytes 4718600 | tf_op jit(solution)/shard_map/ppermute | solution.py:443
  12.3 17.3 %collective-permute-start.1 = (bf16[512,1024]{1,0:T(8,128)(2,1)}, bf16[512,1024]{1,0:T(8,128)(2,1)}, u32[]{:S(2)}, u32[]{:S(2)}) collective-permute-start(bf16[512,1024]{1,0:T(8,128)(2,1)} %shard_map.93), channel_id=1, source_target_pairs={{0,0},{1,4},{2,2},{3,6},{4,1},{5,5},{6,3},{7,7},{8,8},{9,12},{10,1... | collective-permute-start | bytes 3145736 | tf_op jit(solution)/shard_map/ppermute | solution.py:432
  21.7 27.4 %collective-permute-start.2 = (bf16[512,1024]{1,0:T(8,128)(2,1)}, bf16[512,1024]{1,0:T(8,128)(2,1)}, u32[]{:S(2)}, u32[]{:S(2)}) collective-permute-start(bf16[512,1024]{1,0:T(8,128)(2,1)} %shard_map.93), channel_id=1, source_target_pairs={{0,2},{1,6},{2,0},{3,4},{4,3},{5,7},{6,1},{7,5},{8,10},{9,14},{10,... | collective-permute-start | bytes 3145736 | tf_op jit(solution)/shard_map/ppermute | solution.py:432
  24.7 30.5 %collective-permute-start.3 = (bf16[512,1024]{1,0:T(8,128)(2,1)}, bf16[512,1024]{1,0:T(8,128)(2,1)}, u32[]{:S(2)}, u32[]{:S(2)}) collective-permute-start(bf16[512,1024]{1,0:T(8,128)(2,1)} %shard_map.93), channel_id=1, source_target_pairs={{0,4},{1,0},{2,6},{3,2},{4,5},{5,1},{6,7},{7,3},{8,12},{9,8},{10,1... | collective-permute-start | bytes 3145736 | tf_op jit(solution)/shard_map/ppermute | solution.py:432
  24.7 45.0 %collective-permute-start.4 = (bf16[512,1024]{1,0:T(8,128)(2,1)}, bf16[512,1024]{1,0:T(8,128)(2,1)}, u32[]{:S(2)}, u32[]{:S(2)}) collective-permute-start(bf16[512,1024]{1,0:T(8,128)(2,1)} %shard_map.93), channel_id=1, source_target_pairs={{0,6},{1,2},{2,4},{3,0},{4,7},{5,3},{6,5},{7,1},{8,14},{9,10},{10,... | collective-permute-start | bytes 3145736 | tf_op jit(solution)/shard_map/ppermute | solution.py:432
  26.5 61.5 %collective-permute-start.7 = (bf16[256,1024]{1,0:T(8,128)(2,1)}, bf16[256,1024]{1,0:T(8,128)(2,1)}, u32[]{:S(2)}, u32[]{:S(2)}) collective-permute-start(bf16[256,1024]{1,0:T(8,128)(2,1)} %bitcast.23), channel_id=1, source_target_pairs={{2,0},{0,2},{3,1},{1,3},{6,4},{4,6},{7,5},{5,7},{10,8},{8,10},{11,... | collective-permute-start | bytes 1572872 | tf_op jit(solution)/shard_map/ppermute | solution.py:440
  29.6 57.3 %copy-start.4 = (bf16[4,64,1024]{2,1,0:T(8,128)(2,1)S(1)}, bf16[4,64,1024]{2,1,0:T(8,128)(2,1)}, u32[]{:S(2)}) copy-start(bf16[4,64,1024]{2,1,0:T(8,128)(2,1)} %param.9) | copy-start | bytes 1572868
  80.2 30.2 %copy-start.19 = (s32[64]{0:T(128)S(1)}, s32[64]{0:T(128)}, u32[]{:S(2)}) copy-start(s32[64]{0:T(128)} %param.10) | copy-start | bytes 772
  80.2 46.9 %collective-permute-start.5 = (bf16[1536,512]{1,0:T(8,128)(2,1)}, bf16[1536,512]{1,0:T(8,128)(2,1)}, u32[]{:S(2)}, u32[]{:S(2)}) collective-permute-start(bf16[1536,512]{1,0:T(8,128)(2,1)} %get-tuple-element.34), channel_id=1, source_target_pairs={{0,1},{1,8},{8,9},{9,16},{16,17},{17,24},{24,25},{2,3},{3,10},{10,... | collective-permute-start | bytes 4718600 | tf_op jit(solution)/shard_map/ppermute | solution.py:410
  85.5 42.9 %collective-permute-start.6 = (bf16[1536,512]{1,0:T(8,128)(2,1)}, bf16[1536,512]{1,0:T(8,128)(2,1)}, u32[]{:S(2)}, u32[]{:S(2)}) collective-permute-start(bf16[1536,512]{1,0:T(8,128)(2,1)} %get-tuple-element.35), channel_id=1, source_target_pairs={{1,0},{8,1},{9,8},{16,9},{17,16},{24,17},{25,24},{3,2},{10,3},{11,... | collective-permute-start | bytes 4718600 | tf_op jit(solution)/shard_map/ppermute | solution.py:410
  86.8 4.3 %collective-permute-start.8 = (bf16[256,1024]{1,0:T(8,128)(2,1)S(1)}, bf16[256,1024]{1,0:T(8,128)(2,1)S(1)}, u32[]{:S(2)}, u32[]{:S(2)}) collective-permute-start(bf16[256,1024]{1,0:T(8,128)(2,1)S(1)} %bitcast.26), channel_id=1, source_target_pairs={{0,1},{1,0},{2,3},{3,2},{4,5},{5,4},{6,7},{7,6},{8,9},{9,8},{10,11... | collective-permute-start | bytes 1572872 | tf_op jit(solution)/shard_map/ppermute | solution.py:443
  88.0 4.5 %collective-permute-start.9 = (bf16[256,1024]{1,0:T(8,128)(2,1)}, bf16[256,1024]{1,0:T(8,128)(2,1)S(1)}, u32[]{:S(2)}, u32[]{:S(2)}) collective-permute-start(bf16[256,1024]{1,0:T(8,128)(2,1)} %collective-permute-done.7.refs_1_.refs_5_), channel_id=1, source_target_pairs={{0,1},{1,0},{2,3},{3,2},{4,5},{5,4},{6,7},{7,6},{8,9},{9,8},{10,11... | collective-permute-start | bytes 1572872 | tf_op jit(solution)/shard_map/ppermute | solution.py:443
  97.2 4.9 %collective-permute-start.10 = (bf16[512,256]{1,0:T(8,128)(2,1)}, bf16[512,256]{1,0:T(8,128)(2,1)S(1)}, u32[]{:S(2)}, u32[]{:S(2)}) collective-permute-start(bf16[512,256]{1,0:T(8,128)(2,1)} %get-tuple-element.37), channel_id=1, source_target_pairs={{0,0},{1,4},{2,2},{3,6},{4,1},{5,5},{6,3},{7,7},{8,8},{9,12},{10,1... | collective-permute-start | bytes 786440 | tf_op jit(solution)/shard_map/ppermute | solution.py:432
  98.8 12.2 %collective-permute-start.11 = (bf16[512,256]{1,0:T(8,128)(2,1)}, bf16[512,256]{1,0:T(8,128)(2,1)S(1)}, u32[]{:S(2)}, u32[]{:S(2)}) collective-permute-start(bf16[512,256]{1,0:T(8,128)(2,1)} %get-tuple-element.39), channel_id=1, source_target_pairs={{0,2},{1,6},{2,0},{3,4},{4,3},{5,7},{6,1},{7,5},{8,10},{9,14},{10,... | collective-permute-start | bytes 786440 | tf_op jit(solution)/shard_map/ppermute | solution.py:432
  100.3 10.7 %collective-permute-start.12 = (bf16[512,256]{1,0:T(8,128)(2,1)}, bf16[512,256]{1,0:T(8,128)(2,1)S(1)}, u32[]{:S(2)}, u32[]{:S(2)}) collective-permute-start(bf16[512,256]{1,0:T(8,128)(2,1)} %get-tuple-element.41), channel_id=1, source_target_pairs={{0,4},{1,0},{2,6},{3,2},{4,5},{5,1},{6,7},{7,3},{8,12},{9,8},{10,1... | collective-permute-start | bytes 786440 | tf_op jit(solution)/shard_map/ppermute | solution.py:432
  102.1 26.4 %copy-start.15 = (bf16[512,256]{1,0:T(8,128)(2,1)}, bf16[512,256]{1,0:T(8,128)(2,1)S(1)}, u32[]{:S(2)}) copy-start(bf16[512,256]{1,0:T(8,128)(2,1)S(1)} %collective-permute-done.10.refs_0_) | copy-start | bytes 786436
  102.1 15.6 %collective-permute-start.13 = (bf16[512,256]{1,0:T(8,128)(2,1)}, bf16[512,256]{1,0:T(8,128)(2,1)S(1)}, u32[]{:S(2)}, u32[]{:S(2)}) collective-permute-start(bf16[512,256]{1,0:T(8,128)(2,1)} %get-tuple-element.43), channel_id=1, source_target_pairs={{0,6},{1,2},{2,4},{3,0},{4,7},{5,3},{6,5},{7,1},{8,14},{9,10},{10,... | collective-permute-start | bytes 786440 | tf_op jit(solution)/shard_map/ppermute | solution.py:432
  111.0 17.5 %copy-start.16 = (bf16[512,256]{1,0:T(8,128)(2,1)}, bf16[512,256]{1,0:T(8,128)(2,1)S(1)}, u32[]{:S(2)}) copy-start(bf16[512,256]{1,0:T(8,128)(2,1)S(1)} %collective-permute-done.11.refs_1_) | copy-start | bytes 786436
  111.0 17.5 %copy-start.17 = (bf16[512,256]{1,0:T(8,128)(2,1)}, bf16[512,256]{1,0:T(8,128)(2,1)S(1)}, u32[]{:S(2)}) copy-start(bf16[512,256]{1,0:T(8,128)(2,1)S(1)} %collective-permute-done.12.refs_2_) | copy-start | bytes 786436
  117.7 52.8 %collective-permute-start.26 = (bf16[512,1024]{1,0:T(8,128)(2,1)}, bf16[512,1024]{1,0:T(8,128)(2,1)}, u32[]{:S(2)}, u32[]{:S(2)}) collective-permute-start(bf16[512,1024]{1,0:T(8,128)(2,1)} %upstream.1), channel_id=1, source_target_pairs={{0,0},{1,4},{2,2},{3,6},{4,1},{5,5},{6,3},{7,7},{8,8},{9,12},{10,1... | collective-permute-start | bytes 3145736 | tf_op jit(solution)/shard_map/ppermute | solution.py:432
  127.2 48.0 %collective-permute-start.27 = (bf16[512,1024]{1,0:T(8,128)(2,1)}, bf16[512,1024]{1,0:T(8,128)(2,1)}, u32[]{:S(2)}, u32[]{:S(2)}) collective-permute-start(bf16[512,1024]{1,0:T(8,128)(2,1)} %upstream.1), channel_id=1, source_target_pairs={{0,2},{1,6},{2,0},{3,4},{4,3},{5,7},{6,1},{7,5},{8,10},{9,14},{10,... | collective-permute-start | bytes 3145736 | tf_op jit(solution)/shard_map/ppermute | solution.py:432
  127.2 48.0 %collective-permute-start.28 = (bf16[512,1024]{1,0:T(8,128)(2,1)}, bf16[512,1024]{1,0:T(8,128)(2,1)}, u32[]{:S(2)}, u32[]{:S(2)}) collective-permute-start(bf16[512,1024]{1,0:T(8,128)(2,1)} %upstream.1), channel_id=1, source_target_pairs={{0,4},{1,0},{2,6},{3,2},{4,5},{5,1},{6,7},{7,3},{8,12},{9,8},{10,1... | collective-permute-start | bytes 3145736 | tf_op jit(solution)/shard_map/ppermute | solution.py:432
  127.2 48.0 %collective-permute-start.29 = (bf16[512,1024]{1,0:T(8,128)(2,1)}, bf16[512,1024]{1,0:T(8,128)(2,1)}, u32[]{:S(2)}, u32[]{:S(2)}) collective-permute-start(bf16[512,1024]{1,0:T(8,128)(2,1)} %upstream.1), channel_id=1, source_target_pairs={{0,6},{1,2},{2,4},{3,0},{4,7},{5,3},{6,5},{7,1},{8,14},{9,10},{10,... | collective-permute-start | bytes 3145736 | tf_op jit(solution)/shard_map/ppermute | solution.py:432
  169.2 18.2 %collective-permute-start.18 = (bf16[1536,512]{1,0:T(8,128)(2,1)}, bf16[1536,512]{1,0:T(8,128)(2,1)S(1)}, u32[]{:S(2)}, u32[]{:S(2)}) collective-permute-start(bf16[1536,512]{1,0:T(8,128)(2,1)} %get-tuple-element.49), channel_id=1, source_target_pairs={{1,0},{8,1},{9,8},{16,9},{17,16},{24,17},{25,24},{3,2},{10,3},{11,... | collective-permute-start | bytes 4718600 | tf_op jit(solution)/shard_map/ppermute | solution.py:410
  170.5 16.9 %collective-permute-start.19 = (bf16[1536,512]{1,0:T(8,128)(2,1)}, bf16[1536,512]{1,0:T(8,128)(2,1)}, u32[]{:S(2)}, u32[]{:S(2)}) collective-permute-start(bf16[1536,512]{1,0:T(8,128)(2,1)} %get-tuple-element.50), channel_id=1, source_target_pairs={{0,1},{1,8},{8,9},{9,16},{16,17},{17,24},{24,25},{2,3},{3,10},{10,... | collective-permute-start | bytes 4718600 | tf_op jit(solution)/shard_map/ppermute | solution.py:410
  182.7 2.5 collective-permute-start.30
  187.4 77.6 %all-reduce.6.cloned.1.call-start = ((), (), s32[]{:S(2)}) async-start(), calls=%async_computation.2 | async-start | bytes 1048576 | tf_op jit(solution)/shard_map/psum | solution.py:481
  200.1 23.7 %collective-permute-start.33 = (bf16[256,1024]{1,0:T(8,128)(2,1)}, bf16[256,1024]{1,0:T(8,128)(2,1)S(1)}, u32[]{:S(2)}, u32[]{:S(2)}) collective-permute-start(bf16[256,1024]{1,0:T(8,128)(2,1)} %get-tuple-element.61), channel_id=1, source_target_pairs={{0,1},{1,0},{2,3},{3,2},{4,5},{5,4},{6,7},{7,6},{8,9},{9,8},{10,11... | collective-permute-start | bytes 1572872 | tf_op jit(solution)/shard_map/ppermute | solution.py:443
  223.8 13.1 %copy-start.7 = (bf16[256,1024]{1,0:T(8,128)(2,1)S(1)}, bf16[256,1024]{1,0:T(8,128)(2,1)}, u32[]{:S(2)}) copy-start(bf16[256,1024]{1,0:T(8,128)(2,1)} %all-reduce.4.cloned.1.call-done) | copy-start | bytes 1572868
  226.0 77.7 %all-gather.2.cloned.1.call-start = ((), (), s32[]{:S(2)}) async-start(), calls=%async_computation | async-start | bytes 1966080 | tf_op jit(solution)/shard_map/all_gather | solution.py:464
  226.2 10.0 %collective-permute-start.24 = (bf16[192,1024]{1,0:T(8,128)(2,1)S(1)}, bf16[192,1024]{1,0:T(8,128)(2,1)S(1)}, u32[]{:S(2)}, u32[]{:S(2)}) collective-permute-start(bf16[192,1024]{1,0:T(8,128)(2,1)S(1)} %constant_dynamic-slice_fusion), channel_id=1, source_target_pairs={{2,0},{0,2},{3,1},{1,3},{6,4},{4,6},{7,5},{5,7},{10,8},{8,10},{11,... | collective-permute-start | bytes 1179656 | tf_op jit(solution)/shard_map/ppermute | solution.py:440
  236.9 28.1 %collective-permute-start.31 = (bf16[256,1024]{1,0:T(8,128)(2,1)S(1)}, bf16[256,1024]{1,0:T(8,128)(2,1)S(1)}, u32[]{:S(2)}, u32[]{:S(2)}) collective-permute-start(bf16[256,1024]{1,0:T(8,128)(2,1)S(1)} %copy-done.7), channel_id=1, source_target_pairs={{0,1},{1,0},{2,3},{3,2},{4,5},{5,4},{6,7},{7,6},{8,9},{9,8},{10,11... | collective-permute-start | bytes 1572872 | tf_op jit(solution)/shard_map/ppermute | solution.py:443
  265.0 8.7 %collective-permute-start.34 = (bf16[256,1024]{1,0:T(8,128)(2,1)}, bf16[256,1024]{1,0:T(8,128)(2,1)S(1)}, u32[]{:S(2)}, u32[]{:S(2)}) collective-permute-start(bf16[256,1024]{1,0:T(8,128)(2,1)} %all-reduce.6.cloned.1.call-done), channel_id=1, source_target_pairs={{0,1},{1,0},{2,3},{3,2},{4,5},{5,4},{6,7},{7,6},{8,9},{9,8},{10,11... | collective-permute-start | bytes 1572872 | tf_op jit(solution)/shard_map/ppermute | solution.py:443
  266.2 48.5 %collective-permute-start.32 = (bf16[512,1024]{1,0:T(8,128)(2,1)}, bf16[512,1024]{1,0:T(8,128)(2,1)}, u32[]{:S(2)}, u32[]{:S(2)}) collective-permute-start(bf16[512,1024]{1,0:T(8,128)(2,1)} %pad_maximum_fusion.1), channel_id=1, source_target_pairs={{5,1},{7,3},{0,4},{2,6},{13,9},{15,11},{8,12},{10,14},{21,17},{23,... | collective-permute-start | bytes 3145736 | tf_op jit(solution)/shard_map/ppermute | solution.py:490
  270.5 4.7 %collective-permute-start.14 = (bf16[512,512]{1,0:T(8,128)(2,1)}, bf16[512,512]{1,0:T(8,128)(2,1)S(1)}, u32[]{:S(2)}, u32[]{:S(2)}) collective-permute-start(bf16[512,512]{1,0:T(8,128)(2,1)} %get-tuple-element.44.refs_0_), channel_id=1, source_target_pairs={{0,0},{4,1},{2,2},{6,3},{1,4},{5,5},{3,6},{7,7},{8,8},{12,9},{10,1... | collective-permute-start | bytes 1572872 | tf_op jit(solution)/shard_map/ppermute | solution.py:436
  272.2 27.2 %collective-permute-start.15 = (bf16[512,512]{1,0:T(8,128)(2,1)S(1)}, bf16[512,512]{1,0:T(8,128)(2,1)S(1)}, u32[]{:S(2)}, u32[]{:S(2)}) collective-permute-start(bf16[512,512]{1,0:T(8,128)(2,1)S(1)} %copy-done.12), channel_id=1, source_target_pairs={{2,0},{6,1},{0,2},{4,3},{3,4},{7,5},{1,6},{5,7},{10,8},{14,9},{8,1... | collective-permute-start | bytes 1572872 | tf_op jit(solution)/shard_map/ppermute | solution.py:436
  273.7 33.4 %collective-permute-start.16 = (bf16[512,512]{1,0:T(8,128)(2,1)}, bf16[512,512]{1,0:T(8,128)(2,1)}, u32[]{:S(2)}, u32[]{:S(2)}) collective-permute-start(bf16[512,512]{1,0:T(8,128)(2,1)} %get-tuple-element.46.refs_2_), channel_id=1, source_target_pairs={{4,0},{0,1},{6,2},{2,3},{5,4},{1,5},{7,6},{3,7},{12,8},{8,9},{14,1... | collective-permute-start | bytes 1572872 | tf_op jit(solution)/shard_map/ppermute | solution.py:436
  273.7 33.4 %collective-permute-start.17 = (bf16[512,512]{1,0:T(8,128)(2,1)}, bf16[512,512]{1,0:T(8,128)(2,1)}, u32[]{:S(2)}, u32[]{:S(2)}) collective-permute-start(bf16[512,512]{1,0:T(8,128)(2,1)} %get-tuple-element.47.refs_3_), channel_id=1, source_target_pairs={{6,0},{2,1},{4,2},{0,3},{7,4},{3,5},{5,6},{1,7},{14,8},{10,9},{12,... | collective-permute-start | bytes 1572872 | tf_op jit(solution)/shard_map/ppermute | solution.py:436
  275.2 31.9 %copy-start.1 = (bf16[512,512]{1,0:T(8,128)(2,1)}, bf16[512,512]{1,0:T(8,128)(2,1)S(1)}, u32[]{:S(2)}) copy-start(bf16[512,512]{1,0:T(8,128)(2,1)S(1)} %collective-permute-done.14.refs_0_) | copy-start | bytes 1572868
  275.2 45.9 %collective-permute-start.35 = (bf16[512,1024]{1,0:T(8,128)(2,1)}, bf16[512,1024]{1,0:T(8,128)(2,1)}, u32[]{:S(2)}, u32[]{:S(2)}) collective-permute-start(bf16[512,1024]{1,0:T(8,128)(2,1)} %pad_maximum_fusion.2), channel_id=1, source_target_pairs={{5,1},{7,3},{0,4},{2,6},{13,9},{15,11},{8,12},{10,14},{21,17},{23,... | collective-permute-start | bytes 3145736 | tf_op jit(solution)/shard_map/ppermute | solution.py:490
  303.7 35.1 %collective-permute-start.25 = (bf16[768,1024]{1,0:T(8,128)(2,1)}, bf16[768,1024]{1,0:T(8,128)(2,1)}, u32[]{:S(2)}, u32[]{:S(2)}) collective-permute-start(bf16[768,1024]{1,0:T(8,128)(2,1)} %all-gather.2.cloned.1.call-done.refs_9_), channel_id=1, source_target_pairs={{0,1},{1,0},{2,3},{3,2},{4,5},{5,4},{6,7},{7,6},{8,9},{9,8},{10,11... | collective-permute-start | bytes 4718600 | tf_op jit(solution)/shard_map/ppermute | solution.py:443
  311.5 12.3 %collective-permute-start.20 = (bf16[512,512]{1,0:T(8,128)(2,1)}, bf16[512,512]{1,0:T(8,128)(2,1)S(1)}, u32[]{:S(2)}, u32[]{:S(2)}) collective-permute-start(bf16[512,512]{1,0:T(8,128)(2,1)} %get-tuple-element.51.refs_0_), channel_id=1, source_target_pairs={{0,0},{4,1},{2,2},{6,3},{1,4},{5,5},{3,6},{7,7},{8,8},{12,9},{10,1... | collective-permute-start | bytes 1572872 | tf_op jit(solution)/shard_map/ppermute | solution.py:436
  313.2 15.0 %collective-permute-start.21 = (bf16[512,512]{1,0:T(8,128)(2,1)}, bf16[512,512]{1,0:T(8,128)(2,1)S(1)}, u32[]{:S(2)}, u32[]{:S(2)}) collective-permute-start(bf16[512,512]{1,0:T(8,128)(2,1)} %get-tuple-element.52.refs_1_), channel_id=1, source_target_pairs={{2,0},{6,1},{0,2},{4,3},{3,4},{7,5},{1,6},{5,7},{10,8},{14,9},{8,1... | collective-permute-start | bytes 1572872 | tf_op jit(solution)/shard_map/ppermute | solution.py:436
  314.6 24.1 %collective-permute-start.22 = (bf16[512,512]{1,0:T(8,128)(2,1)}, bf16[512,512]{1,0:T(8,128)(2,1)S(1)}, u32[]{:S(2)}, u32[]{:S(2)}) collective-permute-start(bf16[512,512]{1,0:T(8,128)(2,1)} %get-tuple-element.53.refs_2_), channel_id=1, source_target_pairs={{4,0},{0,1},{6,2},{2,3},{5,4},{1,5},{7,6},{3,7},{12,8},{8,9},{14,1... | collective-permute-start | bytes 1572872 | tf_op jit(solution)/shard_map/ppermute | solution.py:436
  321.1 17.7 %collective-permute-start.23 = (bf16[512,512]{1,0:T(8,128)(2,1)S(1)}, bf16[512,512]{1,0:T(8,128)(2,1)}, u32[]{:S(2)}, u32[]{:S(2)}) collective-permute-start(bf16[512,512]{1,0:T(8,128)(2,1)S(1)} %copy-done.14), channel_id=1, source_target_pairs={{6,0},{2,1},{4,2},{0,3},{7,4},{3,5},{5,6},{1,7},{14,8},{10,9},{12,... | collective-permute-start | bytes 1572872 | tf_op jit(solution)/shard_map/ppermute | solution.py:436
  323.8 15.1 %copy-start.9 = (bf16[512,512]{1,0:T(8,128)(2,1)}, bf16[512,512]{1,0:T(8,128)(2,1)S(1)}, u32[]{:S(2)}) copy-start(bf16[512,512]{1,0:T(8,128)(2,1)S(1)} %collective-permute-done.20.refs_4_) | copy-start | bytes 1572868
  (11 other events, 56.4 us)
Sparse Core Ops, SparseCore 0:
  187.5 36.2 all-reduce.3
  226.7 38.2 all-reduce.5
  266.6 37.0 all-gather.1

commit v4 on v3

--- a/solution.py
+++ b/solution.py
@@ -34,16 +34,15 @@
 
 def attention_kernel(
     heads, steps,
-    cells, order, qkv, kv_top, kv_bot, *refs,
+    cells, order, qkv, kv_top, kv_bot, weight, *refs,
 ):
-    go_parts, refs = refs[:steps], refs[steps:]
+    upstream, refs = refs[:steps], refs[steps:]
     outq_parts, refs = refs[:steps], refs[steps:]
-    dkv_own, dkv_top, dkv_bot, outq, go, k_s, v_s, kt_s, vt_s, dk_s, dv_s, live_s, near_s, sems = refs
+    dkv_own, dkv_top, dkv_bot, held, outq, go, k_s, v_s, kt_s, vt_s, dk_s, dv_s, live_s, near_s, sems = refs
     feats = heads * HEAD_WIDTH
     chunk = BAND_ROWS * LONGITUDES // steps
     moves = [
-        pltpu.make_async_copy(part, go.at[pl.ds(pl.multiple_of(order[i], 16), chunk)], sems.at[i])
-        for i, part in enumerate(go_parts)
+        pltpu.make_async_copy(part, held.at[i], sems.at[i]) for i, part in enumerate(upstream)
     ]
     for move in moves:
         move.start()
@@ -154,8 +153,9 @@
             one_tile(upper, tile)
         return carry
 
-    for move in moves:
+    for i, move in enumerate(moves):
         move.wait()
+        go[pl.ds(pl.multiple_of(order[i], 16), chunk)] = nt(held[i], weight[...]).astype(jnp.bfloat16)
     lax.fori_loop(0, LONGITUDES // tile_cols, tile_pair, 0)
     moves = [
         pltpu.make_async_copy(outq.at[pl.ds(pl.multiple_of(order[i], 16), chunk)], part, sems.at[i])
@@ -208,22 +208,23 @@
     )(*args)
 
 
-def attention(cells, order, qkv, kv_top, kv_bot, go_parts):
-    steps, feats = len(go_parts), go_parts[0].shape[-1]
+def attention(cells, order, qkv, kv_top, kv_bot, weight, upstream):
+    steps, (feats, width), chunk = len(upstream), weight.shape, upstream[0].shape[0]
     heads = feats // HEAD_WIDTH
     window = LANES // heads // QUERY_ROWS // BLOCK + 2
-    band, halo, chunk = BAND_ROWS * LONGITUDES, HALO * LONGITUDES, go_parts[0].shape[0]
+    band, halo = BAND_ROWS * LONGITUDES, HALO * LONGITUDES
     pairs = band * heads * KEYS * window
     results = call(
         functools.partial(attention_kernel, heads, steps),
         [shape(chunk, 2 * feats)] * steps
         + [shape(band, 2 * feats, F32), shape(halo, 2 * feats), shape(halo, 2 * feats)],
-        [SMEM, SMEM, VMEM, VMEM, VMEM] + [HBM] * steps,
+        [SMEM, SMEM, VMEM, VMEM, VMEM, VMEM] + [HBM] * steps,
         [HBM] * steps + [VMEM] * 3,
-        (cells, order, qkv, kv_top, kv_bot, *go_parts),
-        flops=12 * pairs * HEAD_WIDTH * heads,
+        (cells, order, qkv, kv_top, kv_bot, weight, *upstream),
+        flops=12 * pairs * HEAD_WIDTH * heads + 2 * band * weight.size,
         transcendentals=pairs,
         scratch=[
+            pltpu.VMEM((steps, chunk, width), BF16),
             pltpu.VMEM((band, 2 * feats), BF16),
             pltpu.VMEM((band, feats), BF16),
             pltpu.VMEM((BLOCKS, EXT_ROWS * BLOCK, feats), BF16),
@@ -252,21 +253,6 @@
     )[0]
 
 
-def grad_heads_kernel(steps, upstream, *refs):
-    for block, out in zip(refs[:steps], refs[steps:]):
-        out[...] = nt(upstream[...], block[...]).astype(BF16)
-
-
-def grad_heads_parts(upstream, blocks):
-    steps, feats = len(blocks), blocks[0].shape[0]
-    return call(
-        functools.partial(grad_heads_kernel, steps),
-        [shape(upstream.shape[0], feats)] * steps,
-        [VMEM] * (1 + steps), [VMEM] * steps, (upstream, *blocks),
-        flops=2 * steps * feats * upstream.size,
-    )
-
-
 def projection_kernel(steps, feats, order, weight, *refs):
     parts, (qkv, kv_up, kv_down, held, sems) = refs[:steps], refs[steps:]
     chunk = held.shape[1]
@@ -277,13 +263,13 @@
         move.wait()
         at = pl.ds(pl.multiple_of(order[i], 16), chunk)
         for first in range(0, 3 * feats, feats):
-            qkv[at, first:first + feats] = nt(held[i], weight[first:first + feats, :]).astype(BF16)
+            qkv[at, first:first + feats] = nn(held[i], weight[:, first:first + feats]).astype(BF16)
     kv_up[...] = qkv[(BAND_ROWS - HALO) * LONGITUDES:, feats:]
     kv_down[...] = qkv[:HALO * LONGITUDES, feats:]
 
 
 def projections(order, weight, parts):
-    steps, feats = len(parts), weight.shape[0] // 3
+    steps, feats = len(parts), weight.shape[1] // 3
     chunk, width = parts[0].shape
     band, halo = BAND_ROWS * LONGITUDES, HALO * LONGITUDES
     return call(
@@ -322,9 +308,9 @@
     )
 
 
-def weight_grad_kernel(steps, sides, core, *refs):
+def weight_grad_kernel(steps, sides, *refs):
     lefts, refs = refs[:steps], refs[steps:]
-    rights, (keep, give, sums) = [refs[i * steps:(i + 1) * steps] for i in range(sides)], refs[sides * steps:]
+    rights, (grad, sums) = [refs[i * steps:(i + 1) * steps] for i in range(sides)], refs[sides * steps:]
     feats = sums.shape[0] // sides
     for side, parts in enumerate(rights):
         at = slice(side * feats, (side + 1) * feats)
@@ -332,46 +318,63 @@
             product = lax.dot_general(
                 left[:, at], right[...], (((0,), (0,)), ((), ())), preferred_element_type=F32
             )
-            sums[at, :] = product if i == 0 else sums[at, :] + product
-    half = sums.shape[0] // 2
-    mine, other = (pl.ds(pl.multiple_of(at * half, 16), half) for at in (core[0], 1 - core[0]))
-    keep[...] = sums[mine, :]
-    give[...] = sums[other, :].astype(BF16)
-
-
-def weight_grad(core, lefts, *rights):
+            if i == 0:
+                sums[at, :] = product
+            elif i < steps - 1:
+                sums[at, :] += product
+            else:
+                grad[at, :] = (sums[at, :] + product).astype(BF16)
+
+
+def weight_grad(lefts, *rights):
     steps, width = len(lefts), rights[0][0].shape[1]
     rows = lefts[0].shape[1]
-    args = (core, *lefts, *(part for parts in rights for part in parts))
+    args = (*lefts, *(part for parts in rights for part in parts))
     return call(
         functools.partial(weight_grad_kernel, steps, len(rights)),
-        [shape(rows // 2, width, F32), shape(rows // 2, width)],
-        [SMEM] + [VMEM] * (len(args) - 1), [VMEM] * 2, args,
+        [shape(rows, width)], [VMEM] * len(args), [VMEM], args,
         flops=2 * steps * lefts[0].size * width,
         scratch=[pltpu.VMEM((rows, width), F32)],
-    )
-
-
-def update_kernel(steps, *refs):
-    out = refs[-1]
-    feats = refs[steps].shape[0]
-    out[...] = sum(nn(part[:, :feats], block[...]) for part, block in zip(refs[:steps], refs[steps:])).astype(BF16)
-
-
-def updates(outq_own, blocks):
-    steps, (feats, width) = len(blocks), blocks[0].shape
-    chunk = outq_own[0].shape[0]
+    )[0]
+
+
+def load_blocks(blocks, held, sems, first):
+    rows = held.shape[1]
+    moves = [
+        pltpu.make_async_copy(block.at[pl.ds(first, rows)], held.at[i], sems.at[i]) for i, block in enumerate(blocks)
+    ]
+    for move in moves:
+        move.start()
+    for move in moves:
+        move.wait()
+
+
+def update_kernel(steps, leads, *refs):
+    parts, blocks, (out, held, sems) = refs[:steps], refs[steps:2 * steps], refs[2 * steps:]
+    feats = held.shape[1]
+    load_blocks(blocks, held, sems, 3 * feats)
+    out[...] = sum(nn(parts[i][:, :feats], held[leads[i]]) for i in range(steps)).astype(BF16)
+
+
+def updates(leads, outq_own, blocks):
+    steps, (rows, width), chunk = len(blocks), blocks[0].shape, outq_own[0].shape[0]
     return call(
-        functools.partial(update_kernel, steps), [shape(chunk, width)], [VMEM] * (2 * steps), [VMEM],
-        (*outq_own, *blocks), flops=2 * steps * chunk * feats * width,
+        functools.partial(update_kernel, steps),
+        [shape(chunk, width)], [SMEM] + [VMEM] * steps + [HBM] * steps, [VMEM], (leads, *outq_own, *blocks),
+        flops=steps * chunk * rows * width // 2,
+        scratch=[pltpu.VMEM((steps, rows // 4, width), BF16), pltpu.SemaphoreType.DMA((steps,))],
     )[0]
 
 
-def grad_input_kernel(steps, tokens, gain, *refs):
-    outq, dkv, blocks, grad = refs[:steps], refs[steps:2 * steps], refs[2 * steps:3 * steps], refs[-1]
-    feats = blocks[0].shape[0] // 3
+def grad_input_kernel(steps, leads, tokens, gain, *refs):
+    outq, dkv, blocks, (grad, held, sems) = (
+        refs[:steps], refs[steps:2 * steps], refs[2 * steps:3 * steps], refs[3 * steps:]
+    )
+    feats = held.shape[1] // 3
+    load_blocks(blocks, held, sems, 0)
     grad_normed = sum(
-        nn(outq[i][:, feats:], blocks[i][:feats, :]) + nn(dkv[i][...], blocks[i][feats:, :]) for i in range(steps)
+        nn(outq[i][:, feats:], held[leads[i], :feats, :]) + nn(dkv[i][...], held[leads[i], feats:, :])
+        for i in range(steps)
     )
     features = tokens[...].astype(F32)
     inverse = lax.rsqrt(jnp.mean(features * features, axis=1, keepdims=True) + 1e-06)
@@ -380,12 +383,14 @@
     grad[...] = (inverse * (scaled - centred * jnp.mean(scaled * centred, axis=1, keepdims=True))).astype(BF16)
 
 
-def grad_inputs(tokens, gain, outq_own, dkv_own, blocks):
-    steps = len(blocks)
+def grad_inputs(leads, tokens, gain, outq_own, dkv_own, blocks):
+    steps, (rows, width) = len(blocks), blocks[0].shape
     return call(
-        functools.partial(grad_input_kernel, steps), [shape(*tokens.shape)], [VMEM] * (2 + 3 * steps), [VMEM],
-        (tokens, gain[None, :], *outq_own, *dkv_own, *blocks),
-        flops=2 * steps * tokens.shape[0] * blocks[0].size,
+        functools.partial(grad_input_kernel, steps),
+        [shape(*tokens.shape)], [SMEM] + [VMEM] * (2 + 2 * steps) + [HBM] * steps, [VMEM],
+        (leads, tokens, gain[None, :], *outq_own, *dkv_own, *blocks),
+        flops=steps * tokens.shape[0] * rows * width * 3 // 2,
+        scratch=[pltpu.VMEM((steps, rows * 3 // 4, width), BF16), pltpu.SemaphoreType.DMA((steps,))],
     )[0]
 
 
@@ -395,12 +400,16 @@
 GROUP = ("y", "m", "c")
 
 
-def to_bands(halves, step):
-    dm, dc = step
-    place = lambda y, m, c: (y * halves + m) * 2 + c
+def owners(halves):
+    if halves == 2:
+        return [
+            lambda y, m, c: (c, 1 - m if c == y else m, y),
+            lambda y, m, c: (c, 1 - m if c == y else m, 1 - y),
+            lambda y, m, c: (c, m if c == y else 1 - m, 1 - y),
+            lambda y, m, c: (c, m if c == y else 1 - m, y),
+        ]
     return [
-        (place(y, m, c), place((c + dc) % 2, (m + dm) % halves, y))
-        for y in range(2) for m in range(halves) for c in range(2)
+        lambda y, m, c, dm=dm, dc=dc: (c, (m + dm) % halves, (y + dc) % 2) for dc in range(2) for dm in range(halves)
     ]
 
 
@@ -421,20 +430,41 @@
     chunk = tokens.shape[0]
     halves, layers = lax.axis_size("m"), lax.axis_size("z")
     z, y, m, c = (lax.axis_index(axis) for axis in ("z",) + GROUP)
-    core = jnp.reshape(c, (1,))
-    steps = [(dm, dc) for dc in range(2) for dm in range(halves)]
-    order = jnp.stack([((m - dm) % halves) * 2 + (y - dc) % 2 for dm, dc in steps]) * chunk
     grad_scale = 4.0 / math.sqrt(band_tokens * layers * 2)
     band_start = (z * 2 + c) * BAND_ROWS
     cells = lax.dynamic_slice_in_dim(jnp.pad(row_cells, (HALO, HALO)), band_start, EXT_ROWS)
 
-    def send(parts):
-        return [lax.ppermute(x, GROUP, to_bands(halves, step)) for x, step in zip(parts, steps)]
+    at = lambda y, m, c: (y * halves + m) * 2 + c
+    spots = [(y, m, c) for y in range(2) for m in range(halves) for c in range(2)]
+    slots = [[owner(*spot) for spot in spots] for owner in owners(halves)]
+    here = lambda table: jnp.asarray(table, jnp.int32)[at(y, m, c)]
+    order = here([[(slot[i][1] * 2 + slot[i][2]) * chunk for slot in slots] for i in range(len(spots))])
+
+    def lead(slot, spot):
+        far = spots[slot.index(spot)]
+        return (far[0] - spot[2]) % 2 * halves + (far[1] - spot[1]) % halves
+
+    leads = here([[lead(slot, spot) for slot in slots] for spot in spots])
+
+    def permuted(x, pairs):
+        return lax.ppermute(x, GROUP, [(at(*a), at(*b)) for a, b in pairs])
 
     def send_back(parts):
-        return [
-            lax.ppermute(x, GROUP, [(b, a) for a, b in to_bands(halves, step)]) for x, step in zip(parts, steps)
-        ]
+        return [permuted(x, list(zip(spots, slot))) for x, slot in zip(parts, slots)]
+
+    def gathered(x):
+        sent = lambda slot: permuted(x, list(zip(slot, spots)))
+        if halves != 2:
+            return [sent(slot) for slot in slots]
+        first, second = sent(slots[0]), sent(slots[1])
+        third = permuted(
+            jnp.where(c == y, first, x),
+            [(spot, (1 - spot[0], spot[1], spot[0]) if spot[2] == spot[0] else (spot[0], spot[1], spot[0])) for spot in spots],
+        )
+        fourth = permuted(
+            first, [(spot, (spot[0], 1 - spot[1], spot[2])) for spot in spots if spot[2] != spot[0]]
+        )
+        return [first, second, third, jnp.where(c == y, x, fourth)]
 
     def from_ahead(x, dm):
         return lax.ppermute(x, "m", [((i + dm) % halves, i) for i in range(halves)])
@@ -442,56 +472,44 @@
     def from_sibling(x):
         return lax.ppermute(x, "c", [(0, 1), (1, 0)])
 
-    out_blocks = [out_weight.reshape(feats, WIDTH)]
-    out_blocks += [from_ahead(out_blocks[0], dm) for dm in range(1, halves)]
-    normed_parts = send([norm(tokens, gain)] * len(steps))
-    out_blocks += [from_sibling(block) for block in out_blocks]
-
     split = qkv_weight.reshape(heads, 3, HEAD_WIDTH, WIDTH).transpose(1, 0, 2, 3).reshape(3 * feats, WIDTH)
     eighth = jnp.where(jnp.arange(3 * feats) < feats, HEAD_WIDTH ** -0.5, 1.0)[:, None].astype(BF16)
-    split = split * eighth
-    sibling_split = from_sibling(split)
-    grad_heads_own = grad_heads_parts(upstream, out_blocks)
-
-    qkv, kv_up, kv_down = projections(order, jnp.where(c == y, split, sibling_split), normed_parts)
+    weight = jnp.concatenate([split * eighth, out_weight.reshape(feats, WIDTH)], axis=0)
+    share = 4 * feats // layers
+    held = lax.dynamic_slice_in_dim(weight, z * share, share, 0)
+    blocks = [weight]
+    blocks += [lax.all_gather(from_ahead(held, dm), "z", axis=0, tiled=True) for dm in range(1, halves)]
+    blocks += [from_sibling(block) for block in blocks]
+    group = jnp.where(c == y, weight, blocks[halves])
+    group_qkv, group_out = group[:3 * feats].T, group[3 * feats:]
+
+    *normed_parts, group_qkv, group_out = lax.optimization_barrier(
+        (*gathered(norm(tokens, gain)), group_qkv, group_out)
+    )
+    upstream_parts = gathered(after(upstream, *normed_parts))
+    qkv, kv_up, kv_down = projections(order, group_qkv, normed_parts)
     kv_top, kv_bot = passed_along(kv_up, 1), passed_along(kv_down, -1)
-    grad_heads = send([after(part, qkv) for part in grad_heads_own])
-
-    upstream_parts = send([after(upstream, *grad_heads)] * len(steps))
-    share = 3 * feats // layers
-    held = after(lax.dynamic_slice_in_dim(split, z * share, share, 0), kv_top, kv_bot)
-    split_blocks = [split]
-    split_blocks += [lax.all_gather(from_ahead(held, dm), "z", axis=0, tiled=True) for dm in range(1, halves)]
-    split_blocks += [sibling_split] + [from_sibling(block) for block in split_blocks[1:]]
-
-    outq_parts, dkv, dkv_top, dkv_bot = attention(cells, order, qkv, kv_top, kv_bot, grad_heads)
+    order, *blocks = lax.optimization_barrier((order, *blocks))
+    outq_parts, dkv, dkv_top, dkv_bot = attention(cells, order, qkv, kv_top, kv_bot, group_out, upstream_parts)
 
     from_above, from_below = passed_along(dkv_top, -1), passed_along(dkv_bot, 1)
     outq_own = send_back(outq_parts)
-    early = weight_grad(core, outq_parts, upstream_parts, normed_parts)
-    dkv_parts = joined(order, dkv, from_above, from_below, len(steps))
+    early = weight_grad(outq_parts, upstream_parts, normed_parts)
+    early_sum = lax.psum(early, ("z", "c"))
+    dkv_parts = joined(after(order, early), dkv, from_above, from_below, len(slots))
     dkv_own = send_back(dkv_parts)
-    late = weight_grad(core, dkv_parts, normed_parts)
-
-    update = updates(outq_own, out_blocks)
-    grad_input = grad_inputs(tokens, gain, outq_own, dkv_own, split_blocks)
-
-    def reduced(keep, give):
-        both = (keep + from_sibling(give).astype(F32)).astype(BF16)
-        return lax.psum(both, "z")
-
-    def spread(half):
-        other = from_sibling(half)
-        whole = jnp.concatenate([jnp.where(c == 0, half, other), jnp.where(c == 0, other, half)], axis=0)
-        pairs = [
-            ((1 - y) * halves * 2 + m * 2 + 1 - y, y * halves * 2 + m * 2 + 1 - y)
-            for y in range(2) for m in range(halves)
-        ]
-        return jnp.where(c == y, whole, lax.ppermute(whole, GROUP, pairs)).astype(F32)
-
-    early_half = reduced(*early)
-    late_half = reduced(after(late[0], early_half), late[1])
-    early, late = spread(early_half), spread(late_half) * grad_scale
+    late = weight_grad(dkv_parts, normed_parts)
+    late_sum = lax.psum(late, ("c", "z"))
+    leads, outq_own, dkv_own = lax.optimization_barrier((leads, outq_own, dkv_own))
+    update = updates(leads, outq_own, blocks)
+    grad_input = grad_inputs(after(leads, late), tokens, gain, outq_own, dkv_own, blocks)
+
+    def spread(grads):
+        pairs = [((1 - y, m, 1 - y), (y, m, 1 - y)) for y in range(2) for m in range(halves)]
+        return jnp.where(c == y, grads, permuted(grads, pairs)).astype(F32)
+
+    early_sum, grad_input, update = lax.optimization_barrier((early_sum, grad_input, update))
+    early, late = spread(early_sum), spread(late_sum) * grad_scale
     by_head = lambda x: x.reshape(heads, HEAD_WIDTH, WIDTH)
     grad_out = by_head(early[:feats] * grad_scale)
     grad_query = early[feats:] * (grad_scale * HEAD_WIDTH ** -0.5)

time: 357 us -> 373 us (1.045)
  waiting for transfers between devices: 132 us -> 180 us
  starting transfers between devices: 100 us -> 63.6 us
  local copies, waits for them, and re-layouts: 5.82 us -> 9.81 us
    psum x2, waiting for transfers between devices: 42.8 us -> 79.5 us  [the longest x1 57.4 us: on_device(): late_sum = lax.psum(late, ('c', 'z'))]
    ppermute x22 -> x18, starting transfers between devices: 72.8 us -> 50.1 us  [permuted(): return lax.ppermute(x, GROUP, [(at(*a), at(*b)) for a, b in pairs])]
    ppermute x22 -> x18, waiting for transfers between devices: 70.2 us -> 81.9 us  [permuted(): return lax.ppermute(x, GROUP, [(at(*a), at(*b)) for a, b in pairs])]
    ppermute x8 -> x2, starting transfers between devices: 11.6 us -> 0.15 us  [from_sibling(): return lax.ppermute(x, 'c', [(0, 1), (1, 0)])]
    ppermute x8 -> x2, waiting for transfers between devices: 6.18 us -> 0.01 us  [from_sibling(): return lax.ppermute(x, 'c', [(0, 1), (1, 0)])]
    ppermute x2 -> x1, waiting for transfers between devices: 8.42 us -> 12.9 us  [from_ahead(): return lax.ppermute(x, 'm', [((i + dm) % halves, i) for i in range(halves)])]
    select_n x3, other arithmetic: 1.7 us -> 6.11 us  [the longest x2 5.12 us: gathered(): return [first, second, third, jnp.where(c == y, x, fourth)]]
    pallas_call x9 -> x8, Pallas kernels: 90.3 us -> 90.8 us  [call(): pl.pallas_call(kernel, out_shape=tuple(out_shape), in_specs=list(in_specs...]
  transfers between devices with their start and end apart: 39 -> 28, of which waited for: 16 -> 12; matrix products, arithmetic and copies ran while one was open for 3% -> 5% of each run, Pallas kernels for 23% -> 12%
where the time goes in v4:
time: 373 us; the launch traced here: 372 us
  waiting for transfers between devices  180 us (48%)
  Pallas kernels  90.8 us (24%)
  starting transfers between devices  63.6 us (17%)
  between operations  14 us (4%)
  other arithmetic  13.4 us (4%)
  local copies, waits for them, and re-layouts  9.81 us (3%)
    pallas_call x8, Pallas kernels, call(): pl.pallas_call(kernel, out_shape=tuple(out_shape), in_specs=list(in_specs...  90.8 us
    ppermute x18, waiting for transfers between devices, permuted(): return lax.ppermute(x, GROUP, [(at(*a), at(*b)) for a, b in pairs])  81.9 us
    psum x1, waiting for transfers between devices, on_device(): late_sum = lax.psum(late, ('c', 'z'))  57.4 us
    ppermute x18, starting transfers between devices, permuted(): return lax.ppermute(x, GROUP, [(at(*a), at(*b)) for a, b in pairs])  50.1 us
    psum x1, waiting for transfers between devices, on_device(): early_sum = lax.psum(early, ('z', 'c'))  22.1 us
    ppermute x1, waiting for transfers between devices, from_ahead(): return lax.ppermute(x, 'm', [((i + dm) % halves, i) for i in range(halves)])  12.9 us
    ppermute x4, starting transfers between devices, passed_along(): return lax.ppermute(x, ('z', 'c'), pairs)  10.9 us
  transfers between devices with their start and end apart: 28, of which 12 were waited for; matrix products, arithmetic and copies ran while one was open for 5% of the time, Pallas kernels for 12%

profile of v4, /device:TPU:0, one launch (start us, length us, event | category | flops | bytes accessed | tf_op | source)
XLA Modules:
  0.0 371.6 jit_solution(3214929108587733331)
XLA Ops:
  7.2 2.7 shard_map.111
  9.9 2.9 collective-permute-start.3
  14.0 1.5 pad_maximum_fusion.1.refs_8_.refs_4_
  15.7 10.3 %collective-permute-done.3.refs_0_.refs_8_.refs_4_ = bf16[512,1024]{1,0:T(8,128)(2,1)} collective-permute-done((bf16[512,1024]{1,0:T(8,128)(2,1)}, bf16[512,1024]{1,0:T(8,128)(2,1)}, u32[]{:S(2)}, u32[]{:S(2)}) %collective-permute-start.3) | collective-permute-done | bytes 1048608 | tf_op jit(solution)/shard_map/ppermute | solution.py:450
  26.0 1.6 collective-permute-start.6
  28.1 2.1 collective-permute-start
  30.2 12.9 %collective-permute-done = bf16[256,1024]{1,0:T(8,128)(2,1)} collective-permute-done((bf16[256,1024]{1,0:T(8,128)(2,1)S(1)}, bf16[256,1024]{1,0:T(8,128)(2,1)}, u32[]{:S(2)}, u32[]{:S(2)}) %collective-permute-start) | collective-permute-done | bytes 524320 | tf_op jit(solution)/shard_map/ppermute | solution.py:470
  43.1 11.4 %collective-permute-start.4 = (bf16[512,1024]{1,0:T(8,128)(2,1)S(1)}, bf16[512,1024]{1,0:T(8,128)(2,1)}, u32[]{:S(2)}, u32[]{:S(2)}) collective-permute-start(bf16[512,1024]{1,0:T(8,128)(2,1)S(1)} %copy-done.2), channel_id=1, source_target_pairs={{3,0},{5,1},{1,2},{7,3},{0,4},{6,5},{2,6},{4,7},{11,8},{13,9},{9,1... | collective-permute-start | bytes 3145736 | tf_op jit(solution)/shard_map/ppermute | solution.py:450
  54.5 2.4 broadcast_select_fusion.3
  58.8 1.3 slice_bitcast_fusion
  60.0 7.0 %collective-permute-done.4.refs_1_.refs_9_.refs_5_ = bf16[512,1024]{1,0:T(8,128)(2,1)} collective-permute-done((bf16[512,1024]{1,0:T(8,128)(2,1)S(1)}, bf16[512,1024]{1,0:T(8,128)(2,1)}, u32[]{:S(2)}, u32[]{:S(2)}) %collective-permute-start.4) | collective-permute-done | bytes 1048608 | tf_op jit(solution)/shard_map/ppermute | solution.py:450
  67.0 11.1 %collective-permute-done.5.refs_2_.refs_10_.refs_6_ = bf16[512,1024]{1,0:T(8,128)(2,1)S(1)} collective-permute-done((bf16[512,1024]{1,0:T(8,128)(2,1)S(1)}, bf16[512,1024]{1,0:T(8,128)(2,1)S(1)}, u32[]{:S(2)}, u32[]{:S(2)}) %collective-permute-start.5) | collective-permute-done | bytes 1048608 | tf_op jit(solution)/shard_map/ppermute | solution.py:450
  78.1 1.5 collective-permute-start.9
  79.6 13.3 %collective-permute-done.9.refs_0_.refs_4_ = bf16[512,1024]{1,0:T(8,128)(2,1)S(1)} collective-permute-done((bf16[512,1024]{1,0:T(8,128)(2,1)S(1)}, bf16[512,1024]{1,0:T(8,128)(2,1)S(1)}, u32[]{:S(2)}, u32[]{:S(2)}) %collective-permute-start.9) | collective-permute-done | bytes 1048608 | tf_op jit(solution)/shard_map/ppermute | solution.py:450
  92.9 1.7 collective-permute-start.12
  94.6 5.7 %all-gather.2.cloned.1.call-done.refs_9_.refs_5_ = bf16[1024,1024]{1,0:T(8,128)(2,1)} async-done(((bf16[256,1024]{1,0:T(8,128)(2,1)}), bf16[1024,1024]{1,0:T(8,128)(2,1)}) %all-gather.2.cloned.1.call-update) | async-done | bytes 2097168 | tf_op jit(solution)/shard_map/all_gather | solution.py:481
  100.2 1.3 fusion.1.order
  101.5 2.6 copy.13.weight
  104.1 10.4 %shard_map.112 = (bf16[2048,768]{1,0:T(8,128)(2,1)}, bf16[1536,512]{1,0:T(8,128)(2,1)}, bf16[1536,512]{1,0:T(8,128)(2,1)}) custom-call(s32[4]{0:T(128)} %fusion.1.order, bf16[1024,768]{1,0:T(8,128)(2,1)} %copy.13.weight, bf16[512,1024]{1,0:T(8,128)(2,1)} %collective-permute-done.3.refs_0_.refs_8_.refs_4_, ...), custom_call_target="tpu_custom_call" | custom-call | flops 3221225472 | bytes 12058640 | tf_op jit(solution)/shard_map/pallas_call | solution.py:198
  114.4 3.6 collective-permute-start.7
  118.0 1.4 collective-permute-start.8
  119.5 1.7 collective-permute-start.10
  121.2 2.8 broadcast_select_fusion.1
  123.9 2.5 collective-permute-start.11
  127.0 7.7 %collective-permute-done.10.refs_1_.refs_5_ = bf16[512,1024]{1,0:T(8,128)(2,1)} collective-permute-done((bf16[512,1024]{1,0:T(8,128)(2,1)}, bf16[512,1024]{1,0:T(8,128)(2,1)}, u32[]{:S(2)}, u32[]{:S(2)}) %collective-permute-start.10) | collective-permute-done | bytes 1048608 | tf_op jit(solution)/shard_map/ppermute | solution.py:450
  134.7 10.3 %collective-permute-done.11.refs_2_.refs_6_ = bf16[512,1024]{1,0:T(8,128)(2,1)S(1)} collective-permute-done((bf16[512,1024]{1,0:T(8,128)(2,1)}, bf16[512,1024]{1,0:T(8,128)(2,1)S(1)}, u32[]{:S(2)}, u32[]{:S(2)}) %collective-permute-start.11) | collective-permute-done | bytes 1048608 | tf_op jit(solution)/shard_map/ppermute | solution.py:450
  146.0 43.7 %shard_map.113 = (bf16[512,512]{1,0:T(8,128)(2,1)}, bf16[512,512]{1,0:T(8,128)(2,1)}, bf16[512,512]{1,0:T(8,128)(2,1)}, bf16[512,512]{1,0:T(8,128)(2,1)}, f32[20...) custom-call(s32[20]{0:T(128)} %pad_dynamic-slice_fusion.2.cells, s32[4]{0:T(128)} %fusion.1.order, ...), custom_call_target="tpu_custom_call" | custom-call | flops 13958643712 | bytes 20447328 | tf_op jit(solution)/shard_map/pallas_call | solution.py:198
  189.8 1.3 collective-permute-start.17
  191.1 4.6 %collective-permute-start.18 = (bf16[1536,512]{1,0:T(8,128)(2,1)}, bf16[1536,512]{1,0:T(8,128)(2,1)}, u32[]{:S(2)}, u32[]{:S(2)}) collective-permute-start(bf16[1536,512]{1,0:T(8,128)(2,1)} %get-tuple-element.62), channel_id=1, source_target_pairs={{0,1},{1,8},{8,9},{9,16},{16,17},{17,24},{24,25},{2,3},{3,10},{10,... | collective-permute-start | bytes 4718600 | tf_op jit(solution)/shard_map/ppermute | solution.py:419
  195.7 1.5 collective-permute-start.13
  197.1 1.7 collective-permute-start.14
  198.8 7.4 %shard_map.114 = bf16[512,1024]{1,0:T(8,128)(2,1)} custom-call(bf16[512,512]{1,0:T(8,128)(2,1)} %get-tuple-element.55.refs_0_, bf16[512,512]{1,0:T(8,128)(2,1)} %get-tuple-element.56.refs_1_, bf16[512,512]{1,0:T(8,128)(2,1)} %get-tuple-element.57.refs_2_, bf16[512,512]{1,0:T(8,128)(2,1)} %get-tuple-element.58.refs_3_, bf16[512,1024]{1,0:T(8,128)(2,1)} %copy-done.3, ...), custom_call_target="tpu_custom_call" | custom-call | flops 2147483648 | bytes 11534336 | tf_op jit(solution)/shard_map/pallas_call | solution.py:198
  206.9 5.0 %shard_map.115 = (bf16[512,512]{1,0:T(8,128)(2,1)}, bf16[512,512]{1,0:T(8,128)(2,1)}, bf16[512,512]{1,0:T(8,128)(2,1)}, bf16[512,512]{1,0:T(8,128)(2,1)}) custom-call(s32[4]{0:T(128)} %fusion.1.order, f32[2048,512]{1,0:T(8,128)} %get-tuple-element.60.own, bf16[1536,512]{1,0:T(8,128)(2,1)} %collective-permute-done.17.above, ...), custom_call_target="tpu_custom_call" | custom-call | flops 2097152 | bytes 9437200 | tf_op jit(solution)/shard_map/pallas_call | solution.py:198
  212.6 10.1 %collective-permute-start.20 = (bf16[512,512]{1,0:T(8,128)(2,1)}, bf16[512,512]{1,0:T(8,128)(2,1)}, u32[]{:S(2)}, u32[]{:S(2)}) collective-permute-start(bf16[512,512]{1,0:T(8,128)(2,1)} %get-tuple-element.64.refs_1_), channel_id=1, source_target_pairs={{0,3},{1,5},{2,1},{3,7},{4,0},{5,6},{6,2},{7,4},{8,11},{9,13},{10,... | collective-permute-start | bytes 1572872 | tf_op jit(solution)/shard_map/ppermute | solution.py:450
  222.7 5.4 %collective-permute-start.22 = (bf16[512,512]{1,0:T(8,128)(2,1)}, bf16[512,512]{1,0:T(8,128)(2,1)}, u32[]{:S(2)}, u32[]{:S(2)}) collective-permute-start(bf16[512,512]{1,0:T(8,128)(2,1)} %get-tuple-element.66.refs_3_), channel_id=1, source_target_pairs={{0,0},{1,6},{2,2},{3,4},{4,3},{5,5},{6,1},{7,7},{8,8},{9,14},{10,1... | collective-permute-start | bytes 1572872 | tf_op jit(solution)/shard_map/ppermute | solution.py:450
  228.1 1.2 fusion.2.leads
  229.6 6.2 %shard_map.116 = bf16[512,1024]{1,0:T(8,128)(2,1)} custom-call(bf16[512,512]{1,0:T(8,128)(2,1)} %get-tuple-element.63.refs_0_, bf16[512,512]{1,0:T(8,128)(2,1)} %get-tuple-element.64.refs_1_, bf16[512,512]{1,0:T(8,128)(2,1)} %get-tuple-element.65.refs_2_, bf16[512,512]{1,0:T(8,128)(2,1)} %get-tuple-element.66.refs_3_, ...), custom_call_target="tpu_custom_call" | custom-call | flops 2147483648 | bytes 7340032 | tf_op jit(solution)/shard_map/pallas_call | solution.py:198
  235.9 12.2 %collective-permute-done.20.refs_5_ = bf16[512,512]{1,0:T(8,128)(2,1)} collective-permute-done((bf16[512,512]{1,0:T(8,128)(2,1)}, bf16[512,512]{1,0:T(8,128)(2,1)}, u32[]{:S(2)}, u32[]{:S(2)}) %collective-permute-start.20) | collective-permute-done | bytes 524320 | tf_op jit(solution)/shard_map/ppermute | solution.py:450
  248.1 5.3 %shard_map.118 = bf16[512,1024]{1,0:T(8,128)(2,1)} custom-call(s32[4]{0:T(128)} %fusion.2.leads, bf16[512,512]{1,0:T(8,128)(2,1)} %copy-done.4, bf16[512,512]{1,0:T(8,128)(2,1)} %copy-done.5, bf16[512,512]{1,0:T(8,128)(2,1)} %copy-done.6, bf16[512,512]{1,0:T(8,128)(2,1)} %copy-done.7, bf16[1024,1024]{1,0:T(8,128)(2,1)} %pad_maximum_fusion.1.refs_8_.refs_4_, ...), custom_call_target="tpu_custom_call" | custom-call | flops 1073741824 | bytes 11534352 | tf_op jit(solution)/shard_map/pallas_call | solution.py:198
  253.4 10.2 %shard_map.117 = bf16[512,1024]{1,0:T(8,128)(2,1)} custom-call(s32[4]{0:T(128)} %fusion.2.leads, bf16[512,1024]{1,0:T(8,128)(2,1)} %tokens.3, f32[1,1024]{1,0:T(1,128)} %bitcast.26, bf16[512,512]{1,0:T(8,128)(2,1)} %copy-done.4, bf16[512,512]{1,0:T(8,128)(2,1)} %copy-done.5, bf16[512,512]{1,0:T(8,128)(2,1)} %copy-done.6, bf16[512,512]{1,0:T(8,128)(2,1)} %copy-done.7, ...), custom_call_target="tpu_custom_call" | custom-call | flops 3221225472 | bytes 14684176 | tf_op jit(solution)/shard_map/pallas_call | solution.py:198
  263.6 22.1 %all-reduce.4.cloned.1.call-done = bf16[512,1024]{1,0:T(8,128)(2,1)} async-done(((bf16[512,1024]{1,0:T(8,128)(2,1)}), bf16[512,1024]{1,0:T(8,128)(2,1)}) %all-reduce.4.cloned.1.call-update) | async-done | bytes 1048592 | tf_op jit(solution)/shard_map/psum | solution.py:498
  285.7 3.4 collective-permute-start.23
  289.1 57.4 %all-reduce.6.cloned.1.call-done = bf16[512,1024]{1,0:T(8,128)(2,1)} async-done(((bf16[512,1024]{1,0:T(8,128)(2,1)}), bf16[512,1024]{1,0:T(8,128)(2,1)}) %all-reduce.6.cloned.1.call-update) | async-done | bytes 1048592 | tf_op jit(solution)/shard_map/psum | solution.py:502
  346.5 3.4 collective-permute-start.24
  349.9 1.4 select_convert_fusion
  351.3 1.1 slice_multiply_fusion
  352.5 10.0 %collective-permute-done.24 = bf16[512,1024]{1,0:T(8,128)(2,1)S(1)} collective-permute-done((bf16[512,1024]{1,0:T(8,128)(2,1)}, bf16[512,1024]{1,0:T(8,128)(2,1)S(1)}, u32[]{:S(2)}, u32[]{:S(2)}) %collective-permute-start.24) | collective-permute-done | bytes 1048608 | tf_op jit(solution)/shard_map/ppermute | solution.py:450
  363.0 2.1 pad_maximum_fusion
  (70 shorter events, 7.6 us)
Async XLA Ops:
  7.2 5.7 %copy-start.8 = (bf16[4,192,1024]{2,1,0:T(8,128)(2,1)S(1)}, bf16[4,192,1024]{2,1,0:T(8,128)(2,1)}, u32[]{:S(2)}) copy-start(bf16[4,192,1024]{2,1,0:T(8,128)(2,1)} %param.10) | copy-start | bytes 4718596
  7.2 93.1 %all-gather.2.cloned.1.call-start = ((), (), s32[]{:S(2)}) async-start(), calls=%async_computation | async-start | bytes 2621440 | tf_op jit(solution)/shard_map/all_gather | solution.py:481
  9.9 16.0 %collective-permute-start.3 = (bf16[512,1024]{1,0:T(8,128)(2,1)}, bf16[512,1024]{1,0:T(8,128)(2,1)}, u32[]{:S(2)}, u32[]{:S(2)}) collective-permute-start(bf16[512,1024]{1,0:T(8,128)(2,1)} %shard_map.111), channel_id=1, source_target_pairs={{2,0},{4,1},{0,2},{6,3},{1,4},{7,5},{3,6},{5,7},{10,8},{12,9},{8,1... | collective-permute-start | bytes 3145736 | tf_op jit(solution)/shard_map/ppermute | solution.py:450
  13.0 1.0 copy-start.1
  15.5 27.6 %copy-start.2 = (bf16[512,1024]{1,0:T(8,128)(2,1)S(1)}, bf16[512,1024]{1,0:T(8,128)(2,1)}, u32[]{:S(2)}) copy-start(bf16[512,1024]{1,0:T(8,128)(2,1)} %shard_map.111) | copy-start | bytes 3145732
  15.5 41.4 %collective-permute-start.1 = (bf16[1024,1024]{1,0:T(8,128)(2,1)}, bf16[1024,1024]{1,0:T(8,128)(2,1)}, u32[]{:S(2)}, u32[]{:S(2)}) collective-permute-start(bf16[1024,1024]{1,0:T(8,128)(2,1)} %pad_maximum_fusion.1.refs_8_.refs_4_), channel_id=1, source_target_pairs={{0,1},{1,0},{2,3},{3,2},{4,5},{5,4},{6,7},{7,6},{8,9},{9,8},{10,11... | collective-permute-start | bytes 6291464 | tf_op jit(solution)/shard_map/ppermute | solution.py:473
  26.0 28.6 %collective-permute-start.6 = (bf16[512,1024]{1,0:T(8,128)(2,1)}, bf16[512,1024]{1,0:T(8,128)(2,1)}, u32[]{:S(2)}, u32[]{:S(2)}) collective-permute-start(bf16[512,1024]{1,0:T(8,128)(2,1)} %collective-permute-done.3.refs_0_.refs_8_.refs_4_), channel_id=1, source_target_pairs={{1,3},{3,1},{4,6},{6,4},{9,11},{11,9},{12,14},{14,12},{17,19},{19,... | collective-permute-start | bytes 3145736 | tf_op jit(solution)/shard_map/ppermute | solution.py:450
  28.1 15.0 %collective-permute-start = (bf16[256,1024]{1,0:T(8,128)(2,1)S(1)}, bf16[256,1024]{1,0:T(8,128)(2,1)}, u32[]{:S(2)}, u32[]{:S(2)}) collective-permute-start(bf16[256,1024]{1,0:T(8,128)(2,1)S(1)} %fusion), channel_id=1, source_target_pairs={{2,0},{0,2},{3,1},{1,3},{6,4},{4,6},{7,5},{5,7},{10,8},{8,10},{11,... | collective-permute-start | bytes 1572872 | tf_op jit(solution)/shard_map/ppermute | solution.py:470
  43.1 242.6 %all-reduce.4.cloned.1.call-start = ((), (), s32[]{:S(2)}) async-start(), calls=%async_computation.1 | async-start | bytes 2097152 | tf_op jit(solution)/shard_map/psum | solution.py:498
  43.1 23.9 %collective-permute-start.4 = (bf16[512,1024]{1,0:T(8,128)(2,1)S(1)}, bf16[512,1024]{1,0:T(8,128)(2,1)}, u32[]{:S(2)}, u32[]{:S(2)}) collective-permute-start(bf16[512,1024]{1,0:T(8,128)(2,1)S(1)} %copy-done.2), channel_id=1, source_target_pairs={{3,0},{5,1},{1,2},{7,3},{0,4},{6,5},{2,6},{4,7},{11,8},{13,9},{9,1... | collective-permute-start | bytes 3145736 | tf_op jit(solution)/shard_map/ppermute | solution.py:450
  56.9 21.2 %collective-permute-start.5 = (bf16[512,1024]{1,0:T(8,128)(2,1)S(1)}, bf16[512,1024]{1,0:T(8,128)(2,1)S(1)}, u32[]{:S(2)}, u32[]{:S(2)}) collective-permute-start(bf16[512,1024]{1,0:T(8,128)(2,1)S(1)} %get-tuple-element.91), channel_id=1, source_target_pairs={{0,4},{1,0},{2,6},{3,2},{4,5},{5,1},{6,7},{7,3},{8,12},{9,8},{10,1... | collective-permute-start | bytes 3145736 | tf_op jit(solution)/shard_map/ppermute | solution.py:450
  57.9 20.1 %copy-start.10 = (bf16[512,1024]{1,0:T(8,128)(2,1)S(1)}, bf16[512,1024]{1,0:T(8,128)(2,1)}, u32[]{:S(2)}) copy-start(bf16[512,1024]{1,0:T(8,128)(2,1)} %param.13) | copy-start | bytes 3145732
  78.1 14.8 %copy-start.11 = (bf16[512,1024]{1,0:T(8,128)(2,1)}, bf16[512,1024]{1,0:T(8,128)(2,1)S(1)}, u32[]{:S(2)}) copy-start(bf16[512,1024]{1,0:T(8,128)(2,1)S(1)} %collective-permute-done.5.refs_2_.refs_10_.refs_6_) | copy-start | bytes 3145732
  78.1 14.8 %collective-permute-start.9 = (bf16[512,1024]{1,0:T(8,128)(2,1)S(1)}, bf16[512,1024]{1,0:T(8,128)(2,1)S(1)}, u32[]{:S(2)}, u32[]{:S(2)}) collective-permute-start(bf16[512,1024]{1,0:T(8,128)(2,1)S(1)} %copy-done.10), channel_id=1, source_target_pairs={{2,0},{4,1},{0,2},{6,3},{1,4},{7,5},{3,6},{5,7},{10,8},{12,9},{8,1... | collective-permute-start | bytes 3145736 | tf_op jit(solution)/shard_map/ppermute | solution.py:450
  92.9 28.3 %copy-start.3 = (bf16[512,1024]{1,0:T(8,128)(2,1)}, bf16[512,1024]{1,0:T(8,128)(2,1)S(1)}, u32[]{:S(2)}) copy-start(bf16[512,1024]{1,0:T(8,128)(2,1)S(1)} %collective-permute-done.9.refs_0_.refs_4_) | copy-start | bytes 3145732
  92.9 28.3 %collective-permute-start.12 = (bf16[512,1024]{1,0:T(8,128)(2,1)S(1)}, bf16[512,1024]{1,0:T(8,128)(2,1)}, u32[]{:S(2)}, u32[]{:S(2)}) collective-permute-start(bf16[512,1024]{1,0:T(8,128)(2,1)S(1)} %collective-permute-done.9.refs_0_.refs_4_), channel_id=1, source_target_pairs={{1,3},{3,1},{4,6},{6,4},{9,11},{11,9},{12,14},{14,12},{17,19},{19,... | collective-permute-start | bytes 3145736 | tf_op jit(solution)/shard_map/ppermute | solution.py:450
  100.2 26.8 %collective-permute-start.2 = (bf16[1024,1024]{1,0:T(8,128)(2,1)}, bf16[1024,1024]{1,0:T(8,128)(2,1)S(1)}, u32[]{:S(2)}, u32[]{:S(2)}) collective-permute-start(bf16[1024,1024]{1,0:T(8,128)(2,1)} %all-gather.2.cloned.1.call-done.refs_9_.refs_5_), channel_id=1, source_target_pairs={{0,1},{1,0},{2,3},{3,2},{4,5},{5,4},{6,7},{7,6},{8,9},{9,8},{10,11... | collective-permute-start | bytes 6291464 | tf_op jit(solution)/shard_map/ppermute | solution.py:473
  114.4 20.2 %collective-permute-start.7 = (bf16[1536,512]{1,0:T(8,128)(2,1)}, bf16[1536,512]{1,0:T(8,128)(2,1)}, u32[]{:S(2)}, u32[]{:S(2)}) collective-permute-start(bf16[1536,512]{1,0:T(8,128)(2,1)} %get-tuple-element.51), channel_id=1, source_target_pairs={{0,1},{1,8},{8,9},{9,16},{16,17},{17,24},{24,25},{2,3},{3,10},{10,... | collective-permute-start | bytes 4718600 | tf_op jit(solution)/shard_map/ppermute | solution.py:419
  118.0 8.4 %copy-start.15 = (s32[64]{0:T(128)S(1)}, s32[64]{0:T(128)}, u32[]{:S(2)}) copy-start(s32[64]{0:T(128)} %param.12) | copy-start | bytes 772
  118.0 16.7 %collective-permute-start.8 = (bf16[1536,512]{1,0:T(8,128)(2,1)}, bf16[1536,512]{1,0:T(8,128)(2,1)}, u32[]{:S(2)}, u32[]{:S(2)}) collective-permute-start(bf16[1536,512]{1,0:T(8,128)(2,1)} %get-tuple-element.52), channel_id=1, source_target_pairs={{1,0},{8,1},{9,8},{16,9},{17,16},{24,17},{25,24},{3,2},{10,3},{11,... | collective-permute-start | bytes 4718600 | tf_op jit(solution)/shard_map/ppermute | solution.py:419
  119.5 15.2 %collective-permute-start.10 = (bf16[512,1024]{1,0:T(8,128)(2,1)}, bf16[512,1024]{1,0:T(8,128)(2,1)}, u32[]{:S(2)}, u32[]{:S(2)}) collective-permute-start(bf16[512,1024]{1,0:T(8,128)(2,1)} %param.13), channel_id=1, source_target_pairs={{3,0},{5,1},{1,2},{7,3},{0,4},{6,5},{2,6},{4,7},{11,8},{13,9},{9,1... | collective-permute-start | bytes 3145736 | tf_op jit(solution)/shard_map/ppermute | solution.py:450
  123.9 21.1 %collective-permute-start.11 = (bf16[512,1024]{1,0:T(8,128)(2,1)}, bf16[512,1024]{1,0:T(8,128)(2,1)S(1)}, u32[]{:S(2)}, u32[]{:S(2)}) collective-permute-start(bf16[512,1024]{1,0:T(8,128)(2,1)} %get-tuple-element.89), channel_id=1, source_target_pairs={{0,4},{1,0},{2,6},{3,2},{4,5},{5,1},{6,7},{7,3},{8,12},{9,8},{10,1... | collective-permute-start | bytes 3145736 | tf_op jit(solution)/shard_map/ppermute | solution.py:450
  127.0 62.8 %copy-start = (bf16[1024,1024]{1,0:T(8,128)(2,1)}, bf16[1024,1024]{1,0:T(8,128)(2,1)S(1)}, u32[]{:S(2)}) copy-start(bf16[1024,1024]{1,0:T(8,128)(2,1)S(1)} %collective-permute-done.2.refs_11_.refs_7_) | copy-start | bytes 6291460
  145.0 1.0 copy-start.12
  189.8 16.5 %collective-permute-start.17 = (bf16[1536,512]{1,0:T(8,128)(2,1)}, bf16[1536,512]{1,0:T(8,128)(2,1)}, u32[]{:S(2)}, u32[]{:S(2)}) collective-permute-start(bf16[1536,512]{1,0:T(8,128)(2,1)} %get-tuple-element.61), channel_id=1, source_target_pairs={{1,0},{8,1},{9,8},{16,9},{17,16},{24,17},{25,24},{3,2},{10,3},{11,... | collective-permute-start | bytes 4718600 | tf_op jit(solution)/shard_map/ppermute | solution.py:419
  191.1 15.9 %collective-permute-start.18 = (bf16[1536,512]{1,0:T(8,128)(2,1)}, bf16[1536,512]{1,0:T(8,128)(2,1)}, u32[]{:S(2)}, u32[]{:S(2)}) collective-permute-start(bf16[1536,512]{1,0:T(8,128)(2,1)} %get-tuple-element.62), channel_id=1, source_target_pairs={{0,1},{1,8},{8,9},{9,16},{16,17},{17,24},{24,25},{2,3},{3,10},{10,... | collective-permute-start | bytes 4718600 | tf_op jit(solution)/shard_map/ppermute | solution.py:419
  195.7 16.9 %collective-permute-start.13 = (bf16[512,512]{1,0:T(8,128)(2,1)}, bf16[512,512]{1,0:T(8,128)(2,1)S(1)}, u32[]{:S(2)}, u32[]{:S(2)}) collective-permute-start(bf16[512,512]{1,0:T(8,128)(2,1)} %get-tuple-element.55.refs_0_), channel_id=1, source_target_pairs={{0,2},{1,4},{2,0},{3,6},{4,1},{5,7},{6,3},{7,5},{8,10},{9,12},{10,... | collective-permute-start | bytes 1572872 | tf_op jit(solution)/shard_map/ppermute | solution.py:450
  197.1 25.5 %collective-permute-start.14 = (bf16[512,512]{1,0:T(8,128)(2,1)}, bf16[512,512]{1,0:T(8,128)(2,1)S(1)}, u32[]{:S(2)}, u32[]{:S(2)}) collective-permute-start(bf16[512,512]{1,0:T(8,128)(2,1)} %get-tuple-element.56.refs_1_), channel_id=1, source_target_pairs={{0,3},{1,5},{2,1},{3,7},{4,0},{5,6},{6,2},{7,4},{8,11},{9,13},{10,... | collective-permute-start | bytes 1572872 | tf_op jit(solution)/shard_map/ppermute | solution.py:450
  198.8 23.8 %collective-permute-start.15 = (bf16[512,512]{1,0:T(8,128)(2,1)}, bf16[512,512]{1,0:T(8,128)(2,1)S(1)}, u32[]{:S(2)}, u32[]{:S(2)}) collective-permute-start(bf16[512,512]{1,0:T(8,128)(2,1)} %get-tuple-element.57.refs_2_), channel_id=1, source_target_pairs={{0,1},{1,7},{2,3},{3,5},{4,2},{5,4},{6,0},{7,6},{8,9},{9,15},{10,1... | collective-permute-start | bytes 1572872 | tf_op jit(solution)/shard_map/ppermute | solution.py:450
  198.8 7.4 %copy-start.13 = (bf16[512,512]{1,0:T(8,128)(2,1)S(1)}, bf16[512,512]{1,0:T(8,128)(2,1)}, u32[]{:S(2)}) copy-start(bf16[512,512]{1,0:T(8,128)(2,1)} %get-tuple-element.58.refs_3_) | copy-start | bytes 1572868
  206.2 29.6 %collective-permute-start.16 = (bf16[512,512]{1,0:T(8,128)(2,1)S(1)}, bf16[512,512]{1,0:T(8,128)(2,1)S(1)}, u32[]{:S(2)}, u32[]{:S(2)}) collective-permute-start(bf16[512,512]{1,0:T(8,128)(2,1)S(1)} %copy-done.13), channel_id=1, source_target_pairs={{0,0},{1,6},{2,2},{3,4},{4,3},{5,5},{6,1},{7,7},{8,8},{9,14},{10,1... | collective-permute-start | bytes 1572872 | tf_op jit(solution)/shard_map/ppermute | solution.py:450
  211.9 23.9 %collective-permute-start.19 = (bf16[512,512]{1,0:T(8,128)(2,1)}, bf16[512,512]{1,0:T(8,128)(2,1)S(1)}, u32[]{:S(2)}, u32[]{:S(2)}) collective-permute-start(bf16[512,512]{1,0:T(8,128)(2,1)} %get-tuple-element.63.refs_0_), channel_id=1, source_target_pairs={{0,2},{1,4},{2,0},{3,6},{4,1},{5,7},{6,3},{7,5},{8,10},{9,12},{10,... | collective-permute-start | bytes 1572872 | tf_op jit(solution)/shard_map/ppermute | solution.py:450
  212.5 23.3 %copy-start.4 = (bf16[512,512]{1,0:T(8,128)(2,1)}, bf16[512,512]{1,0:T(8,128)(2,1)S(1)}, u32[]{:S(2)}) copy-start(bf16[512,512]{1,0:T(8,128)(2,1)S(1)} %collective-permute-done.13.refs_0_) | copy-start | bytes 1572868
  212.6 35.5 %collective-permute-start.20 = (bf16[512,512]{1,0:T(8,128)(2,1)}, bf16[512,512]{1,0:T(8,128)(2,1)}, u32[]{:S(2)}, u32[]{:S(2)}) collective-permute-start(bf16[512,512]{1,0:T(8,128)(2,1)} %get-tuple-element.64.refs_1_), channel_id=1, source_target_pairs={{0,3},{1,5},{2,1},{3,7},{4,0},{5,6},{6,2},{7,4},{8,11},{9,13},{10,... | collective-permute-start | bytes 1572872 | tf_op jit(solution)/shard_map/ppermute | solution.py:450
  222.7 13.1 %copy-start.5 = (bf16[512,512]{1,0:T(8,128)(2,1)}, bf16[512,512]{1,0:T(8,128)(2,1)S(1)}, u32[]{:S(2)}) copy-start(bf16[512,512]{1,0:T(8,128)(2,1)S(1)} %collective-permute-done.14.refs_1_) | copy-start | bytes 1572868
  222.7 25.4 %collective-permute-start.21 = (bf16[512,512]{1,0:T(8,128)(2,1)}, bf16[512,512]{1,0:T(8,128)(2,1)}, u32[]{:S(2)}, u32[]{:S(2)}) collective-permute-start(bf16[512,512]{1,0:T(8,128)(2,1)} %get-tuple-element.65.refs_2_), channel_id=1, source_target_pairs={{0,1},{1,7},{2,3},{3,5},{4,2},{5,4},{6,0},{7,6},{8,9},{9,15},{10,1... | collective-permute-start | bytes 1572872 | tf_op jit(solution)/shard_map/ppermute | solution.py:450
  222.7 13.1 %copy-start.6 = (bf16[512,512]{1,0:T(8,128)(2,1)}, bf16[512,512]{1,0:T(8,128)(2,1)S(1)}, u32[]{:S(2)}) copy-start(bf16[512,512]{1,0:T(8,128)(2,1)S(1)} %collective-permute-done.15.refs_2_) | copy-start | bytes 1572868
  222.7 25.4 %collective-permute-start.22 = (bf16[512,512]{1,0:T(8,128)(2,1)}, bf16[512,512]{1,0:T(8,128)(2,1)}, u32[]{:S(2)}, u32[]{:S(2)}) collective-permute-start(bf16[512,512]{1,0:T(8,128)(2,1)} %get-tuple-element.66.refs_3_), channel_id=1, source_target_pairs={{0,0},{1,6},{2,2},{3,4},{4,3},{5,5},{6,1},{7,7},{8,8},{9,14},{10,1... | collective-permute-start | bytes 1572872 | tf_op jit(solution)/shard_map/ppermute | solution.py:450
  229.3 117.2 %all-reduce.6.cloned.1.call-start = ((), (), s32[]{:S(2)}) async-start(), calls=%async_computation.2 | async-start | bytes 2097152 | tf_op jit(solution)/shard_map/psum | solution.py:502
  235.8 12.2 %copy-start.7 = (bf16[512,512]{1,0:T(8,128)(2,1)}, bf16[512,512]{1,0:T(8,128)(2,1)S(1)}, u32[]{:S(2)}) copy-start(bf16[512,512]{1,0:T(8,128)(2,1)S(1)} %collective-permute-done.16.refs_3_) | copy-start | bytes 1572868
  235.8 17.5 %copy-start.14 = (bf16[512,512]{1,0:T(8,128)(2,1)}, bf16[512,512]{1,0:T(8,128)(2,1)S(1)}, u32[]{:S(2)}) copy-start(bf16[512,512]{1,0:T(8,128)(2,1)S(1)} %collective-permute-done.19.refs_4_) | copy-start | bytes 1572868
  285.7 64.2 %collective-permute-start.23 = (bf16[512,1024]{1,0:T(8,128)(2,1)}, bf16[512,1024]{1,0:T(8,128)(2,1)S(1)}, u32[]{:S(2)}, u32[]{:S(2)}) collective-permute-start(bf16[512,1024]{1,0:T(8,128)(2,1)} %all-reduce.4.cloned.1.call-done), channel_id=1, source_target_pairs={{5,1},{7,3},{0,4},{2,6},{13,9},{15,11},{8,12},{10,14},{21,17},{23,... | collective-permute-start | bytes 3145736 | tf_op jit(solution)/shard_map/ppermute | solution.py:450
  346.5 16.0 %collective-permute-start.24 = (bf16[512,1024]{1,0:T(8,128)(2,1)}, bf16[512,1024]{1,0:T(8,128)(2,1)S(1)}, u32[]{:S(2)}, u32[]{:S(2)}) collective-permute-start(bf16[512,1024]{1,0:T(8,128)(2,1)} %all-reduce.6.cloned.1.call-done), channel_id=1, source_target_pairs={{5,1},{7,3},{0,4},{2,6},{13,9},{15,11},{8,12},{10,14},{21,17},{23,... | collective-permute-start | bytes 3145736 | tf_op jit(solution)/shard_map/ppermute | solution.py:450
  351.3 11.2 %copy-start.9 = (bf16[512,1024]{1,0:T(8,128)(2,1)S(1)}, bf16[512,1024]{1,0:T(8,128)(2,1)}, u32[]{:S(2)}) copy-start(bf16[512,1024]{1,0:T(8,128)(2,1)} %all-reduce.6.cloned.1.call-done) | copy-start | bytes 3145732
Sparse Core Ops, SparseCore 0:
  43.2 56.9 all-gather.1
  229.5 56.2 all-reduce.3
  289.3 57.2 all-reduce.5

commit v5 on v4

--- a/solution.py
+++ b/solution.py
@@ -42,7 +42,7 @@
     feats = heads * HEAD_WIDTH
     chunk = BAND_ROWS * LONGITUDES // steps
     moves = [
-        pltpu.make_async_copy(part, held.at[i], sems.at[i]) for i, part in enumerate(upstream)
+        pltpu.make_async_copy(part, held.at[pl.ds(i * chunk, chunk)], sems.at[i]) for i, part in enumerate(upstream)
     ]
     for move in moves:
         move.start()
@@ -153,9 +153,11 @@
             one_tile(upper, tile)
         return carry
 
-    for i, move in enumerate(moves):
+    for move in moves:
         move.wait()
-        go[pl.ds(pl.multiple_of(order[i], 16), chunk)] = nt(held[i], weight[...]).astype(jnp.bfloat16)
+    grad_heads = nt(held[...], weight[...]).astype(jnp.bfloat16)
+    for i in range(steps):
+        go[pl.ds(pl.multiple_of(order[i], 16), chunk)] = grad_heads[i * chunk:(i + 1) * chunk]
     lax.fori_loop(0, LONGITUDES // tile_cols, tile_pair, 0)
     moves = [
         pltpu.make_async_copy(outq.at[pl.ds(pl.multiple_of(order[i], 16), chunk)], part, sems.at[i])
@@ -224,7 +226,7 @@
         flops=12 * pairs * HEAD_WIDTH * heads + 2 * band * weight.size,
         transcendentals=pairs,
         scratch=[
-            pltpu.VMEM((steps, chunk, width), BF16),
+            pltpu.VMEM((band, width), BF16),
             pltpu.VMEM((band, 2 * feats), BF16),
             pltpu.VMEM((band, feats), BF16),
             pltpu.VMEM((BLOCKS, EXT_ROWS * BLOCK, feats), BF16),
@@ -253,31 +255,42 @@
     )[0]
 
 
+def stacked_moves(parts, held, sems, first=0):
+    chunk = parts[0].shape[0]
+    return [
+        pltpu.make_async_copy(part, held.at[pl.ds(i * chunk, chunk)], sems.at[first + i]) for i, part in enumerate(parts)
+    ]
+
+
+def carry_out(moves):
+    for move in moves:
+        move.start()
+    for move in moves:
+        move.wait()
+
+
 def projection_kernel(steps, feats, order, weight, *refs):
     parts, (qkv, kv_up, kv_down, held, sems) = refs[:steps], refs[steps:]
-    chunk = held.shape[1]
-    moves = [pltpu.make_async_copy(part, held.at[i], sems.at[i]) for i, part in enumerate(parts)]
-    for move in moves:
-        move.start()
-    for i, move in enumerate(moves):
-        move.wait()
-        at = pl.ds(pl.multiple_of(order[i], 16), chunk)
-        for first in range(0, 3 * feats, feats):
-            qkv[at, first:first + feats] = nn(held[i], weight[:, first:first + feats]).astype(BF16)
+    chunk = parts[0].shape[0]
+    carry_out(stacked_moves(parts, held, sems))
+    for first in range(0, 3 * feats, feats):
+        product = nn(held[...], weight[:, first:first + feats]).astype(BF16)
+        for i in range(steps):
+            qkv[pl.ds(pl.multiple_of(order[i], 16), chunk), first:first + feats] = product[i * chunk:(i + 1) * chunk]
     kv_up[...] = qkv[(BAND_ROWS - HALO) * LONGITUDES:, feats:]
     kv_down[...] = qkv[:HALO * LONGITUDES, feats:]
 
 
 def projections(order, weight, parts):
     steps, feats = len(parts), weight.shape[1] // 3
-    chunk, width = parts[0].shape
+    width = parts[0].shape[1]
     band, halo = BAND_ROWS * LONGITUDES, HALO * LONGITUDES
     return call(
         functools.partial(projection_kernel, steps, feats),
         [shape(band, 3 * feats), shape(halo, 2 * feats), shape(halo, 2 * feats)],
         [SMEM, VMEM] + [HBM] * steps, [VMEM] * 3, (order, weight, *parts),
         flops=2 * band * weight.size,
-        scratch=[pltpu.VMEM((steps, chunk, width), BF16), pltpu.SemaphoreType.DMA((steps,))],
+        scratch=[pltpu.VMEM((band, width), BF16), pltpu.SemaphoreType.DMA((steps,))],
     )
 
 
@@ -310,50 +323,44 @@
 
 def weight_grad_kernel(steps, sides, *refs):
     lefts, refs = refs[:steps], refs[steps:]
-    rights, (grad, sums) = [refs[i * steps:(i + 1) * steps] for i in range(sides)], refs[sides * steps:]
-    feats = sums.shape[0] // sides
+    rights, (grad, left, right, sems) = [refs[i * steps:(i + 1) * steps] for i in range(sides)], refs[sides * steps:]
+    feats = left.shape[1] // sides
+    moves = stacked_moves(lefts, left, sems)
     for side, parts in enumerate(rights):
+        moves += stacked_moves(parts, right.at[side], sems, (side + 1) * steps)
+    carry_out(moves)
+    for side in range(sides):
         at = slice(side * feats, (side + 1) * feats)
-        for i, (left, right) in enumerate(zip(lefts, parts)):
-            product = lax.dot_general(
-                left[:, at], right[...], (((0,), (0,)), ((), ())), preferred_element_type=F32
-            )
-            if i == 0:
-                sums[at, :] = product
-            elif i < steps - 1:
-                sums[at, :] += product
-            else:
-                grad[at, :] = (sums[at, :] + product).astype(BF16)
+        grad[at, :] = lax.dot_general(
+            left[:, at], right[side], (((0,), (0,)), ((), ())), preferred_element_type=F32
+        ).astype(BF16)
 
 
 def weight_grad(lefts, *rights):
-    steps, width = len(lefts), rights[0][0].shape[1]
-    rows = lefts[0].shape[1]
+    steps, (chunk, rows), width = len(lefts), lefts[0].shape, rights[0][0].shape[1]
     args = (*lefts, *(part for parts in rights for part in parts))
     return call(
         functools.partial(weight_grad_kernel, steps, len(rights)),
-        [shape(rows, width)], [VMEM] * len(args), [VMEM], args,
+        [shape(rows, width)], [HBM] * len(args), [VMEM], args,
         flops=2 * steps * lefts[0].size * width,
-        scratch=[pltpu.VMEM((rows, width), F32)],
+        scratch=[
+            pltpu.VMEM((steps * chunk, rows), BF16),
+            pltpu.VMEM((len(rights), steps * chunk, width), BF16),
+            pltpu.SemaphoreType.DMA((len(args),)),
+        ],
     )[0]
 
 
-def load_blocks(blocks, held, sems, first):
-    rows = held.shape[1]
-    moves = [
-        pltpu.make_async_copy(block.at[pl.ds(first, rows)], held.at[i], sems.at[i]) for i, block in enumerate(blocks)
-    ]
-    for move in moves:
-        move.start()
-    for move in moves:
-        move.wait()
-
-
 def update_kernel(steps, leads, *refs):
-    parts, blocks, (out, held, sems) = refs[:steps], refs[steps:2 * steps], refs[2 * steps:]
-    feats = held.shape[1]
-    load_blocks(blocks, held, sems, 3 * feats)
-    out[...] = sum(nn(parts[i][:, :feats], held[leads[i]]) for i in range(steps)).astype(BF16)
+    parts, blocks, (out, left, right, sems) = refs[:steps], refs[steps:2 * steps], refs[2 * steps:]
+    feats = right.shape[0] // steps
+    carry_out([
+        pltpu.make_async_copy(block.at[pl.ds(3 * feats, feats)], right.at[pl.ds(i * feats, feats)], sems.at[i])
+        for i, block in enumerate(blocks)
+    ])
+    for i, part in enumerate(parts):
+        left[leads[i]] = part[:, :feats]
+    out[...] = nn(jnp.concatenate([left[i] for i in range(steps)], axis=1), right[...]).astype(BF16)
 
 
 def updates(leads, outq_own, blocks):
@@ -362,20 +369,28 @@
         functools.partial(update_kernel, steps),
         [shape(chunk, width)], [SMEM] + [VMEM] * steps + [HBM] * steps, [VMEM], (leads, *outq_own, *blocks),
         flops=steps * chunk * rows * width // 2,
-        scratch=[pltpu.VMEM((steps, rows // 4, width), BF16), pltpu.SemaphoreType.DMA((steps,))],
+        scratch=[
+            pltpu.VMEM((steps, chunk, rows // 4), BF16),
+            pltpu.VMEM((steps * rows // 4, width), BF16),
+            pltpu.SemaphoreType.DMA((steps,)),
+        ],
     )[0]
 
 
 def grad_input_kernel(steps, leads, tokens, gain, *refs):
-    outq, dkv, blocks, (grad, held, sems) = (
+    outq, dkv, blocks, (grad, left, right, sems) = (
         refs[:steps], refs[steps:2 * steps], refs[2 * steps:3 * steps], refs[3 * steps:]
     )
-    feats = held.shape[1] // 3
-    load_blocks(blocks, held, sems, 0)
-    grad_normed = sum(
-        nn(outq[i][:, feats:], held[leads[i], :feats, :]) + nn(dkv[i][...], held[leads[i], feats:, :])
-        for i in range(steps)
-    )
+    rows = right.shape[0] // steps
+    feats = rows // 3
+    carry_out([
+        pltpu.make_async_copy(block.at[pl.ds(0, rows)], right.at[pl.ds(i * rows, rows)], sems.at[i])
+        for i, block in enumerate(blocks)
+    ])
+    for i in range(steps):
+        left[leads[i], :, :feats] = outq[i][:, feats:]
+        left[leads[i], :, feats:] = dkv[i][...]
+    grad_normed = nn(jnp.concatenate([left[i] for i in range(steps)], axis=1), right[...])
     features = tokens[...].astype(F32)
     inverse = lax.rsqrt(jnp.mean(features * features, axis=1, keepdims=True) + 1e-06)
     centred = features * inverse
@@ -384,13 +399,18 @@
 
 
 def grad_inputs(leads, tokens, gain, outq_own, dkv_own, blocks):
-    steps, (rows, width) = len(blocks), blocks[0].shape
+    steps, (rows, width), chunk = len(blocks), blocks[0].shape, tokens.shape[0]
+    rows = rows * 3 // 4
     return call(
         functools.partial(grad_input_kernel, steps),
         [shape(*tokens.shape)], [SMEM] + [VMEM] * (2 + 2 * steps) + [HBM] * steps, [VMEM],
         (leads, tokens, gain[None, :], *outq_own, *dkv_own, *blocks),
-        flops=steps * tokens.shape[0] * rows * width * 3 // 2,
-        scratch=[pltpu.VMEM((steps, rows * 3 // 4, width), BF16), pltpu.SemaphoreType.DMA((steps,))],
+        flops=2 * steps * chunk * rows * width,
+        scratch=[
+            pltpu.VMEM((steps, chunk, rows), BF16),
+            pltpu.VMEM((steps * rows, width), BF16),
+            pltpu.SemaphoreType.DMA((steps,)),
+        ],
     )[0]
 
 
@@ -452,11 +472,11 @@
     def send_back(parts):
         return [permuted(x, list(zip(spots, slot))) for x, slot in zip(parts, slots)]
 
-    def gathered(x):
+    def gathered(x, *others):
         sent = lambda slot: permuted(x, list(zip(slot, spots)))
         if halves != 2:
             return [sent(slot) for slot in slots]
-        first, second = sent(slots[0]), sent(slots[1])
+        first, second, *others = lax.optimization_barrier((sent(slots[0]), sent(slots[1]), *others))
         third = permuted(
             jnp.where(c == y, first, x),
             [(spot, (1 - spot[0], spot[1], spot[0]) if spot[2] == spot[0] else (spot[0], spot[1], spot[0])) for spot in spots],
@@ -464,6 +484,7 @@
         fourth = permuted(
             first, [(spot, (spot[0], 1 - spot[1], spot[2])) for spot in spots if spot[2] != spot[0]]
         )
+        third, fourth = lax.optimization_barrier((third, fourth))
         return [first, second, third, jnp.where(c == y, x, fourth)]
 
     def from_ahead(x, dm):
@@ -472,47 +493,54 @@
     def from_sibling(x):
         return lax.ppermute(x, "c", [(0, 1), (1, 0)])
 
-    split = qkv_weight.reshape(heads, 3, HEAD_WIDTH, WIDTH).transpose(1, 0, 2, 3).reshape(3 * feats, WIDTH)
-    eighth = jnp.where(jnp.arange(3 * feats) < feats, HEAD_WIDTH ** -0.5, 1.0)[:, None].astype(BF16)
-    weight = jnp.concatenate([split * eighth, out_weight.reshape(feats, WIDTH)], axis=0)
+    raw = jnp.concatenate([qkv_weight.reshape(3 * feats, WIDTH), out_weight.reshape(feats, WIDTH)], axis=0)
     share = 4 * feats // layers
-    held = lax.dynamic_slice_in_dim(weight, z * share, share, 0)
-    blocks = [weight]
-    blocks += [lax.all_gather(from_ahead(held, dm), "z", axis=0, tiled=True) for dm in range(1, halves)]
-    blocks += [from_sibling(block) for block in blocks]
-    group = jnp.where(c == y, weight, blocks[halves])
+    held = lax.dynamic_slice_in_dim(raw, z * share, share, 0)
+    shares = [from_ahead(held, dm) for dm in range(1, halves)]
+
+    def split(block):
+        qkv = block[:3 * feats].reshape(heads, 3, HEAD_WIDTH, WIDTH)
+        eighth = jnp.asarray([HEAD_WIDTH ** -0.5, 1.0, 1.0], BF16)[None, :, None, None]
+        qkv = (qkv * eighth).transpose(1, 0, 2, 3).reshape(3 * feats, WIDTH)
+        return jnp.concatenate([qkv, block[3 * feats:]], axis=0)
+
+    blocks = [split(raw)]
+    sibling = from_sibling(blocks[0])
+    group = jnp.where(c == y, blocks[0], sibling)
     group_qkv, group_out = group[:3 * feats].T, group[3 * feats:]
 
     *normed_parts, group_qkv, group_out = lax.optimization_barrier(
         (*gathered(norm(tokens, gain)), group_qkv, group_out)
     )
-    upstream_parts = gathered(after(upstream, *normed_parts))
     qkv, kv_up, kv_down = projections(order, group_qkv, normed_parts)
+    upstream_parts = gathered(after(upstream, *normed_parts), qkv)
     kv_top, kv_bot = passed_along(kv_up, 1), passed_along(kv_down, -1)
-    order, *blocks = lax.optimization_barrier((order, *blocks))
+    shares = lax.optimization_barrier((shares, normed_parts))[0]
+    ahead = [split(lax.all_gather(part, "z", axis=0, tiled=True)) for part in shares]
+    order, kv_top, kv_bot, *ahead = lax.optimization_barrier((order, kv_top, kv_bot, *ahead))
     outq_parts, dkv, dkv_top, dkv_bot = attention(cells, order, qkv, kv_top, kv_bot, group_out, upstream_parts)
 
+    blocks += ahead + [sibling] + [from_sibling(after(block, dkv_top)) for block in ahead]
     from_above, from_below = passed_along(dkv_top, -1), passed_along(dkv_bot, 1)
     outq_own = send_back(outq_parts)
     early = weight_grad(outq_parts, upstream_parts, normed_parts)
-    early_sum = lax.psum(early, ("z", "c"))
     dkv_parts = joined(after(order, early), dkv, from_above, from_below, len(slots))
     dkv_own = send_back(dkv_parts)
     late = weight_grad(dkv_parts, normed_parts)
-    late_sum = lax.psum(late, ("c", "z"))
-    leads, outq_own, dkv_own = lax.optimization_barrier((leads, outq_own, dkv_own))
-    update = updates(leads, outq_own, blocks)
+    grads = lax.psum(jnp.concatenate([early, late], axis=0), ("z", "c"))
+    update = updates(after(leads, late), outq_own, blocks)
     grad_input = grad_inputs(after(leads, late), tokens, gain, outq_own, dkv_own, blocks)
 
     def spread(grads):
         pairs = [((1 - y, m, 1 - y), (y, m, 1 - y)) for y in range(2) for m in range(halves)]
         return jnp.where(c == y, grads, permuted(grads, pairs)).astype(F32)
 
-    early_sum, grad_input, update = lax.optimization_barrier((early_sum, grad_input, update))
-    early, late = spread(early_sum), spread(late_sum) * grad_scale
+    grads, grad_input, update = lax.optimization_barrier((grads, grad_input, update))
+    grads = spread(grads) * grad_scale
+    early, late = grads[:2 * feats], grads[2 * feats:]
     by_head = lambda x: x.reshape(heads, HEAD_WIDTH, WIDTH)
-    grad_out = by_head(early[:feats] * grad_scale)
-    grad_query = early[feats:] * (grad_scale * HEAD_WIDTH ** -0.5)
+    grad_out = by_head(early[:feats])
+    grad_query = early[feats:] * HEAD_WIDTH ** -0.5
     grad_qkv = jnp.concatenate([by_head(grad_query), by_head(late[:feats]), by_head(late[feats:])], axis=1)
     return update, grad_input, grad_qkv, grad_out
 

time: 373 us -> 322 us (0.86)
  waiting for transfers between devices: 180 us -> 114 us
  starting transfers between devices: 63.6 us -> 72.3 us
  other arithmetic: 13.4 us -> 19.1 us
    psum x2 -> x1, waiting for transfers between devices: 79.5 us -> 33 us  [on_device(): grads = lax.psum(jnp.concatenate([early, late], axis=0), ('z', 'c'))]
    ppermute x18 -> x17, waiting for transfers between devices: 81.9 us -> 70.6 us  [permuted(): return lax.ppermute(x, GROUP, [(at(*a), at(*b)) for a, b in pairs])]
    ppermute x1, waiting for transfers between devices: 12.9 us -> 2.18 us  [from_ahead(): return lax.ppermute(x, 'm', [((i + dm) % halves, i) for i in range(halves)])]
    ppermute x4, starting transfers between devices: 10.9 us -> 20 us  [passed_along(): return lax.ppermute(x, ('z', 'c'), pairs)]
    concatenate x2 -> x4, other arithmetic: 2.04 us -> 5.99 us  [the longest x1 2.72 us: on_device(): grads = lax.psum(jnp.concatenate([early, late], axis=0), ('z', 'c'))]
    ppermute x18 -> x17, starting transfers between devices: 50.1 us -> 50 us  [permuted(): return lax.ppermute(x, GROUP, [(at(*a), at(*b)) for a, b in pairs])]
  transfers between devices with their start and end apart: 28 -> 26, of which waited for: 12 -> 9; matrix products, arithmetic and copies ran while one was open for 5% -> 6% of each run, Pallas kernels for 12% -> 14%
where the time goes in v5:
time: 322 us; the launch traced here: 321 us
  waiting for transfers between devices  114 us (35%)
  Pallas kernels  90.1 us (28%)
  starting transfers between devices  72.3 us (22%)
  other arithmetic  19.1 us (6%)
  between operations  14.4 us (4%)
  local copies, waits for them, and re-layouts  10.5 us (3%)
    pallas_call x8, Pallas kernels, call(): pl.pallas_call(kernel, out_shape=tuple(out_shape), in_specs=list(in_specs...  90.1 us
    ppermute x17, waiting for transfers between devices, permuted(): return lax.ppermute(x, GROUP, [(at(*a), at(*b)) for a, b in pairs])  70.6 us
    ppermute x17, starting transfers between devices, permuted(): return lax.ppermute(x, GROUP, [(at(*a), at(*b)) for a, b in pairs])  50 us
    psum x1, waiting for transfers between devices, on_device(): grads = lax.psum(jnp.concatenate([early, late], axis=0), ('z', 'c'))  33 us
    ppermute x4, starting transfers between devices, passed_along(): return lax.ppermute(x, ('z', 'c'), pairs)  20 us
    all_gather x1, waiting for transfers between devices, on_device(): lax.all_gather(part, 'z', axis=0, tiled=True)  8.57 us
  transfers between devices with their start and end apart: 26, of which 9 were waited for; matrix products, arithmetic and copies ran while one was open for 6% of the time, Pallas kernels for 14%

profile of v5, /device:TPU:0, one launch (start us, length us, event | category | flops | bytes accessed | tf_op | source)
XLA Modules:
  0.0 320.8 jit_solution(15240827271317980519)
XLA Ops:
  7.2 2.7 shard_map.129
  9.9 3.0 collective-permute-start.1
  12.9 1.5 collective-permute-start
  15.6 1.5 pad_maximum_fusion.1.refs_8_.refs_4_
  17.2 19.4 %collective-permute-done.1.refs_1_.refs_9_.refs_5_ = bf16[512,1024]{1,0:T(8,128)(2,1)} collective-permute-done((bf16[512,1024]{1,0:T(8,128)(2,1)}, bf16[512,1024]{1,0:T(8,128)(2,1)}, u32[]{:S(2)}, u32[]{:S(2)}) %collective-permute-start.1) | collective-permute-done | bytes 1048608 | tf_op jit(solution)/shard_map/ppermute | solution.py:470
  36.5 2.3 broadcast_select_fusion.4
  38.8 1.5 collective-permute-start.2
  40.3 1.7 collective-permute-start.3
  42.0 1.6 fusion
  44.6 8.4 %collective-permute-done.2.refs_2_.refs_10_.refs_6_ = bf16[512,1024]{1,0:T(8,128)(2,1)} collective-permute-done((bf16[512,1024]{1,0:T(8,128)(2,1)}, bf16[512,1024]{1,0:T(8,128)(2,1)}, u32[]{:S(2)}, u32[]{:S(2)}) %collective-permute-start.2) | collective-permute-done | bytes 1048608 | tf_op jit(solution)/shard_map/ppermute | solution.py:470
  56.4 2.2 collective-permute-done.7
  58.7 10.3 %collective-permute-start.9 = (bf16[512,1024]{1,0:T(8,128)(2,1)}, bf16[512,1024]{1,0:T(8,128)(2,1)}, u32[]{:S(2)}, u32[]{:S(2)}) collective-permute-start(bf16[512,1024]{1,0:T(8,128)(2,1)} %param.15), channel_id=1, source_target_pairs={{3,0},{5,1},{1,2},{7,3},{0,4},{6,5},{2,6},{4,7},{11,8},{13,9},{9,1... | collective-permute-start | bytes 3145736 | tf_op jit(solution)/shard_map/ppermute | solution.py:470
  69.0 1.7 collective-permute-start.8
  71.8 1.6 copy.15.weight
  73.4 10.2 %shard_map.130 = (bf16[2048,768]{1,0:T(8,128)(2,1)}, bf16[1536,512]{1,0:T(8,128)(2,1)}, bf16[1536,512]{1,0:T(8,128)(2,1)}) custom-call(s32[4]{0:T(128)} %fusion.1.order, bf16[1024,768]{1,0:T(8,128)(2,1)} %copy.15.weight, bf16[512,1024]{1,0:T(8,128)(2,1)} %collective-permute-done.refs_0_.refs_8_.refs_4_, ...), custom_call_target="tpu_custom_call" | custom-call | flops 3221225472 | bytes 12058640 | tf_op jit(solution)/shard_map/pallas_call | solution.py:200
  83.6 8.7 %collective-permute-done.9.refs_1_.refs_5_ = bf16[512,1024]{1,0:T(8,128)(2,1)} collective-permute-done((bf16[512,1024]{1,0:T(8,128)(2,1)}, bf16[512,1024]{1,0:T(8,128)(2,1)}, u32[]{:S(2)}, u32[]{:S(2)}) %collective-permute-start.9) | collective-permute-done | bytes 1048608 | tf_op jit(solution)/shard_map/ppermute | solution.py:470
  92.3 1.3 broadcast_select_fusion.2
  93.7 1.3 collective-permute-start.10
  95.7 4.9 %collective-permute-start.5 = (bf16[1536,512]{1,0:T(8,128)(2,1)}, bf16[1536,512]{1,0:T(8,128)(2,1)}, u32[]{:S(2)}, u32[]{:S(2)}) collective-permute-start(bf16[1536,512]{1,0:T(8,128)(2,1)} %get-tuple-element.53), channel_id=1, source_target_pairs={{0,1},{1,8},{8,9},{9,16},{16,17},{17,24},{24,25},{2,3},{3,10},{10,... | collective-permute-start | bytes 4718600 | tf_op jit(solution)/shard_map/ppermute | solution.py:439
  100.6 1.5 collective-permute-start.6
  102.7 4.5 %collective-permute-done.10.refs_2_.refs_6_ = bf16[512,1024]{1,0:T(8,128)(2,1)} collective-permute-done((bf16[512,1024]{1,0:T(8,128)(2,1)S(1)}, bf16[512,1024]{1,0:T(8,128)(2,1)}, u32[]{:S(2)}, u32[]{:S(2)}) %collective-permute-start.10) | collective-permute-done | bytes 1048608 | tf_op jit(solution)/shard_map/ppermute | solution.py:470
  108.4 8.6 %all-gather.2.cloned.1.call-done = bf16[1024,1024]{1,0:T(8,128)(2,1)} async-done(((bf16[256,1024]{1,0:T(8,128)(2,1)}), bf16[1024,1024]{1,0:T(8,128)(2,1)}) %all-gather.2.cloned.1.call-update) | async-done | bytes 2097168 | tf_op jit(solution)/shard_map/all_gather | solution.py:519
  116.9 1.4 slice-done
  119.8 42.8 %shard_map.131 = (bf16[512,512]{1,0:T(8,128)(2,1)}, bf16[512,512]{1,0:T(8,128)(2,1)}, bf16[512,512]{1,0:T(8,128)(2,1)}, bf16[512,512]{1,0:T(8,128)(2,1)}, f32[20...) custom-call(s32[20]{0:T(128)} %pad_dynamic-slice_fusion.2.cells, s32[4]{0:T(128)} %fusion.1.order, ...), custom_call_target="tpu_custom_call" | custom-call | flops 13958643712 | bytes 20447328 | tf_op jit(solution)/shard_map/pallas_call | solution.py:200
  162.6 12.4 %collective-permute-start.13 = (bf16[1536,512]{1,0:T(8,128)(2,1)}, bf16[1536,512]{1,0:T(8,128)(2,1)}, u32[]{:S(2)}, u32[]{:S(2)}) collective-permute-start(bf16[1536,512]{1,0:T(8,128)(2,1)} %get-tuple-element.73), channel_id=1, source_target_pairs={{0,1},{1,8},{8,9},{9,16},{16,17},{17,24},{24,25},{2,3},{3,10},{10,... | collective-permute-start | bytes 4718600 | tf_op jit(solution)/shard_map/ppermute | solution.py:439
  175.0 1.3 collective-permute-start.12
  177.5 1.5 collective-permute-start.14
  178.9 1.2 collective-permute-start.15
  180.1 7.4 %shard_map.132 = bf16[512,1024]{1,0:T(8,128)(2,1)} custom-call(bf16[512,512]{1,0:T(8,128)(2,1)} %get-tuple-element.66.refs_0_, bf16[512,512]{1,0:T(8,128)(2,1)} %get-tuple-element.67.refs_1_, bf16[512,512]{1,0:T(8,128)(2,1)} %get-tuple-element.68.refs_2_, bf16[512,512]{1,0:T(8,128)(2,1)} %get-tuple-element.69.refs_3_, ...), custom_call_target="tpu_custom_call" | custom-call | flops 2147483648 | bytes 11534336 | tf_op jit(solution)/shard_map/pallas_call | solution.py:200
  187.6 4.8 %collective-permute-start.16 = (bf16[512,512]{1,0:T(8,128)(2,1)}, bf16[512,512]{1,0:T(8,128)(2,1)}, u32[]{:S(2)}, u32[]{:S(2)}) collective-permute-start(bf16[512,512]{1,0:T(8,128)(2,1)} %get-tuple-element.68.refs_2_), channel_id=1, source_target_pairs={{0,1},{1,7},{2,3},{3,5},{4,2},{5,4},{6,0},{7,6},{8,9},{9,15},{10,1... | collective-permute-start | bytes 1572872 | tf_op jit(solution)/shard_map/ppermute | solution.py:470
  192.4 5.4 %collective-permute-start.17 = (bf16[512,512]{1,0:T(8,128)(2,1)}, bf16[512,512]{1,0:T(8,128)(2,1)}, u32[]{:S(2)}, u32[]{:S(2)}) collective-permute-start(bf16[512,512]{1,0:T(8,128)(2,1)} %get-tuple-element.69.refs_3_), channel_id=1, source_target_pairs={{0,0},{1,6},{2,2},{3,4},{4,3},{5,5},{6,1},{7,7},{8,8},{9,14},{10,1... | collective-permute-start | bytes 1572872 | tf_op jit(solution)/shard_map/ppermute | solution.py:470
  197.8 4.9 %shard_map.133 = (bf16[512,512]{1,0:T(8,128)(2,1)}, bf16[512,512]{1,0:T(8,128)(2,1)}, bf16[512,512]{1,0:T(8,128)(2,1)}, bf16[512,512]{1,0:T(8,128)(2,1)}) custom-call(s32[4]{0:T(128)} %fusion.1.order, f32[2048,512]{1,0:T(8,128)} %get-tuple-element.71.own, bf16[1536,512]{1,0:T(8,128)(2,1)} %collective-permute-done.12.above, ...), custom_call_target="tpu_custom_call" | custom-call | flops 2097152 | bytes 9437200 | tf_op jit(solution)/shard_map/pallas_call | solution.py:200
  202.7 6.3 %shard_map.134 = bf16[512,1024]{1,0:T(8,128)(2,1)} custom-call(bf16[512,512]{1,0:T(8,128)(2,1)} %get-tuple-element.74.refs_0_, bf16[512,512]{1,0:T(8,128)(2,1)} %get-tuple-element.75.refs_1_, bf16[512,512]{1,0:T(8,128)(2,1)} %get-tuple-element.76.refs_2_, bf16[512,512]{1,0:T(8,128)(2,1)} %get-tuple-element.77.refs_3_, ...), custom_call_target="tpu_custom_call" | custom-call | flops 2147483648 | bytes 7340032 | tf_op jit(solution)/shard_map/pallas_call | solution.py:200
  209.0 2.7 pad_maximum_fusion.3
  211.8 1.5 collective-permute-start.18
  213.2 2.7 collective-permute-start.19
  215.9 2.7 collective-permute-start.20
  218.6 5.4 %collective-permute-start.21 = (bf16[512,512]{1,0:T(8,128)(2,1)}, bf16[512,512]{1,0:T(8,128)(2,1)}, u32[]{:S(2)}, u32[]{:S(2)}) collective-permute-start(bf16[512,512]{1,0:T(8,128)(2,1)} %get-tuple-element.77.refs_3_), channel_id=1, source_target_pairs={{0,0},{1,6},{2,2},{3,4},{4,3},{5,5},{6,1},{7,7},{8,8},{9,14},{10,1... | collective-permute-start | bytes 1572872 | tf_op jit(solution)/shard_map/ppermute | solution.py:470
  223.9 1.3 fusion.2.leads
  225.2 5.4 %shard_map.136 = bf16[512,1024]{1,0:T(8,128)(2,1)} custom-call(s32[4]{0:T(128)} %fusion.2.leads, bf16[512,512]{1,0:T(8,128)(2,1)} %collective-permute-done.14.refs_0_, bf16[512,512]{1,0:T(8,128)(2,1)} %collective-permute-done.15.refs_1_, bf16[512,512]{1,0:T(8,128)(2,1)} %collective-permute-done.16.refs_2_, bf16[512,512]{1,0:T(8,128)(2,1)} %collective-permute-done.17.refs_3_, ...), custom_call_target="tpu_custom_call" | custom-call | flops 1073741824 | bytes 11534352 | tf_op jit(solution)/shard_map/pallas_call | solution.py:200
  230.6 5.9 %collective-permute-done.19.refs_5_ = bf16[512,512]{1,0:T(8,128)(2,1)S(1)} collective-permute-done((bf16[512,512]{1,0:T(8,128)(2,1)}, bf16[512,512]{1,0:T(8,128)(2,1)S(1)}, u32[]{:S(2)}, u32[]{:S(2)}) %collective-permute-start.19) | collective-permute-done | bytes 524320 | tf_op jit(solution)/shard_map/ppermute | solution.py:470
  237.5 10.3 %shard_map.135 = bf16[512,1024]{1,0:T(8,128)(2,1)} custom-call(s32[4]{0:T(128)} %fusion.2.leads, bf16[512,1024]{1,0:T(8,128)(2,1)} %tokens.3, f32[1,1024]{1,0:T(1,128)} %bitcast.35, bf16[512,512]{1,0:T(8,128)(2,1)} %collective-permute-done.14.refs_0_, bf16[512,512]{1,0:T(8,128)(2,1)} %collective-permute-done.15.refs_1_, ...), custom_call_target="tpu_custom_call" | custom-call | flops 3221225472 | bytes 14684176 | tf_op jit(solution)/shard_map/pallas_call | solution.py:200
  247.8 33.0 %all-reduce.3.cloned.1.call-done = bf16[1024,1024]{1,0:T(8,128)(2,1)} async-done(((bf16[1024,1024]{1,0:T(8,128)(2,1)}), bf16[1024,1024]{1,0:T(8,128)(2,1)}) %all-reduce.3.cloned.1.call-update) | async-done | bytes 2097168 | tf_op jit(solution)/shard_map/psum | solution.py:530
  280.8 3.5 %collective-permute-start.23 = (bf16[1024,1024]{1,0:T(8,128)(2,1)}, bf16[1024,1024]{1,0:T(8,128)(2,1)S(1)}, u32[]{:S(2)}, u32[]{:S(2)}) collective-permute-start(bf16[1024,1024]{1,0:T(8,128)(2,1)} %all-reduce.3.cloned.1.call-done), channel_id=1, source_target_pairs={{5,1},{7,3},{0,4},{2,6},{13,9},{15,11},{8,12},{10,14},{21,17},{23,... | collective-permute-start | bytes 6291464 | tf_op jit(solution)/shard_map/ppermute | solution.py:470
  284.3 23.7 %collective-permute-done.23 = bf16[1024,1024]{1,0:T(8,128)(2,1)S(1)} collective-permute-done((bf16[1024,1024]{1,0:T(8,128)(2,1)}, bf16[1024,1024]{1,0:T(8,128)(2,1)S(1)}, u32[]{:S(2)}, u32[]{:S(2)}) %collective-permute-start.23) | collective-permute-done | bytes 2097184 | tf_op jit(solution)/shard_map/ppermute | solution.py:470
  308.0 2.5 convert_multiply_fusion
  310.5 1.6 fusion.3
  312.1 1.9 pad_maximum_fusion
  (70 shorter events, 13.0 us)
Async XLA Ops:
  7.2 7.2 %copy-start.13 = (bf16[3]{0:T(256)(128)(2,1)S(1)}, bf16[3]{0:T(256)(128)(2,1)}, u32[]{:S(2)}) copy-start(bf16[3]{0:T(256)(128)(2,1)} %constant.38.clone) | copy-start | bytes 22
  7.2 7.2 %copy-start.5 = (bf16[4,192,1024]{2,1,0:T(8,128)(2,1)S(1)}, bf16[4,192,1024]{2,1,0:T(8,128)(2,1)}, u32[]{:S(2)}) copy-start(bf16[4,192,1024]{2,1,0:T(8,128)(2,1)} %param.12) | copy-start | bytes 4718596
  7.2 109.7 %all-gather.2.cloned.1.call-start = ((), (), s32[]{:S(2)}) async-start(), calls=%async_computation | async-start | bytes 2621440 | tf_op jit(solution)/shard_map/all_gather | solution.py:519
  9.9 26.6 %collective-permute-start.1 = (bf16[512,1024]{1,0:T(8,128)(2,1)}, bf16[512,1024]{1,0:T(8,128)(2,1)}, u32[]{:S(2)}, u32[]{:S(2)}) collective-permute-start(bf16[512,1024]{1,0:T(8,128)(2,1)} %shard_map.129), channel_id=1, source_target_pairs={{3,0},{5,1},{1,2},{7,3},{0,4},{6,5},{2,6},{4,7},{11,8},{13,9},{9,1... | collective-permute-start | bytes 3145736 | tf_op jit(solution)/shard_map/ppermute | solution.py:470
  12.9 23.6 %collective-permute-start = (bf16[512,1024]{1,0:T(8,128)(2,1)}, bf16[512,1024]{1,0:T(8,128)(2,1)}, u32[]{:S(2)}, u32[]{:S(2)}) collective-permute-start(bf16[512,1024]{1,0:T(8,128)(2,1)} %shard_map.129), channel_id=1, source_target_pairs={{2,0},{4,1},{0,2},{6,3},{1,4},{7,5},{3,6},{5,7},{10,8},{12,9},{8,1... | collective-permute-start | bytes 3145736 | tf_op jit(solution)/shard_map/ppermute | solution.py:470
  14.6 1.0 copy-start.6
  14.7 2.4 copy-start.2
  15.6 20.9 %copy-start.4 = (bf16[512,1024]{1,0:T(8,128)(2,1)S(1)}, bf16[512,1024]{1,0:T(8,128)(2,1)}, u32[]{:S(2)}) copy-start(bf16[512,1024]{1,0:T(8,128)(2,1)} %shard_map.129) | copy-start | bytes 3145732
  17.1 35.8 %collective-permute-start.4 = (bf16[1024,1024]{1,0:T(8,128)(2,1)}, bf16[1024,1024]{1,0:T(8,128)(2,1)S(1)}, u32[]{:S(2)}, u32[]{:S(2)}) collective-permute-start(bf16[1024,1024]{1,0:T(8,128)(2,1)} %pad_maximum_fusion.1.refs_8_.refs_4_), channel_id=1, source_target_pairs={{0,1},{1,0},{2,3},{3,2},{4,5},{5,4},{6,7},{7,6},{8,9},{9,8},{10,11... | collective-permute-start | bytes 6291464 | tf_op jit(solution)/shard_map/ppermute | solution.py:494
  38.8 14.2 %collective-permute-start.2 = (bf16[512,1024]{1,0:T(8,128)(2,1)}, bf16[512,1024]{1,0:T(8,128)(2,1)}, u32[]{:S(2)}, u32[]{:S(2)}) collective-permute-start(bf16[512,1024]{1,0:T(8,128)(2,1)} %broadcast_select_fusion.4), channel_id=1, source_target_pairs={{0,4},{1,0},{2,6},{3,2},{4,5},{5,1},{6,7},{7,3},{8,12},{9,8},{10,1... | collective-permute-start | bytes 3145736 | tf_op jit(solution)/shard_map/ppermute | solution.py:470
  40.3 12.6 %collective-permute-start.3 = (bf16[512,1024]{1,0:T(8,128)(2,1)}, bf16[512,1024]{1,0:T(8,128)(2,1)}, u32[]{:S(2)}, u32[]{:S(2)}) collective-permute-start(bf16[512,1024]{1,0:T(8,128)(2,1)} %collective-permute-done.refs_0_.refs_8_.refs_4_), channel_id=1, source_target_pairs={{1,3},{3,1},{4,6},{6,4},{9,11},{11,9},{12,14},{14,12},{17,19},{19,... | collective-permute-start | bytes 3145736 | tf_op jit(solution)/shard_map/ppermute | solution.py:470
  42.0 11.0 %copy-start.3 = (bf16[3,4,64,1024]{3,2,1,0:T(8,128)(2,1)S(1)}, bf16[3,4,64,1024]{3,2,1,0:T(8,128)(2,1)}, u32[]{:S(2)}) copy-start(bf16[3,4,64,1024]{3,2,1,0:T(8,128)(2,1)} %copy-done.2) | copy-start | bytes 4718596
  42.0 11.0 %copy-start.7 = (bf16[4,64,1024]{2,1,0:T(8,128)(2,1)S(1)}, bf16[4,64,1024]{2,1,0:T(8,128)(2,1)}, u32[]{:S(2)}) copy-start(bf16[4,64,1024]{2,1,0:T(8,128)(2,1)} %param.13) | copy-start | bytes 1572868
  43.6 15.0 %collective-permute-start.7 = (bf16[256,1024]{1,0:T(8,128)(2,1)S(1)}, bf16[256,1024]{1,0:T(8,128)(2,1)}, u32[]{:S(2)}, u32[]{:S(2)}) collective-permute-start(bf16[256,1024]{1,0:T(8,128)(2,1)S(1)} %fusion), channel_id=1, source_target_pairs={{2,0},{0,2},{3,1},{1,3},{6,4},{4,6},{7,5},{5,7},{10,8},{8,10},{11,... | collective-permute-start | bytes 1572872 | tf_op jit(solution)/shard_map/ppermute | solution.py:491
  53.0 1.4 copy-start
  58.6 222.1 %all-reduce.3.cloned.1.call-start = ((), (), s32[]{:S(2)}) async-start(), calls=%async_computation.1 | async-start | bytes 4194304 | tf_op jit(solution)/shard_map/psum | solution.py:530
  58.7 33.7 %collective-permute-start.9 = (bf16[512,1024]{1,0:T(8,128)(2,1)}, bf16[512,1024]{1,0:T(8,128)(2,1)}, u32[]{:S(2)}, u32[]{:S(2)}) collective-permute-start(bf16[512,1024]{1,0:T(8,128)(2,1)} %param.15), channel_id=1, source_target_pairs={{3,0},{5,1},{1,2},{7,3},{0,4},{6,5},{2,6},{4,7},{11,8},{13,9},{9,1... | collective-permute-start | bytes 3145736 | tf_op jit(solution)/shard_map/ppermute | solution.py:470
  69.0 23.4 %collective-permute-start.8 = (bf16[512,1024]{1,0:T(8,128)(2,1)}, bf16[512,1024]{1,0:T(8,128)(2,1)}, u32[]{:S(2)}, u32[]{:S(2)}) collective-permute-start(bf16[512,1024]{1,0:T(8,128)(2,1)} %param.15), channel_id=1, source_target_pairs={{2,0},{4,1},{0,2},{6,3},{1,4},{7,5},{3,6},{5,7},{10,8},{12,9},{8,1... | collective-permute-start | bytes 3145736 | tf_op jit(solution)/shard_map/ppermute | solution.py:470
  73.4 19.0 %copy-start.8 = (bf16[512,1024]{1,0:T(8,128)(2,1)S(1)}, bf16[512,1024]{1,0:T(8,128)(2,1)}, u32[]{:S(2)}) copy-start(bf16[512,1024]{1,0:T(8,128)(2,1)} %param.15) | copy-start | bytes 3145732
  83.6 18.5 %copy-start.14 = (s32[64]{0:T(128)S(1)}, s32[64]{0:T(128)}, u32[]{:S(2)}) copy-start(s32[64]{0:T(128)} %param.14) | copy-start | bytes 772
  93.7 13.6 %collective-permute-start.10 = (bf16[512,1024]{1,0:T(8,128)(2,1)S(1)}, bf16[512,1024]{1,0:T(8,128)(2,1)}, u32[]{:S(2)}, u32[]{:S(2)}) collective-permute-start(bf16[512,1024]{1,0:T(8,128)(2,1)S(1)} %broadcast_select_fusion.2), channel_id=1, source_target_pairs={{0,4},{1,0},{2,6},{3,2},{4,5},{5,1},{6,7},{7,3},{8,12},{9,8},{10,1... | collective-permute-start | bytes 3145736 | tf_op jit(solution)/shard_map/ppermute | solution.py:470
  95.0 12.3 %collective-permute-start.11 = (bf16[512,1024]{1,0:T(8,128)(2,1)}, bf16[512,1024]{1,0:T(8,128)(2,1)S(1)}, u32[]{:S(2)}, u32[]{:S(2)}) collective-permute-start(bf16[512,1024]{1,0:T(8,128)(2,1)} %collective-permute-done.8.refs_0_.refs_4_), channel_id=1, source_target_pairs={{1,3},{3,1},{4,6},{6,4},{9,11},{11,9},{12,14},{14,12},{17,19},{19,... | collective-permute-start | bytes 3145736 | tf_op jit(solution)/shard_map/ppermute | solution.py:470
  95.7 24.1 %collective-permute-start.5 = (bf16[1536,512]{1,0:T(8,128)(2,1)}, bf16[1536,512]{1,0:T(8,128)(2,1)}, u32[]{:S(2)}, u32[]{:S(2)}) collective-permute-start(bf16[1536,512]{1,0:T(8,128)(2,1)} %get-tuple-element.53), channel_id=1, source_target_pairs={{0,1},{1,8},{8,9},{9,16},{16,17},{17,24},{24,25},{2,3},{3,10},{10,... | collective-permute-start | bytes 4718600 | tf_op jit(solution)/shard_map/ppermute | solution.py:439
  100.6 19.2 %collective-permute-start.6 = (bf16[1536,512]{1,0:T(8,128)(2,1)}, bf16[1536,512]{1,0:T(8,128)(2,1)}, u32[]{:S(2)}, u32[]{:S(2)}) collective-permute-start(bf16[1536,512]{1,0:T(8,128)(2,1)} %get-tuple-element.54), channel_id=1, source_target_pairs={{1,0},{8,1},{9,8},{16,9},{17,16},{24,17},{25,24},{3,2},{10,3},{11,... | collective-permute-start | bytes 4718600 | tf_op jit(solution)/shard_map/ppermute | solution.py:439
  116.9 1.4 slice-start
  118.5 1.0 slice-start.1
  119.7 56.5 %copy-start.1 = (bf16[1024,1024]{1,0:T(8,128)(2,1)}, bf16[1024,1024]{1,0:T(8,128)(2,1)S(1)}, u32[]{:S(2)}) copy-start(bf16[1024,1024]{1,0:T(8,128)(2,1)S(1)} %pad_maximum_fusion.2.refs_9_.refs_5_) | copy-start | bytes 6291460
  162.6 25.0 %collective-permute-start.13 = (bf16[1536,512]{1,0:T(8,128)(2,1)}, bf16[1536,512]{1,0:T(8,128)(2,1)}, u32[]{:S(2)}, u32[]{:S(2)}) collective-permute-start(bf16[1536,512]{1,0:T(8,128)(2,1)} %get-tuple-element.73), channel_id=1, source_target_pairs={{0,1},{1,8},{8,9},{9,16},{16,17},{17,24},{24,25},{2,3},{3,10},{10,... | collective-permute-start | bytes 4718600 | tf_op jit(solution)/shard_map/ppermute | solution.py:439
  175.0 17.4 %collective-permute-start.12 = (bf16[1536,512]{1,0:T(8,128)(2,1)}, bf16[1536,512]{1,0:T(8,128)(2,1)}, u32[]{:S(2)}, u32[]{:S(2)}) collective-permute-start(bf16[1536,512]{1,0:T(8,128)(2,1)} %get-tuple-element.72), channel_id=1, source_target_pairs={{1,0},{8,1},{9,8},{16,9},{17,16},{24,17},{25,24},{3,2},{10,3},{11,... | collective-permute-start | bytes 4718600 | tf_op jit(solution)/shard_map/ppermute | solution.py:439
  176.3 48.9 %collective-permute-start.22 = (bf16[1024,1024]{1,0:T(8,128)(2,1)S(1)}, bf16[1024,1024]{1,0:T(8,128)(2,1)}, u32[]{:S(2)}, u32[]{:S(2)}) collective-permute-start(bf16[1024,1024]{1,0:T(8,128)(2,1)S(1)} %pad_maximum_fusion.2.refs_9_.refs_5_), channel_id=1, source_target_pairs={{0,1},{1,0},{2,3},{3,2},{4,5},{5,4},{6,7},{7,6},{8,9},{9,8},{10,11... | collective-permute-start | bytes 6291464 | tf_op jit(solution)/shard_map/ppermute | solution.py:494
  177.5 34.3 %collective-permute-start.14 = (bf16[512,512]{1,0:T(8,128)(2,1)}, bf16[512,512]{1,0:T(8,128)(2,1)}, u32[]{:S(2)}, u32[]{:S(2)}) collective-permute-start(bf16[512,512]{1,0:T(8,128)(2,1)} %get-tuple-element.66.refs_0_), channel_id=1, source_target_pairs={{0,2},{1,4},{2,0},{3,6},{4,1},{5,7},{6,3},{7,5},{8,10},{9,12},{10,... | collective-permute-start | bytes 1572872 | tf_op jit(solution)/shard_map/ppermute | solution.py:470
  178.9 34.3 %collective-permute-start.15 = (bf16[512,512]{1,0:T(8,128)(2,1)}, bf16[512,512]{1,0:T(8,128)(2,1)}, u32[]{:S(2)}, u32[]{:S(2)}) collective-permute-start(bf16[512,512]{1,0:T(8,128)(2,1)} %get-tuple-element.67.refs_1_), channel_id=1, source_target_pairs={{0,3},{1,5},{2,1},{3,7},{4,0},{5,6},{6,2},{7,4},{8,11},{9,13},{10,... | collective-permute-start | bytes 1572872 | tf_op jit(solution)/shard_map/ppermute | solution.py:470
  187.6 28.3 %collective-permute-start.16 = (bf16[512,512]{1,0:T(8,128)(2,1)}, bf16[512,512]{1,0:T(8,128)(2,1)}, u32[]{:S(2)}, u32[]{:S(2)}) collective-permute-start(bf16[512,512]{1,0:T(8,128)(2,1)} %get-tuple-element.68.refs_2_), channel_id=1, source_target_pairs={{0,1},{1,7},{2,3},{3,5},{4,2},{5,4},{6,0},{7,6},{8,9},{9,15},{10,1... | collective-permute-start | bytes 1572872 | tf_op jit(solution)/shard_map/ppermute | solution.py:470
  192.4 26.2 %collective-permute-start.17 = (bf16[512,512]{1,0:T(8,128)(2,1)}, bf16[512,512]{1,0:T(8,128)(2,1)}, u32[]{:S(2)}, u32[]{:S(2)}) collective-permute-start(bf16[512,512]{1,0:T(8,128)(2,1)} %get-tuple-element.69.refs_3_), channel_id=1, source_target_pairs={{0,0},{1,6},{2,2},{3,4},{4,3},{5,5},{6,1},{7,7},{8,8},{9,14},{10,1... | collective-permute-start | bytes 1572872 | tf_op jit(solution)/shard_map/ppermute | solution.py:470
  202.7 6.3 %copy-start.9 = (bf16[512,1024]{1,0:T(8,128)(2,1)S(1)}, bf16[512,1024]{1,0:T(8,128)(2,1)}, u32[]{:S(2)}) copy-start(bf16[512,1024]{1,0:T(8,128)(2,1)} %shard_map.132) | copy-start | bytes 3145732
  211.8 18.8 %collective-permute-start.18 = (bf16[512,512]{1,0:T(8,128)(2,1)}, bf16[512,512]{1,0:T(8,128)(2,1)S(1)}, u32[]{:S(2)}, u32[]{:S(2)}) collective-permute-start(bf16[512,512]{1,0:T(8,128)(2,1)} %get-tuple-element.74.refs_0_), channel_id=1, source_target_pairs={{0,2},{1,4},{2,0},{3,6},{4,1},{5,7},{6,3},{7,5},{8,10},{9,12},{10,... | collective-permute-start | bytes 1572872 | tf_op jit(solution)/shard_map/ppermute | solution.py:470
  213.2 23.3 %collective-permute-start.19 = (bf16[512,512]{1,0:T(8,128)(2,1)}, bf16[512,512]{1,0:T(8,128)(2,1)S(1)}, u32[]{:S(2)}, u32[]{:S(2)}) collective-permute-start(bf16[512,512]{1,0:T(8,128)(2,1)} %get-tuple-element.75.refs_1_), channel_id=1, source_target_pairs={{0,3},{1,5},{2,1},{3,7},{4,0},{5,6},{6,2},{7,4},{8,11},{9,13},{10,... | collective-permute-start | bytes 1572872 | tf_op jit(solution)/shard_map/ppermute | solution.py:470
  215.9 20.6 %collective-permute-start.20 = (bf16[512,512]{1,0:T(8,128)(2,1)}, bf16[512,512]{1,0:T(8,128)(2,1)S(1)}, u32[]{:S(2)}, u32[]{:S(2)}) collective-permute-start(bf16[512,512]{1,0:T(8,128)(2,1)} %get-tuple-element.76.refs_2_), channel_id=1, source_target_pairs={{0,1},{1,7},{2,3},{3,5},{4,2},{5,4},{6,0},{7,6},{8,9},{9,15},{10,1... | collective-permute-start | bytes 1572872 | tf_op jit(solution)/shard_map/ppermute | solution.py:470
  218.6 18.0 %collective-permute-start.21 = (bf16[512,512]{1,0:T(8,128)(2,1)}, bf16[512,512]{1,0:T(8,128)(2,1)}, u32[]{:S(2)}, u32[]{:S(2)}) collective-permute-start(bf16[512,512]{1,0:T(8,128)(2,1)} %get-tuple-element.77.refs_3_), channel_id=1, source_target_pairs={{0,0},{1,6},{2,2},{3,4},{4,3},{5,5},{6,1},{7,7},{8,8},{9,14},{10,1... | collective-permute-start | bytes 1572872 | tf_op jit(solution)/shard_map/ppermute | solution.py:470
  230.6 5.9 %copy-start.10 = (bf16[512,512]{1,0:T(8,128)(2,1)}, bf16[512,512]{1,0:T(8,128)(2,1)S(1)}, u32[]{:S(2)}) copy-start(bf16[512,512]{1,0:T(8,128)(2,1)S(1)} %collective-permute-done.18.refs_4_) | copy-start | bytes 1572868
  236.5 0.8 copy-start.11
  236.5 1.0 copy-start.12
  280.8 27.2 %collective-permute-start.23 = (bf16[1024,1024]{1,0:T(8,128)(2,1)}, bf16[1024,1024]{1,0:T(8,128)(2,1)S(1)}, u32[]{:S(2)}, u32[]{:S(2)}) collective-permute-start(bf16[1024,1024]{1,0:T(8,128)(2,1)} %all-reduce.3.cloned.1.call-done), channel_id=1, source_target_pairs={{5,1},{7,3},{0,4},{2,6},{13,9},{15,11},{8,12},{10,14},{21,17},{23,... | collective-permute-start | bytes 6291464 | tf_op jit(solution)/shard_map/ppermute | solution.py:470
Sparse Core Ops, SparseCore 0:
  58.8 58.1 all-gather.1
  211.9 68.8 all-reduce.2

commit v6 on v5

--- a/solution.py
+++ b/solution.py
@@ -475,8 +475,11 @@
     def gathered(x, *others):
         sent = lambda slot: permuted(x, list(zip(slot, spots)))
         if halves != 2:
-            return [sent(slot) for slot in slots]
-        first, second, *others = lax.optimization_barrier((sent(slots[0]), sent(slots[1]), *others))
+            parts = [sent(slot) for slot in slots]
+            return parts, parts
+        first, second = lax.optimization_barrier((sent(slots[0]), sent(slots[1])))
+        hop = first, second
+        first = after(first, *others)
         third = permuted(
             jnp.where(c == y, first, x),
             [(spot, (1 - spot[0], spot[1], spot[0]) if spot[2] == spot[0] else (spot[0], spot[1], spot[0])) for spot in spots],
@@ -485,7 +488,7 @@
             first, [(spot, (spot[0], 1 - spot[1], spot[2])) for spot in spots if spot[2] != spot[0]]
         )
         third, fourth = lax.optimization_barrier((third, fourth))
-        return [first, second, third, jnp.where(c == y, x, fourth)]
+        return [first, second, third, jnp.where(c == y, x, fourth)], hop
 
     def from_ahead(x, dm):
         return lax.ppermute(x, "m", [((i + dm) % halves, i) for i in range(halves)])
@@ -493,51 +496,81 @@
     def from_sibling(x):
         return lax.ppermute(x, "c", [(0, 1), (1, 0)])
 
-    raw = jnp.concatenate([qkv_weight.reshape(3 * feats, WIDTH), out_weight.reshape(feats, WIDTH)], axis=0)
-    share = 4 * feats // layers
-    held = lax.dynamic_slice_in_dim(raw, z * share, share, 0)
+    rows = 3 * feats // layers, feats // layers
+    flat_qkv, flat_out = qkv_weight.reshape(3 * feats, WIDTH), out_weight.reshape(feats, WIDTH)
+    held = jnp.concatenate([
+        lax.dynamic_slice_in_dim(flat, z * size, size, 0) for flat, size in zip((flat_qkv, flat_out), rows)
+    ], axis=0)
     shares = [from_ahead(held, dm) for dm in range(1, halves)]
 
-    def split(block):
-        qkv = block[:3 * feats].reshape(heads, 3, HEAD_WIDTH, WIDTH)
+    def split(qkv, out):
         eighth = jnp.asarray([HEAD_WIDTH ** -0.5, 1.0, 1.0], BF16)[None, :, None, None]
-        qkv = (qkv * eighth).transpose(1, 0, 2, 3).reshape(3 * feats, WIDTH)
-        return jnp.concatenate([qkv, block[3 * feats:]], axis=0)
-
-    blocks = [split(raw)]
+        qkv = (qkv.reshape(heads, 3, HEAD_WIDTH, WIDTH) * eighth).transpose(1, 0, 2, 3)
+        return jnp.concatenate([qkv.reshape(3 * feats, WIDTH), out.reshape(feats, WIDTH)], axis=0)
+
+    tokens, *shares = lax.optimization_barrier((tokens, *shares))
+    ahead = [lax.all_gather(part, "z") for part in shares]
+    blocks = [split(flat_qkv, flat_out)]
     sibling = from_sibling(blocks[0])
     group = jnp.where(c == y, blocks[0], sibling)
     group_qkv, group_out = group[:3 * feats].T, group[3 * feats:]
 
-    *normed_parts, group_qkv, group_out = lax.optimization_barrier(
-        (*gathered(norm(tokens, gain)), group_qkv, group_out)
-    )
+    normed_parts, hop = gathered(norm(tokens, gain))
+    *normed_parts, group_qkv, group_out = lax.optimization_barrier((*normed_parts, group_qkv, group_out))
     qkv, kv_up, kv_down = projections(order, group_qkv, normed_parts)
-    upstream_parts = gathered(after(upstream, *normed_parts), qkv)
+    upstream_parts, _ = gathered(after(upstream, *hop), qkv)
     kv_top, kv_bot = passed_along(kv_up, 1), passed_along(kv_down, -1)
-    shares = lax.optimization_barrier((shares, normed_parts))[0]
-    ahead = [split(lax.all_gather(part, "z", axis=0, tiled=True)) for part in shares]
     order, kv_top, kv_bot, *ahead = lax.optimization_barrier((order, kv_top, kv_bot, *ahead))
     outq_parts, dkv, dkv_top, dkv_bot = attention(cells, order, qkv, kv_top, kv_bot, group_out, upstream_parts)
 
-    blocks += ahead + [sibling] + [from_sibling(after(block, dkv_top)) for block in ahead]
+    ahead = [after(block, dkv_top) for block in ahead]
+    ahead = [split(block[:, :rows[0]], block[:, rows[0]:]) for block in ahead]
+    blocks += ahead + [sibling] + [from_sibling(block) for block in ahead]
     from_above, from_below = passed_along(dkv_top, -1), passed_along(dkv_bot, 1)
     outq_own = send_back(outq_parts)
-    early = weight_grad(outq_parts, upstream_parts, normed_parts)
-    dkv_parts = joined(after(order, early), dkv, from_above, from_below, len(slots))
+
+    bits = range((layers - 1).bit_length())
+    partners = [("c", c, from_sibling)] + [
+        ("z", z // 2 ** bit % 2, lambda x, bit=bit: lax.ppermute(x, "z", [(i, i ^ 2 ** bit) for i in range(layers)]))
+        for bit in bits
+    ]
+
+    def halved(x, partner):
+        _, side, swap = partner
+        half = x.shape[0] // 2
+        keep, give = (lax.dynamic_slice_in_dim(x, at * half, half, 0) for at in (side, 1 - side))
+        return (keep.astype(F32) + swap(give).astype(F32)).astype(BF16)
+
+    def in_turn(side, mine, other):
+        return jnp.concatenate([jnp.where(side == 0, mine, other), jnp.where(side == 0, other, mine)], axis=1)
+
+    def begun(grads):
+        return halved(halved(grads, partners[0]), partners[1])
+
+    early = begun(weight_grad(outq_parts, upstream_parts, normed_parts))
+    early, from_above, from_below, *outq_own = lax.optimization_barrier((early, from_above, from_below, *outq_own))
+    dkv_parts = joined(order, dkv, from_above, from_below, len(slots))
     dkv_own = send_back(dkv_parts)
-    late = weight_grad(dkv_parts, normed_parts)
-    grads = lax.psum(jnp.concatenate([early, late], axis=0), ("z", "c"))
+    late = begun(weight_grad(dkv_parts, normed_parts))
     update = updates(after(leads, late), outq_own, blocks)
-    grad_input = grad_inputs(after(leads, late), tokens, gain, outq_own, dkv_own, blocks)
-
-    def spread(grads):
-        pairs = [((1 - y, m, 1 - y), (y, m, 1 - y)) for y in range(2) for m in range(halves)]
-        return jnp.where(c == y, grads, permuted(grads, pairs)).astype(F32)
-
-    grads, grad_input, update = lax.optimization_barrier((grads, grad_input, update))
-    grads = spread(grads) * grad_scale
-    early, late = grads[:2 * feats], grads[2 * feats:]
+    late, update, *dkv_own = lax.optimization_barrier((late, update, *dkv_own))
+    grad_input = grad_inputs(leads, tokens, gain, outq_own, dkv_own, blocks)
+
+    both = jnp.concatenate([early, late], axis=0)
+    for partner in partners[2:]:
+        both = halved(both, partner)
+    for _, side, swap in reversed(partners[2:]):
+        other = swap(both)
+        both = jnp.concatenate([jnp.where(side == 0, both, other), jnp.where(side == 0, other, both)], axis=0)
+    both = both.reshape(2, feats // 2, WIDTH)
+    _, side, swap = partners[1]
+    over_y = lambda x: lax.ppermute(x, "y", [(0, 1), (1, 0)])
+    other, both_y = lax.optimization_barrier((swap(both), over_y(both)))
+    own = in_turn(side, both, other)
+    far = in_turn(side, both_y, over_y(other))
+    own, far, grad_input = lax.optimization_barrier((own, far, grad_input))
+    mine, give = jnp.where(c == y, own, far), jnp.where(c == y, far, own)
+    early, late = in_turn(c, mine, from_sibling(give)).astype(F32) * grad_scale
     by_head = lambda x: x.reshape(heads, HEAD_WIDTH, WIDTH)
     grad_out = by_head(early[:feats])
     grad_query = early[feats:] * HEAD_WIDTH ** -0.5

time: 322 us -> 336 us (1.043)
  waiting for transfers between devices: 114 us -> 153 us
  starting transfers between devices: 72.3 us -> 43.3 us
    ppermute x0 -> x7, waiting for transfers between devices: none -> 51.9 us  [the longest x5 49.4 us: on_device(): lax.ppermute(x, 'z', [(i, i ^ 2 ** bit) for i in range(layers)])]
    psum x1 -> x0, waiting for transfers between devices: 33 us -> none  [on_device(): grads = lax.psum(jnp.concatenate([early, late], axis=0), ('z', 'c'))]
    ppermute x17 -> x16, starting transfers between devices: 50 us -> 18.1 us  [permuted(): return lax.ppermute(x, GROUP, [(at(*a), at(*b)) for a, b in pairs])]
    ppermute x17 -> x16, waiting for transfers between devices: 70.6 us -> 86.6 us  [permuted(): return lax.ppermute(x, GROUP, [(at(*a), at(*b)) for a, b in pairs])]
    ppermute x4, starting transfers between devices: 20 us -> 9.21 us  [passed_along(): return lax.ppermute(x, ('z', 'c'), pairs)]
    all_gather x1, waiting for transfers between devices: 8.57 us -> 0.01 us  [on_device(): ahead = [lax.all_gather(part, 'z') for part in shares]]
    ppermute x1, waiting for transfers between devices: 2.18 us -> 10 us  [from_ahead(): return lax.ppermute(x, 'm', [((i + dm) % halves, i) for i in range(halves)])]
    ppermute x2 -> x5, starting transfers between devices: 1.2 us -> 7.7 us  [from_sibling(): return lax.ppermute(x, 'c', [(0, 1), (1, 0)])]
  transfers between devices with their start and end apart: 26 -> 34, of which waited for: 9 -> 19; matrix products, arithmetic and copies ran while one was open for 6% -> 7% of each run, Pallas kernels for 14% -> 12%
where the time goes in v6:
time: 336 us; the launch traced here: 335 us
  waiting for transfers between devices  153 us (46%)
  Pallas kernels  88.9 us (26%)
  starting transfers between devices  43.3 us (13%)
  other arithmetic  21.2 us (6%)
  between operations  14.6 us (4%)
  local copies, waits for them, and re-layouts  13.8 us (4%)
    pallas_call x8, Pallas kernels, call(): pl.pallas_call(kernel, out_shape=tuple(out_shape), in_specs=list(in_specs...  88.9 us
    ppermute x16, waiting for transfers between devices, permuted(): return lax.ppermute(x, GROUP, [(at(*a), at(*b)) for a, b in pairs])  86.6 us
    ppermute x5, waiting for transfers between devices, on_device(): lax.ppermute(x, 'z', [(i, i ^ 2 ** bit) for i in range(layers)])  49.4 us
    ppermute x16, starting transfers between devices, permuted(): return lax.ppermute(x, GROUP, [(at(*a), at(*b)) for a, b in pairs])  18.1 us
    ppermute x1, waiting for transfers between devices, from_ahead(): return lax.ppermute(x, 'm', [((i + dm) % halves, i) for i in range(halves)])  10 us
    ppermute x4, starting transfers between devices, passed_along(): return lax.ppermute(x, ('z', 'c'), pairs)  9.21 us
    ppermute x5, starting transfers between devices, from_sibling(): return lax.ppermute(x, 'c', [(0, 1), (1, 0)])  7.7 us
  transfers between devices with their start and end apart: 34, of which 19 were waited for; matrix products, arithmetic and copies ran while one was open for 7% of the time, Pallas kernels for 12%

profile of v6, /device:TPU:0, one launch (start us, length us, event | category | flops | bytes accessed | tf_op | source)
XLA Modules:
  0.0 334.7 jit_solution(16210301702088843307)
XLA Ops:
  9.4 3.0 collective-permute-start
  12.6 1.7 pad_maximum_fusion.1.refs_4_.refs_8_
  14.4 10.0 %collective-permute-done = bf16[256,1024]{1,0:T(8,128)(2,1)} collective-permute-done((bf16[256,1024]{1,0:T(8,128)(2,1)S(1)}, bf16[256,1024]{1,0:T(8,128)(2,1)}, u32[]{:S(2)}, u32[]{:S(2)}) %collective-permute-start) | collective-permute-done | bytes 524320 | tf_op jit(solution)/shard_map/ppermute | solution.py:494
  24.4 2.6 shard_map.129
  27.0 1.7 collective-permute-start.1
  28.8 23.5 %collective-permute-done.1.refs_0_.refs_8_.refs_4_ = bf16[512,1024]{1,0:T(8,128)(2,1)} collective-permute-done((bf16[512,1024]{1,0:T(8,128)(2,1)}, bf16[512,1024]{1,0:T(8,128)(2,1)}, u32[]{:S(2)}, u32[]{:S(2)}) %collective-permute-start.1) | collective-permute-done | bytes 1048608 | tf_op jit(solution)/shard_map/ppermute | solution.py:470
  53.3 2.3 broadcast_select_fusion.8
  56.8 1.7 collective-permute-start.4
  58.6 1.6 collective-permute-start.8
  62.2 3.3 broadcast_select_fusion
  66.5 11.4 %collective-permute-done.3.refs_2_.refs_10_.refs_6_ = bf16[512,1024]{1,0:T(8,128)(2,1)} collective-permute-done((bf16[512,1024]{1,0:T(8,128)(2,1)}, bf16[512,1024]{1,0:T(8,128)(2,1)}, u32[]{:S(2)}, u32[]{:S(2)}) %collective-permute-start.3) | collective-permute-done | bytes 1048608 | tf_op jit(solution)/shard_map/ppermute | solution.py:470
  79.0 1.6 copy.15.weight
  80.6 4.2 %collective-permute-done.8.refs_0_.refs_4_ = bf16[512,1024]{1,0:T(8,128)(2,1)} collective-permute-done((bf16[512,1024]{1,0:T(8,128)(2,1)S(1)}, bf16[512,1024]{1,0:T(8,128)(2,1)}, u32[]{:S(2)}, u32[]{:S(2)}) %collective-permute-start.8) | collective-permute-done | bytes 1048608 | tf_op jit(solution)/shard_map/ppermute | solution.py:470
  84.8 9.9 %collective-permute-done.9.refs_1_.refs_5_ = bf16[512,1024]{1,0:T(8,128)(2,1)} collective-permute-done((bf16[512,1024]{1,0:T(8,128)(2,1)S(1)}, bf16[512,1024]{1,0:T(8,128)(2,1)}, u32[]{:S(2)}, u32[]{:S(2)}) %collective-permute-start.9) | collective-permute-done | bytes 1048608 | tf_op jit(solution)/shard_map/ppermute | solution.py:470
  94.7 9.9 %shard_map.130 = (bf16[2048,768]{1,0:T(8,128)(2,1)}, bf16[1536,512]{1,0:T(8,128)(2,1)}, bf16[1536,512]{1,0:T(8,128)(2,1)}) custom-call(s32[4]{0:T(128)} %fusion.order, bf16[1024,768]{1,0:T(8,128)(2,1)} %copy.15.weight, bf16[512,1024]{1,0:T(8,128)(2,1)} %collective-permute-done.1.refs_0_.refs_8_.refs_4_, ...), custom_call_target="tpu_custom_call" | custom-call | flops 3221225472 | bytes 12058640 | tf_op jit(solution)/shard_map/pallas_call | solution.py:200
  104.5 2.5 collective-permute-start.6
  111.5 10.7 %collective-permute-done.10.refs_2_.refs_6_ = bf16[512,1024]{1,0:T(8,128)(2,1)} collective-permute-done((bf16[512,1024]{1,0:T(8,128)(2,1)S(1)}, bf16[512,1024]{1,0:T(8,128)(2,1)}, u32[]{:S(2)}, u32[]{:S(2)}) %collective-permute-start.10) | collective-permute-done | bytes 1048608 | tf_op jit(solution)/shard_map/ppermute | solution.py:470
  123.4 42.1 %shard_map.131 = (bf16[512,512]{1,0:T(8,128)(2,1)}, bf16[512,512]{1,0:T(8,128)(2,1)}, bf16[512,512]{1,0:T(8,128)(2,1)}, bf16[512,512]{1,0:T(8,128)(2,1)}, f32[20...) custom-call(s32[20]{0:T(128)} %pad_dynamic-slice_fusion.cells, s32[4]{0:T(128)} %fusion.order, ...), custom_call_target="tpu_custom_call" | custom-call | flops 13958643712 | bytes 20447328 | tf_op jit(solution)/shard_map/pallas_call | solution.py:200
  165.5 7.5 %shard_map.132 = bf16[512,1024]{1,0:T(8,128)(2,1)} custom-call(bf16[512,512]{1,0:T(8,128)(2,1)} %get-tuple-element.85.refs_0_, bf16[512,512]{1,0:T(8,128)(2,1)} %get-tuple-element.86.refs_1_, bf16[512,512]{1,0:T(8,128)(2,1)} %get-tuple-element.87.refs_2_, bf16[512,512]{1,0:T(8,128)(2,1)} %get-tuple-element.88.refs_3_, ...), custom_call_target="tpu_custom_call" | custom-call | flops 2147483648 | bytes 11534336 | tf_op jit(solution)/shard_map/pallas_call | solution.py:200
  173.0 2.0 constant_dynamic-slice_fusion.5
  175.0 7.1 %collective-permute-start.12 = (bf16[256,1024]{1,0:T(8,128)(2,1)}, bf16[256,1024]{1,0:T(8,128)(2,1)}, u32[]{:S(2)}, u32[]{:S(2)}) collective-permute-start(bf16[256,1024]{1,0:T(8,128)(2,1)} %constant_dynamic-slice_fusion.5), channel_id=1, source_target_pairs={{0,1},{1,0},{2,3},{3,2},{4,5},{5,4},{6,7},{7,6},{8,9},{9,8},{10,11... | collective-permute-start | bytes 1572872 | tf_op jit(solution)/shard_map/ppermute | solution.py:497
  183.3 4.2 %collective-permute-start.15 = (bf16[1536,512]{1,0:T(8,128)(2,1)}, bf16[1536,512]{1,0:T(8,128)(2,1)}, u32[]{:S(2)}, u32[]{:S(2)}) collective-permute-start(bf16[1536,512]{1,0:T(8,128)(2,1)} %get-tuple-element.90), channel_id=1, source_target_pairs={{0,1},{1,8},{8,9},{9,16},{16,17},{17,24},{24,25},{2,3},{3,10},{10,... | collective-permute-start | bytes 4718600 | tf_op jit(solution)/shard_map/ppermute | solution.py:439
  187.5 1.5 collective-permute-start.16
  189.0 1.6 slice.34
  192.0 6.5 %collective-permute-done.16.refs_0_ = bf16[512,512]{1,0:T(8,128)(2,1)S(1)} collective-permute-done((bf16[512,512]{1,0:T(8,128)(2,1)S(1)}, bf16[512,512]{1,0:T(8,128)(2,1)S(1)}, u32[]{:S(2)}, u32[]{:S(2)}) %collective-permute-start.16) | collective-permute-done | bytes 524320 | tf_op jit(solution)/shard_map/ppermute | solution.py:470
  198.5 1.5 collective-permute-start.19
  200.0 13.4 %collective-permute-done.17.refs_1_ = bf16[512,512]{1,0:T(8,128)(2,1)S(1)} collective-permute-done((bf16[512,512]{1,0:T(8,128)(2,1)S(1)}, bf16[512,512]{1,0:T(8,128)(2,1)S(1)}, u32[]{:S(2)}, u32[]{:S(2)}) %collective-permute-start.17) | collective-permute-done | bytes 524320 | tf_op jit(solution)/shard_map/ppermute | solution.py:470
  213.3 1.6 collective-permute-start.13
  216.4 3.3 collective-permute-done.13
  219.8 5.1 %shard_map.133 = (bf16[512,512]{1,0:T(8,128)(2,1)}, bf16[512,512]{1,0:T(8,128)(2,1)}, bf16[512,512]{1,0:T(8,128)(2,1)}, bf16[512,512]{1,0:T(8,128)(2,1)}) custom-call(s32[4]{0:T(128)} %fusion.order, f32[2048,512]{1,0:T(8,128)} %get-tuple-element.84.own, bf16[1536,512]{1,0:T(8,128)(2,1)} %collective-permute-done.14.above, ...), custom_call_target="tpu_custom_call" | custom-call | flops 2097152 | bytes 9437200 | tf_op jit(solution)/shard_map/pallas_call | solution.py:200
  224.9 6.2 %shard_map.134 = bf16[512,1024]{1,0:T(8,128)(2,1)} custom-call(bf16[512,512]{1,0:T(8,128)(2,1)} %get-tuple-element.93.refs_0_, bf16[512,512]{1,0:T(8,128)(2,1)} %get-tuple-element.94.refs_1_, bf16[512,512]{1,0:T(8,128)(2,1)} %get-tuple-element.95.refs_2_, bf16[512,512]{1,0:T(8,128)(2,1)} %get-tuple-element.96.refs_3_, ...), custom_call_target="tpu_custom_call" | custom-call | flops 2147483648 | bytes 7340032 | tf_op jit(solution)/shard_map/pallas_call | solution.py:200
  232.8 1.5 collective-permute-done.20
  235.6 1.7 collective-permute-start.21
  237.3 1.5 collective-permute-start.23
  238.7 5.5 %collective-permute-done.21 = bf16[128,1024]{1,0:T(8,128)(2,1)S(1)} collective-permute-done((bf16[128,1024]{1,0:T(8,128)(2,1)S(1)}, bf16[128,1024]{1,0:T(8,128)(2,1)S(1)}, u32[]{:S(2)}, u32[]{:S(2)}) %collective-permute-start.21) | collective-permute-done | bytes 262176 | tf_op jit(solution)/shard_map/ppermute | solution.py:534
  244.2 5.4 %collective-permute-start.26 = (bf16[512,512]{1,0:T(8,128)(2,1)}, bf16[512,512]{1,0:T(8,128)(2,1)}, u32[]{:S(2)}, u32[]{:S(2)}) collective-permute-start(bf16[512,512]{1,0:T(8,128)(2,1)} %get-tuple-element.96.refs_3_), channel_id=1, source_target_pairs={{0,0},{1,6},{2,2},{3,4},{4,3},{5,5},{6,1},{7,7},{8,8},{9,14},{10,1... | collective-permute-start | bytes 1572872 | tf_op jit(solution)/shard_map/ppermute | solution.py:470
  251.9 5.4 %shard_map.135 = bf16[512,1024]{1,0:T(8,128)(2,1)} custom-call(s32[4]{0:T(128)} %fusion.1.leads, bf16[512,512]{1,0:T(8,128)(2,1)} %copy-done.8, bf16[512,512]{1,0:T(8,128)(2,1)} %copy-done.9, bf16[512,512]{1,0:T(8,128)(2,1)} %collective-permute-done.18.refs_2_, bf16[512,512]{1,0:T(8,128)(2,1)} %collective-permute-done.19.refs_3_, ...), custom_call_target="tpu_custom_call" | custom-call | flops 1073741824 | bytes 11534352 | tf_op jit(solution)/shard_map/pallas_call | solution.py:200
  257.3 6.0 %collective-permute-done.24.refs_5_ = bf16[512,512]{1,0:T(8,128)(2,1)} collective-permute-done((bf16[512,512]{1,0:T(8,128)(2,1)}, bf16[512,512]{1,0:T(8,128)(2,1)}, u32[]{:S(2)}, u32[]{:S(2)}) %collective-permute-start.24) | collective-permute-done | bytes 524320 | tf_op jit(solution)/shard_map/ppermute | solution.py:470
  263.4 1.5 collective-permute-start.27
  264.8 12.6 %collective-permute-done.27 = bf16[128,1024]{1,0:T(8,128)(2,1)S(1)} collective-permute-done((bf16[128,1024]{1,0:T(8,128)(2,1)S(1)}, bf16[128,1024]{1,0:T(8,128)(2,1)S(1)}, u32[]{:S(2)}, u32[]{:S(2)}) %collective-permute-start.27) | collective-permute-done | bytes 262176 | tf_op jit(solution)/shard_map/ppermute | solution.py:534
  277.6 14.2 %collective-permute-done.28 = bf16[128,1024]{1,0:T(8,128)(2,1)S(1)} collective-permute-done((bf16[128,1024]{1,0:T(8,128)(2,1)S(1)}, bf16[128,1024]{1,0:T(8,128)(2,1)S(1)}, u32[]{:S(2)}, u32[]{:S(2)}) %collective-permute-start.28) | collective-permute-done | bytes 262176 | tf_op jit(solution)/shard_map/ppermute | solution.py:534
  292.1 13.8 %collective-permute-done.29 = bf16[2,128,1024]{2,1,0:T(8,128)(2,1)S(1)} collective-permute-done((bf16[2,128,1024]{2,1,0:T(8,128)(2,1)S(1)}, bf16[2,128,1024]{2,1,0:T(8,128)(2,1)S(1)}, u32[]{:S(2)}, u32[]{:S(2)}) %collective-permute-start.29) | collective-permute-done | bytes 524320 | tf_op jit(solution)/shard_map/ppermute | solution.py:534
  306.2 10.2 %shard_map.136 = bf16[512,1024]{1,0:T(8,128)(2,1)} custom-call(s32[4]{0:T(128)} %fusion.1.leads, bf16[512,1024]{1,0:T(8,128)(2,1)} %tokens.1, f32[1,1024]{1,0:T(1,128)} %bitcast.44, bf16[512,512]{1,0:T(8,128)(2,1)} %copy-done.8, bf16[512,512]{1,0:T(8,128)(2,1)} %copy-done.9, bf16[512,512]{1,0:T(8,128)(2,1)} %collective-permute-done.18.refs_2_, ...), custom_call_target="tpu_custom_call" | custom-call | flops 3221225472 | bytes 14684176 | tf_op jit(solution)/shard_map/pallas_call | solution.py:200
  316.5 2.4 collective-permute-done.31
  319.4 2.8 collective-permute-done.32
  322.1 1.4 broadcast_select_fusion.4
  324.1 1.7 fusion.2
  325.8 2.1 pad_maximum_fusion
  (103 shorter events, 25.8 us)
Async XLA Ops:
  7.2 5.2 %copy-start.14 = (bf16[3]{0:T(256)(128)(2,1)S(1)}, bf16[3]{0:T(256)(128)(2,1)}, u32[]{:S(2)}) copy-start(bf16[3]{0:T(256)(128)(2,1)} %constant.80.clone) | copy-start | bytes 22
  7.2 5.2 %copy-start.7 = (bf16[4,192,1024]{2,1,0:T(8,128)(2,1)S(1)}, bf16[4,192,1024]{2,1,0:T(8,128)(2,1)}, u32[]{:S(2)}) copy-start(bf16[4,192,1024]{2,1,0:T(8,128)(2,1)} %param.12) | copy-start | bytes 4718596
  7.2 116.2 %all-gather.3.cloned.1.call-start = ((), (), s32[]{:S(2)}) async-start(), calls=%async_computation | async-start | bytes 2621440 | tf_op jit(solution)/shard_map/all_gather | solution.py:512
  9.3 3.3 copy-start.6
  9.4 15.0 %collective-permute-start = (bf16[256,1024]{1,0:T(8,128)(2,1)S(1)}, bf16[256,1024]{1,0:T(8,128)(2,1)}, u32[]{:S(2)}, u32[]{:S(2)}) collective-permute-start(bf16[256,1024]{1,0:T(8,128)(2,1)S(1)} %pad_maximum_fusion.5), channel_id=1, source_target_pairs={{2,0},{0,2},{3,1},{1,3},{6,4},{4,6},{7,5},{5,7},{10,8},{8,10},{11,... | collective-permute-start | bytes 1572872 | tf_op jit(solution)/shard_map/ppermute | solution.py:494
  14.4 47.8 %collective-permute-start.5 = (bf16[1024,1024]{1,0:T(8,128)(2,1)}, bf16[1024,1024]{1,0:T(8,128)(2,1)S(1)}, u32[]{:S(2)}, u32[]{:S(2)}) collective-permute-start(bf16[1024,1024]{1,0:T(8,128)(2,1)} %pad_maximum_fusion.1.refs_4_.refs_8_), channel_id=1, source_target_pairs={{0,1},{1,0},{2,3},{3,2},{4,5},{5,4},{6,7},{7,6},{8,9},{9,8},{10,11... | collective-permute-start | bytes 6291464 | tf_op jit(solution)/shard_map/ppermute | solution.py:497
  27.0 31.6 %copy-start.4 = (bf16[512,1024]{1,0:T(8,128)(2,1)S(1)}, bf16[512,1024]{1,0:T(8,128)(2,1)}, u32[]{:S(2)}) copy-start(bf16[512,1024]{1,0:T(8,128)(2,1)} %param.15) | copy-start | bytes 3145732
  27.0 25.3 %collective-permute-start.1 = (bf16[512,1024]{1,0:T(8,128)(2,1)}, bf16[512,1024]{1,0:T(8,128)(2,1)}, u32[]{:S(2)}, u32[]{:S(2)}) collective-permute-start(bf16[512,1024]{1,0:T(8,128)(2,1)} %shard_map.129), channel_id=1, source_target_pairs={{2,0},{4,1},{0,2},{6,3},{1,4},{7,5},{3,6},{5,7},{10,8},{12,9},{8,1... | collective-permute-start | bytes 3145736 | tf_op jit(solution)/shard_map/ppermute | solution.py:470
  28.7 24.6 %collective-permute-start.2 = (bf16[512,1024]{1,0:T(8,128)(2,1)}, bf16[512,1024]{1,0:T(8,128)(2,1)}, u32[]{:S(2)}, u32[]{:S(2)}) collective-permute-start(bf16[512,1024]{1,0:T(8,128)(2,1)} %shard_map.129), channel_id=1, source_target_pairs={{3,0},{5,1},{1,2},{7,3},{0,4},{6,5},{2,6},{4,7},{11,8},{13,9},{9,1... | collective-permute-start | bytes 3145736 | tf_op jit(solution)/shard_map/ppermute | solution.py:470
  55.6 22.3 %collective-permute-start.3 = (bf16[512,1024]{1,0:T(8,128)(2,1)}, bf16[512,1024]{1,0:T(8,128)(2,1)}, u32[]{:S(2)}, u32[]{:S(2)}) collective-permute-start(bf16[512,1024]{1,0:T(8,128)(2,1)} %broadcast_select_fusion.8), channel_id=1, source_target_pairs={{0,4},{1,0},{2,6},{3,2},{4,5},{5,1},{6,7},{7,3},{8,12},{9,8},{10,1... | collective-permute-start | bytes 3145736 | tf_op jit(solution)/shard_map/ppermute | solution.py:470
  56.8 21.1 %collective-permute-start.4 = (bf16[512,1024]{1,0:T(8,128)(2,1)}, bf16[512,1024]{1,0:T(8,128)(2,1)}, u32[]{:S(2)}, u32[]{:S(2)}) collective-permute-start(bf16[512,1024]{1,0:T(8,128)(2,1)} %collective-permute-done.1.refs_0_.refs_8_.refs_4_), channel_id=1, source_target_pairs={{1,3},{3,1},{4,6},{6,4},{9,11},{11,9},{12,14},{14,12},{17,19},{19,... | collective-permute-start | bytes 3145736 | tf_op jit(solution)/shard_map/ppermute | solution.py:470
  58.6 26.2 %collective-permute-start.8 = (bf16[512,1024]{1,0:T(8,128)(2,1)S(1)}, bf16[512,1024]{1,0:T(8,128)(2,1)}, u32[]{:S(2)}, u32[]{:S(2)}) collective-permute-start(bf16[512,1024]{1,0:T(8,128)(2,1)S(1)} %copy-done.4), channel_id=1, source_target_pairs={{2,0},{4,1},{0,2},{6,3},{1,4},{7,5},{3,6},{5,7},{10,8},{12,9},{8,1... | collective-permute-start | bytes 3145736 | tf_op jit(solution)/shard_map/ppermute | solution.py:470
  60.1 34.5 %collective-permute-start.9 = (bf16[512,1024]{1,0:T(8,128)(2,1)S(1)}, bf16[512,1024]{1,0:T(8,128)(2,1)}, u32[]{:S(2)}, u32[]{:S(2)}) collective-permute-start(bf16[512,1024]{1,0:T(8,128)(2,1)S(1)} %copy-done.4), channel_id=1, source_target_pairs={{3,0},{5,1},{1,2},{7,3},{0,4},{6,5},{2,6},{4,7},{11,8},{13,9},{9,1... | collective-permute-start | bytes 3145736 | tf_op jit(solution)/shard_map/ppermute | solution.py:470
  62.2 3.3 copy-start
  65.6 12.4 %copy-start.3 = (bf16[512,1024]{1,0:T(8,128)(2,1)S(1)}, bf16[512,1024]{1,0:T(8,128)(2,1)}, u32[]{:S(2)}) copy-start(bf16[512,1024]{1,0:T(8,128)(2,1)} %shard_map.129) | copy-start | bytes 3145732
  104.5 6.4 %copy-start.15 = (s32[64]{0:T(128)S(1)}, s32[64]{0:T(128)}, u32[]{:S(2)}) copy-start(s32[64]{0:T(128)} %param.14) | copy-start | bytes 772
  104.5 18.8 %collective-permute-start.6 = (bf16[1536,512]{1,0:T(8,128)(2,1)}, bf16[1536,512]{1,0:T(8,128)(2,1)}, u32[]{:S(2)}, u32[]{:S(2)}) collective-permute-start(bf16[1536,512]{1,0:T(8,128)(2,1)} %get-tuple-element.70), channel_id=1, source_target_pairs={{0,1},{1,8},{8,9},{9,16},{16,17},{17,24},{24,25},{2,3},{3,10},{10,... | collective-permute-start | bytes 4718600 | tf_op jit(solution)/shard_map/ppermute | solution.py:439
  107.0 16.4 %collective-permute-start.7 = (bf16[1536,512]{1,0:T(8,128)(2,1)}, bf16[1536,512]{1,0:T(8,128)(2,1)}, u32[]{:S(2)}, u32[]{:S(2)}) collective-permute-start(bf16[1536,512]{1,0:T(8,128)(2,1)} %get-tuple-element.71), channel_id=1, source_target_pairs={{1,0},{8,1},{9,8},{16,9},{17,16},{24,17},{25,24},{3,2},{10,3},{11,... | collective-permute-start | bytes 4718600 | tf_op jit(solution)/shard_map/ppermute | solution.py:439
  109.7 12.6 %collective-permute-start.10 = (bf16[512,1024]{1,0:T(8,128)(2,1)S(1)}, bf16[512,1024]{1,0:T(8,128)(2,1)}, u32[]{:S(2)}, u32[]{:S(2)}) collective-permute-start(bf16[512,1024]{1,0:T(8,128)(2,1)S(1)} %broadcast_select_fusion.6), channel_id=1, source_target_pairs={{0,4},{1,0},{2,6},{3,2},{4,5},{5,1},{6,7},{7,3},{8,12},{9,8},{10,1... | collective-permute-start | bytes 3145736 | tf_op jit(solution)/shard_map/ppermute | solution.py:470
  110.0 12.3 %collective-permute-start.11 = (bf16[512,1024]{1,0:T(8,128)(2,1)}, bf16[512,1024]{1,0:T(8,128)(2,1)S(1)}, u32[]{:S(2)}, u32[]{:S(2)}) collective-permute-start(bf16[512,1024]{1,0:T(8,128)(2,1)} %collective-permute-done.8.refs_0_.refs_4_), channel_id=1, source_target_pairs={{1,3},{3,1},{4,6},{6,4},{9,11},{11,9},{12,14},{14,12},{17,19},{19,... | collective-permute-start | bytes 3145736 | tf_op jit(solution)/shard_map/ppermute | solution.py:470
  165.5 22.0 %copy-start.12 = (bf16[512,512]{1,0:T(8,128)(2,1)S(1)}, bf16[512,512]{1,0:T(8,128)(2,1)}, u32[]{:S(2)}) copy-start(bf16[512,512]{1,0:T(8,128)(2,1)} %get-tuple-element.85.refs_0_) | copy-start | bytes 1572868
  165.5 23.5 %copy-start.11 = (bf16[512,512]{1,0:T(8,128)(2,1)S(1)}, bf16[512,512]{1,0:T(8,128)(2,1)}, u32[]{:S(2)}) copy-start(bf16[512,512]{1,0:T(8,128)(2,1)} %get-tuple-element.86.refs_1_) | copy-start | bytes 1572868
  173.0 17.7 %copy-start.5 = (bf16[512,1024]{1,0:T(8,128)(2,1)S(1)}, bf16[512,1024]{1,0:T(8,128)(2,1)}, u32[]{:S(2)}) copy-start(bf16[512,1024]{1,0:T(8,128)(2,1)} %shard_map.132) | copy-start | bytes 3145732
  175.0 15.6 %collective-permute-start.12 = (bf16[256,1024]{1,0:T(8,128)(2,1)}, bf16[256,1024]{1,0:T(8,128)(2,1)}, u32[]{:S(2)}, u32[]{:S(2)}) collective-permute-start(bf16[256,1024]{1,0:T(8,128)(2,1)} %constant_dynamic-slice_fusion.5), channel_id=1, source_target_pairs={{0,1},{1,0},{2,3},{3,2},{4,5},{5,4},{6,7},{7,6},{8,9},{9,8},{10,11... | collective-permute-start | bytes 1572872 | tf_op jit(solution)/shard_map/ppermute | solution.py:497
  182.1 37.8 %collective-permute-start.14 = (bf16[1536,512]{1,0:T(8,128)(2,1)}, bf16[1536,512]{1,0:T(8,128)(2,1)}, u32[]{:S(2)}, u32[]{:S(2)}) collective-permute-start(bf16[1536,512]{1,0:T(8,128)(2,1)} %get-tuple-element.89), channel_id=1, source_target_pairs={{1,0},{8,1},{9,8},{16,9},{17,16},{24,17},{25,24},{3,2},{10,3},{11,... | collective-permute-start | bytes 4718600 | tf_op jit(solution)/shard_map/ppermute | solution.py:439
  183.3 36.5 %collective-permute-start.15 = (bf16[1536,512]{1,0:T(8,128)(2,1)}, bf16[1536,512]{1,0:T(8,128)(2,1)}, u32[]{:S(2)}, u32[]{:S(2)}) collective-permute-start(bf16[1536,512]{1,0:T(8,128)(2,1)} %get-tuple-element.90), channel_id=1, source_target_pairs={{0,1},{1,8},{8,9},{9,16},{16,17},{17,24},{24,25},{2,3},{3,10},{10,... | collective-permute-start | bytes 4718600 | tf_op jit(solution)/shard_map/ppermute | solution.py:439
  187.5 11.0 %collective-permute-start.16 = (bf16[512,512]{1,0:T(8,128)(2,1)S(1)}, bf16[512,512]{1,0:T(8,128)(2,1)S(1)}, u32[]{:S(2)}, u32[]{:S(2)}) collective-permute-start(bf16[512,512]{1,0:T(8,128)(2,1)S(1)} %copy-done.12), channel_id=1, source_target_pairs={{0,2},{1,4},{2,0},{3,6},{4,1},{5,7},{6,3},{7,5},{8,10},{9,12},{10,... | collective-permute-start | bytes 1572872 | tf_op jit(solution)/shard_map/ppermute | solution.py:470
  189.0 24.4 %collective-permute-start.17 = (bf16[512,512]{1,0:T(8,128)(2,1)S(1)}, bf16[512,512]{1,0:T(8,128)(2,1)S(1)}, u32[]{:S(2)}, u32[]{:S(2)}) collective-permute-start(bf16[512,512]{1,0:T(8,128)(2,1)S(1)} %copy-done.11), channel_id=1, source_target_pairs={{0,3},{1,5},{2,1},{3,7},{4,0},{5,6},{6,2},{7,4},{8,11},{9,13},{10,... | collective-permute-start | bytes 1572872 | tf_op jit(solution)/shard_map/ppermute | solution.py:470
  189.0 9.5 %copy-start.10 = (bf16[512,512]{1,0:T(8,128)(2,1)S(1)}, bf16[512,512]{1,0:T(8,128)(2,1)}, u32[]{:S(2)}) copy-start(bf16[512,512]{1,0:T(8,128)(2,1)} %get-tuple-element.88.refs_3_) | copy-start | bytes 1572868
  190.6 29.2 %collective-permute-start.18 = (bf16[512,512]{1,0:T(8,128)(2,1)}, bf16[512,512]{1,0:T(8,128)(2,1)}, u32[]{:S(2)}, u32[]{:S(2)}) collective-permute-start(bf16[512,512]{1,0:T(8,128)(2,1)} %get-tuple-element.87.refs_2_), channel_id=1, source_target_pairs={{0,1},{1,7},{2,3},{3,5},{4,2},{5,4},{6,0},{7,6},{8,9},{9,15},{10,1... | collective-permute-start | bytes 1572872 | tf_op jit(solution)/shard_map/ppermute | solution.py:470
  198.5 17.7 %copy-start.8 = (bf16[512,512]{1,0:T(8,128)(2,1)}, bf16[512,512]{1,0:T(8,128)(2,1)S(1)}, u32[]{:S(2)}) copy-start(bf16[512,512]{1,0:T(8,128)(2,1)S(1)} %collective-permute-done.16.refs_0_) | copy-start | bytes 1572868
  198.5 21.3 %collective-permute-start.19 = (bf16[512,512]{1,0:T(8,128)(2,1)S(1)}, bf16[512,512]{1,0:T(8,128)(2,1)}, u32[]{:S(2)}, u32[]{:S(2)}) collective-permute-start(bf16[512,512]{1,0:T(8,128)(2,1)S(1)} %copy-done.10), channel_id=1, source_target_pairs={{0,0},{1,6},{2,2},{3,4},{4,3},{5,5},{6,1},{7,7},{8,8},{9,14},{10,1... | collective-permute-start | bytes 1572872 | tf_op jit(solution)/shard_map/ppermute | solution.py:470
  213.3 6.4 %collective-permute-start.13 = (bf16[128,1024]{1,0:T(8,128)(2,1)S(1)}, bf16[128,1024]{1,0:T(8,128)(2,1)S(1)}, u32[]{:S(2)}, u32[]{:S(2)}) collective-permute-start(bf16[128,1024]{1,0:T(8,128)(2,1)S(1)} %constant_dynamic-slice_fusion.4), channel_id=1, source_target_pairs={{0,8},{8,0},{16,24},{24,16},{1,9},{9,1},{17,25},{25,17},{2,10},{10... | collective-permute-start | bytes 786440 | tf_op jit(solution)/shard_map/ppermute | solution.py:534
  216.4 8.5 %copy-start.1 = (bf16[1024,1024]{1,0:T(8,128)(2,1)}, bf16[1024,1024]{1,0:T(8,128)(2,1)S(1)}, u32[]{:S(2)}) copy-start(bf16[1024,1024]{1,0:T(8,128)(2,1)S(1)} %pad_maximum_fusion.2.refs_5_.refs_9_) | copy-start | bytes 6291460
  219.7 32.2 %collective-permute-start.22 = (bf16[1024,1024]{1,0:T(8,128)(2,1)S(1)}, bf16[1024,1024]{1,0:T(8,128)(2,1)}, u32[]{:S(2)}, u32[]{:S(2)}) collective-permute-start(bf16[1024,1024]{1,0:T(8,128)(2,1)S(1)} %pad_maximum_fusion.2.refs_5_.refs_9_), channel_id=1, source_target_pairs={{0,1},{1,0},{2,3},{3,2},{4,5},{5,4},{6,7},{7,6},{8,9},{9,8},{10,11... | collective-permute-start | bytes 6291464 | tf_op jit(solution)/shard_map/ppermute | solution.py:497
  232.2 2.1 collective-permute-start.20
  235.6 8.7 %collective-permute-start.21 = (bf16[128,1024]{1,0:T(8,128)(2,1)S(1)}, bf16[128,1024]{1,0:T(8,128)(2,1)S(1)}, u32[]{:S(2)}, u32[]{:S(2)}) collective-permute-start(bf16[128,1024]{1,0:T(8,128)(2,1)S(1)} %constant_dynamic-slice_fusion.2), channel_id=1, source_target_pairs={{0,8},{8,0},{16,24},{24,16},{1,9},{9,1},{17,25},{25,17},{2,10},{10... | collective-permute-start | bytes 786440 | tf_op jit(solution)/shard_map/ppermute | solution.py:534
  237.3 20.0 %collective-permute-start.23 = (bf16[512,512]{1,0:T(8,128)(2,1)}, bf16[512,512]{1,0:T(8,128)(2,1)}, u32[]{:S(2)}, u32[]{:S(2)}) collective-permute-start(bf16[512,512]{1,0:T(8,128)(2,1)} %get-tuple-element.93.refs_0_), channel_id=1, source_target_pairs={{0,2},{1,4},{2,0},{3,6},{4,1},{5,7},{6,3},{7,5},{8,10},{9,12},{10,... | collective-permute-start | bytes 1572872 | tf_op jit(solution)/shard_map/ppermute | solution.py:470
  238.7 24.6 %collective-permute-start.24 = (bf16[512,512]{1,0:T(8,128)(2,1)}, bf16[512,512]{1,0:T(8,128)(2,1)}, u32[]{:S(2)}, u32[]{:S(2)}) collective-permute-start(bf16[512,512]{1,0:T(8,128)(2,1)} %get-tuple-element.94.refs_1_), channel_id=1, source_target_pairs={{0,3},{1,5},{2,1},{3,7},{4,0},{5,6},{6,2},{7,4},{8,11},{9,13},{10,... | collective-permute-start | bytes 1572872 | tf_op jit(solution)/shard_map/ppermute | solution.py:470
  238.7 24.6 %collective-permute-start.25 = (bf16[512,512]{1,0:T(8,128)(2,1)}, bf16[512,512]{1,0:T(8,128)(2,1)}, u32[]{:S(2)}, u32[]{:S(2)}) collective-permute-start(bf16[512,512]{1,0:T(8,128)(2,1)} %get-tuple-element.95.refs_2_), channel_id=1, source_target_pairs={{0,1},{1,7},{2,3},{3,5},{4,2},{5,4},{6,0},{7,6},{8,9},{9,15},{10,1... | collective-permute-start | bytes 1572872 | tf_op jit(solution)/shard_map/ppermute | solution.py:470
  244.2 5.4 %copy-start.13 = (bf16[128,1024]{1,0:T(8,128)(2,1)}, bf16[128,1024]{1,0:T(8,128)(2,1)S(1)}, u32[]{:S(2)}) copy-start(bf16[128,1024]{1,0:T(8,128)(2,1)S(1)} %collective-permute-done.21) | copy-start | bytes 786436
  244.2 19.1 %collective-permute-start.26 = (bf16[512,512]{1,0:T(8,128)(2,1)}, bf16[512,512]{1,0:T(8,128)(2,1)}, u32[]{:S(2)}, u32[]{:S(2)}) collective-permute-start(bf16[512,512]{1,0:T(8,128)(2,1)} %get-tuple-element.96.refs_3_), channel_id=1, source_target_pairs={{0,0},{1,6},{2,2},{3,4},{4,3},{5,5},{6,1},{7,7},{8,8},{9,14},{10,1... | collective-permute-start | bytes 1572872 | tf_op jit(solution)/shard_map/ppermute | solution.py:470
  263.4 14.1 %collective-permute-start.27 = (bf16[128,1024]{1,0:T(8,128)(2,1)S(1)}, bf16[128,1024]{1,0:T(8,128)(2,1)S(1)}, u32[]{:S(2)}, u32[]{:S(2)}) collective-permute-start(bf16[128,1024]{1,0:T(8,128)(2,1)S(1)} %constant_dynamic-slice_fusion), channel_id=1, source_target_pairs={{0,16},{8,24},{16,0},{24,8},{1,17},{9,25},{17,1},{25,9},{2,18},{10... | collective-permute-start | bytes 786440 | tf_op jit(solution)/shard_map/ppermute | solution.py:534
  277.5 14.3 %collective-permute-start.28 = (bf16[128,1024]{1,0:T(8,128)(2,1)S(1)}, bf16[128,1024]{1,0:T(8,128)(2,1)S(1)}, u32[]{:S(2)}, u32[]{:S(2)}) collective-permute-start(bf16[128,1024]{1,0:T(8,128)(2,1)S(1)} %add_convert_fusion.2), channel_id=1, source_target_pairs={{0,16},{8,24},{16,0},{24,8},{1,17},{9,25},{17,1},{25,9},{2,18},{10... | collective-permute-start | bytes 786440 | tf_op jit(solution)/shard_map/ppermute | solution.py:534
  291.9 13.9 %collective-permute-start.29 = (bf16[2,128,1024]{2,1,0:T(8,128)(2,1)S(1)}, bf16[2,128,1024]{2,1,0:T(8,128)(2,1)S(1)}, u32[]{:S(2)}, u32[]{:S(2)}) collective-permute-start(bf16[2,128,1024]{2,1,0:T(8,128)(2,1)S(1)} %bitcast.36), channel_id=1, source_target_pairs={{0,8},{8,0},{16,24},{24,16},{1,9},{9,1},{17,25},{25,17},{2,10},{10... | collective-permute-start | bytes 1572872 | tf_op jit(solution)/shard_map/ppermute | solution.py:534
  292.0 13.9 %collective-permute-start.30 = (bf16[2,128,1024]{2,1,0:T(8,128)(2,1)S(1)}, bf16[2,128,1024]{2,1,0:T(8,128)(2,1)S(1)}, u32[]{:S(2)}, u32[]{:S(2)}) collective-permute-start(bf16[2,128,1024]{2,1,0:T(8,128)(2,1)S(1)} %bitcast.37), channel_id=1, source_target_pairs={{0,4},{4,0},{1,5},{5,1},{2,6},{6,2},{3,7},{7,3},{8,12},{12,8},{9,1... | collective-permute-start | bytes 1572872 | tf_op jit(solution)/shard_map/ppermute | solution.py:567
  305.9 13.0 %collective-permute-start.31 = (bf16[2,128,1024]{2,1,0:T(8,128)(2,1)S(1)}, bf16[2,128,1024]{2,1,0:T(8,128)(2,1)S(1)}, u32[]{:S(2)}, u32[]{:S(2)}) collective-permute-start(bf16[2,128,1024]{2,1,0:T(8,128)(2,1)S(1)} %collective-permute-done.29), channel_id=1, source_target_pairs={{0,4},{4,0},{1,5},{5,1},{2,6},{6,2},{3,7},{7,3},{8,12},{12,8},{9,1... | collective-permute-start | bytes 1572872 | tf_op jit(solution)/shard_map/ppermute | solution.py:567
  319.3 2.9 collective-permute-start.32
  (2 other events, 4.7 us)
Sparse Core Ops, SparseCore 0:
  58.7 46.4 all-gather.2

commit v7 on v6

--- a/solution.py
+++ b/solution.py
@@ -269,29 +269,48 @@
         move.wait()
 
 
+def halo_kernel(steps, order, *refs):
+    parts, (up, down, held, sems) = refs[:steps], refs[steps:]
+    chunk = parts[0].shape[0]
+    carry_out([
+        pltpu.make_async_copy(part, held.at[pl.ds(pl.multiple_of(order[i], 16), chunk)], sems.at[i])
+        for i, part in enumerate(parts)
+    ])
+    halo, rest = HALO * LONGITUDES, (BAND_ROWS - HALO) * LONGITUDES
+    carry_out([
+        pltpu.make_async_copy(held.at[pl.ds(rest, halo)], up, sems.at[0]),
+        pltpu.make_async_copy(held.at[pl.ds(0, halo)], down, sems.at[1]),
+    ])
+
+
+def halo_rows(order, parts):
+    steps, width = len(parts), parts[0].shape[1]
+    halo = shape(HALO * LONGITUDES, width)
+    return call(
+        functools.partial(halo_kernel, steps), [halo, halo], [SMEM] + [HBM] * steps, [HBM] * 2, (order, *parts), flops=0,
+        scratch=[pltpu.VMEM((BAND_ROWS * LONGITUDES, width), BF16), pltpu.SemaphoreType.DMA((steps,))],
+    )
+
+
 def projection_kernel(steps, feats, order, weight, *refs):
-    parts, (qkv, kv_up, kv_down, held, sems) = refs[:steps], refs[steps:]
+    parts, (qkv, held, sems) = refs[:steps], refs[steps:]
     chunk = parts[0].shape[0]
     carry_out(stacked_moves(parts, held, sems))
     for first in range(0, 3 * feats, feats):
         product = nn(held[...], weight[:, first:first + feats]).astype(BF16)
         for i in range(steps):
             qkv[pl.ds(pl.multiple_of(order[i], 16), chunk), first:first + feats] = product[i * chunk:(i + 1) * chunk]
-    kv_up[...] = qkv[(BAND_ROWS - HALO) * LONGITUDES:, feats:]
-    kv_down[...] = qkv[:HALO * LONGITUDES, feats:]
 
 
 def projections(order, weight, parts):
-    steps, feats = len(parts), weight.shape[1] // 3
-    width = parts[0].shape[1]
-    band, halo = BAND_ROWS * LONGITUDES, HALO * LONGITUDES
+    steps, feats, width = len(parts), weight.shape[1] // 3, parts[0].shape[1]
+    band = BAND_ROWS * LONGITUDES
     return call(
         functools.partial(projection_kernel, steps, feats),
-        [shape(band, 3 * feats), shape(halo, 2 * feats), shape(halo, 2 * feats)],
-        [SMEM, VMEM] + [HBM] * steps, [VMEM] * 3, (order, weight, *parts),
+        [shape(band, 3 * feats)], [SMEM, VMEM] + [HBM] * steps, [VMEM], (order, weight, *parts),
         flops=2 * band * weight.size,
         scratch=[pltpu.VMEM((band, width), BF16), pltpu.SemaphoreType.DMA((steps,))],
-    )
+    )[0]
 
 
 def join_kernel(steps, order, own, above, below, *refs):
@@ -321,32 +340,46 @@
     )
 
 
-def weight_grad_kernel(steps, sides, *refs):
-    lefts, refs = refs[:steps], refs[steps:]
-    rights, (grad, left, right, sems) = [refs[i * steps:(i + 1) * steps] for i in range(sides)], refs[sides * steps:]
-    feats = left.shape[1] // sides
-    moves = stacked_moves(lefts, left, sems)
-    for side, parts in enumerate(rights):
-        moves += stacked_moves(parts, right.at[side], sems, (side + 1) * steps)
-    carry_out(moves)
-    for side in range(sides):
-        at = slice(side * feats, (side + 1) * feats)
-        grad[at, :] = lax.dot_general(
-            left[:, at], right[side], (((0,), (0,)), ((), ())), preferred_element_type=F32
-        ).astype(BF16)
-
-
-def weight_grad(lefts, *rights):
-    steps, (chunk, rows), width = len(lefts), lefts[0].shape, rights[0][0].shape[1]
-    args = (*lefts, *(part for parts in rights for part in parts))
-    return call(
-        functools.partial(weight_grad_kernel, steps, len(rights)),
-        [shape(rows, width)], [HBM] * len(args), [VMEM], args,
-        flops=2 * steps * lefts[0].size * width,
+def weight_grad_kernel(steps, order, *refs):
+    (outq_parts, upstream, normed), refs = [refs[i * steps:(i + 1) * steps] for i in range(3)], refs[3 * steps:]
+    dkv, dkv_top, dkv_bot, normed_top, normed_bot, grad, outq, up, own, sems = refs
+    feats, chunk = outq.shape[1] // 2, outq_parts[0].shape[0]
+    groups = [
+        [
+            pltpu.make_async_copy(part, held.at[pl.ds(pl.multiple_of(order[i], 16), chunk)], sems.at[group, i])
+            for i, part in enumerate(parts)
+        ]
+        for group, (parts, held) in enumerate(((outq_parts, outq), (normed, own), (upstream, up)))
+    ]
+    for moves in groups:
+        for move in moves:
+            move.start()
+
+    def product(left, right):
+        return lax.dot_general(left, right, (((0,), (0,)), ((), ())), preferred_element_type=F32)
+
+    keyval = product(dkv_top[...], normed_top[...]) + product(dkv_bot[...], normed_bot[...])
+    for moves in groups[:2]:
+        for move in moves:
+            move.wait()
+    grad[2 * feats:, :] = (keyval + product(dkv[...].astype(BF16), own[...])).astype(BF16)
+    grad[feats:2 * feats, :] = product(outq[:, feats:], own[...]).astype(BF16)
+    for move in groups[2]:
+        move.wait()
+    grad[:feats, :] = product(outq[:, :feats], up[...]).astype(BF16)
+
+
+def weight_grads(order, outq_parts, upstream, normed, dkv, dkv_halos, normed_halos):
+    steps, (chunk, rows), width = len(normed), outq_parts[0].shape, normed[0].shape[1]
+    band = steps * chunk
+    return call(
+        functools.partial(weight_grad_kernel, steps),
+        [shape(2 * rows, width)], [SMEM] + [HBM] * (3 * steps) + [VMEM] * 5, [VMEM],
+        (order, *outq_parts, *upstream, *normed, dkv, *dkv_halos, *normed_halos),
+        flops=2 * width * rows * (2 * band + 2 * HALO * LONGITUDES),
         scratch=[
-            pltpu.VMEM((steps * chunk, rows), BF16),
-            pltpu.VMEM((len(rights), steps * chunk, width), BF16),
-            pltpu.SemaphoreType.DMA((len(args),)),
+            pltpu.VMEM((band, rows), BF16), pltpu.VMEM((band, width), BF16), pltpu.VMEM((band, width), BF16),
+            pltpu.SemaphoreType.DMA((3, steps)),
         ],
     )[0]
 
@@ -501,15 +534,12 @@
     held = jnp.concatenate([
         lax.dynamic_slice_in_dim(flat, z * size, size, 0) for flat, size in zip((flat_qkv, flat_out), rows)
     ], axis=0)
-    shares = [from_ahead(held, dm) for dm in range(1, halves)]
 
     def split(qkv, out):
         eighth = jnp.asarray([HEAD_WIDTH ** -0.5, 1.0, 1.0], BF16)[None, :, None, None]
         qkv = (qkv.reshape(heads, 3, HEAD_WIDTH, WIDTH) * eighth).transpose(1, 0, 2, 3)
         return jnp.concatenate([qkv.reshape(3 * feats, WIDTH), out.reshape(feats, WIDTH)], axis=0)
 
-    tokens, *shares = lax.optimization_barrier((tokens, *shares))
-    ahead = [lax.all_gather(part, "z") for part in shares]
     blocks = [split(flat_qkv, flat_out)]
     sibling = from_sibling(blocks[0])
     group = jnp.where(c == y, blocks[0], sibling)
@@ -517,10 +547,14 @@
 
     normed_parts, hop = gathered(norm(tokens, gain))
     *normed_parts, group_qkv, group_out = lax.optimization_barrier((*normed_parts, group_qkv, group_out))
-    qkv, kv_up, kv_down = projections(order, group_qkv, normed_parts)
-    upstream_parts, _ = gathered(after(upstream, *hop), qkv)
-    kv_top, kv_bot = passed_along(kv_up, 1), passed_along(kv_down, -1)
-    order, kv_top, kv_bot, *ahead = lax.optimization_barrier((order, kv_top, kv_bot, *ahead))
+    normed_up, normed_down = halo_rows(order, normed_parts)
+    normed_halos = passed_along(normed_up, 1), passed_along(normed_down, -1)
+    qkv = projections(order, group_qkv, normed_parts)
+    shares = [from_ahead(after(held, qkv), dm) for dm in range(1, halves)]
+    upstream_parts, _ = gathered(after(upstream, *normed_parts), qkv)
+    kv_top, kv_bot = (nn(x, group_qkv[:, feats:]).astype(BF16) for x in normed_halos)
+    order, kv_top, kv_bot, *shares = lax.optimization_barrier((order, kv_top, kv_bot, *shares))
+    ahead = [lax.all_gather(part, "z") for part in shares]
     outq_parts, dkv, dkv_top, dkv_bot = attention(cells, order, qkv, kv_top, kv_bot, group_out, upstream_parts)
 
     ahead = [after(block, dkv_top) for block in ahead]
@@ -529,48 +563,16 @@
     from_above, from_below = passed_along(dkv_top, -1), passed_along(dkv_bot, 1)
     outq_own = send_back(outq_parts)
 
-    bits = range((layers - 1).bit_length())
-    partners = [("c", c, from_sibling)] + [
-        ("z", z // 2 ** bit % 2, lambda x, bit=bit: lax.ppermute(x, "z", [(i, i ^ 2 ** bit) for i in range(layers)]))
-        for bit in bits
-    ]
-
-    def halved(x, partner):
-        _, side, swap = partner
-        half = x.shape[0] // 2
-        keep, give = (lax.dynamic_slice_in_dim(x, at * half, half, 0) for at in (side, 1 - side))
-        return (keep.astype(F32) + swap(give).astype(F32)).astype(BF16)
-
-    def in_turn(side, mine, other):
-        return jnp.concatenate([jnp.where(side == 0, mine, other), jnp.where(side == 0, other, mine)], axis=1)
-
-    def begun(grads):
-        return halved(halved(grads, partners[0]), partners[1])
-
-    early = begun(weight_grad(outq_parts, upstream_parts, normed_parts))
-    early, from_above, from_below, *outq_own = lax.optimization_barrier((early, from_above, from_below, *outq_own))
+    grads = weight_grads(order, outq_parts, upstream_parts, normed_parts, dkv, (dkv_top, dkv_bot), normed_halos)
+    grads = lax.psum(grads, ("z", "c"))
     dkv_parts = joined(order, dkv, from_above, from_below, len(slots))
     dkv_own = send_back(dkv_parts)
-    late = begun(weight_grad(dkv_parts, normed_parts))
-    update = updates(after(leads, late), outq_own, blocks)
-    late, update, *dkv_own = lax.optimization_barrier((late, update, *dkv_own))
+    update = updates(leads, outq_own, blocks)
     grad_input = grad_inputs(leads, tokens, gain, outq_own, dkv_own, blocks)
-
-    both = jnp.concatenate([early, late], axis=0)
-    for partner in partners[2:]:
-        both = halved(both, partner)
-    for _, side, swap in reversed(partners[2:]):
-        other = swap(both)
-        both = jnp.concatenate([jnp.where(side == 0, both, other), jnp.where(side == 0, other, both)], axis=0)
-    both = both.reshape(2, feats // 2, WIDTH)
-    _, side, swap = partners[1]
-    over_y = lambda x: lax.ppermute(x, "y", [(0, 1), (1, 0)])
-    other, both_y = lax.optimization_barrier((swap(both), over_y(both)))
-    own = in_turn(side, both, other)
-    far = in_turn(side, both_y, over_y(other))
-    own, far, grad_input = lax.optimization_barrier((own, far, grad_input))
-    mine, give = jnp.where(c == y, own, far), jnp.where(c == y, far, own)
-    early, late = in_turn(c, mine, from_sibling(give)).astype(F32) * grad_scale
+    grads, grad_input, update = lax.optimization_barrier((grads, grad_input, update))
+    pairs = [((1 - y, m, 1 - y), (y, m, 1 - y)) for y in range(2) for m in range(halves)]
+    grads = jnp.where(c == y, grads, permuted(grads, pairs)).astype(F32) * grad_scale
+    early, late = grads[:2 * feats], grads[2 * feats:]
     by_head = lambda x: x.reshape(heads, HEAD_WIDTH, WIDTH)
     grad_out = by_head(early[:feats])
     grad_query = early[feats:] * HEAD_WIDTH ** -0.5

time: 336 us -> 330 us (0.982)
  waiting for transfers between devices: 153 us -> 108 us
  starting transfers between devices: 43.3 us -> 71.2 us
  matrix products: 0 us -> 9.78 us
  Pallas kernels: 88.9 us -> 94.7 us
    ppermute x7 -> x0, waiting for transfers between devices: 51.9 us -> none  [the longest x5 49.4 us: on_device(): lax.ppermute(x, 'z', [(i, i ^ 2 ** bit) for i in range(layers)])]
    psum x0 -> x1, waiting for transfers between devices: none -> 30.1 us  [on_device(): grads = lax.psum(grads, ('z', 'c'))]
    ppermute x16 -> x17, starting transfers between devices: 18.1 us -> 47.2 us  [permuted(): return lax.ppermute(x, GROUP, [(at(*a), at(*b)) for a, b in pairs])]
    ppermute x4, starting transfers between devices: 9.21 us -> 21 us  [passed_along(): return lax.ppermute(x, ('z', 'c'), pairs)]
    ppermute x1, waiting for transfers between devices: 10 us -> 0.01 us  [from_ahead(): return lax.ppermute(x, 'm', [((i + dm) % halves, i) for i in range(halves)])]
    dot_general x0 -> x2, matrix products: none -> 9.78 us  [nn(): lax.dot_general(a, b, (((1,), (0,)), ((), ())), preferred_element_type=jn...]
    ppermute x16 -> x17, waiting for transfers between devices: 86.6 us -> 77.9 us  [permuted(): return lax.ppermute(x, GROUP, [(at(*a), at(*b)) for a, b in pairs])]
    ppermute x5 -> x2, starting transfers between devices: 7.7 us -> 1.09 us  [from_sibling(): return lax.ppermute(x, 'c', [(0, 1), (1, 0)])]
  transfers between devices with their start and end apart: 34 -> 26, of which waited for: 19 -> 9; matrix products, arithmetic and copies ran while one was open for 7% -> 9% of each run, Pallas kernels for 12% -> 27%
where the time goes in v7:
time: 330 us; the launch traced here: 329 us
  waiting for transfers between devices  108 us (33%)
  Pallas kernels  94.7 us (29%)
  starting transfers between devices  71.2 us (22%)
  other arithmetic  18.3 us (6%)
  between operations  15.8 us (5%)
  local copies, waits for them, and re-layouts  11.3 us (3%)
  matrix products  9.78 us (3%)
    pallas_call x8, Pallas kernels, call(): pl.pallas_call(kernel, out_shape=tuple(out_shape), in_specs=list(in_specs...  94.7 us
    ppermute x17, waiting for transfers between devices, permuted(): return lax.ppermute(x, GROUP, [(at(*a), at(*b)) for a, b in pairs])  77.9 us
    ppermute x17, starting transfers between devices, permuted(): return lax.ppermute(x, GROUP, [(at(*a), at(*b)) for a, b in pairs])  47.2 us
    psum x1, waiting for transfers between devices, on_device(): grads = lax.psum(grads, ('z', 'c'))  30.1 us
    ppermute x4, starting transfers between devices, passed_along(): return lax.ppermute(x, ('z', 'c'), pairs)  21 us
    dot_general x2, matrix products, nn(): lax.dot_general(a, b, (((1,), (0,)), ((), ())), preferred_element_type=jn...  9.78 us
  transfers between devices with their start and end apart: 26, of which 9 were waited for; matrix products, arithmetic and copies ran while one was open for 9% of the time, Pallas kernels for 27%

profile of v7, /device:TPU:0, one launch (start us, length us, event | category | flops | bytes accessed | tf_op | source)
XLA Modules:
  0.0 329.1 jit_solution(15669704495570236131)
XLA Ops:
  8.1 1.6 copy_multiply_fusion.1
  9.7 1.6 pad_maximum_fusion.1.refs_8_.refs_4_
  12.0 2.6 shard_map.129
  14.6 2.5 collective-permute-start
  17.1 23.3 %collective-permute-done.refs_0_.refs_8_ = bf16[512,1024]{1,0:T(8,128)(2,1)S(1)} collective-permute-done((bf16[512,1024]{1,0:T(8,128)(2,1)}, bf16[512,1024]{1,0:T(8,128)(2,1)S(1)}, u32[]{:S(2)}, u32[]{:S(2)}) %collective-permute-start) | collective-permute-done | bytes 1048608 | tf_op jit(solution)/shard_map/ppermute | solution.py:503
  42.5 2.7 collective-permute-start.2
  45.2 1.6 collective-permute-start.3
  46.8 1.3 fusion.2.order
  48.1 3.3 %broadcast_select_fusion = bf16[1024,1024]{1,0:T(8,128)(2,1)S(1)} fusion(bf16[1024,1024]{1,0:T(8,128)(2,1)S(1)} %collective-permute-done.4.refs_10_.refs_6_, pred[]{:T(512)S(6)} %eq.2, bf16[256,1024]{1,0:T(8,128)(2,1)} %bitcast.32, bf16[768,1024]{1,0:T(8,128)(2,1)} %bitcast.26), kind=kLoop, calls=%fused_computation.6 | loop fusion | flops 5242880 | bytes 6291457 | tf_op jit(solution)/shard_map/jit(_where)/select_n | solution.py:545
  52.4 5.4 %collective-permute-done.2.refs_2_.refs_10_ = bf16[512,1024]{1,0:T(8,128)(2,1)} collective-permute-done((bf16[512,1024]{1,0:T(8,128)(2,1)}, bf16[512,1024]{1,0:T(8,128)(2,1)}, u32[]{:S(2)}, u32[]{:S(2)}) %collective-permute-start.2) | collective-permute-done | bytes 1048608 | tf_op jit(solution)/shard_map/ppermute | solution.py:503
  58.9 5.7 %shard_map.130 = (bf16[1536,1024]{1,0:T(8,128)(2,1)}, bf16[1536,1024]{1,0:T(8,128)(2,1)}) custom-call(s32[4]{0:T(128)} %fusion.2.order, bf16[512,1024]{1,0:T(8,128)(2,1)} %copy-done.4, bf16[512,1024]{1,0:T(8,128)(2,1)} %collective-permute-done.1.refs_1_.refs_9_, bf16[512,1024]{1,0:T(8,128)(2,1)} %collective-permute-done.2.refs_2_.refs_10_, ...), custom_call_target="tpu_custom_call" | custom-call | bytes 10485776 | tf_op jit(solution)/shard_map/pallas_call | solution.py:200
  64.6 6.5 %collective-permute-start.5 = (bf16[1536,1024]{1,0:T(8,128)(2,1)}, bf16[1536,1024]{1,0:T(8,128)(2,1)}, u32[]{:S(2)}, u32[]{:S(2)}) collective-permute-start(bf16[1536,1024]{1,0:T(8,128)(2,1)} %get-tuple-element.50), channel_id=1, source_target_pairs={{0,1},{1,8},{8,9},{9,16},{16,17},{17,24},{24,25},{2,3},{3,10},{10,... | collective-permute-start | bytes 9437192 | tf_op jit(solution)/shard_map/ppermute | solution.py:472
  71.1 1.3 collective-permute-start.6
  72.4 1.8 collective-permute-start.8
  78.0 1.6 copy.15.weight
  79.6 8.9 %shard_map.131.qkv = bf16[2048,768]{1,0:T(8,128)(2,1)} custom-call(s32[4]{0:T(128)} %fusion.2.order, bf16[1024,768]{1,0:T(8,128)(2,1)} %copy.15.weight, bf16[512,1024]{1,0:T(8,128)(2,1)} %copy-done.4, bf16[512,1024]{1,0:T(8,128)(2,1)} %collective-permute-done.1.refs_1_.refs_9_, bf16[512,1024]{1,0:T(8,128)(2,1)} %collective-permute-done.2.refs_2_.refs_10_, ...), custom_call_target="tpu_custom_call" | custom-call | flops 3221225472 | bytes 8912912 | tf_op jit(solution)/shard_map/pallas_call | solution.py:200
  88.5 1.8 collective-permute-start.7
  90.3 7.5 %collective-permute-done.8.refs_0_.refs_4_ = bf16[512,1024]{1,0:T(8,128)(2,1)} collective-permute-done((bf16[512,1024]{1,0:T(8,128)(2,1)S(1)}, bf16[512,1024]{1,0:T(8,128)(2,1)}, u32[]{:S(2)}, u32[]{:S(2)}) %collective-permute-start.8) | collective-permute-done | bytes 1048608 | tf_op jit(solution)/shard_map/ppermute | solution.py:503
  97.8 2.0 collective-permute-done.9.refs_1_.refs_5_
  99.8 4.9 %convolution_convert_fusion.1.kv_top = bf16[1536,512]{1,0:T(8,128)(2,1)} fusion(bf16[1536,1024]{1,0:T(8,128)(2,1)} %collective-permute-done.5.refs_15_, bf16[1024,768]{0,1:T(8,128)(2,1)S(1)} %slice_bitcast_fusion), kind=kOutput, calls=%fused_computation.3 | convolution fusion | flops 1611399168 | bytes 5767168 | tf_op jit(solution)/shard_map/dot_general | solution.py:24
  104.7 4.9 %convolution_convert_fusion.kv_bot = bf16[1536,512]{1,0:T(8,128)(2,1)} fusion(bf16[1536,1024]{1,0:T(8,128)(2,1)} %collective-permute-done.6.refs_16_, bf16[1024,768]{0,1:T(8,128)(2,1)S(1)} %slice_bitcast_fusion), kind=kOutput, calls=%fused_computation.2 | convolution fusion | flops 1611399168 | bytes 5767168 | tf_op jit(solution)/shard_map/dot_general | solution.py:24
  110.5 1.3 broadcast_select_fusion.2
  112.9 1.7 collective-permute-start.11
  115.2 10.0 %collective-permute-done.10.refs_2_.refs_6_ = bf16[512,1024]{1,0:T(8,128)(2,1)} collective-permute-done((bf16[512,1024]{1,0:T(8,128)(2,1)S(1)}, bf16[512,1024]{1,0:T(8,128)(2,1)}, u32[]{:S(2)}, u32[]{:S(2)}) %collective-permute-start.10) | collective-permute-done | bytes 1048608 | tf_op jit(solution)/shard_map/ppermute | solution.py:503
  126.3 42.4 %shard_map.132 = (bf16[512,512]{1,0:T(8,128)(2,1)}, bf16[512,512]{1,0:T(8,128)(2,1)}, bf16[512,512]{1,0:T(8,128)(2,1)}, bf16[512,512]{1,0:T(8,128)(2,1)}, f32[20...) custom-call(s32[20]{0:T(128)} %pad_dynamic-slice_fusion.cells, s32[4]{0:T(128)} %fusion.2.order, ...), custom_call_target="tpu_custom_call" | custom-call | flops 13958643712 | bytes 20447328 | tf_op jit(solution)/shard_map/pallas_call | solution.py:200
  168.7 1.3 collective-permute-start.16
  170.0 11.9 %collective-permute-start.17 = (bf16[1536,512]{1,0:T(8,128)(2,1)}, bf16[1536,512]{1,0:T(8,128)(2,1)}, u32[]{:S(2)}, u32[]{:S(2)}) collective-permute-start(bf16[1536,512]{1,0:T(8,128)(2,1)} %get-tuple-element.70.refs_14_), channel_id=1, source_target_pairs={{0,1},{1,8},{8,9},{9,16},{16,17},{17,24},{24,25},{2,3},{3,10},{10,... | collective-permute-start | bytes 4718600 | tf_op jit(solution)/shard_map/ppermute | solution.py:472
  183.0 1.6 slice.37
  185.6 1.5 collective-permute-start.12
  187.0 4.5 %collective-permute-start.13 = (bf16[512,512]{1,0:T(8,128)(2,1)}, bf16[512,512]{1,0:T(8,128)(2,1)S(1)}, u32[]{:S(2)}, u32[]{:S(2)}) collective-permute-start(bf16[512,512]{1,0:T(8,128)(2,1)} %get-tuple-element.65.refs_1_), channel_id=1, source_target_pairs={{0,3},{1,5},{2,1},{3,7},{4,0},{5,6},{6,2},{7,4},{8,11},{9,13},{10,... | collective-permute-start | bytes 1572872 | tf_op jit(solution)/shard_map/ppermute | solution.py:503
  191.5 7.7 %collective-permute-start.14 = (bf16[512,512]{1,0:T(8,128)(2,1)}, bf16[512,512]{1,0:T(8,128)(2,1)}, u32[]{:S(2)}, u32[]{:S(2)}) collective-permute-start(bf16[512,512]{1,0:T(8,128)(2,1)} %get-tuple-element.66.refs_2_), channel_id=1, source_target_pairs={{0,1},{1,7},{2,3},{3,5},{4,2},{5,4},{6,0},{7,6},{8,9},{9,15},{10,1... | collective-permute-start | bytes 1572872 | tf_op jit(solution)/shard_map/ppermute | solution.py:503
  199.2 5.4 %collective-permute-start.15 = (bf16[512,512]{1,0:T(8,128)(2,1)}, bf16[512,512]{1,0:T(8,128)(2,1)}, u32[]{:S(2)}, u32[]{:S(2)}) collective-permute-start(bf16[512,512]{1,0:T(8,128)(2,1)} %get-tuple-element.67.refs_3_), channel_id=1, source_target_pairs={{0,0},{1,6},{2,2},{3,4},{4,3},{5,5},{6,1},{7,7},{8,8},{9,14},{10,1... | collective-permute-start | bytes 1572872 | tf_op jit(solution)/shard_map/ppermute | solution.py:503
  204.5 14.6 %shard_map.133 = bf16[1024,1024]{1,0:T(8,128)(2,1)} custom-call(s32[4]{0:T(128)} %fusion.2.order, bf16[512,512]{1,0:T(8,128)(2,1)} %get-tuple-element.64.refs_0_, bf16[512,512]{1,0:T(8,128)(2,1)} %get-tuple-element.65.refs_1_, bf16[512,512]{1,0:T(8,128)(2,1)} %get-tuple-element.66.refs_2_, bf16[512,512]{1,0:T(8,128)(2,1)} %get-tuple-element.67.refs_3_, ...), custom_call_target="tpu_custom_call" | custom-call | flops 7516192768 | bytes 26214416 | tf_op jit(solution)/shard_map/pallas_call | solution.py:200
  219.1 4.9 %shard_map.134 = (bf16[512,512]{1,0:T(8,128)(2,1)}, bf16[512,512]{1,0:T(8,128)(2,1)}, bf16[512,512]{1,0:T(8,128)(2,1)}, bf16[512,512]{1,0:T(8,128)(2,1)}) custom-call(s32[4]{0:T(128)} %fusion.2.order, f32[2048,512]{1,0:T(8,128)} %get-tuple-element.68.refs_12_.own, bf16[1536,512]{1,0:T(8,128)(2,1)} %collective-permute-done.16.above, ...), custom_call_target="tpu_custom_call" | custom-call | flops 2097152 | bytes 9437200 | tf_op jit(solution)/shard_map/pallas_call | solution.py:200
  224.1 1.5 collective-permute-start.18
  225.7 3.1 collective-permute-start.19
  228.8 1.9 collective-permute-start.20
  230.7 5.4 %collective-permute-start.21 = (bf16[512,512]{1,0:T(8,128)(2,1)}, bf16[512,512]{1,0:T(8,128)(2,1)}, u32[]{:S(2)}, u32[]{:S(2)}) collective-permute-start(bf16[512,512]{1,0:T(8,128)(2,1)} %get-tuple-element.74), channel_id=1, source_target_pairs={{0,0},{1,6},{2,2},{3,4},{4,3},{5,5},{6,1},{7,7},{8,8},{9,14},{10,1... | collective-permute-start | bytes 1572872 | tf_op jit(solution)/shard_map/ppermute | solution.py:503
  236.1 1.2 fusion.3.leads
  237.3 5.4 %shard_map.136 = bf16[512,1024]{1,0:T(8,128)(2,1)} custom-call(s32[4]{0:T(128)} %fusion.3.leads, bf16[512,512]{1,0:T(8,128)(2,1)} %copy-done.7, bf16[512,512]{1,0:T(8,128)(2,1)} %copy-done.8, bf16[512,512]{1,0:T(8,128)(2,1)} %collective-permute-done.14.refs_2_, bf16[512,512]{1,0:T(8,128)(2,1)} %collective-permute-done.15.refs_3_, ...), custom_call_target="tpu_custom_call" | custom-call | flops 1073741824 | bytes 11534352 | tf_op jit(solution)/shard_map/pallas_call | solution.py:200
  242.7 5.1 %collective-permute-done.19.refs_5_ = bf16[512,512]{1,0:T(8,128)(2,1)} collective-permute-done((bf16[512,512]{1,0:T(8,128)(2,1)}, bf16[512,512]{1,0:T(8,128)(2,1)}, u32[]{:S(2)}, u32[]{:S(2)}) %collective-permute-start.19) | collective-permute-done | bytes 524320 | tf_op jit(solution)/shard_map/ppermute | solution.py:503
  247.8 10.3 %shard_map.135 = bf16[512,1024]{1,0:T(8,128)(2,1)} custom-call(s32[4]{0:T(128)} %fusion.3.leads, bf16[512,1024]{1,0:T(8,128)(2,1)} %tokens.3, f32[1,1024]{1,0:T(1,128)} %bitcast.42, bf16[512,512]{1,0:T(8,128)(2,1)} %copy-done.7, bf16[512,512]{1,0:T(8,128)(2,1)} %copy-done.8, bf16[512,512]{1,0:T(8,128)(2,1)} %collective-permute-done.14.refs_2_, ...), custom_call_target="tpu_custom_call" | custom-call | flops 3221225472 | bytes 14684176 | tf_op jit(solution)/shard_map/pallas_call | solution.py:200
  258.1 30.1 %all-reduce.3.cloned.1.call-done = bf16[1024,1024]{1,0:T(8,128)(2,1)} async-done(((bf16[1024,1024]{1,0:T(8,128)(2,1)}), bf16[1024,1024]{1,0:T(8,128)(2,1)}) %all-reduce.3.cloned.1.call-update) | async-done | bytes 2097168 | tf_op jit(solution)/shard_map/psum | solution.py:567
  288.2 3.8 %collective-permute-start.23 = (bf16[1024,1024]{1,0:T(8,128)(2,1)}, bf16[1024,1024]{1,0:T(8,128)(2,1)S(1)}, u32[]{:S(2)}, u32[]{:S(2)}) collective-permute-start(bf16[1024,1024]{1,0:T(8,128)(2,1)} %all-reduce.3.cloned.1.call-done), channel_id=1, source_target_pairs={{5,1},{7,3},{0,4},{2,6},{13,9},{15,11},{8,12},{10,14},{21,17},{23,... | collective-permute-start | bytes 6291464 | tf_op jit(solution)/shard_map/ppermute | solution.py:503
  292.0 23.7 %collective-permute-done.23 = bf16[1024,1024]{1,0:T(8,128)(2,1)S(1)} collective-permute-done((bf16[1024,1024]{1,0:T(8,128)(2,1)}, bf16[1024,1024]{1,0:T(8,128)(2,1)S(1)}, u32[]{:S(2)}, u32[]{:S(2)}) %collective-permute-start.23) | collective-permute-done | bytes 2097184 | tf_op jit(solution)/shard_map/ppermute | solution.py:503
  315.7 2.5 convert_multiply_fusion
  318.2 1.6 fusion.4
  319.8 1.9 pad_maximum_fusion
  (67 shorter events, 14.5 us)
Async XLA Ops:
  8.0 1.7 copy-start.6
  8.0 173.9 %all-gather.3.cloned.1.call-start = ((), (), s32[]{:S(2)}) async-start(), calls=%async_computation.1 | async-start | bytes 2621440 | tf_op jit(solution)/shard_map/all_gather | solution.py:557
  9.7 1.8 copy-start.2
  11.5 36.6 %collective-permute-start.4 = (bf16[1024,1024]{1,0:T(8,128)(2,1)}, bf16[1024,1024]{1,0:T(8,128)(2,1)S(1)}, u32[]{:S(2)}, u32[]{:S(2)}) collective-permute-start(bf16[1024,1024]{1,0:T(8,128)(2,1)} %pad_maximum_fusion.1.refs_8_.refs_4_), channel_id=1, source_target_pairs={{0,1},{1,0},{2,3},{3,2},{4,5},{5,4},{6,7},{7,6},{8,9},{9,8},{10,11... | collective-permute-start | bytes 6291464 | tf_op jit(solution)/shard_map/ppermute | solution.py:530
  14.6 25.8 %collective-permute-start = (bf16[512,1024]{1,0:T(8,128)(2,1)}, bf16[512,1024]{1,0:T(8,128)(2,1)S(1)}, u32[]{:S(2)}, u32[]{:S(2)}) collective-permute-start(bf16[512,1024]{1,0:T(8,128)(2,1)} %shard_map.129), channel_id=1, source_target_pairs={{2,0},{4,1},{0,2},{6,3},{1,4},{7,5},{3,6},{5,7},{10,8},{12,9},{8,1... | collective-permute-start | bytes 3145736 | tf_op jit(solution)/shard_map/ppermute | solution.py:503
  17.1 24.3 %collective-permute-start.1 = (bf16[512,1024]{1,0:T(8,128)(2,1)}, bf16[512,1024]{1,0:T(8,128)(2,1)}, u32[]{:S(2)}, u32[]{:S(2)}) collective-permute-start(bf16[512,1024]{1,0:T(8,128)(2,1)} %shard_map.129), channel_id=1, source_target_pairs={{3,0},{5,1},{1,2},{7,3},{0,4},{6,5},{2,6},{4,7},{11,8},{13,9},{9,1... | collective-permute-start | bytes 3145736 | tf_op jit(solution)/shard_map/ppermute | solution.py:503
  40.4 11.0 %copy-start.4 = (bf16[512,1024]{1,0:T(8,128)(2,1)}, bf16[512,1024]{1,0:T(8,128)(2,1)S(1)}, u32[]{:S(2)}) copy-start(bf16[512,1024]{1,0:T(8,128)(2,1)S(1)} %collective-permute-done.refs_0_.refs_8_) | copy-start | bytes 3145732
  42.5 15.3 %collective-permute-start.2 = (bf16[512,1024]{1,0:T(8,128)(2,1)}, bf16[512,1024]{1,0:T(8,128)(2,1)}, u32[]{:S(2)}, u32[]{:S(2)}) collective-permute-start(bf16[512,1024]{1,0:T(8,128)(2,1)} %broadcast_select_fusion.4), channel_id=1, source_target_pairs={{0,4},{1,0},{2,6},{3,2},{4,5},{5,1},{6,7},{7,3},{8,12},{9,8},{10,1... | collective-permute-start | bytes 3145736 | tf_op jit(solution)/shard_map/ppermute | solution.py:503
  45.2 12.6 %collective-permute-start.3 = (bf16[512,1024]{1,0:T(8,128)(2,1)S(1)}, bf16[512,1024]{1,0:T(8,128)(2,1)}, u32[]{:S(2)}, u32[]{:S(2)}) collective-permute-start(bf16[512,1024]{1,0:T(8,128)(2,1)S(1)} %collective-permute-done.refs_0_.refs_8_), channel_id=1, source_target_pairs={{1,3},{3,1},{4,6},{6,4},{9,11},{11,9},{12,14},{14,12},{17,19},{19,... | collective-permute-start | bytes 3145736 | tf_op jit(solution)/shard_map/ppermute | solution.py:503
  48.1 3.3 %copy-start = (bf16[1024,1024]{1,0:T(8,128)(2,1)}, bf16[1024,1024]{1,0:T(8,128)(2,1)S(1)}, u32[]{:S(2)}) copy-start(bf16[1024,1024]{1,0:T(8,128)(2,1)S(1)} %collective-permute-done.4.refs_10_.refs_6_) | copy-start | bytes 6291460
  51.4 6.4 %copy-start.3 = (bf16[512,1024]{1,0:T(8,128)(2,1)S(1)}, bf16[512,1024]{1,0:T(8,128)(2,1)}, u32[]{:S(2)}) copy-start(bf16[512,1024]{1,0:T(8,128)(2,1)} %shard_map.129) | copy-start | bytes 3145732
  58.9 13.5 %copy-start.5 = (bf16[512,1024]{1,0:T(8,128)(2,1)S(1)}, bf16[512,1024]{1,0:T(8,128)(2,1)}, u32[]{:S(2)}) copy-start(bf16[512,1024]{1,0:T(8,128)(2,1)} %param.15) | copy-start | bytes 3145732
  64.6 35.2 %collective-permute-start.5 = (bf16[1536,1024]{1,0:T(8,128)(2,1)}, bf16[1536,1024]{1,0:T(8,128)(2,1)}, u32[]{:S(2)}, u32[]{:S(2)}) collective-permute-start(bf16[1536,1024]{1,0:T(8,128)(2,1)} %get-tuple-element.50), channel_id=1, source_target_pairs={{0,1},{1,8},{8,9},{9,16},{16,17},{17,24},{24,25},{2,3},{3,10},{10,... | collective-permute-start | bytes 9437192 | tf_op jit(solution)/shard_map/ppermute | solution.py:472
  71.1 33.6 %collective-permute-start.6 = (bf16[1536,1024]{1,0:T(8,128)(2,1)}, bf16[1536,1024]{1,0:T(8,128)(2,1)}, u32[]{:S(2)}, u32[]{:S(2)}) collective-permute-start(bf16[1536,1024]{1,0:T(8,128)(2,1)} %get-tuple-element.52), channel_id=1, source_target_pairs={{1,0},{8,1},{9,8},{16,9},{17,16},{24,17},{25,24},{3,2},{10,3},{11,... | collective-permute-start | bytes 9437192 | tf_op jit(solution)/shard_map/ppermute | solution.py:472
  72.4 25.3 %collective-permute-start.8 = (bf16[512,1024]{1,0:T(8,128)(2,1)S(1)}, bf16[512,1024]{1,0:T(8,128)(2,1)}, u32[]{:S(2)}, u32[]{:S(2)}) collective-permute-start(bf16[512,1024]{1,0:T(8,128)(2,1)S(1)} %copy-done.5), channel_id=1, source_target_pairs={{2,0},{4,1},{0,2},{6,3},{1,4},{7,5},{3,6},{5,7},{10,8},{12,9},{8,1... | collective-permute-start | bytes 3145736 | tf_op jit(solution)/shard_map/ppermute | solution.py:503
  74.2 25.6 %collective-permute-start.9 = (bf16[512,1024]{1,0:T(8,128)(2,1)S(1)}, bf16[512,1024]{1,0:T(8,128)(2,1)}, u32[]{:S(2)}, u32[]{:S(2)}) collective-permute-start(bf16[512,1024]{1,0:T(8,128)(2,1)S(1)} %copy-done.5), channel_id=1, source_target_pairs={{3,0},{5,1},{1,2},{7,3},{0,4},{6,5},{2,6},{4,7},{11,8},{13,9},{9,1... | collective-permute-start | bytes 3145736 | tf_op jit(solution)/shard_map/ppermute | solution.py:503
  79.6 8.9 %copy-start.11 = (bf16[256,1024]{1,0:T(8,128)(2,1)S(1)}, bf16[256,1024]{1,0:T(8,128)(2,1)}, u32[]{:S(2)}) copy-start(bf16[256,1024]{1,0:T(8,128)(2,1)} %pad_maximum_fusion.3) | copy-start | bytes 1572868
  88.5 21.1 %collective-permute-start.7 = (bf16[256,1024]{1,0:T(8,128)(2,1)S(1)}, bf16[256,1024]{1,0:T(8,128)(2,1)S(1)}, u32[]{:S(2)}, u32[]{:S(2)}) collective-permute-start(bf16[256,1024]{1,0:T(8,128)(2,1)S(1)} %copy-done.11), channel_id=1, source_target_pairs={{2,0},{0,2},{3,1},{1,3},{6,4},{4,6},{7,5},{5,7},{10,8},{8,10},{11,... | collective-permute-start | bytes 1572872 | tf_op jit(solution)/shard_map/ppermute | solution.py:527
  109.6 5.0 %copy-start.13 = (s32[64]{0:T(128)S(1)}, s32[64]{0:T(128)}, u32[]{:S(2)}) copy-start(s32[64]{0:T(128)} %param.14) | copy-start | bytes 772
  109.6 0.8 copy-start.10
  110.4 177.8 %all-reduce.3.cloned.1.call-start = ((), (), s32[]{:S(2)}) async-start(), calls=%async_computation | async-start | bytes 4194304 | tf_op jit(solution)/shard_map/psum | solution.py:567
  111.8 13.4 %collective-permute-start.10 = (bf16[512,1024]{1,0:T(8,128)(2,1)S(1)}, bf16[512,1024]{1,0:T(8,128)(2,1)}, u32[]{:S(2)}, u32[]{:S(2)}) collective-permute-start(bf16[512,1024]{1,0:T(8,128)(2,1)S(1)} %broadcast_select_fusion.2), channel_id=1, source_target_pairs={{0,4},{1,0},{2,6},{3,2},{4,5},{5,1},{6,7},{7,3},{8,12},{9,8},{10,1... | collective-permute-start | bytes 3145736 | tf_op jit(solution)/shard_map/ppermute | solution.py:503
  112.9 12.3 %collective-permute-start.11 = (bf16[512,1024]{1,0:T(8,128)(2,1)}, bf16[512,1024]{1,0:T(8,128)(2,1)}, u32[]{:S(2)}, u32[]{:S(2)}) collective-permute-start(bf16[512,1024]{1,0:T(8,128)(2,1)} %collective-permute-done.8.refs_0_.refs_4_), channel_id=1, source_target_pairs={{1,3},{3,1},{4,6},{6,4},{9,11},{11,9},{12,14},{14,12},{17,19},{19,... | collective-permute-start | bytes 3145736 | tf_op jit(solution)/shard_map/ppermute | solution.py:503
  168.7 22.8 %collective-permute-start.16 = (bf16[1536,512]{1,0:T(8,128)(2,1)}, bf16[1536,512]{1,0:T(8,128)(2,1)}, u32[]{:S(2)}, u32[]{:S(2)}) collective-permute-start(bf16[1536,512]{1,0:T(8,128)(2,1)} %get-tuple-element.69.refs_13_), channel_id=1, source_target_pairs={{1,0},{8,1},{9,8},{16,9},{17,16},{24,17},{25,24},{3,2},{10,3},{11,... | collective-permute-start | bytes 4718600 | tf_op jit(solution)/shard_map/ppermute | solution.py:472
  170.0 29.2 %collective-permute-start.17 = (bf16[1536,512]{1,0:T(8,128)(2,1)}, bf16[1536,512]{1,0:T(8,128)(2,1)}, u32[]{:S(2)}, u32[]{:S(2)}) collective-permute-start(bf16[1536,512]{1,0:T(8,128)(2,1)} %get-tuple-element.70.refs_14_), channel_id=1, source_target_pairs={{0,1},{1,8},{8,9},{9,16},{16,17},{17,24},{24,25},{2,3},{3,10},{10,... | collective-permute-start | bytes 4718600 | tf_op jit(solution)/shard_map/ppermute | solution.py:472
  181.9 2.7 copy-start.12
  184.9 34.2 %copy-start.1 = (bf16[1024,1024]{1,0:T(8,128)(2,1)}, bf16[1024,1024]{1,0:T(8,128)(2,1)S(1)}, u32[]{:S(2)}) copy-start(bf16[1024,1024]{1,0:T(8,128)(2,1)S(1)} %pad_maximum_fusion.2.refs_9_.refs_5_) | copy-start | bytes 6291460
  184.9 52.4 %collective-permute-start.22 = (bf16[1024,1024]{1,0:T(8,128)(2,1)S(1)}, bf16[1024,1024]{1,0:T(8,128)(2,1)}, u32[]{:S(2)}, u32[]{:S(2)}) collective-permute-start(bf16[1024,1024]{1,0:T(8,128)(2,1)S(1)} %pad_maximum_fusion.2.refs_9_.refs_5_), channel_id=1, source_target_pairs={{0,1},{1,0},{2,3},{3,2},{4,5},{5,4},{6,7},{7,6},{8,9},{9,8},{10,11... | collective-permute-start | bytes 6291464 | tf_op jit(solution)/shard_map/ppermute | solution.py:530
  185.6 38.5 %collective-permute-start.12 = (bf16[512,512]{1,0:T(8,128)(2,1)}, bf16[512,512]{1,0:T(8,128)(2,1)S(1)}, u32[]{:S(2)}, u32[]{:S(2)}) collective-permute-start(bf16[512,512]{1,0:T(8,128)(2,1)} %get-tuple-element.64.refs_0_), channel_id=1, source_target_pairs={{0,2},{1,4},{2,0},{3,6},{4,1},{5,7},{6,3},{7,5},{8,10},{9,12},{10,... | collective-permute-start | bytes 1572872 | tf_op jit(solution)/shard_map/ppermute | solution.py:503
  187.0 38.6 %collective-permute-start.13 = (bf16[512,512]{1,0:T(8,128)(2,1)}, bf16[512,512]{1,0:T(8,128)(2,1)S(1)}, u32[]{:S(2)}, u32[]{:S(2)}) collective-permute-start(bf16[512,512]{1,0:T(8,128)(2,1)} %get-tuple-element.65.refs_1_), channel_id=1, source_target_pairs={{0,3},{1,5},{2,1},{3,7},{4,0},{5,6},{6,2},{7,4},{8,11},{9,13},{10,... | collective-permute-start | bytes 1572872 | tf_op jit(solution)/shard_map/ppermute | solution.py:503
  191.5 37.3 %collective-permute-start.14 = (bf16[512,512]{1,0:T(8,128)(2,1)}, bf16[512,512]{1,0:T(8,128)(2,1)}, u32[]{:S(2)}, u32[]{:S(2)}) collective-permute-start(bf16[512,512]{1,0:T(8,128)(2,1)} %get-tuple-element.66.refs_2_), channel_id=1, source_target_pairs={{0,1},{1,7},{2,3},{3,5},{4,2},{5,4},{6,0},{7,6},{8,9},{9,15},{10,1... | collective-permute-start | bytes 1572872 | tf_op jit(solution)/shard_map/ppermute | solution.py:503
  199.2 31.5 %collective-permute-start.15 = (bf16[512,512]{1,0:T(8,128)(2,1)}, bf16[512,512]{1,0:T(8,128)(2,1)}, u32[]{:S(2)}, u32[]{:S(2)}) collective-permute-start(bf16[512,512]{1,0:T(8,128)(2,1)} %get-tuple-element.67.refs_3_), channel_id=1, source_target_pairs={{0,0},{1,6},{2,2},{3,4},{4,3},{5,5},{6,1},{7,7},{8,8},{9,14},{10,1... | collective-permute-start | bytes 1572872 | tf_op jit(solution)/shard_map/ppermute | solution.py:503
  224.1 13.2 %copy-start.7 = (bf16[512,512]{1,0:T(8,128)(2,1)}, bf16[512,512]{1,0:T(8,128)(2,1)S(1)}, u32[]{:S(2)}) copy-start(bf16[512,512]{1,0:T(8,128)(2,1)S(1)} %collective-permute-done.12.refs_0_) | copy-start | bytes 1572868
  224.1 18.6 %collective-permute-start.18 = (bf16[512,512]{1,0:T(8,128)(2,1)}, bf16[512,512]{1,0:T(8,128)(2,1)S(1)}, u32[]{:S(2)}, u32[]{:S(2)}) collective-permute-start(bf16[512,512]{1,0:T(8,128)(2,1)} %get-tuple-element.71), channel_id=1, source_target_pairs={{0,2},{1,4},{2,0},{3,6},{4,1},{5,7},{6,3},{7,5},{8,10},{9,12},{10,... | collective-permute-start | bytes 1572872 | tf_op jit(solution)/shard_map/ppermute | solution.py:503
  225.7 11.6 %copy-start.8 = (bf16[512,512]{1,0:T(8,128)(2,1)}, bf16[512,512]{1,0:T(8,128)(2,1)S(1)}, u32[]{:S(2)}) copy-start(bf16[512,512]{1,0:T(8,128)(2,1)S(1)} %collective-permute-done.13.refs_1_) | copy-start | bytes 1572868
  225.7 22.1 %collective-permute-start.19 = (bf16[512,512]{1,0:T(8,128)(2,1)}, bf16[512,512]{1,0:T(8,128)(2,1)}, u32[]{:S(2)}, u32[]{:S(2)}) collective-permute-start(bf16[512,512]{1,0:T(8,128)(2,1)} %get-tuple-element.72), channel_id=1, source_target_pairs={{0,3},{1,5},{2,1},{3,7},{4,0},{5,6},{6,2},{7,4},{8,11},{9,13},{10,... | collective-permute-start | bytes 1572872 | tf_op jit(solution)/shard_map/ppermute | solution.py:503
  228.8 19.0 %collective-permute-start.20 = (bf16[512,512]{1,0:T(8,128)(2,1)}, bf16[512,512]{1,0:T(8,128)(2,1)}, u32[]{:S(2)}, u32[]{:S(2)}) collective-permute-start(bf16[512,512]{1,0:T(8,128)(2,1)} %get-tuple-element.73), channel_id=1, source_target_pairs={{0,1},{1,7},{2,3},{3,5},{4,2},{5,4},{6,0},{7,6},{8,9},{9,15},{10,1... | collective-permute-start | bytes 1572872 | tf_op jit(solution)/shard_map/ppermute | solution.py:503
  230.7 17.1 %collective-permute-start.21 = (bf16[512,512]{1,0:T(8,128)(2,1)}, bf16[512,512]{1,0:T(8,128)(2,1)}, u32[]{:S(2)}, u32[]{:S(2)}) collective-permute-start(bf16[512,512]{1,0:T(8,128)(2,1)} %get-tuple-element.74), channel_id=1, source_target_pairs={{0,0},{1,6},{2,2},{3,4},{4,3},{5,5},{6,1},{7,7},{8,8},{9,14},{10,1... | collective-permute-start | bytes 1572872 | tf_op jit(solution)/shard_map/ppermute | solution.py:503
  242.7 5.1 %copy-start.9 = (bf16[512,512]{1,0:T(8,128)(2,1)}, bf16[512,512]{1,0:T(8,128)(2,1)S(1)}, u32[]{:S(2)}) copy-start(bf16[512,512]{1,0:T(8,128)(2,1)S(1)} %collective-permute-done.18.refs_4_) | copy-start | bytes 1572868
  288.2 27.5 %collective-permute-start.23 = (bf16[1024,1024]{1,0:T(8,128)(2,1)}, bf16[1024,1024]{1,0:T(8,128)(2,1)S(1)}, u32[]{:S(2)}, u32[]{:S(2)}) collective-permute-start(bf16[1024,1024]{1,0:T(8,128)(2,1)} %all-reduce.3.cloned.1.call-done), channel_id=1, source_target_pairs={{5,1},{7,3},{0,4},{2,6},{13,9},{15,11},{8,12},{10,14},{21,17},{23,... | collective-permute-start | bytes 6291464 | tf_op jit(solution)/shard_map/ppermute | solution.py:503
Sparse Core Ops, SparseCore 0:
  110.5 54.7 all-gather.2
Sparse Core Ops, SparseCore 1:
  219.2 68.9 all-reduce.2

commit v8 on v7

--- a/solution.py
+++ b/solution.py
@@ -196,7 +196,7 @@
 
 
 def call(kernel, out_shape, in_specs, out_specs, args, flops, scratch=(), transcendentals=0):
-    moved = sum(x.size * x.dtype.itemsize for x in (*args, *out_shape))
+    moved = sum(x.size * x.dtype.itemsize for x in (*args, *out_shape)) if flops else 0
     return pl.pallas_call(
         kernel,
         out_shape=tuple(out_shape),
@@ -313,30 +313,49 @@
     )[0]
 
 
+def halo_projection_kernel(weight, top, bot, kv_top, kv_bot):
+    for halo, out in ((top, kv_top), (bot, kv_bot)):
+        out[...] = nn(halo[...], weight[...]).astype(BF16)
+
+
+def halo_projections(weight, top, bot):
+    out = shape(top.shape[0], weight.shape[1])
+    return call(
+        halo_projection_kernel, [out, out], [VMEM] * 3, [VMEM] * 2, (weight, top, bot),
+        flops=4 * top.shape[0] * weight.size,
+    )
+
+
 def join_kernel(steps, order, own, above, below, *refs):
-    parts, (whole, sems) = refs[:steps], refs[steps:]
-    chunk = parts[0].shape[0]
+    outq_parts, parts, (whole, sems) = refs[:steps], refs[steps:2 * steps], refs[2 * steps:]
+    chunk, feats = outq_parts[0].shape
+    moves = [
+        pltpu.make_async_copy(outq, part.at[:, pl.ds(0, feats)], sems.at[steps + i])
+        for i, (outq, part) in enumerate(zip(outq_parts, parts))
+    ]
+    for move in moves:
+        move.start()
     low, high = (BAND_ROWS - HALO) * LONGITUDES, HALO * LONGITUDES
     whole[:low] = (own[:low] + below[:low].astype(F32)).astype(BF16)
     whole[low:high] = (own[low:high] + below[low:].astype(F32) + above[:high - low].astype(F32)).astype(BF16)
     whole[high:] = (own[high:] + above[high - low:].astype(F32)).astype(BF16)
-    moves = [
-        pltpu.make_async_copy(whole.at[pl.ds(pl.multiple_of(order[i], 16), chunk)], part, sems.at[i])
+    carry_out([
+        pltpu.make_async_copy(
+            whole.at[pl.ds(pl.multiple_of(order[i], 16), chunk)], part.at[:, pl.ds(feats, feats)], sems.at[i]
+        )
         for i, part in enumerate(parts)
-    ]
-    for move in moves:
-        move.start()
+    ])
     for move in moves:
         move.wait()
 
 
-def joined(order, own, above, below, steps):
-    band, feats = own.shape
+def joined(order, own, above, below, outq_parts):
+    steps, (chunk, feats) = len(outq_parts), outq_parts[0].shape
     return call(
         functools.partial(join_kernel, steps),
-        [shape(band // steps, feats)] * steps,
-        [SMEM] + [VMEM] * 3, [HBM] * steps, (order, own, above, below), flops=2 * own.size,
-        scratch=[pltpu.VMEM((band, feats), BF16), pltpu.SemaphoreType.DMA((steps,))],
+        [shape(chunk, 2 * feats)] * steps,
+        [SMEM] + [VMEM] * 3 + [HBM] * steps, [HBM] * steps, (order, own, above, below, *outq_parts), flops=0,
+        scratch=[pltpu.VMEM((steps * chunk, feats), BF16), pltpu.SemaphoreType.DMA((2 * steps,))],
     )
 
 
@@ -384,46 +403,20 @@
     )[0]
 
 
-def update_kernel(steps, leads, *refs):
-    parts, blocks, (out, left, right, sems) = refs[:steps], refs[steps:2 * steps], refs[2 * steps:]
-    feats = right.shape[0] // steps
+def token_kernel(steps, leads, tokens, gain, *refs):
+    parts, blocks, (update, grad, left, qkv, out, sems) = refs[:steps], refs[steps:2 * steps], refs[2 * steps:]
+    feats = out.shape[0] // steps
     carry_out([
-        pltpu.make_async_copy(block.at[pl.ds(3 * feats, feats)], right.at[pl.ds(i * feats, feats)], sems.at[i])
-        for i, block in enumerate(blocks)
+        move for i, block in enumerate(blocks) for move in (
+            pltpu.make_async_copy(block.at[pl.ds(0, 3 * feats)], qkv.at[pl.ds(3 * i * feats, 3 * feats)], sems.at[i]),
+            pltpu.make_async_copy(block.at[pl.ds(3 * feats, feats)], out.at[pl.ds(i * feats, feats)], sems.at[steps + i]),
+        )
     ])
     for i, part in enumerate(parts):
-        left[leads[i]] = part[:, :feats]
-    out[...] = nn(jnp.concatenate([left[i] for i in range(steps)], axis=1), right[...]).astype(BF16)
-
-
-def updates(leads, outq_own, blocks):
-    steps, (rows, width), chunk = len(blocks), blocks[0].shape, outq_own[0].shape[0]
-    return call(
-        functools.partial(update_kernel, steps),
-        [shape(chunk, width)], [SMEM] + [VMEM] * steps + [HBM] * steps, [VMEM], (leads, *outq_own, *blocks),
-        flops=steps * chunk * rows * width // 2,
-        scratch=[
-            pltpu.VMEM((steps, chunk, rows // 4), BF16),
-            pltpu.VMEM((steps * rows // 4, width), BF16),
-            pltpu.SemaphoreType.DMA((steps,)),
-        ],
-    )[0]
-
-
-def grad_input_kernel(steps, leads, tokens, gain, *refs):
-    outq, dkv, blocks, (grad, left, right, sems) = (
-        refs[:steps], refs[steps:2 * steps], refs[2 * steps:3 * steps], refs[3 * steps:]
-    )
-    rows = right.shape[0] // steps
-    feats = rows // 3
-    carry_out([
-        pltpu.make_async_copy(block.at[pl.ds(0, rows)], right.at[pl.ds(i * rows, rows)], sems.at[i])
-        for i, block in enumerate(blocks)
-    ])
-    for i in range(steps):
-        left[leads[i], :, :feats] = outq[i][:, feats:]
-        left[leads[i], :, feats:] = dkv[i][...]
-    grad_normed = nn(jnp.concatenate([left[i] for i in range(steps)], axis=1), right[...])
+        left[leads[i]] = part[...]
+    side_by_side = lambda cut: jnp.concatenate([left[i, :, cut] for i in range(steps)], axis=1)
+    update[...] = nn(side_by_side(slice(0, feats)), out[...]).astype(BF16)
+    grad_normed = nn(side_by_side(slice(feats, None)), qkv[...])
     features = tokens[...].astype(F32)
     inverse = lax.rsqrt(jnp.mean(features * features, axis=1, keepdims=True) + 1e-06)
     centred = features * inverse
@@ -431,20 +424,42 @@
     grad[...] = (inverse * (scaled - centred * jnp.mean(scaled * centred, axis=1, keepdims=True))).astype(BF16)
 
 
-def grad_inputs(leads, tokens, gain, outq_own, dkv_own, blocks):
+def token_outputs(leads, tokens, gain, parts, blocks):
     steps, (rows, width), chunk = len(blocks), blocks[0].shape, tokens.shape[0]
-    rows = rows * 3 // 4
-    return call(
-        functools.partial(grad_input_kernel, steps),
-        [shape(*tokens.shape)], [SMEM] + [VMEM] * (2 + 2 * steps) + [HBM] * steps, [VMEM],
-        (leads, tokens, gain[None, :], *outq_own, *dkv_own, *blocks),
-        flops=2 * steps * chunk * rows * width,
+    feats = rows // 4
+    return call(
+        functools.partial(token_kernel, steps),
+        [shape(chunk, width)] * 2, [SMEM] + [VMEM] * (2 + steps) + [HBM] * steps, [VMEM] * 2,
+        (leads, tokens, gain[None, :], *parts, *blocks), flops=2 * steps * chunk * rows * width,
         scratch=[
             pltpu.VMEM((steps, chunk, rows), BF16),
-            pltpu.VMEM((steps * rows, width), BF16),
-            pltpu.SemaphoreType.DMA((steps,)),
+            pltpu.VMEM((3 * steps * feats, width), BF16),
+            pltpu.VMEM((steps * feats, width), BF16),
+            pltpu.SemaphoreType.DMA((2 * steps,)),
         ],
-    )[0]
+    )
+
+
+def finish_kernel(scale, flag, mine, other, grad_qkv, grad_out):
+    heads = grad_out.shape[0]
+    for h in range(heads):
+        for i in range(4):
+            at = pl.ds((i * heads + h) * HEAD_WIDTH, HEAD_WIDTH)
+            part = jnp.where(flag[0] == 1, mine[at, :], other[at, :]).astype(F32)
+            if i == 0:
+                grad_out[h] = part * scale
+            else:
+                factor = scale * HEAD_WIDTH ** -0.5 if i == 1 else scale
+                grad_qkv[h, (i - 1) * HEAD_WIDTH:i * HEAD_WIDTH, :] = part * factor
+
+
+def finished(scale, flag, mine, other):
+    heads, width = mine.shape[0] // (4 * HEAD_WIDTH), mine.shape[1]
+    return call(
+        functools.partial(finish_kernel, scale),
+        [jax.ShapeDtypeStruct((heads, 3 * HEAD_WIDTH, width), F32), jax.ShapeDtypeStruct((heads, HEAD_WIDTH, width), F32)],
+        [SMEM, VMEM, VMEM], [VMEM] * 2, (flag, mine, other), flops=mine.size,
+    )
 
 
 from jax.sharding import Mesh, PartitionSpec as P
@@ -552,31 +567,27 @@
     qkv = projections(order, group_qkv, normed_parts)
     shares = [from_ahead(after(held, qkv), dm) for dm in range(1, halves)]
     upstream_parts, _ = gathered(after(upstream, *normed_parts), qkv)
-    kv_top, kv_bot = (nn(x, group_qkv[:, feats:]).astype(BF16) for x in normed_halos)
-    order, kv_top, kv_bot, *shares = lax.optimization_barrier((order, kv_top, kv_bot, *shares))
+    kv_top, kv_bot = halo_projections(group_qkv[:, feats:], *normed_halos)
+    kv_top, kv_bot, *upstream_parts = lax.optimization_barrier((kv_top, kv_bot, *upstream_parts))
+    order, *shares = lax.optimization_barrier((order, *shares))
     ahead = [lax.all_gather(part, "z") for part in shares]
     outq_parts, dkv, dkv_top, dkv_bot = attention(cells, order, qkv, kv_top, kv_bot, group_out, upstream_parts)
 
-    ahead = [after(block, dkv_top) for block in ahead]
+    from_above, from_below = passed_along(dkv_top, -1), passed_along(dkv_bot, 1)
+    grads = weight_grads(
+        after(order, ahead), outq_parts, upstream_parts, normed_parts, dkv, (dkv_top, dkv_bot), normed_halos
+    )
+    grads_sum = lax.psum(grads, ("z", "c"))
+    parts = joined(after(order, grads), dkv, from_above, from_below, outq_parts)
+    parts, ahead = lax.optimization_barrier((parts, ahead))
+    parts_own = send_back(parts)
     ahead = [split(block[:, :rows[0]], block[:, rows[0]:]) for block in ahead]
     blocks += ahead + [sibling] + [from_sibling(block) for block in ahead]
-    from_above, from_below = passed_along(dkv_top, -1), passed_along(dkv_bot, 1)
-    outq_own = send_back(outq_parts)
-
-    grads = weight_grads(order, outq_parts, upstream_parts, normed_parts, dkv, (dkv_top, dkv_bot), normed_halos)
-    grads = lax.psum(grads, ("z", "c"))
-    dkv_parts = joined(order, dkv, from_above, from_below, len(slots))
-    dkv_own = send_back(dkv_parts)
-    update = updates(leads, outq_own, blocks)
-    grad_input = grad_inputs(leads, tokens, gain, outq_own, dkv_own, blocks)
-    grads, grad_input, update = lax.optimization_barrier((grads, grad_input, update))
+    update, grad_input = token_outputs(leads, tokens, gain, parts_own, blocks)
+    grads = after(grads_sum, *parts_own)
     pairs = [((1 - y, m, 1 - y), (y, m, 1 - y)) for y in range(2) for m in range(halves)]
-    grads = jnp.where(c == y, grads, permuted(grads, pairs)).astype(F32) * grad_scale
-    early, late = grads[:2 * feats], grads[2 * feats:]
-    by_head = lambda x: x.reshape(heads, HEAD_WIDTH, WIDTH)
-    grad_out = by_head(early[:feats])
-    grad_query = early[feats:] * HEAD_WIDTH ** -0.5
-    grad_qkv = jnp.concatenate([by_head(grad_query), by_head(late[:feats]), by_head(late[feats:])], axis=1)
+    flag = after(jnp.reshape(c == y, (1,)).astype(jnp.int32), grad_input, update)
+    grad_qkv, grad_out = finished(grad_scale, flag, grads, permuted(grads, pairs))
     return update, grad_input, grad_qkv, grad_out
 
 

time: 330 us -> 363 us (1.10)
  Pallas kernels: 94.7 us -> 166 us
  starting transfers between devices: 71.2 us -> 60.4 us
  matrix products: 9.78 us -> 0 us
  waiting for transfers between devices: 108 us -> 98.7 us
  other arithmetic: 18.3 us -> 10.1 us
    pallas_call x8 -> x9, Pallas kernels: 94.7 us -> 166 us  [call(): pl.pallas_call(kernel, out_shape=tuple(out_shape), in_specs=list(in_specs...]
    psum x1, waiting for transfers between devices: 30.1 us -> 0.02 us  [on_device(): grads_sum = lax.psum(grads, ('z', 'c'))]
    ppermute x1, waiting for transfers between devices: 0.01 us -> 14.3 us  [from_ahead(): return lax.ppermute(x, 'm', [((i + dm) % halves, i) for i in range(halves)])]
    dot_general x2 -> x0, matrix products: 9.78 us -> none  [nn(): lax.dot_general(a, b, (((1,), (0,)), ((), ())), preferred_element_type=jn...]
    ppermute x17 -> x13, starting transfers between devices: 47.2 us -> 38.1 us  [permuted(): return lax.ppermute(x, GROUP, [(at(*a), at(*b)) for a, b in pairs])]
    ppermute x17 -> x13, waiting for transfers between devices: 77.9 us -> 84.3 us  [permuted(): return lax.ppermute(x, GROUP, [(at(*a), at(*b)) for a, b in pairs])]
  transfers between devices with their start and end apart: 26 -> 22, of which waited for: 9 -> 9; matrix products, arithmetic and copies ran while one was open for 9% -> 4% of each run, Pallas kernels for 27% -> 43%
where the time goes in v8:
time: 363 us; the launch traced here: 362 us
  Pallas kernels  166 us (46%)
  waiting for transfers between devices  98.7 us (27%)
  starting transfers between devices  60.4 us (17%)
  between operations  14.3 us (4%)
  local copies, waits for them, and re-layouts  12.2 us (3%)
  other arithmetic  10.1 us (3%)
    pallas_call x9, Pallas kernels, call(): pl.pallas_call(kernel, out_shape=tuple(out_shape), in_specs=list(in_specs...  166 us
    ppermute x13, waiting for transfers between devices, permuted(): return lax.ppermute(x, GROUP, [(at(*a), at(*b)) for a, b in pairs])  84.3 us
    ppermute x13, starting transfers between devices, permuted(): return lax.ppermute(x, GROUP, [(at(*a), at(*b)) for a, b in pairs])  38.1 us
    ppermute x4, starting transfers between devices, passed_along(): return lax.ppermute(x, ('z', 'c'), pairs)  20.9 us
    ppermute x1, waiting for transfers between devices, from_ahead(): return lax.ppermute(x, 'm', [((i + dm) % halves, i) for i in range(halves)])  14.3 us
  transfers between devices with their start and end apart: 22, of which 9 were waited for; matrix products, arithmetic and copies ran while one was open for 4% of the time, Pallas kernels for 43%

profile of v8, /device:TPU:0, one launch (start us, length us, event | category | flops | bytes accessed | tf_op | source)
XLA Modules:
  0.0 361.6 jit_solution(10533438773385344678)
XLA Ops:
  7.2 1.6 copy_multiply_fusion.1
  8.9 1.5 pad_maximum_fusion.refs_4_
  10.8 2.6 shard_map.129
  13.4 2.5 collective-permute-start
  16.0 23.3 %collective-permute-done.refs_0_.refs_8_ = bf16[512,1024]{1,0:T(8,128)(2,1)S(1)} collective-permute-done((bf16[512,1024]{1,0:T(8,128)(2,1)}, bf16[512,1024]{1,0:T(8,128)(2,1)S(1)}, u32[]{:S(2)}, u32[]{:S(2)}) %collective-permute-start) | collective-permute-done | bytes 1048608 | tf_op jit(solution)/shard_map/ppermute | solution.py:518
  39.3 1.0 collective-permute-done.1.refs_1_.refs_9_
  40.3 1.1 broadcast_select_fusion.4
  41.3 2.7 collective-permute-start.2
  44.0 1.7 collective-permute-start.3
  45.7 1.3 fusion.1.order
  47.0 1.0 broadcast_select_fusion
  48.9 7.7 %collective-permute-done.2.refs_2_.refs_10_ = bf16[512,1024]{1,0:T(8,128)(2,1)} collective-permute-done((bf16[512,1024]{1,0:T(8,128)(2,1)}, bf16[512,1024]{1,0:T(8,128)(2,1)}, u32[]{:S(2)}, u32[]{:S(2)}) %collective-permute-start.2) | collective-permute-done | bytes 1048608 | tf_op jit(solution)/shard_map/ppermute | solution.py:518
  56.7 1.1 broadcast_select_fusion.3.refs_3_.refs_11_
  57.8 5.7 %shard_map.131 = (bf16[1536,1024]{1,0:T(8,128)(2,1)}, bf16[1536,1024]{1,0:T(8,128)(2,1)}) custom-call(s32[4]{0:T(128)} %fusion.1.order, bf16[512,1024]{1,0:T(8,128)(2,1)} %copy-done.1, bf16[512,1024]{1,0:T(8,128)(2,1)} %collective-permute-done.1.refs_1_.refs_9_, bf16[512,1024]{1,0:T(8,128)(2,1)} %collective-permute-done.2.refs_2_.refs_10_, ...), custom_call_target="tpu_custom_call" | custom-call | tf_op jit(solution)/shard_map/pallas_call | solution.py:200
  63.5 6.5 %collective-permute-start.6 = (bf16[1536,1024]{1,0:T(8,128)(2,1)}, bf16[1536,1024]{1,0:T(8,128)(2,1)}, u32[]{:S(2)}, u32[]{:S(2)}) collective-permute-start(bf16[1536,1024]{1,0:T(8,128)(2,1)} %get-tuple-element.70), channel_id=1, source_target_pairs={{0,1},{1,8},{8,9},{9,16},{16,17},{17,24},{24,25},{2,3},{3,10},{10,... | collective-permute-start | bytes 9437192 | tf_op jit(solution)/shard_map/ppermute | solution.py:487
  70.0 1.3 collective-permute-start.7
  71.3 1.8 collective-permute-start.8
  73.1 1.0 collective-permute-start.9
  74.1 1.0 constant_dynamic-slice_fusion.1
  75.2 1.6 copy.15.weight
  76.8 8.8 %shard_map.130.qkv = bf16[2048,768]{1,0:T(8,128)(2,1)} custom-call(s32[4]{0:T(128)} %fusion.1.order, bf16[1024,768]{1,0:T(8,128)(2,1)} %copy.15.weight, bf16[512,1024]{1,0:T(8,128)(2,1)} %copy-done.1, bf16[512,1024]{1,0:T(8,128)(2,1)} %collective-permute-done.1.refs_1_.refs_9_, bf16[512,1024]{1,0:T(8,128)(2,1)} %collective-permute-done.2.refs_2_.refs_10_, ...), custom_call_target="tpu_custom_call" | custom-call | flops 3221225472 | bytes 8912912 | tf_op jit(solution)/shard_map/pallas_call | solution.py:200
  85.6 10.8 %collective-permute-done.8.refs_0_.refs_4_ = bf16[512,1024]{1,0:T(8,128)(2,1)} collective-permute-done((bf16[512,1024]{1,0:T(8,128)(2,1)S(1)}, bf16[512,1024]{1,0:T(8,128)(2,1)}, u32[]{:S(2)}, u32[]{:S(2)}) %collective-permute-start.8) | collective-permute-done | bytes 1048608 | tf_op jit(solution)/shard_map/ppermute | solution.py:518
  96.4 1.1 collective-permute-done.9.refs_1_.refs_5_
  97.5 1.7 collective-permute-start.11
  99.2 2.3 broadcast_select_fusion.2
  101.5 1.7 collective-permute-start.10
  103.9 14.3 %collective-permute-done.5 = bf16[256,1024]{1,0:T(8,128)(2,1)S(1)} collective-permute-done((bf16[256,1024]{1,0:T(8,128)(2,1)S(1)}, bf16[256,1024]{1,0:T(8,128)(2,1)S(1)}, u32[]{:S(2)}, u32[]{:S(2)}) %collective-permute-start.5) | collective-permute-done | bytes 524320 | tf_op jit(solution)/shard_map/ppermute | solution.py:542
  119.9 1.0 slice.17
  121.0 2.3 copy.16.weight
  123.3 1.1 broadcast_select_fusion.1.refs_3_.refs_7_
  124.4 7.8 %shard_map.132 = (bf16[1536,512]{1,0:T(8,128)(2,1)}, bf16[1536,512]{1,0:T(8,128)(2,1)}) custom-call(bf16[1024,512]{1,0:T(8,128)(2,1)} %copy.16.weight, bf16[1536,1024]{1,0:T(8,128)(2,1)} %collective-permute-done.6.top.refs_15_, bf16[1536,1024]{1,0:T(8,128)(2,1)} %collective-permute-done.7.bot.refs_16_), custom_call_target="tpu_custom_call" | custom-call | flops 3221225472 | bytes 10485760 | tf_op jit(solution)/shard_map/pallas_call | solution.py:200
  132.1 42.1 %shard_map.133 = (bf16[512,512]{1,0:T(8,128)(2,1)}, bf16[512,512]{1,0:T(8,128)(2,1)}, bf16[512,512]{1,0:T(8,128)(2,1)}, bf16[512,512]{1,0:T(8,128)(2,1)}, f32[20...) custom-call(s32[20]{0:T(128)} %pad_dynamic-slice_fusion.cells, s32[4]{0:T(128)} %fusion.1.order, ...), custom_call_target="tpu_custom_call" | custom-call | flops 13958643712 | bytes 20447328 | tf_op jit(solution)/shard_map/pallas_call | solution.py:200
  174.2 1.3 collective-permute-start.12
  175.5 11.8 %collective-permute-start.13 = (bf16[1536,512]{1,0:T(8,128)(2,1)}, bf16[1536,512]{1,0:T(8,128)(2,1)}, u32[]{:S(2)}, u32[]{:S(2)}) collective-permute-start(bf16[1536,512]{1,0:T(8,128)(2,1)} %get-tuple-element.93.refs_14_), channel_id=1, source_target_pairs={{0,1},{1,8},{8,9},{9,16},{16,17},{17,24},{24,25},{2,3},{3,10},{10,... | collective-permute-start | bytes 4718600 | tf_op jit(solution)/shard_map/ppermute | solution.py:487
  187.3 14.5 %shard_map.134 = bf16[1024,1024]{1,0:T(8,128)(2,1)} custom-call(s32[4]{0:T(128)} %fusion.1.order, bf16[512,512]{1,0:T(8,128)(2,1)} %get-tuple-element.87.refs_0_, bf16[512,512]{1,0:T(8,128)(2,1)} %get-tuple-element.88.refs_1_, bf16[512,512]{1,0:T(8,128)(2,1)} %get-tuple-element.89.refs_2_, bf16[512,512]{1,0:T(8,128)(2,1)} %get-tuple-element.90.refs_3_, ...), custom_call_target="tpu_custom_call" | custom-call | flops 7516192768 | bytes 26214416 | tf_op jit(solution)/shard_map/pallas_call | solution.py:200
  201.9 1.1 copy-done.6
  203.0 67.8 %shard_map.135 = (bf16[512,1024]{1,0:T(8,128)(2,1)}, bf16[512,1024]{1,0:T(8,128)(2,1)}, bf16[512,1024]{1,0:T(8,128)(2,1)}, bf16[512,1024]{1,0:T(8,128)(2,1)}) custom-call(s32[4]{0:T(128)} %fusion.1.order, f32[2048,512]{1,0:T(8,128)} %get-tuple-element.91.refs_12_.own, bf16[1536,512]{1,0:T(8,128)(2,1)} %copy-done.6, ...), custom_call_target="tpu_custom_call" | custom-call | tf_op jit(solution)/shard_map/pallas_call | solution.py:200
  270.9 1.8 collective-permute-start.14
  272.6 2.2 collective-permute-start.15
  274.9 3.1 collective-permute-start.16
  277.9 9.4 %collective-permute-start.17 = (bf16[512,1024]{1,0:T(8,128)(2,1)}, bf16[512,1024]{1,0:T(8,128)(2,1)}, u32[]{:S(2)}, u32[]{:S(2)}) collective-permute-start(bf16[512,1024]{1,0:T(8,128)(2,1)} %get-tuple-element.102), channel_id=1, source_target_pairs={{0,0},{1,6},{2,2},{3,4},{4,3},{5,5},{6,1},{7,7},{8,8},{9,14},{10,1... | collective-permute-start | bytes 3145736 | tf_op jit(solution)/shard_map/ppermute | solution.py:518
  288.0 3.8 %collective-permute-done.14.refs_0_ = bf16[512,1024]{1,0:T(8,128)(2,1)S(1)} collective-permute-done((bf16[512,1024]{1,0:T(8,128)(2,1)}, bf16[512,1024]{1,0:T(8,128)(2,1)S(1)}, u32[]{:S(2)}, u32[]{:S(2)}) %collective-permute-start.14) | collective-permute-done | bytes 1048608 | tf_op jit(solution)/shard_map/ppermute | solution.py:518
  291.9 27.3 %collective-permute-done.15.refs_1_ = bf16[512,1024]{1,0:T(8,128)(2,1)} collective-permute-done((bf16[512,1024]{1,0:T(8,128)(2,1)}, bf16[512,1024]{1,0:T(8,128)(2,1)}, u32[]{:S(2)}, u32[]{:S(2)}) %collective-permute-start.15) | collective-permute-done | bytes 1048608 | tf_op jit(solution)/shard_map/ppermute | solution.py:518
  319.2 8.5 %collective-permute-start.19 = (bf16[1024,1024]{1,0:T(8,128)(2,1)}, bf16[1024,1024]{1,0:T(8,128)(2,1)}, u32[]{:S(2)}, u32[]{:S(2)}) collective-permute-start(bf16[1024,1024]{1,0:T(8,128)(2,1)} %all-reduce.3.cloned.1.call-done.mine), channel_id=1, source_target_pairs={{5,1},{7,3},{0,4},{2,6},{13,9},{15,11},{8,12},{10,14},{21,17},{23,... | collective-permute-start | bytes 6291464 | tf_op jit(solution)/shard_map/ppermute | solution.py:518
  327.7 1.3 fusion.leads
  329.0 12.0 %shard_map.136 = (bf16[512,1024]{1,0:T(8,128)(2,1)}, bf16[512,1024]{1,0:T(8,128)(2,1)}) custom-call(s32[4]{0:T(128)} %fusion.leads, bf16[512,1024]{1,0:T(8,128)(2,1)} %tokens.3, f32[1,1024]{1,0:T(1,128)} %bitcast.33, bf16[512,1024]{1,0:T(8,128)(2,1)} %copy-done.9, bf16[512,1024]{1,0:T(8,128)(2,1)} %collective-permute-done.15.refs_1_, ...), custom_call_target="tpu_custom_call" | custom-call | flops 4294967296 | bytes 15732752 | tf_op jit(solution)/shard_map/pallas_call | solution.py:200
  341.0 9.2 %collective-permute-done.19.other = bf16[1024,1024]{1,0:T(8,128)(2,1)} collective-permute-done((bf16[1024,1024]{1,0:T(8,128)(2,1)}, bf16[1024,1024]{1,0:T(8,128)(2,1)}, u32[]{:S(2)}, u32[]{:S(2)}) %collective-permute-start.19) | collective-permute-done | bytes 2097184 | tf_op jit(solution)/shard_map/ppermute | solution.py:518
  350.3 4.5 %shard_map.137 = (f32[4,192,1024]{2,1,0:T(8,128)}, f32[4,64,1024]{2,1,0:T(8,128)}) custom-call(s32[1]{0:T(128)} %bitcast.14.flag, bf16[1024,1024]{1,0:T(8,128)(2,1)} %all-reduce.3.cloned.1.call-done.mine, bf16[1024,1024]{1,0:T(8,128)(2,1)} %collective-permute-done.19.other), custom_call_target="tpu_custom_call" | custom-call | flops 1048576 | bytes 8388612 | tf_op jit(solution)/shard_map/pallas_call | solution.py:200
  (51 shorter events, 4.5 us)
Async XLA Ops:
  7.2 1.7 copy-start.3
  7.2 180.1 %all-gather.3.cloned.1.call-start = ((), (), s32[]{:S(2)}) async-start(), calls=%async_computation.1 | async-start | bytes 2621440 | tf_op jit(solution)/shard_map/all_gather | solution.py:573
  10.4 36.6 %collective-permute-start.4 = (bf16[1024,1024]{1,0:T(8,128)(2,1)}, bf16[1024,1024]{1,0:T(8,128)(2,1)}, u32[]{:S(2)}, u32[]{:S(2)}) collective-permute-start(bf16[1024,1024]{1,0:T(8,128)(2,1)} %pad_maximum_fusion.refs_4_), channel_id=1, source_target_pairs={{0,1},{1,0},{2,3},{3,2},{4,5},{5,4},{6,7},{7,6},{8,9},{9,8},{10,11... | collective-permute-start | bytes 6291464 | tf_op jit(solution)/shard_map/ppermute | solution.py:545
  13.4 25.8 %collective-permute-start = (bf16[512,1024]{1,0:T(8,128)(2,1)}, bf16[512,1024]{1,0:T(8,128)(2,1)S(1)}, u32[]{:S(2)}, u32[]{:S(2)}) collective-permute-start(bf16[512,1024]{1,0:T(8,128)(2,1)} %shard_map.129), channel_id=1, source_target_pairs={{2,0},{4,1},{0,2},{6,3},{1,4},{7,5},{3,6},{5,7},{10,8},{12,9},{8,1... | collective-permute-start | bytes 3145736 | tf_op jit(solution)/shard_map/ppermute | solution.py:518
  15.9 24.3 %collective-permute-start.1 = (bf16[512,1024]{1,0:T(8,128)(2,1)}, bf16[512,1024]{1,0:T(8,128)(2,1)}, u32[]{:S(2)}, u32[]{:S(2)}) collective-permute-start(bf16[512,1024]{1,0:T(8,128)(2,1)} %shard_map.129), channel_id=1, source_target_pairs={{3,0},{5,1},{1,2},{7,3},{0,4},{6,5},{2,6},{4,7},{11,8},{13,9},{9,1... | collective-permute-start | bytes 3145736 | tf_op jit(solution)/shard_map/ppermute | solution.py:518
  39.3 8.7 %copy-start.1 = (bf16[512,1024]{1,0:T(8,128)(2,1)}, bf16[512,1024]{1,0:T(8,128)(2,1)S(1)}, u32[]{:S(2)}) copy-start(bf16[512,1024]{1,0:T(8,128)(2,1)S(1)} %collective-permute-done.refs_0_.refs_8_) | copy-start | bytes 3145732
  41.3 15.3 %collective-permute-start.2 = (bf16[512,1024]{1,0:T(8,128)(2,1)}, bf16[512,1024]{1,0:T(8,128)(2,1)}, u32[]{:S(2)}, u32[]{:S(2)}) collective-permute-start(bf16[512,1024]{1,0:T(8,128)(2,1)} %broadcast_select_fusion.4), channel_id=1, source_target_pairs={{0,4},{1,0},{2,6},{3,2},{4,5},{5,1},{6,7},{7,3},{8,12},{9,8},{10,1... | collective-permute-start | bytes 3145736 | tf_op jit(solution)/shard_map/ppermute | solution.py:518
  44.0 12.6 %collective-permute-start.3 = (bf16[512,1024]{1,0:T(8,128)(2,1)S(1)}, bf16[512,1024]{1,0:T(8,128)(2,1)}, u32[]{:S(2)}, u32[]{:S(2)}) collective-permute-start(bf16[512,1024]{1,0:T(8,128)(2,1)S(1)} %collective-permute-done.refs_0_.refs_8_), channel_id=1, source_target_pairs={{1,3},{3,1},{4,6},{6,4},{9,11},{11,9},{12,14},{14,12},{17,19},{19,... | collective-permute-start | bytes 3145736 | tf_op jit(solution)/shard_map/ppermute | solution.py:518
  48.0 8.7 %copy-start = (bf16[512,1024]{1,0:T(8,128)(2,1)S(1)}, bf16[512,1024]{1,0:T(8,128)(2,1)}, u32[]{:S(2)}) copy-start(bf16[512,1024]{1,0:T(8,128)(2,1)} %shard_map.129) | copy-start | bytes 3145732
  57.8 13.5 %copy-start.2 = (bf16[512,1024]{1,0:T(8,128)(2,1)S(1)}, bf16[512,1024]{1,0:T(8,128)(2,1)}, u32[]{:S(2)}) copy-start(bf16[512,1024]{1,0:T(8,128)(2,1)} %param.15) | copy-start | bytes 3145732
  63.5 60.8 %collective-permute-start.6 = (bf16[1536,1024]{1,0:T(8,128)(2,1)}, bf16[1536,1024]{1,0:T(8,128)(2,1)}, u32[]{:S(2)}, u32[]{:S(2)}) collective-permute-start(bf16[1536,1024]{1,0:T(8,128)(2,1)} %get-tuple-element.70), channel_id=1, source_target_pairs={{0,1},{1,8},{8,9},{9,16},{16,17},{17,24},{24,25},{2,3},{3,10},{10,... | collective-permute-start | bytes 9437192 | tf_op jit(solution)/shard_map/ppermute | solution.py:487
  70.0 54.3 %collective-permute-start.7 = (bf16[1536,1024]{1,0:T(8,128)(2,1)}, bf16[1536,1024]{1,0:T(8,128)(2,1)}, u32[]{:S(2)}, u32[]{:S(2)}) collective-permute-start(bf16[1536,1024]{1,0:T(8,128)(2,1)} %get-tuple-element.71), channel_id=1, source_target_pairs={{1,0},{8,1},{9,8},{16,9},{17,16},{24,17},{25,24},{3,2},{10,3},{11,... | collective-permute-start | bytes 9437192 | tf_op jit(solution)/shard_map/ppermute | solution.py:487
  71.3 25.1 %collective-permute-start.8 = (bf16[512,1024]{1,0:T(8,128)(2,1)S(1)}, bf16[512,1024]{1,0:T(8,128)(2,1)}, u32[]{:S(2)}, u32[]{:S(2)}) collective-permute-start(bf16[512,1024]{1,0:T(8,128)(2,1)S(1)} %copy-done.2), channel_id=1, source_target_pairs={{2,0},{4,1},{0,2},{6,3},{1,4},{7,5},{3,6},{5,7},{10,8},{12,9},{8,1... | collective-permute-start | bytes 3145736 | tf_op jit(solution)/shard_map/ppermute | solution.py:518
  73.1 24.4 %collective-permute-start.9 = (bf16[512,1024]{1,0:T(8,128)(2,1)S(1)}, bf16[512,1024]{1,0:T(8,128)(2,1)}, u32[]{:S(2)}, u32[]{:S(2)}) collective-permute-start(bf16[512,1024]{1,0:T(8,128)(2,1)S(1)} %copy-done.2), channel_id=1, source_target_pairs={{3,0},{5,1},{1,2},{7,3},{0,4},{6,5},{2,6},{4,7},{11,8},{13,9},{9,1... | collective-permute-start | bytes 3145736 | tf_op jit(solution)/shard_map/ppermute | solution.py:518
  85.6 33.7 %copy-start.10 = (s32[64]{0:T(128)S(1)}, s32[64]{0:T(128)}, u32[]{:S(2)}) copy-start(s32[64]{0:T(128)} %param.14) | copy-start | bytes 772
  97.5 25.7 %collective-permute-start.11 = (bf16[512,1024]{1,0:T(8,128)(2,1)}, bf16[512,1024]{1,0:T(8,128)(2,1)}, u32[]{:S(2)}, u32[]{:S(2)}) collective-permute-start(bf16[512,1024]{1,0:T(8,128)(2,1)} %collective-permute-done.8.refs_0_.refs_4_), channel_id=1, source_target_pairs={{1,3},{3,1},{4,6},{6,4},{9,11},{11,9},{12,14},{14,12},{17,19},{19,... | collective-permute-start | bytes 3145736 | tf_op jit(solution)/shard_map/ppermute | solution.py:518
  101.5 21.8 %collective-permute-start.10 = (bf16[512,1024]{1,0:T(8,128)(2,1)}, bf16[512,1024]{1,0:T(8,128)(2,1)}, u32[]{:S(2)}, u32[]{:S(2)}) collective-permute-start(bf16[512,1024]{1,0:T(8,128)(2,1)} %broadcast_select_fusion.2), channel_id=1, source_target_pairs={{0,4},{1,0},{2,6},{3,2},{4,5},{5,1},{6,7},{7,3},{8,12},{9,8},{10,1... | collective-permute-start | bytes 3145736 | tf_op jit(solution)/shard_map/ppermute | solution.py:518
  103.3 14.9 %collective-permute-start.5 = (bf16[256,1024]{1,0:T(8,128)(2,1)S(1)}, bf16[256,1024]{1,0:T(8,128)(2,1)S(1)}, u32[]{:S(2)}, u32[]{:S(2)}) collective-permute-start(bf16[256,1024]{1,0:T(8,128)(2,1)S(1)} %pad_maximum_fusion.2), channel_id=1, source_target_pairs={{2,0},{0,2},{3,1},{1,3},{6,4},{4,6},{7,5},{5,7},{10,8},{8,10},{11,... | collective-permute-start | bytes 1572872 | tf_op jit(solution)/shard_map/ppermute | solution.py:542
  118.2 0.8 copy-start.7
  119.0 169.0 %all-reduce.3.cloned.1.call-start = ((), (), s32[]{:S(2)}) async-start(), calls=%async_computation | async-start | bytes 4194304 | tf_op jit(solution)/shard_map/psum | solution.py:580
  174.2 27.6 %collective-permute-start.12 = (bf16[1536,512]{1,0:T(8,128)(2,1)}, bf16[1536,512]{1,0:T(8,128)(2,1)S(1)}, u32[]{:S(2)}, u32[]{:S(2)}) collective-permute-start(bf16[1536,512]{1,0:T(8,128)(2,1)} %get-tuple-element.92.refs_13_), channel_id=1, source_target_pairs={{1,0},{8,1},{9,8},{16,9},{17,16},{24,17},{25,24},{3,2},{10,3},{11,... | collective-permute-start | bytes 4718600 | tf_op jit(solution)/shard_map/ppermute | solution.py:487
  175.5 26.3 %collective-permute-start.13 = (bf16[1536,512]{1,0:T(8,128)(2,1)}, bf16[1536,512]{1,0:T(8,128)(2,1)}, u32[]{:S(2)}, u32[]{:S(2)}) collective-permute-start(bf16[1536,512]{1,0:T(8,128)(2,1)} %get-tuple-element.93.refs_14_), channel_id=1, source_target_pairs={{0,1},{1,8},{8,9},{9,16},{16,17},{17,24},{24,25},{2,3},{3,10},{10,... | collective-permute-start | bytes 4718600 | tf_op jit(solution)/shard_map/ppermute | solution.py:487
  201.8 85.5 %copy-start.4 = (bf16[1024,1024]{1,0:T(8,128)(2,1)S(1)}, bf16[1024,1024]{1,0:T(8,128)(2,1)}, u32[]{:S(2)}) copy-start(bf16[1024,1024]{1,0:T(8,128)(2,1)} %all-gather.3.cloned.1.call-done) | copy-start | bytes 6291460
  201.9 1.1 copy-start.6
  270.9 16.7 %copy-start.8 = (bf16[3]{0:T(256)(128)(2,1)S(1)}, bf16[3]{0:T(256)(128)(2,1)}, u32[]{:S(2)}) copy-start(bf16[3]{0:T(256)(128)(2,1)} %constant.38.clone) | copy-start | bytes 22
  270.9 21.0 %collective-permute-start.14 = (bf16[512,1024]{1,0:T(8,128)(2,1)}, bf16[512,1024]{1,0:T(8,128)(2,1)S(1)}, u32[]{:S(2)}, u32[]{:S(2)}) collective-permute-start(bf16[512,1024]{1,0:T(8,128)(2,1)} %get-tuple-element.99), channel_id=1, source_target_pairs={{0,2},{1,4},{2,0},{3,6},{4,1},{5,7},{6,3},{7,5},{8,10},{9,12},{10,... | collective-permute-start | bytes 3145736 | tf_op jit(solution)/shard_map/ppermute | solution.py:518
  272.6 46.6 %collective-permute-start.15 = (bf16[512,1024]{1,0:T(8,128)(2,1)}, bf16[512,1024]{1,0:T(8,128)(2,1)}, u32[]{:S(2)}, u32[]{:S(2)}) collective-permute-start(bf16[512,1024]{1,0:T(8,128)(2,1)} %get-tuple-element.100), channel_id=1, source_target_pairs={{0,3},{1,5},{2,1},{3,7},{4,0},{5,6},{6,2},{7,4},{8,11},{9,13},{10,... | collective-permute-start | bytes 3145736 | tf_op jit(solution)/shard_map/ppermute | solution.py:518
  274.9 44.4 %collective-permute-start.16 = (bf16[512,1024]{1,0:T(8,128)(2,1)}, bf16[512,1024]{1,0:T(8,128)(2,1)}, u32[]{:S(2)}, u32[]{:S(2)}) collective-permute-start(bf16[512,1024]{1,0:T(8,128)(2,1)} %get-tuple-element.101), channel_id=1, source_target_pairs={{0,1},{1,7},{2,3},{3,5},{4,2},{5,4},{6,0},{7,6},{8,9},{9,15},{10,1... | collective-permute-start | bytes 3145736 | tf_op jit(solution)/shard_map/ppermute | solution.py:518
  277.9 41.3 %collective-permute-start.17 = (bf16[512,1024]{1,0:T(8,128)(2,1)}, bf16[512,1024]{1,0:T(8,128)(2,1)}, u32[]{:S(2)}, u32[]{:S(2)}) collective-permute-start(bf16[512,1024]{1,0:T(8,128)(2,1)} %get-tuple-element.102), channel_id=1, source_target_pairs={{0,0},{1,6},{2,2},{3,4},{4,3},{5,5},{6,1},{7,7},{8,8},{9,14},{10,1... | collective-permute-start | bytes 3145736 | tf_op jit(solution)/shard_map/ppermute | solution.py:518
  287.9 41.1 %copy-start.5 = (bf16[1024,1024]{1,0:T(8,128)(2,1)}, bf16[1024,1024]{1,0:T(8,128)(2,1)S(1)}, u32[]{:S(2)}) copy-start(bf16[1024,1024]{1,0:T(8,128)(2,1)S(1)} %pad_maximum_fusion.1.refs_5_) | copy-start | bytes 6291460
  287.9 41.1 %collective-permute-start.18 = (bf16[1024,1024]{1,0:T(8,128)(2,1)S(1)}, bf16[1024,1024]{1,0:T(8,128)(2,1)}, u32[]{:S(2)}, u32[]{:S(2)}) collective-permute-start(bf16[1024,1024]{1,0:T(8,128)(2,1)S(1)} %pad_maximum_fusion.1.refs_5_), channel_id=1, source_target_pairs={{0,1},{1,0},{2,3},{3,2},{4,5},{5,4},{6,7},{7,6},{8,9},{9,8},{10,11... | collective-permute-start | bytes 6291464 | tf_op jit(solution)/shard_map/ppermute | solution.py:545
  291.9 37.1 %copy-start.9 = (bf16[512,1024]{1,0:T(8,128)(2,1)}, bf16[512,1024]{1,0:T(8,128)(2,1)S(1)}, u32[]{:S(2)}) copy-start(bf16[512,1024]{1,0:T(8,128)(2,1)S(1)} %collective-permute-done.14.refs_0_) | copy-start | bytes 3145732
  319.2 31.0 %collective-permute-start.19 = (bf16[1024,1024]{1,0:T(8,128)(2,1)}, bf16[1024,1024]{1,0:T(8,128)(2,1)}, u32[]{:S(2)}, u32[]{:S(2)}) collective-permute-start(bf16[1024,1024]{1,0:T(8,128)(2,1)} %all-reduce.3.cloned.1.call-done.mine), channel_id=1, source_target_pairs={{5,1},{7,3},{0,4},{2,6},{13,9},{15,11},{8,12},{10,14},{21,17},{23,... | collective-permute-start | bytes 6291464 | tf_op jit(solution)/shard_map/ppermute | solution.py:518
Sparse Core Ops, SparseCore 0:
  119.2 55.6 all-gather.2
  202.0 67.8 all-reduce.2

commit v9 on v8

--- a/solution.py
+++ b/solution.py
@@ -327,26 +327,16 @@
 
 
 def join_kernel(steps, order, own, above, below, *refs):
-    outq_parts, parts, (whole, sems) = refs[:steps], refs[steps:2 * steps], refs[2 * steps:]
+    outq_parts, parts, whole = refs[:steps], refs[steps:2 * steps], refs[-1]
     chunk, feats = outq_parts[0].shape
-    moves = [
-        pltpu.make_async_copy(outq, part.at[:, pl.ds(0, feats)], sems.at[steps + i])
-        for i, (outq, part) in enumerate(zip(outq_parts, parts))
-    ]
-    for move in moves:
-        move.start()
     low, high = (BAND_ROWS - HALO) * LONGITUDES, HALO * LONGITUDES
+    for outq, part in zip(outq_parts, parts):
+        part[:, :feats] = outq[...]
     whole[:low] = (own[:low] + below[:low].astype(F32)).astype(BF16)
     whole[low:high] = (own[low:high] + below[low:].astype(F32) + above[:high - low].astype(F32)).astype(BF16)
     whole[high:] = (own[high:] + above[high - low:].astype(F32)).astype(BF16)
-    carry_out([
-        pltpu.make_async_copy(
-            whole.at[pl.ds(pl.multiple_of(order[i], 16), chunk)], part.at[:, pl.ds(feats, feats)], sems.at[i]
-        )
-        for i, part in enumerate(parts)
-    ])
-    for move in moves:
-        move.wait()
+    for i, part in enumerate(parts):
+        part[:, feats:] = whole[pl.ds(pl.multiple_of(order[i], 16), chunk), :]
 
 
 def joined(order, own, above, below, outq_parts):
@@ -354,8 +344,8 @@
     return call(
         functools.partial(join_kernel, steps),
         [shape(chunk, 2 * feats)] * steps,
-        [SMEM] + [VMEM] * 3 + [HBM] * steps, [HBM] * steps, (order, own, above, below, *outq_parts), flops=0,
-        scratch=[pltpu.VMEM((steps * chunk, feats), BF16), pltpu.SemaphoreType.DMA((2 * steps,))],
+        [SMEM] + [VMEM] * (3 + steps), [VMEM] * steps, (order, own, above, below, *outq_parts), flops=0,
+        scratch=[pltpu.VMEM((steps * chunk, feats), BF16)],
     )
 
 
@@ -544,18 +534,12 @@
     def from_sibling(x):
         return lax.ppermute(x, "c", [(0, 1), (1, 0)])
 
-    rows = 3 * feats // layers, feats // layers
-    flat_qkv, flat_out = qkv_weight.reshape(3 * feats, WIDTH), out_weight.reshape(feats, WIDTH)
-    held = jnp.concatenate([
-        lax.dynamic_slice_in_dim(flat, z * size, size, 0) for flat, size in zip((flat_qkv, flat_out), rows)
-    ], axis=0)
-
     def split(qkv, out):
         eighth = jnp.asarray([HEAD_WIDTH ** -0.5, 1.0, 1.0], BF16)[None, :, None, None]
         qkv = (qkv.reshape(heads, 3, HEAD_WIDTH, WIDTH) * eighth).transpose(1, 0, 2, 3)
         return jnp.concatenate([qkv.reshape(3 * feats, WIDTH), out.reshape(feats, WIDTH)], axis=0)
 
-    blocks = [split(flat_qkv, flat_out)]
+    blocks = [split(qkv_weight, out_weight)]
     sibling = from_sibling(blocks[0])
     group = jnp.where(c == y, blocks[0], sibling)
     group_qkv, group_out = group[:3 * feats].T, group[3 * feats:]
@@ -565,23 +549,20 @@
     normed_up, normed_down = halo_rows(order, normed_parts)
     normed_halos = passed_along(normed_up, 1), passed_along(normed_down, -1)
     qkv = projections(order, group_qkv, normed_parts)
-    shares = [from_ahead(after(held, qkv), dm) for dm in range(1, halves)]
     upstream_parts, _ = gathered(after(upstream, *normed_parts), qkv)
     kv_top, kv_bot = halo_projections(group_qkv[:, feats:], *normed_halos)
     kv_top, kv_bot, *upstream_parts = lax.optimization_barrier((kv_top, kv_bot, *upstream_parts))
-    order, *shares = lax.optimization_barrier((order, *shares))
-    ahead = [lax.all_gather(part, "z") for part in shares]
+    ahead = [from_ahead(after(blocks[0], *upstream_parts), dm) for dm in range(1, halves)]
     outq_parts, dkv, dkv_top, dkv_bot = attention(cells, order, qkv, kv_top, kv_bot, group_out, upstream_parts)
 
     from_above, from_below = passed_along(dkv_top, -1), passed_along(dkv_bot, 1)
     grads = weight_grads(
-        after(order, ahead), outq_parts, upstream_parts, normed_parts, dkv, (dkv_top, dkv_bot), normed_halos
+        order, outq_parts, upstream_parts, normed_parts, dkv, (dkv_top, dkv_bot), normed_halos
     )
     grads_sum = lax.psum(grads, ("z", "c"))
     parts = joined(after(order, grads), dkv, from_above, from_below, outq_parts)
     parts, ahead = lax.optimization_barrier((parts, ahead))
     parts_own = send_back(parts)
-    ahead = [split(block[:, :rows[0]], block[:, rows[0]:]) for block in ahead]
     blocks += ahead + [sibling] + [from_sibling(block) for block in ahead]
     update, grad_input = token_outputs(leads, tokens, gain, parts_own, blocks)
     grads = after(grads_sum, *parts_own)

time: 363 us -> 299 us (0.82)
  Pallas kernels: 166 us -> 105 us
  starting transfers between devices: 60.4 us -> 49.7 us
  waiting for transfers between devices: 98.7 us -> 105 us
    pallas_call x9, Pallas kernels: 166 us -> 105 us  [call(): pl.pallas_call(kernel, out_shape=tuple(out_shape), in_specs=list(in_specs...]
    psum x1, waiting for transfers between devices: 0.02 us -> 42.9 us  [on_device(): grads_sum = lax.psum(grads, ('z', 'c'))]
    ppermute x13, waiting for transfers between devices: 84.3 us -> 62.5 us  [permuted(): return lax.ppermute(x, GROUP, [(at(*a), at(*b)) for a, b in pairs])]
    ppermute x1, waiting for transfers between devices: 14.3 us -> 0.01 us  [from_ahead(): return lax.ppermute(x, 'm', [((i + dm) % halves, i) for i in range(halves)])]
    ppermute x13, starting transfers between devices: 38.1 us -> 31.1 us  [permuted(): return lax.ppermute(x, GROUP, [(at(*a), at(*b)) for a, b in pairs])]
    ppermute x4, starting transfers between devices: 20.9 us -> 16.6 us  [passed_along(): return lax.ppermute(x, ('z', 'c'), pairs)]
    unnamed x22, local copies, waits for them, and re-layouts: 1.99 us -> 5.7 us
  transfers between devices with their start and end apart: 22 -> 21, of which waited for: 9 -> 8; matrix products, arithmetic and copies ran while one was open for 4% -> 5% of each run, Pallas kernels for 43% -> 29%
where the time goes in v9:
time: 299 us; the launch traced here: 298 us
  Pallas kernels  105 us (35%)
  waiting for transfers between devices  105 us (35%)
  starting transfers between devices  49.7 us (17%)
  local copies, waits for them, and re-layouts  14.7 us (5%)
  between operations  14.2 us (5%)
  other arithmetic  9.7 us (3%)
    pallas_call x9, Pallas kernels, call(): pl.pallas_call(kernel, out_shape=tuple(out_shape), in_specs=list(in_specs...  105 us
    ppermute x13, waiting for transfers between devices, permuted(): return lax.ppermute(x, GROUP, [(at(*a), at(*b)) for a, b in pairs])  62.5 us
    psum x1, waiting for transfers between devices, on_device(): grads_sum = lax.psum(grads, ('z', 'c'))  42.9 us
    ppermute x13, starting transfers between devices, permuted(): return lax.ppermute(x, GROUP, [(at(*a), at(*b)) for a, b in pairs])  31.1 us
    ppermute x4, starting transfers between devices, passed_along(): return lax.ppermute(x, ('z', 'c'), pairs)  16.6 us
  transfers between devices with their start and end apart: 21, of which 8 were waited for; matrix products, arithmetic and copies ran while one was open for 5% of the time, Pallas kernels for 29%

profile of v9, /device:TPU:0, one launch (start us, length us, event | category | flops | bytes accessed | tf_op | source)
XLA Modules:
  0.0 298.4 jit_solution(3419951197832600166)
XLA Ops:
  7.2 1.6 copy_multiply_fusion
  8.9 1.5 pad_maximum_fusion.refs_4_
  10.8 2.6 shard_map.120
  13.4 2.5 collective-permute-start
  16.0 23.3 %collective-permute-done.refs_0_.refs_8_ = bf16[512,1024]{1,0:T(8,128)(2,1)S(1)} collective-permute-done((bf16[512,1024]{1,0:T(8,128)(2,1)}, bf16[512,1024]{1,0:T(8,128)(2,1)S(1)}, u32[]{:S(2)}, u32[]{:S(2)}) %collective-permute-start) | collective-permute-done | bytes 1048608 | tf_op jit(solution)/shard_map/ppermute | solution.py:508
  40.2 1.1 broadcast_select_fusion.4
  41.3 2.7 collective-permute-start.2
  44.0 1.6 collective-permute-start.3
  45.6 1.3 dynamic-slice_bitcast_fusion.order
  46.9 1.0 broadcast_select_fusion
  48.9 7.8 %collective-permute-done.2.refs_2_.refs_10_ = bf16[512,1024]{1,0:T(8,128)(2,1)} collective-permute-done((bf16[512,1024]{1,0:T(8,128)(2,1)}, bf16[512,1024]{1,0:T(8,128)(2,1)}, u32[]{:S(2)}, u32[]{:S(2)}) %collective-permute-start.2) | collective-permute-done | bytes 1048608 | tf_op jit(solution)/shard_map/ppermute | solution.py:508
  56.6 1.1 broadcast_select_fusion.3.refs_3_.refs_11_
  57.8 5.7 %shard_map.122 = (bf16[1536,1024]{1,0:T(8,128)(2,1)}, bf16[1536,1024]{1,0:T(8,128)(2,1)}) custom-call(s32[4]{0:T(128)} %dynamic-slice_bitcast_fusion.order, bf16[512,1024]{1,0:T(8,128)(2,1)} %copy-done.1, bf16[512,1024]{1,0:T(8,128)(2,1)} %collective-permute-done.1.refs_1_.refs_9_, bf16[512,1024]{1,0:T(8,128)(2,1)} %collective-permute-done.2.refs_2_.refs_10_, ...), custom_call_target="tpu_custom_call" | custom-call | tf_op jit(solution)/shard_map/pallas_call | solution.py:200
  63.5 6.5 %collective-permute-start.5 = (bf16[1536,1024]{1,0:T(8,128)(2,1)}, bf16[1536,1024]{1,0:T(8,128)(2,1)}, u32[]{:S(2)}, u32[]{:S(2)}) collective-permute-start(bf16[1536,1024]{1,0:T(8,128)(2,1)} %get-tuple-element.63), channel_id=1, source_target_pairs={{0,1},{1,8},{8,9},{9,16},{16,17},{17,24},{24,25},{2,3},{3,10},{10,... | collective-permute-start | bytes 9437192 | tf_op jit(solution)/shard_map/ppermute | solution.py:477
  70.0 1.3 collective-permute-start.6
  71.3 1.8 collective-permute-start.7
  73.1 1.0 collective-permute-start.8
  74.1 1.6 copy.14.weight
  75.7 8.8 %shard_map.121.qkv = bf16[2048,768]{1,0:T(8,128)(2,1)} custom-call(s32[4]{0:T(128)} %dynamic-slice_bitcast_fusion.order, bf16[1024,768]{1,0:T(8,128)(2,1)} %copy.14.weight, bf16[512,1024]{1,0:T(8,128)(2,1)} %copy-done.1, bf16[512,1024]{1,0:T(8,128)(2,1)} %collective-permute-done.1.refs_1_.refs_9_, bf16[512,1024]{1,0:T(8,128)(2,1)} %collective-permute-done.2.refs_2_.refs_10_, ...), custom_call_target="tpu_custom_call" | custom-call | flops 3221225472 | bytes 8912912 | tf_op jit(solution)/shard_map/pallas_call | solution.py:200
  84.5 11.8 %collective-permute-done.7.refs_0_.refs_4_ = bf16[512,1024]{1,0:T(8,128)(2,1)} collective-permute-done((bf16[512,1024]{1,0:T(8,128)(2,1)S(1)}, bf16[512,1024]{1,0:T(8,128)(2,1)}, u32[]{:S(2)}, u32[]{:S(2)}) %collective-permute-start.7) | collective-permute-done | bytes 1048608 | tf_op jit(solution)/shard_map/ppermute | solution.py:508
  96.4 1.1 collective-permute-done.8.refs_1_.refs_5_
  97.5 2.3 broadcast_select_fusion.2
  99.8 1.7 collective-permute-start.10
  102.2 1.0 slice.11
  103.2 2.3 copy.15.weight
  105.5 7.0 %collective-permute-done.9.refs_2_.refs_6_ = bf16[512,1024]{1,0:T(8,128)(2,1)} collective-permute-done((bf16[512,1024]{1,0:T(8,128)(2,1)}, bf16[512,1024]{1,0:T(8,128)(2,1)}, u32[]{:S(2)}, u32[]{:S(2)}) %collective-permute-start.9) | collective-permute-done | bytes 1048608 | tf_op jit(solution)/shard_map/ppermute | solution.py:508
  112.5 1.1 broadcast_select_fusion.1.refs_3_.refs_7_
  113.5 7.7 %shard_map.123 = (bf16[1536,512]{1,0:T(8,128)(2,1)}, bf16[1536,512]{1,0:T(8,128)(2,1)}) custom-call(bf16[1024,512]{1,0:T(8,128)(2,1)} %copy.15.weight, bf16[1536,1024]{1,0:T(8,128)(2,1)} %collective-permute-done.5.top.refs_15_, bf16[1536,1024]{1,0:T(8,128)(2,1)} %collective-permute-done.6.bot.refs_16_), custom_call_target="tpu_custom_call" | custom-call | flops 3221225472 | bytes 10485760 | tf_op jit(solution)/shard_map/pallas_call | solution.py:200
  121.3 1.5 collective-permute-start.13
  122.8 42.1 %shard_map.124 = (bf16[512,512]{1,0:T(8,128)(2,1)}, bf16[512,512]{1,0:T(8,128)(2,1)}, bf16[512,512]{1,0:T(8,128)(2,1)}, bf16[512,512]{1,0:T(8,128)(2,1)}, f32[20...) custom-call(s32[20]{0:T(128)} %pad_dynamic-slice_fusion.cells, ...), custom_call_target="tpu_custom_call" | custom-call | flops 13958643712 | bytes 20447328 | tf_op jit(solution)/shard_map/pallas_call | solution.py:200
  164.9 1.3 collective-permute-start.11
  166.2 7.5 %collective-permute-start.12 = (bf16[1536,512]{1,0:T(8,128)(2,1)}, bf16[1536,512]{1,0:T(8,128)(2,1)S(1)}, u32[]{:S(2)}, u32[]{:S(2)}) collective-permute-start(bf16[1536,512]{1,0:T(8,128)(2,1)} %get-tuple-element.86.refs_14_), channel_id=1, source_target_pairs={{0,1},{1,8},{8,9},{9,16},{16,17},{17,24},{24,25},{2,3},{3,10},{10,... | collective-permute-start | bytes 4718600 | tf_op jit(solution)/shard_map/ppermute | solution.py:477
  173.7 14.5 %shard_map.125 = bf16[1024,1024]{1,0:T(8,128)(2,1)} custom-call(s32[4]{0:T(128)} %dynamic-slice_bitcast_fusion.order, bf16[512,512]{1,0:T(8,128)(2,1)} %get-tuple-element.80.refs_0_, bf16[512,512]{1,0:T(8,128)(2,1)} %get-tuple-element.81.refs_1_, bf16[512,512]{1,0:T(8,128)(2,1)} %get-tuple-element.82.refs_2_, bf16[512,512]{1,0:T(8,128)(2,1)} %get-tuple-element.83.refs_3_, ...), custom_call_target="tpu_custom_call" | custom-call | flops 7516192768 | bytes 26214416 | tf_op jit(solution)/shard_map/pallas_call | solution.py:200
  188.3 1.1 copy-done.5
  189.4 1.2 copy-done.6
  190.6 6.7 %shard_map.126 = (bf16[512,1024]{1,0:T(8,128)(2,1)}, bf16[512,1024]{1,0:T(8,128)(2,1)}, bf16[512,1024]{1,0:T(8,128)(2,1)}, bf16[512,1024]{1,0:T(8,128)(2,1)}) custom-call(s32[4]{0:T(128)} %dynamic-slice_bitcast_fusion.order, f32[2048,512]{1,0:T(8,128)} %get-tuple-element.84.refs_12_.own, bf16[1536,512]{1,0:T(8,128)(2,1)} %copy-done.5, ...), custom_call_target="tpu_custom_call" | custom-call | tf_op jit(solution)/shard_map/pallas_call | solution.py:200
  197.9 3.1 %collective-permute-start.15 = (bf16[512,1024]{1,0:T(8,128)(2,1)}, bf16[512,1024]{1,0:T(8,128)(2,1)S(1)}, u32[]{:S(2)}, u32[]{:S(2)}) collective-permute-start(bf16[512,1024]{1,0:T(8,128)(2,1)} %get-tuple-element.94), channel_id=1, source_target_pairs={{0,3},{1,5},{2,1},{3,7},{4,0},{5,6},{6,2},{7,4},{8,11},{9,13},{10,... | collective-permute-start | bytes 3145736 | tf_op jit(solution)/shard_map/ppermute | solution.py:508
  201.0 3.1 %collective-permute-start.16 = (bf16[512,1024]{1,0:T(8,128)(2,1)}, bf16[512,1024]{1,0:T(8,128)(2,1)S(1)}, u32[]{:S(2)}, u32[]{:S(2)}) collective-permute-start(bf16[512,1024]{1,0:T(8,128)(2,1)} %get-tuple-element.95), channel_id=1, source_target_pairs={{0,1},{1,7},{2,3},{3,5},{4,2},{5,4},{6,0},{7,6},{8,9},{9,15},{10,1... | collective-permute-start | bytes 3145736 | tf_op jit(solution)/shard_map/ppermute | solution.py:508
  204.1 9.4 %collective-permute-start.17 = (bf16[512,1024]{1,0:T(8,128)(2,1)}, bf16[512,1024]{1,0:T(8,128)(2,1)}, u32[]{:S(2)}, u32[]{:S(2)}) collective-permute-start(bf16[512,1024]{1,0:T(8,128)(2,1)} %get-tuple-element.96), channel_id=1, source_target_pairs={{0,0},{1,6},{2,2},{3,4},{4,3},{5,5},{6,1},{7,7},{8,8},{9,14},{10,1... | collective-permute-start | bytes 3145736 | tf_op jit(solution)/shard_map/ppermute | solution.py:508
  213.5 42.9 %all-reduce.3.cloned.1.call-done.mine = bf16[1024,1024]{1,0:T(8,128)(2,1)} async-done(((bf16[1024,1024]{1,0:T(8,128)(2,1)}), bf16[1024,1024]{1,0:T(8,128)(2,1)}) %all-reduce.3.cloned.1.call-update) | async-done | bytes 2097168 | tf_op jit(solution)/shard_map/psum | solution.py:562
  256.4 1.0 copy-done.8
  257.4 1.0 copy-done.9
  258.4 3.6 %collective-permute-start.19 = (bf16[1024,1024]{1,0:T(8,128)(2,1)}, bf16[1024,1024]{1,0:T(8,128)(2,1)S(1)}, u32[]{:S(2)}, u32[]{:S(2)}) collective-permute-start(bf16[1024,1024]{1,0:T(8,128)(2,1)} %all-reduce.3.cloned.1.call-done.mine), channel_id=1, source_target_pairs={{5,1},{7,3},{0,4},{2,6},{13,9},{15,11},{8,12},{10,14},{21,17},{23,... | collective-permute-start | bytes 6291464 | tf_op jit(solution)/shard_map/ppermute | solution.py:508
  262.0 1.2 dynamic-slice_bitcast_fusion.1.leads
  263.2 12.0 %shard_map.127 = (bf16[512,1024]{1,0:T(8,128)(2,1)}, bf16[512,1024]{1,0:T(8,128)(2,1)}) custom-call(s32[4]{0:T(128)} %dynamic-slice_bitcast_fusion.1.leads, bf16[512,1024]{1,0:T(8,128)(2,1)} %tokens.3, f32[1,1024]{1,0:T(1,128)} %bitcast.19, bf16[512,1024]{1,0:T(8,128)(2,1)} %copy-done.7, bf16[512,1024]{1,0:T(8,128)(2,1)} %copy-done.8, ...), custom_call_target="tpu_custom_call" | custom-call | flops 4294967296 | bytes 15732752 | tf_op jit(solution)/shard_map/pallas_call | solution.py:200
  275.2 10.5 %collective-permute-done.19.other = bf16[1024,1024]{1,0:T(8,128)(2,1)S(1)} collective-permute-done((bf16[1024,1024]{1,0:T(8,128)(2,1)}, bf16[1024,1024]{1,0:T(8,128)(2,1)S(1)}, u32[]{:S(2)}, u32[]{:S(2)}) %collective-permute-start.19) | collective-permute-done | bytes 2097184 | tf_op jit(solution)/shard_map/ppermute | solution.py:508
  285.7 1.4 copy-done.3
  287.0 4.5 %shard_map.128 = (f32[4,192,1024]{2,1,0:T(8,128)}, f32[4,64,1024]{2,1,0:T(8,128)}) custom-call(s32[1]{0:T(128)} %bitcast.8.flag, bf16[1024,1024]{1,0:T(8,128)(2,1)} %all-reduce.3.cloned.1.call-done.mine, bf16[1024,1024]{1,0:T(8,128)(2,1)} %copy-done.3), custom_call_target="tpu_custom_call" | custom-call | flops 1048576 | bytes 8388612 | tf_op jit(solution)/shard_map/pallas_call | solution.py:200
  (41 shorter events, 3.8 us)
Async XLA Ops:
  7.2 1.7 copy-start.4
  7.2 249.2 %all-reduce.3.cloned.1.call-start = ((), (), s32[]{:S(2)}) async-start(), calls=%async_computation | async-start | bytes 4194304 | tf_op jit(solution)/shard_map/psum | solution.py:562
  10.4 36.5 %collective-permute-start.4 = (bf16[1024,1024]{1,0:T(8,128)(2,1)}, bf16[1024,1024]{1,0:T(8,128)(2,1)}, u32[]{:S(2)}, u32[]{:S(2)}) collective-permute-start(bf16[1024,1024]{1,0:T(8,128)(2,1)} %pad_maximum_fusion.refs_4_), channel_id=1, source_target_pairs={{0,1},{1,0},{2,3},{3,2},{4,5},{5,4},{6,7},{7,6},{8,9},{9,8},{10,11... | collective-permute-start | bytes 6291464 | tf_op jit(solution)/shard_map/ppermute | solution.py:535
  13.4 25.8 %collective-permute-start = (bf16[512,1024]{1,0:T(8,128)(2,1)}, bf16[512,1024]{1,0:T(8,128)(2,1)S(1)}, u32[]{:S(2)}, u32[]{:S(2)}) collective-permute-start(bf16[512,1024]{1,0:T(8,128)(2,1)} %shard_map.120), channel_id=1, source_target_pairs={{2,0},{4,1},{0,2},{6,3},{1,4},{7,5},{3,6},{5,7},{10,8},{12,9},{8,1... | collective-permute-start | bytes 3145736 | tf_op jit(solution)/shard_map/ppermute | solution.py:508
  15.9 24.3 %collective-permute-start.1 = (bf16[512,1024]{1,0:T(8,128)(2,1)}, bf16[512,1024]{1,0:T(8,128)(2,1)}, u32[]{:S(2)}, u32[]{:S(2)}) collective-permute-start(bf16[512,1024]{1,0:T(8,128)(2,1)} %shard_map.120), channel_id=1, source_target_pairs={{3,0},{5,1},{1,2},{7,3},{0,4},{6,5},{2,6},{4,7},{11,8},{13,9},{9,1... | collective-permute-start | bytes 3145736 | tf_op jit(solution)/shard_map/ppermute | solution.py:508
  39.3 8.6 %copy-start.1 = (bf16[512,1024]{1,0:T(8,128)(2,1)}, bf16[512,1024]{1,0:T(8,128)(2,1)S(1)}, u32[]{:S(2)}) copy-start(bf16[512,1024]{1,0:T(8,128)(2,1)S(1)} %collective-permute-done.refs_0_.refs_8_) | copy-start | bytes 3145732
  41.3 15.3 %collective-permute-start.2 = (bf16[512,1024]{1,0:T(8,128)(2,1)}, bf16[512,1024]{1,0:T(8,128)(2,1)}, u32[]{:S(2)}, u32[]{:S(2)}) collective-permute-start(bf16[512,1024]{1,0:T(8,128)(2,1)} %broadcast_select_fusion.4), channel_id=1, source_target_pairs={{0,4},{1,0},{2,6},{3,2},{4,5},{5,1},{6,7},{7,3},{8,12},{9,8},{10,1... | collective-permute-start | bytes 3145736 | tf_op jit(solution)/shard_map/ppermute | solution.py:508
  44.0 12.6 %collective-permute-start.3 = (bf16[512,1024]{1,0:T(8,128)(2,1)S(1)}, bf16[512,1024]{1,0:T(8,128)(2,1)}, u32[]{:S(2)}, u32[]{:S(2)}) collective-permute-start(bf16[512,1024]{1,0:T(8,128)(2,1)S(1)} %collective-permute-done.refs_0_.refs_8_), channel_id=1, source_target_pairs={{1,3},{3,1},{4,6},{6,4},{9,11},{11,9},{12,14},{14,12},{17,19},{19,... | collective-permute-start | bytes 3145736 | tf_op jit(solution)/shard_map/ppermute | solution.py:508
  47.9 8.8 %copy-start = (bf16[512,1024]{1,0:T(8,128)(2,1)S(1)}, bf16[512,1024]{1,0:T(8,128)(2,1)}, u32[]{:S(2)}) copy-start(bf16[512,1024]{1,0:T(8,128)(2,1)} %shard_map.120) | copy-start | bytes 3145732
  57.8 13.5 %copy-start.2 = (bf16[512,1024]{1,0:T(8,128)(2,1)S(1)}, bf16[512,1024]{1,0:T(8,128)(2,1)}, u32[]{:S(2)}) copy-start(bf16[512,1024]{1,0:T(8,128)(2,1)} %param.14) | copy-start | bytes 3145732
  63.5 50.1 %collective-permute-start.5 = (bf16[1536,1024]{1,0:T(8,128)(2,1)}, bf16[1536,1024]{1,0:T(8,128)(2,1)}, u32[]{:S(2)}, u32[]{:S(2)}) collective-permute-start(bf16[1536,1024]{1,0:T(8,128)(2,1)} %get-tuple-element.63), channel_id=1, source_target_pairs={{0,1},{1,8},{8,9},{9,16},{16,17},{17,24},{24,25},{2,3},{3,10},{10,... | collective-permute-start | bytes 9437192 | tf_op jit(solution)/shard_map/ppermute | solution.py:477
  70.0 43.5 %collective-permute-start.6 = (bf16[1536,1024]{1,0:T(8,128)(2,1)}, bf16[1536,1024]{1,0:T(8,128)(2,1)}, u32[]{:S(2)}, u32[]{:S(2)}) collective-permute-start(bf16[1536,1024]{1,0:T(8,128)(2,1)} %get-tuple-element.64), channel_id=1, source_target_pairs={{1,0},{8,1},{9,8},{16,9},{17,16},{24,17},{25,24},{3,2},{10,3},{11,... | collective-permute-start | bytes 9437192 | tf_op jit(solution)/shard_map/ppermute | solution.py:477
  71.3 25.1 %collective-permute-start.7 = (bf16[512,1024]{1,0:T(8,128)(2,1)S(1)}, bf16[512,1024]{1,0:T(8,128)(2,1)}, u32[]{:S(2)}, u32[]{:S(2)}) collective-permute-start(bf16[512,1024]{1,0:T(8,128)(2,1)S(1)} %copy-done.2), channel_id=1, source_target_pairs={{2,0},{4,1},{0,2},{6,3},{1,4},{7,5},{3,6},{5,7},{10,8},{12,9},{8,1... | collective-permute-start | bytes 3145736 | tf_op jit(solution)/shard_map/ppermute | solution.py:508
  73.1 24.4 %collective-permute-start.8 = (bf16[512,1024]{1,0:T(8,128)(2,1)S(1)}, bf16[512,1024]{1,0:T(8,128)(2,1)}, u32[]{:S(2)}, u32[]{:S(2)}) collective-permute-start(bf16[512,1024]{1,0:T(8,128)(2,1)S(1)} %copy-done.2), channel_id=1, source_target_pairs={{3,0},{5,1},{1,2},{7,3},{0,4},{6,5},{2,6},{4,7},{11,8},{13,9},{9,1... | collective-permute-start | bytes 3145736 | tf_op jit(solution)/shard_map/ppermute | solution.py:508
  84.5 17.0 %copy-start.10 = (s32[64]{0:T(128)S(1)}, s32[64]{0:T(128)}, u32[]{:S(2)}) copy-start(s32[64]{0:T(128)} %param.13) | copy-start | bytes 772
  99.8 12.6 %collective-permute-start.9 = (bf16[512,1024]{1,0:T(8,128)(2,1)}, bf16[512,1024]{1,0:T(8,128)(2,1)}, u32[]{:S(2)}, u32[]{:S(2)}) collective-permute-start(bf16[512,1024]{1,0:T(8,128)(2,1)} %broadcast_select_fusion.2), channel_id=1, source_target_pairs={{0,4},{1,0},{2,6},{3,2},{4,5},{5,1},{6,7},{7,3},{8,12},{9,8},{10,1... | collective-permute-start | bytes 3145736 | tf_op jit(solution)/shard_map/ppermute | solution.py:508
  99.8 12.6 %collective-permute-start.10 = (bf16[512,1024]{1,0:T(8,128)(2,1)}, bf16[512,1024]{1,0:T(8,128)(2,1)}, u32[]{:S(2)}, u32[]{:S(2)}) collective-permute-start(bf16[512,1024]{1,0:T(8,128)(2,1)} %collective-permute-done.7.refs_0_.refs_4_), channel_id=1, source_target_pairs={{1,3},{3,1},{4,6},{6,4},{9,11},{11,9},{12,14},{14,12},{17,19},{19,... | collective-permute-start | bytes 3145736 | tf_op jit(solution)/shard_map/ppermute | solution.py:508
  121.3 76.1 %collective-permute-start.13 = (bf16[1024,1024]{1,0:T(8,128)(2,1)}, bf16[1024,1024]{1,0:T(8,128)(2,1)}, u32[]{:S(2)}, u32[]{:S(2)}) collective-permute-start(bf16[1024,1024]{1,0:T(8,128)(2,1)} %pad_maximum_fusion.refs_4_), channel_id=1, source_target_pairs={{2,0},{0,2},{3,1},{1,3},{6,4},{4,6},{7,5},{5,7},{10,8},{8,10},{11,... | collective-permute-start | bytes 6291464 | tf_op jit(solution)/shard_map/ppermute | solution.py:532
  164.9 23.3 %collective-permute-start.11 = (bf16[1536,512]{1,0:T(8,128)(2,1)}, bf16[1536,512]{1,0:T(8,128)(2,1)S(1)}, u32[]{:S(2)}, u32[]{:S(2)}) collective-permute-start(bf16[1536,512]{1,0:T(8,128)(2,1)} %get-tuple-element.85.refs_13_), channel_id=1, source_target_pairs={{1,0},{8,1},{9,8},{16,9},{17,16},{24,17},{25,24},{3,2},{10,3},{11,... | collective-permute-start | bytes 4718600 | tf_op jit(solution)/shard_map/ppermute | solution.py:477
  166.2 22.0 %collective-permute-start.12 = (bf16[1536,512]{1,0:T(8,128)(2,1)}, bf16[1536,512]{1,0:T(8,128)(2,1)S(1)}, u32[]{:S(2)}, u32[]{:S(2)}) collective-permute-start(bf16[1536,512]{1,0:T(8,128)(2,1)} %get-tuple-element.86.refs_14_), channel_id=1, source_target_pairs={{0,1},{1,8},{8,9},{9,16},{16,17},{17,24},{24,25},{2,3},{3,10},{10,... | collective-permute-start | bytes 4718600 | tf_op jit(solution)/shard_map/ppermute | solution.py:477
  188.2 1.2 copy-start.5
  189.4 1.2 copy-start.6
  197.4 59.0 %collective-permute-start.14 = (bf16[512,1024]{1,0:T(8,128)(2,1)}, bf16[512,1024]{1,0:T(8,128)(2,1)S(1)}, u32[]{:S(2)}, u32[]{:S(2)}) collective-permute-start(bf16[512,1024]{1,0:T(8,128)(2,1)} %get-tuple-element.93), channel_id=1, source_target_pairs={{0,2},{1,4},{2,0},{3,6},{4,1},{5,7},{6,3},{7,5},{8,10},{9,12},{10,... | collective-permute-start | bytes 3145736 | tf_op jit(solution)/shard_map/ppermute | solution.py:508
  197.9 58.5 %collective-permute-start.15 = (bf16[512,1024]{1,0:T(8,128)(2,1)}, bf16[512,1024]{1,0:T(8,128)(2,1)S(1)}, u32[]{:S(2)}, u32[]{:S(2)}) collective-permute-start(bf16[512,1024]{1,0:T(8,128)(2,1)} %get-tuple-element.94), channel_id=1, source_target_pairs={{0,3},{1,5},{2,1},{3,7},{4,0},{5,6},{6,2},{7,4},{8,11},{9,13},{10,... | collective-permute-start | bytes 3145736 | tf_op jit(solution)/shard_map/ppermute | solution.py:508
  201.0 55.4 %collective-permute-start.16 = (bf16[512,1024]{1,0:T(8,128)(2,1)}, bf16[512,1024]{1,0:T(8,128)(2,1)S(1)}, u32[]{:S(2)}, u32[]{:S(2)}) collective-permute-start(bf16[512,1024]{1,0:T(8,128)(2,1)} %get-tuple-element.95), channel_id=1, source_target_pairs={{0,1},{1,7},{2,3},{3,5},{4,2},{5,4},{6,0},{7,6},{8,9},{9,15},{10,1... | collective-permute-start | bytes 3145736 | tf_op jit(solution)/shard_map/ppermute | solution.py:508
  204.1 54.3 %collective-permute-start.17 = (bf16[512,1024]{1,0:T(8,128)(2,1)}, bf16[512,1024]{1,0:T(8,128)(2,1)}, u32[]{:S(2)}, u32[]{:S(2)}) collective-permute-start(bf16[512,1024]{1,0:T(8,128)(2,1)} %get-tuple-element.96), channel_id=1, source_target_pairs={{0,0},{1,6},{2,2},{3,4},{4,3},{5,5},{6,1},{7,7},{8,8},{9,14},{10,1... | collective-permute-start | bytes 3145736 | tf_op jit(solution)/shard_map/ppermute | solution.py:508
  213.5 49.7 %collective-permute-start.18 = (bf16[1024,1024]{1,0:T(8,128)(2,1)}, bf16[1024,1024]{1,0:T(8,128)(2,1)}, u32[]{:S(2)}, u32[]{:S(2)}) collective-permute-start(bf16[1024,1024]{1,0:T(8,128)(2,1)} %collective-permute-done.13.refs_5_), channel_id=1, source_target_pairs={{0,1},{1,0},{2,3},{3,2},{4,5},{5,4},{6,7},{7,6},{8,9},{9,8},{10,11... | collective-permute-start | bytes 6291464 | tf_op jit(solution)/shard_map/ppermute | solution.py:535
  256.4 6.8 %copy-start.7 = (bf16[512,1024]{1,0:T(8,128)(2,1)}, bf16[512,1024]{1,0:T(8,128)(2,1)S(1)}, u32[]{:S(2)}) copy-start(bf16[512,1024]{1,0:T(8,128)(2,1)S(1)} %collective-permute-done.14.refs_0_) | copy-start | bytes 3145732
  256.4 1.0 copy-start.8
  257.4 1.0 copy-start.9
  258.4 27.3 %collective-permute-start.19 = (bf16[1024,1024]{1,0:T(8,128)(2,1)}, bf16[1024,1024]{1,0:T(8,128)(2,1)S(1)}, u32[]{:S(2)}, u32[]{:S(2)}) collective-permute-start(bf16[1024,1024]{1,0:T(8,128)(2,1)} %all-reduce.3.cloned.1.call-done.mine), channel_id=1, source_target_pairs={{5,1},{7,3},{0,4},{2,6},{13,9},{15,11},{8,12},{10,14},{21,17},{23,... | collective-permute-start | bytes 6291464 | tf_op jit(solution)/shard_map/ppermute | solution.py:508
  285.7 1.4 copy-start.3
Sparse Core Ops, SparseCore 0:
  188.3 68.0 all-reduce.2

commit v10 on v9

--- a/solution.py
+++ b/solution.py
@@ -269,60 +269,39 @@
         move.wait()
 
 
-def halo_kernel(steps, order, *refs):
-    parts, (up, down, held, sems) = refs[:steps], refs[steps:]
+def projection_kernel(steps, feats, order, weight, *refs):
+    parts, (qkv, kv_up, kv_down, normed_up, normed_down, held, sems) = refs[:steps], refs[steps:]
     chunk = parts[0].shape[0]
+    halo, rest = HALO * LONGITUDES, (BAND_ROWS - HALO) * LONGITUDES
     carry_out([
         pltpu.make_async_copy(part, held.at[pl.ds(pl.multiple_of(order[i], 16), chunk)], sems.at[i])
         for i, part in enumerate(parts)
     ])
-    halo, rest = HALO * LONGITUDES, (BAND_ROWS - HALO) * LONGITUDES
-    carry_out([
-        pltpu.make_async_copy(held.at[pl.ds(rest, halo)], up, sems.at[0]),
-        pltpu.make_async_copy(held.at[pl.ds(0, halo)], down, sems.at[1]),
-    ])
-
-
-def halo_rows(order, parts):
-    steps, width = len(parts), parts[0].shape[1]
-    halo = shape(HALO * LONGITUDES, width)
-    return call(
-        functools.partial(halo_kernel, steps), [halo, halo], [SMEM] + [HBM] * steps, [HBM] * 2, (order, *parts), flops=0,
-        scratch=[pltpu.VMEM((BAND_ROWS * LONGITUDES, width), BF16), pltpu.SemaphoreType.DMA((steps,))],
-    )
-
-
-def projection_kernel(steps, feats, order, weight, *refs):
-    parts, (qkv, held, sems) = refs[:steps], refs[steps:]
-    chunk = parts[0].shape[0]
-    carry_out(stacked_moves(parts, held, sems))
-    for first in range(0, 3 * feats, feats):
-        product = nn(held[...], weight[:, first:first + feats]).astype(BF16)
-        for i in range(steps):
-            qkv[pl.ds(pl.multiple_of(order[i], 16), chunk), first:first + feats] = product[i * chunk:(i + 1) * chunk]
+    moves = [
+        pltpu.make_async_copy(held.at[pl.ds(rest, halo)], normed_up, sems.at[0]),
+        pltpu.make_async_copy(held.at[pl.ds(0, halo)], normed_down, sems.at[1]),
+    ]
+    for move in moves:
+        move.start()
+    for i in range(3):
+        product = nn(held[...], weight[:, i * feats:(i + 1) * feats]).astype(BF16)
+        qkv[:, i * feats:(i + 1) * feats] = product
+        if i:
+            kv_up[:, (i - 1) * feats:i * feats] = product[rest:]
+            kv_down[:, (i - 1) * feats:i * feats] = product[:halo]
+    for move in moves:
+        move.wait()
 
 
 def projections(order, weight, parts):
     steps, feats, width = len(parts), weight.shape[1] // 3, parts[0].shape[1]
-    band = BAND_ROWS * LONGITUDES
+    band, halo = BAND_ROWS * LONGITUDES, HALO * LONGITUDES
     return call(
         functools.partial(projection_kernel, steps, feats),
-        [shape(band, 3 * feats)], [SMEM, VMEM] + [HBM] * steps, [VMEM], (order, weight, *parts),
+        [shape(band, 3 * feats)] + [shape(halo, 2 * feats)] * 2 + [shape(halo, width)] * 2,
+        [SMEM, VMEM] + [HBM] * steps, [VMEM] * 3 + [HBM] * 2, (order, weight, *parts),
         flops=2 * band * weight.size,
         scratch=[pltpu.VMEM((band, width), BF16), pltpu.SemaphoreType.DMA((steps,))],
-    )[0]
-
-
-def halo_projection_kernel(weight, top, bot, kv_top, kv_bot):
-    for halo, out in ((top, kv_top), (bot, kv_bot)):
-        out[...] = nn(halo[...], weight[...]).astype(BF16)
-
-
-def halo_projections(weight, top, bot):
-    out = shape(top.shape[0], weight.shape[1])
-    return call(
-        halo_projection_kernel, [out, out], [VMEM] * 3, [VMEM] * 2, (weight, top, bot),
-        flops=4 * top.shape[0] * weight.size,
     )
 
 
@@ -546,12 +525,14 @@
 
     normed_parts, hop = gathered(norm(tokens, gain))
     *normed_parts, group_qkv, group_out = lax.optimization_barrier((*normed_parts, group_qkv, group_out))
-    normed_up, normed_down = halo_rows(order, normed_parts)
+    qkv, kv_up, kv_down, normed_up, normed_down = projections(order, group_qkv, normed_parts)
+    kv_top, kv_bot = passed_along(kv_up, 1), passed_along(kv_down, -1)
+    upstream_parts, _ = gathered(after(upstream, *hop), qkv)
+
+    kv_top, kv_bot, normed_up, normed_down, *upstream_parts = lax.optimization_barrier(
+        (kv_top, kv_bot, normed_up, normed_down, *upstream_parts)
+    )
     normed_halos = passed_along(normed_up, 1), passed_along(normed_down, -1)
-    qkv = projections(order, group_qkv, normed_parts)
-    upstream_parts, _ = gathered(after(upstream, *normed_parts), qkv)
-    kv_top, kv_bot = halo_projections(group_qkv[:, feats:], *normed_halos)
-    kv_top, kv_bot, *upstream_parts = lax.optimization_barrier((kv_top, kv_bot, *upstream_parts))
     ahead = [from_ahead(after(blocks[0], *upstream_parts), dm) for dm in range(1, halves)]
     outq_parts, dkv, dkv_top, dkv_bot = attention(cells, order, qkv, kv_top, kv_bot, group_out, upstream_parts)
 

time: 299 us -> 309 us (1.033)
  waiting for transfers between devices: 105 us -> 124 us
  Pallas kernels: 105 us -> 92.3 us
  starting transfers between devices: 49.7 us -> 55.9 us
  local copies, waits for them, and re-layouts: 14.7 us -> 11.6 us
    ppermute x13, waiting for transfers between devices: 62.5 us -> 92.1 us  [permuted(): return lax.ppermute(x, GROUP, [(at(*a), at(*b)) for a, b in pairs])]
    pallas_call x9 -> x7, Pallas kernels: 105 us -> 92.3 us  [call(): pl.pallas_call(kernel, out_shape=tuple(out_shape), in_specs=list(in_specs...]
    psum x1, waiting for transfers between devices: 42.9 us -> 31.9 us  [on_device(): grads_sum = lax.psum(grads, ('z', 'c'))]
    ppermute x4 -> x6, starting transfers between devices: 16.6 us -> 21.4 us  [passed_along(): return lax.ppermute(x, ('z', 'c'), pairs)]
    slice x2 -> x0, local copies, waits for them, and re-layouts: 3.33 us -> none  [on_device(): kv_top, kv_bot = halo_projections(group_qkv[:, feats:], *normed_halos)]
  transfers between devices with their start and end apart: 21 -> 23, of which waited for: 8 -> 8; matrix products, arithmetic and copies ran while one was open for 5% -> 4% of each run, Pallas kernels for 29% -> 28%
where the time goes in v10:
time: 309 us; the launch traced here: 308 us
  waiting for transfers between devices  124 us (40%)
  Pallas kernels  92.3 us (30%)
  starting transfers between devices  55.9 us (18%)
  between operations  14.3 us (5%)
  local copies, waits for them, and re-layouts  11.6 us (4%)
  other arithmetic  10 us (3%)
    pallas_call x7, Pallas kernels, call(): pl.pallas_call(kernel, out_shape=tuple(out_shape), in_specs=list(in_specs...  92.3 us
    ppermute x13, waiting for transfers between devices, permuted(): return lax.ppermute(x, GROUP, [(at(*a), at(*b)) for a, b in pairs])  92.1 us
    ppermute x13, starting transfers between devices, permuted(): return lax.ppermute(x, GROUP, [(at(*a), at(*b)) for a, b in pairs])  32.3 us
    psum x1, waiting for transfers between devices, on_device(): grads_sum = lax.psum(grads, ('z', 'c'))  31.9 us
    ppermute x6, starting transfers between devices, passed_along(): return lax.ppermute(x, ('z', 'c'), pairs)  21.4 us
  transfers between devices with their start and end apart: 23, of which 8 were waited for; matrix products, arithmetic and copies ran while one was open for 4% of the time, Pallas kernels for 28%

profile of v10, /device:TPU:0, one launch (start us, length us, event | category | flops | bytes accessed | tf_op | source)
XLA Modules:
  0.0 308.1 jit_solution(16708165721937303701)
XLA Ops:
  7.2 1.6 copy_multiply_fusion
  8.9 1.5 pad_maximum_fusion.refs_4_
  10.9 2.6 shard_map.120
  13.4 2.5 collective-permute-start
  16.0 23.3 %collective-permute-done.refs_0_.refs_8_ = bf16[512,1024]{1,0:T(8,128)(2,1)} collective-permute-done((bf16[512,1024]{1,0:T(8,128)(2,1)}, bf16[512,1024]{1,0:T(8,128)(2,1)}, u32[]{:S(2)}, u32[]{:S(2)}) %collective-permute-start) | collective-permute-done | bytes 1048608 | tf_op jit(solution)/shard_map/ppermute | solution.py:487
  39.3 1.0 collective-permute-done.1.refs_1_.refs_9_
  40.3 2.3 broadcast_select_fusion.4
  42.6 1.5 collective-permute-start.2
  44.0 1.7 collective-permute-start.3
  45.7 1.3 dynamic-slice_bitcast_fusion.order
  47.0 1.5 collective-permute-start.7
  49.1 1.0 broadcast_select_fusion
  50.2 13.7 %collective-permute-done.2.refs_2_.refs_10_ = bf16[512,1024]{1,0:T(8,128)(2,1)} collective-permute-done((bf16[512,1024]{1,0:T(8,128)(2,1)}, bf16[512,1024]{1,0:T(8,128)(2,1)}, u32[]{:S(2)}, u32[]{:S(2)}) %collective-permute-start.2) | collective-permute-done | bytes 1048608 | tf_op jit(solution)/shard_map/ppermute | solution.py:487
  63.8 0.8 slice.9.weight
  64.8 1.1 broadcast_select_fusion.3.refs_3_.refs_11_
  65.9 1.6 copy.14.weight
  67.5 9.8 %shard_map.121 = (bf16[2048,768]{1,0:T(8,128)(2,1)}, bf16[1536,512]{1,0:T(8,128)(2,1)}, bf16[1536,512]{1,0:T(8,128)(2,1)}, bf16[1536,1024]{1,0:T(8,128)(2,1)}, bf16[1536,1024]{1,0:T(8,128)(2,1)}) custom-call(s32[4]{0:T(128)} %dynamic-slice_bitcast_fusion.order, bf16[1024,768]{1,0:T(8,128)(2,1)} %copy.14.weight, ...), custom_call_target="tpu_custom_call" | custom-call | flops 3221225472 | bytes 18350096 | tf_op jit(solution)/shard_map/pallas_call | solution.py:200
  77.3 7.0 %collective-permute-start.5 = (bf16[1536,512]{1,0:T(8,128)(2,1)}, bf16[1536,512]{1,0:T(8,128)(2,1)S(1)}, u32[]{:S(2)}, u32[]{:S(2)}) collective-permute-start(bf16[1536,512]{1,0:T(8,128)(2,1)} %get-tuple-element.67), channel_id=1, source_target_pairs={{0,1},{1,8},{8,9},{9,16},{16,17},{17,24},{24,25},{2,3},{3,10},{10,... | collective-permute-start | bytes 4718600 | tf_op jit(solution)/shard_map/ppermute | solution.py:456
  84.4 1.3 collective-permute-start.6
  85.7 1.3 broadcast_select_fusion.2
  87.0 2.7 collective-permute-start.9
  89.8 0.7 collective-permute-start.10
  90.5 11.6 %collective-permute-done.9.refs_2_.refs_6_ = bf16[512,1024]{1,0:T(8,128)(2,1)S(1)} collective-permute-done((bf16[512,1024]{1,0:T(8,128)(2,1)S(1)}, bf16[512,1024]{1,0:T(8,128)(2,1)S(1)}, u32[]{:S(2)}, u32[]{:S(2)}) %collective-permute-start.9) | collective-permute-done | bytes 1048608 | tf_op jit(solution)/shard_map/ppermute | solution.py:487
  102.1 1.0 copy-done.7
  103.0 1.1 broadcast_select_fusion.1.refs_3_.refs_7_
  104.1 6.9 %collective-permute-start.11 = (bf16[1536,1024]{1,0:T(8,128)(2,1)}, bf16[1536,1024]{1,0:T(8,128)(2,1)}, u32[]{:S(2)}, u32[]{:S(2)}) collective-permute-start(bf16[1536,1024]{1,0:T(8,128)(2,1)} %get-tuple-element.91), channel_id=1, source_target_pairs={{0,1},{1,8},{8,9},{9,16},{16,17},{17,24},{24,25},{2,3},{3,10},{10,... | collective-permute-start | bytes 9437192 | tf_op jit(solution)/shard_map/ppermute | solution.py:456
  111.1 1.3 collective-permute-start.12
  113.0 1.5 collective-permute-start.15
  114.6 42.1 %shard_map.122 = (bf16[512,512]{1,0:T(8,128)(2,1)}, bf16[512,512]{1,0:T(8,128)(2,1)}, bf16[512,512]{1,0:T(8,128)(2,1)}, bf16[512,512]{1,0:T(8,128)(2,1)}, f32[20...) custom-call(s32[20]{0:T(128)} %pad_dynamic-slice_fusion.cells, ...), custom_call_target="tpu_custom_call" | custom-call | flops 13958643712 | bytes 20447328 | tf_op jit(solution)/shard_map/pallas_call | solution.py:200
  156.6 1.3 collective-permute-start.13
  157.9 3.7 %collective-permute-start.14 = (bf16[1536,512]{1,0:T(8,128)(2,1)}, bf16[1536,512]{1,0:T(8,128)(2,1)S(1)}, u32[]{:S(2)}, u32[]{:S(2)}) collective-permute-start(bf16[1536,512]{1,0:T(8,128)(2,1)} %get-tuple-element.90.refs_14_), channel_id=1, source_target_pairs={{0,1},{1,8},{8,9},{9,16},{16,17},{17,24},{24,25},{2,3},{3,10},{10,... | collective-permute-start | bytes 4718600 | tf_op jit(solution)/shard_map/ppermute | solution.py:456
  161.6 14.5 %shard_map.123 = bf16[1024,1024]{1,0:T(8,128)(2,1)} custom-call(s32[4]{0:T(128)} %dynamic-slice_bitcast_fusion.order, bf16[512,512]{1,0:T(8,128)(2,1)} %get-tuple-element.84.refs_0_, bf16[512,512]{1,0:T(8,128)(2,1)} %get-tuple-element.85.refs_1_, bf16[512,512]{1,0:T(8,128)(2,1)} %get-tuple-element.86.refs_2_, bf16[512,512]{1,0:T(8,128)(2,1)} %get-tuple-element.87.refs_3_, ...), custom_call_target="tpu_custom_call" | custom-call | flops 7516192768 | bytes 26214416 | tf_op jit(solution)/shard_map/pallas_call | solution.py:200
  176.1 1.2 copy-done.4
  177.3 1.1 copy-done.5
  178.4 6.8 %shard_map.124 = (bf16[512,1024]{1,0:T(8,128)(2,1)}, bf16[512,1024]{1,0:T(8,128)(2,1)}, bf16[512,1024]{1,0:T(8,128)(2,1)}, bf16[512,1024]{1,0:T(8,128)(2,1)}) custom-call(s32[4]{0:T(128)} %dynamic-slice_bitcast_fusion.order, f32[2048,512]{1,0:T(8,128)} %get-tuple-element.88.refs_12_.own, bf16[1536,512]{1,0:T(8,128)(2,1)} %copy-done.4, ...), custom_call_target="tpu_custom_call" | custom-call | tf_op jit(solution)/shard_map/pallas_call | solution.py:200
  185.7 4.5 %collective-permute-start.17 = (bf16[512,1024]{1,0:T(8,128)(2,1)}, bf16[512,1024]{1,0:T(8,128)(2,1)S(1)}, u32[]{:S(2)}, u32[]{:S(2)}) collective-permute-start(bf16[512,1024]{1,0:T(8,128)(2,1)} %get-tuple-element.100), channel_id=1, source_target_pairs={{0,3},{1,5},{2,1},{3,7},{4,0},{5,6},{6,2},{7,4},{8,11},{9,13},{10,... | collective-permute-start | bytes 3145736 | tf_op jit(solution)/shard_map/ppermute | solution.py:487
  190.2 3.2 %collective-permute-start.18 = (bf16[512,1024]{1,0:T(8,128)(2,1)}, bf16[512,1024]{1,0:T(8,128)(2,1)S(1)}, u32[]{:S(2)}, u32[]{:S(2)}) collective-permute-start(bf16[512,1024]{1,0:T(8,128)(2,1)} %get-tuple-element.101), channel_id=1, source_target_pairs={{0,1},{1,7},{2,3},{3,5},{4,2},{5,4},{6,0},{7,6},{8,9},{9,15},{10,1... | collective-permute-start | bytes 3145736 | tf_op jit(solution)/shard_map/ppermute | solution.py:487
  193.4 9.4 %collective-permute-start.19 = (bf16[512,1024]{1,0:T(8,128)(2,1)}, bf16[512,1024]{1,0:T(8,128)(2,1)}, u32[]{:S(2)}, u32[]{:S(2)}) collective-permute-start(bf16[512,1024]{1,0:T(8,128)(2,1)} %get-tuple-element.102), channel_id=1, source_target_pairs={{0,0},{1,6},{2,2},{3,4},{4,3},{5,5},{6,1},{7,7},{8,8},{9,14},{10,1... | collective-permute-start | bytes 3145736 | tf_op jit(solution)/shard_map/ppermute | solution.py:487
  202.9 1.6 collective-permute-done.16.refs_0_
  204.5 30.4 %collective-permute-done.17.refs_1_ = bf16[512,1024]{1,0:T(8,128)(2,1)S(1)} collective-permute-done((bf16[512,1024]{1,0:T(8,128)(2,1)}, bf16[512,1024]{1,0:T(8,128)(2,1)S(1)}, u32[]{:S(2)}, u32[]{:S(2)}) %collective-permute-start.17) | collective-permute-done | bytes 1048608 | tf_op jit(solution)/shard_map/ppermute | solution.py:487
  234.9 1.0 copy-done.9
  236.2 31.9 %all-reduce.3.cloned.1.call-done.mine = bf16[1024,1024]{1,0:T(8,128)(2,1)} async-done(((bf16[1024,1024]{1,0:T(8,128)(2,1)}), bf16[1024,1024]{1,0:T(8,128)(2,1)}) %all-reduce.3.cloned.1.call-update) | async-done | bytes 2097168 | tf_op jit(solution)/shard_map/psum | solution.py:543
  268.2 3.5 %collective-permute-start.21 = (bf16[1024,1024]{1,0:T(8,128)(2,1)}, bf16[1024,1024]{1,0:T(8,128)(2,1)S(1)}, u32[]{:S(2)}, u32[]{:S(2)}) collective-permute-start(bf16[1024,1024]{1,0:T(8,128)(2,1)} %all-reduce.3.cloned.1.call-done.mine), channel_id=1, source_target_pairs={{5,1},{7,3},{0,4},{2,6},{13,9},{15,11},{8,12},{10,14},{21,17},{23,... | collective-permute-start | bytes 6291464 | tf_op jit(solution)/shard_map/ppermute | solution.py:487
  271.7 1.2 dynamic-slice_bitcast_fusion.1.leads
  272.9 12.0 %shard_map.125 = (bf16[512,1024]{1,0:T(8,128)(2,1)}, bf16[512,1024]{1,0:T(8,128)(2,1)}) custom-call(s32[4]{0:T(128)} %dynamic-slice_bitcast_fusion.1.leads, bf16[512,1024]{1,0:T(8,128)(2,1)} %tokens.3, f32[1,1024]{1,0:T(1,128)} %bitcast.19, bf16[512,1024]{1,0:T(8,128)(2,1)} %copy-done.8, bf16[512,1024]{1,0:T(8,128)(2,1)} %copy-done.9, ...), custom_call_target="tpu_custom_call" | custom-call | flops 4294967296 | bytes 15732752 | tf_op jit(solution)/shard_map/pallas_call | solution.py:200
  284.9 10.5 %collective-permute-done.21.other = bf16[1024,1024]{1,0:T(8,128)(2,1)S(1)} collective-permute-done((bf16[1024,1024]{1,0:T(8,128)(2,1)}, bf16[1024,1024]{1,0:T(8,128)(2,1)S(1)}, u32[]{:S(2)}, u32[]{:S(2)}) %collective-permute-start.21) | collective-permute-done | bytes 2097184 | tf_op jit(solution)/shard_map/ppermute | solution.py:487
  295.4 1.3 copy-done.2
  296.7 4.5 %shard_map.126 = (f32[4,192,1024]{2,1,0:T(8,128)}, f32[4,64,1024]{2,1,0:T(8,128)}) custom-call(s32[1]{0:T(128)} %bitcast.8.flag, bf16[1024,1024]{1,0:T(8,128)(2,1)} %all-reduce.3.cloned.1.call-done.mine, bf16[1024,1024]{1,0:T(8,128)(2,1)} %copy-done.2), custom_call_target="tpu_custom_call" | custom-call | flops 1048576 | bytes 8388612 | tf_op jit(solution)/shard_map/pallas_call | solution.py:200
  (43 shorter events, 3.0 us)
Async XLA Ops:
  7.2 1.7 copy-start.3
  7.2 261.0 %all-reduce.3.cloned.1.call-start = ((), (), s32[]{:S(2)}) async-start(), calls=%async_computation | async-start | bytes 4194304 | tf_op jit(solution)/shard_map/psum | solution.py:543
  10.4 38.7 %collective-permute-start.4 = (bf16[1024,1024]{1,0:T(8,128)(2,1)}, bf16[1024,1024]{1,0:T(8,128)(2,1)}, u32[]{:S(2)}, u32[]{:S(2)}) collective-permute-start(bf16[1024,1024]{1,0:T(8,128)(2,1)} %pad_maximum_fusion.refs_4_), channel_id=1, source_target_pairs={{0,1},{1,0},{2,3},{3,2},{4,5},{5,4},{6,7},{7,6},{8,9},{9,8},{10,11... | collective-permute-start | bytes 6291464 | tf_op jit(solution)/shard_map/ppermute | solution.py:514
  13.4 33.5 %copy-start.1 = (bf16[512,1024]{1,0:T(8,128)(2,1)S(1)}, bf16[512,1024]{1,0:T(8,128)(2,1)}, u32[]{:S(2)}) copy-start(bf16[512,1024]{1,0:T(8,128)(2,1)} %param.14) | copy-start | bytes 3145732
  13.4 25.8 %collective-permute-start = (bf16[512,1024]{1,0:T(8,128)(2,1)}, bf16[512,1024]{1,0:T(8,128)(2,1)}, u32[]{:S(2)}, u32[]{:S(2)}) collective-permute-start(bf16[512,1024]{1,0:T(8,128)(2,1)} %shard_map.120), channel_id=1, source_target_pairs={{2,0},{4,1},{0,2},{6,3},{1,4},{7,5},{3,6},{5,7},{10,8},{12,9},{8,1... | collective-permute-start | bytes 3145736 | tf_op jit(solution)/shard_map/ppermute | solution.py:487
  15.9 24.3 %collective-permute-start.1 = (bf16[512,1024]{1,0:T(8,128)(2,1)}, bf16[512,1024]{1,0:T(8,128)(2,1)}, u32[]{:S(2)}, u32[]{:S(2)}) collective-permute-start(bf16[512,1024]{1,0:T(8,128)(2,1)} %shard_map.120), channel_id=1, source_target_pairs={{3,0},{5,1},{1,2},{7,3},{0,4},{6,5},{2,6},{4,7},{11,8},{13,9},{9,1... | collective-permute-start | bytes 3145736 | tf_op jit(solution)/shard_map/ppermute | solution.py:487
  42.6 21.3 %collective-permute-start.2 = (bf16[512,1024]{1,0:T(8,128)(2,1)}, bf16[512,1024]{1,0:T(8,128)(2,1)}, u32[]{:S(2)}, u32[]{:S(2)}) collective-permute-start(bf16[512,1024]{1,0:T(8,128)(2,1)} %broadcast_select_fusion.4), channel_id=1, source_target_pairs={{0,4},{1,0},{2,6},{3,2},{4,5},{5,1},{6,7},{7,3},{8,12},{9,8},{10,1... | collective-permute-start | bytes 3145736 | tf_op jit(solution)/shard_map/ppermute | solution.py:487
  44.0 19.8 %collective-permute-start.3 = (bf16[512,1024]{1,0:T(8,128)(2,1)}, bf16[512,1024]{1,0:T(8,128)(2,1)}, u32[]{:S(2)}, u32[]{:S(2)}) collective-permute-start(bf16[512,1024]{1,0:T(8,128)(2,1)} %collective-permute-done.refs_0_.refs_8_), channel_id=1, source_target_pairs={{1,3},{3,1},{4,6},{6,4},{9,11},{11,9},{12,14},{14,12},{17,19},{19,... | collective-permute-start | bytes 3145736 | tf_op jit(solution)/shard_map/ppermute | solution.py:487
  47.0 38.7 %collective-permute-start.7 = (bf16[512,1024]{1,0:T(8,128)(2,1)S(1)}, bf16[512,1024]{1,0:T(8,128)(2,1)}, u32[]{:S(2)}, u32[]{:S(2)}) collective-permute-start(bf16[512,1024]{1,0:T(8,128)(2,1)S(1)} %copy-done.1), channel_id=1, source_target_pairs={{2,0},{4,1},{0,2},{6,3},{1,4},{7,5},{3,6},{5,7},{10,8},{12,9},{8,1... | collective-permute-start | bytes 3145736 | tf_op jit(solution)/shard_map/ppermute | solution.py:487
  48.5 37.2 %collective-permute-start.8 = (bf16[512,1024]{1,0:T(8,128)(2,1)S(1)}, bf16[512,1024]{1,0:T(8,128)(2,1)}, u32[]{:S(2)}, u32[]{:S(2)}) collective-permute-start(bf16[512,1024]{1,0:T(8,128)(2,1)S(1)} %copy-done.1), channel_id=1, source_target_pairs={{3,0},{5,1},{1,2},{7,3},{0,4},{6,5},{2,6},{4,7},{11,8},{13,9},{9,1... | collective-permute-start | bytes 3145736 | tf_op jit(solution)/shard_map/ppermute | solution.py:487
  50.1 14.7 %copy-start = (bf16[512,1024]{1,0:T(8,128)(2,1)S(1)}, bf16[512,1024]{1,0:T(8,128)(2,1)}, u32[]{:S(2)}) copy-start(bf16[512,1024]{1,0:T(8,128)(2,1)} %shard_map.120) | copy-start | bytes 3145732
  77.3 26.8 %collective-permute-start.5 = (bf16[1536,512]{1,0:T(8,128)(2,1)}, bf16[1536,512]{1,0:T(8,128)(2,1)S(1)}, u32[]{:S(2)}, u32[]{:S(2)}) collective-permute-start(bf16[1536,512]{1,0:T(8,128)(2,1)} %get-tuple-element.67), channel_id=1, source_target_pairs={{0,1},{1,8},{8,9},{9,16},{16,17},{17,24},{24,25},{2,3},{3,10},{10,... | collective-permute-start | bytes 4718600 | tf_op jit(solution)/shard_map/ppermute | solution.py:456
  84.4 19.8 %collective-permute-start.6 = (bf16[1536,512]{1,0:T(8,128)(2,1)}, bf16[1536,512]{1,0:T(8,128)(2,1)}, u32[]{:S(2)}, u32[]{:S(2)}) collective-permute-start(bf16[1536,512]{1,0:T(8,128)(2,1)} %get-tuple-element.68), channel_id=1, source_target_pairs={{1,0},{8,1},{9,8},{16,9},{17,16},{24,17},{25,24},{3,2},{10,3},{11,... | collective-permute-start | bytes 4718600 | tf_op jit(solution)/shard_map/ppermute | solution.py:456
  87.0 25.4 %copy-start.11 = (s32[64]{0:T(128)S(1)}, s32[64]{0:T(128)}, u32[]{:S(2)}) copy-start(s32[64]{0:T(128)} %param.13) | copy-start | bytes 772
  87.0 15.0 %collective-permute-start.9 = (bf16[512,1024]{1,0:T(8,128)(2,1)S(1)}, bf16[512,1024]{1,0:T(8,128)(2,1)S(1)}, u32[]{:S(2)}, u32[]{:S(2)}) collective-permute-start(bf16[512,1024]{1,0:T(8,128)(2,1)S(1)} %broadcast_select_fusion.2), channel_id=1, source_target_pairs={{0,4},{1,0},{2,6},{3,2},{4,5},{5,1},{6,7},{7,3},{8,12},{9,8},{10,1... | collective-permute-start | bytes 3145736 | tf_op jit(solution)/shard_map/ppermute | solution.py:487
  89.8 13.3 %collective-permute-start.10 = (bf16[512,1024]{1,0:T(8,128)(2,1)}, bf16[512,1024]{1,0:T(8,128)(2,1)S(1)}, u32[]{:S(2)}, u32[]{:S(2)}) collective-permute-start(bf16[512,1024]{1,0:T(8,128)(2,1)} %collective-permute-done.7.refs_0_.refs_4_), channel_id=1, source_target_pairs={{1,3},{3,1},{4,6},{6,4},{9,11},{11,9},{12,14},{14,12},{17,19},{19,... | collective-permute-start | bytes 3145736 | tf_op jit(solution)/shard_map/ppermute | solution.py:487
  102.1 1.0 copy-start.7
  104.1 10.4 %copy-start.6 = (bf16[1536,512]{1,0:T(8,128)(2,1)}, bf16[1536,512]{1,0:T(8,128)(2,1)S(1)}, u32[]{:S(2)}) copy-start(bf16[1536,512]{1,0:T(8,128)(2,1)S(1)} %collective-permute-done.5.kv_top) | copy-start | bytes 4718596
  104.1 57.5 %collective-permute-start.11 = (bf16[1536,1024]{1,0:T(8,128)(2,1)}, bf16[1536,1024]{1,0:T(8,128)(2,1)}, u32[]{:S(2)}, u32[]{:S(2)}) collective-permute-start(bf16[1536,1024]{1,0:T(8,128)(2,1)} %get-tuple-element.91), channel_id=1, source_target_pairs={{0,1},{1,8},{8,9},{9,16},{16,17},{17,24},{24,25},{2,3},{3,10},{10,... | collective-permute-start | bytes 9437192 | tf_op jit(solution)/shard_map/ppermute | solution.py:456
  111.1 50.5 %collective-permute-start.12 = (bf16[1536,1024]{1,0:T(8,128)(2,1)}, bf16[1536,1024]{1,0:T(8,128)(2,1)}, u32[]{:S(2)}, u32[]{:S(2)}) collective-permute-start(bf16[1536,1024]{1,0:T(8,128)(2,1)} %get-tuple-element.92), channel_id=1, source_target_pairs={{1,0},{8,1},{9,8},{16,9},{17,16},{24,17},{25,24},{3,2},{10,3},{11,... | collective-permute-start | bytes 9437192 | tf_op jit(solution)/shard_map/ppermute | solution.py:456
  113.0 72.2 %collective-permute-start.15 = (bf16[1024,1024]{1,0:T(8,128)(2,1)}, bf16[1024,1024]{1,0:T(8,128)(2,1)}, u32[]{:S(2)}, u32[]{:S(2)}) collective-permute-start(bf16[1024,1024]{1,0:T(8,128)(2,1)} %pad_maximum_fusion.refs_4_), channel_id=1, source_target_pairs={{2,0},{0,2},{3,1},{1,3},{6,4},{4,6},{7,5},{5,7},{10,8},{8,10},{11,... | collective-permute-start | bytes 6291464 | tf_op jit(solution)/shard_map/ppermute | solution.py:511
  156.6 19.5 %collective-permute-start.13 = (bf16[1536,512]{1,0:T(8,128)(2,1)}, bf16[1536,512]{1,0:T(8,128)(2,1)S(1)}, u32[]{:S(2)}, u32[]{:S(2)}) collective-permute-start(bf16[1536,512]{1,0:T(8,128)(2,1)} %get-tuple-element.89.refs_13_), channel_id=1, source_target_pairs={{1,0},{8,1},{9,8},{16,9},{17,16},{24,17},{25,24},{3,2},{10,3},{11,... | collective-permute-start | bytes 4718600 | tf_op jit(solution)/shard_map/ppermute | solution.py:456
  157.9 18.2 %collective-permute-start.14 = (bf16[1536,512]{1,0:T(8,128)(2,1)}, bf16[1536,512]{1,0:T(8,128)(2,1)S(1)}, u32[]{:S(2)}, u32[]{:S(2)}) collective-permute-start(bf16[1536,512]{1,0:T(8,128)(2,1)} %get-tuple-element.90.refs_14_), channel_id=1, source_target_pairs={{0,1},{1,8},{8,9},{9,16},{16,17},{17,24},{24,25},{2,3},{3,10},{10,... | collective-permute-start | bytes 4718600 | tf_op jit(solution)/shard_map/ppermute | solution.py:456
  176.1 1.2 copy-start.4
  177.3 1.1 copy-start.5
  185.2 19.2 %collective-permute-start.16 = (bf16[512,1024]{1,0:T(8,128)(2,1)}, bf16[512,1024]{1,0:T(8,128)(2,1)S(1)}, u32[]{:S(2)}, u32[]{:S(2)}) collective-permute-start(bf16[512,1024]{1,0:T(8,128)(2,1)} %get-tuple-element.99), channel_id=1, source_target_pairs={{0,2},{1,4},{2,0},{3,6},{4,1},{5,7},{6,3},{7,5},{8,10},{9,12},{10,... | collective-permute-start | bytes 3145736 | tf_op jit(solution)/shard_map/ppermute | solution.py:487
  185.7 49.2 %collective-permute-start.17 = (bf16[512,1024]{1,0:T(8,128)(2,1)}, bf16[512,1024]{1,0:T(8,128)(2,1)S(1)}, u32[]{:S(2)}, u32[]{:S(2)}) collective-permute-start(bf16[512,1024]{1,0:T(8,128)(2,1)} %get-tuple-element.100), channel_id=1, source_target_pairs={{0,3},{1,5},{2,1},{3,7},{4,0},{5,6},{6,2},{7,4},{8,11},{9,13},{10,... | collective-permute-start | bytes 3145736 | tf_op jit(solution)/shard_map/ppermute | solution.py:487
  190.2 44.7 %collective-permute-start.18 = (bf16[512,1024]{1,0:T(8,128)(2,1)}, bf16[512,1024]{1,0:T(8,128)(2,1)S(1)}, u32[]{:S(2)}, u32[]{:S(2)}) collective-permute-start(bf16[512,1024]{1,0:T(8,128)(2,1)} %get-tuple-element.101), channel_id=1, source_target_pairs={{0,1},{1,7},{2,3},{3,5},{4,2},{5,4},{6,0},{7,6},{8,9},{9,15},{10,1... | collective-permute-start | bytes 3145736 | tf_op jit(solution)/shard_map/ppermute | solution.py:487
  193.4 41.6 %collective-permute-start.19 = (bf16[512,1024]{1,0:T(8,128)(2,1)}, bf16[512,1024]{1,0:T(8,128)(2,1)}, u32[]{:S(2)}, u32[]{:S(2)}) collective-permute-start(bf16[512,1024]{1,0:T(8,128)(2,1)} %get-tuple-element.102), channel_id=1, source_target_pairs={{0,0},{1,6},{2,2},{3,4},{4,3},{5,5},{6,1},{7,7},{8,8},{9,14},{10,1... | collective-permute-start | bytes 3145736 | tf_op jit(solution)/shard_map/ppermute | solution.py:487
  202.8 70.1 %collective-permute-start.20 = (bf16[1024,1024]{1,0:T(8,128)(2,1)}, bf16[1024,1024]{1,0:T(8,128)(2,1)}, u32[]{:S(2)}, u32[]{:S(2)}) collective-permute-start(bf16[1024,1024]{1,0:T(8,128)(2,1)} %collective-permute-done.15.refs_5_), channel_id=1, source_target_pairs={{0,1},{1,0},{2,3},{3,2},{4,5},{5,4},{6,7},{7,6},{8,9},{9,8},{10,11... | collective-permute-start | bytes 6291464 | tf_op jit(solution)/shard_map/ppermute | solution.py:514
  204.5 68.4 %copy-start.8 = (bf16[512,1024]{1,0:T(8,128)(2,1)}, bf16[512,1024]{1,0:T(8,128)(2,1)S(1)}, u32[]{:S(2)}) copy-start(bf16[512,1024]{1,0:T(8,128)(2,1)S(1)} %collective-permute-done.16.refs_0_) | copy-start | bytes 3145732
  234.9 1.0 copy-start.9
  234.9 1.3 copy-start.10
  268.2 27.2 %collective-permute-start.21 = (bf16[1024,1024]{1,0:T(8,128)(2,1)}, bf16[1024,1024]{1,0:T(8,128)(2,1)S(1)}, u32[]{:S(2)}, u32[]{:S(2)}) collective-permute-start(bf16[1024,1024]{1,0:T(8,128)(2,1)} %all-reduce.3.cloned.1.call-done.mine), channel_id=1, source_target_pairs={{5,1},{7,3},{0,4},{2,6},{13,9},{15,11},{8,12},{10,14},{21,17},{23,... | collective-permute-start | bytes 6291464 | tf_op jit(solution)/shard_map/ppermute | solution.py:487
  295.4 1.3 copy-start.2
Sparse Core Ops, SparseCore 0:
  202.9 65.1 all-reduce.2

commit v11 on v10

--- a/solution.py
+++ b/solution.py
@@ -527,7 +527,7 @@
     *normed_parts, group_qkv, group_out = lax.optimization_barrier((*normed_parts, group_qkv, group_out))
     qkv, kv_up, kv_down, normed_up, normed_down = projections(order, group_qkv, normed_parts)
     kv_top, kv_bot = passed_along(kv_up, 1), passed_along(kv_down, -1)
-    upstream_parts, _ = gathered(after(upstream, *hop), qkv)
+    upstream_parts, _ = gathered(after(upstream, *normed_parts), qkv)
 
     kv_top, kv_bot, normed_up, normed_down, *upstream_parts = lax.optimization_barrier(
         (kv_top, kv_bot, normed_up, normed_down, *upstream_parts)
@@ -544,6 +544,7 @@
     parts = joined(after(order, grads), dkv, from_above, from_below, outq_parts)
     parts, ahead = lax.optimization_barrier((parts, ahead))
     parts_own = send_back(parts)
+    ahead = [after(block, grads_sum) for block in ahead]
     blocks += ahead + [sibling] + [from_sibling(block) for block in ahead]
     update, grad_input = token_outputs(leads, tokens, gain, parts_own, blocks)
     grads = after(grads_sum, *parts_own)

time: 309 us -> 282 us (0.913)
  waiting for transfers between devices: 124 us -> 105 us
  starting transfers between devices: 55.9 us -> 46.9 us
    ppermute x13, waiting for transfers between devices: 92.1 us -> 62.7 us  [permuted(): return lax.ppermute(x, GROUP, [(at(*a), at(*b)) for a, b in pairs])]
    psum x1, waiting for transfers between devices: 31.9 us -> 42.2 us  [on_device(): grads_sum = lax.psum(grads, ('z', 'c'))]
    ppermute x6, starting transfers between devices: 21.4 us -> 14.8 us  [passed_along(): return lax.ppermute(x, ('z', 'c'), pairs)]
    unnamed x24 -> x28, local copies, waits for them, and re-layouts: 5.92 us -> 6.84 us
  transfers between devices with their start and end apart: 23 -> 23, of which waited for: 8 -> 8; matrix products, arithmetic and copies ran while one was open for 4% -> 4% of each run, Pallas kernels for 28% -> 31%
where the time goes in v11:
time: 282 us; the launch traced here: 281 us
  waiting for transfers between devices  105 us (37%)
  Pallas kernels  92.2 us (33%)
  starting transfers between devices  46.9 us (17%)
  between operations  14.3 us (5%)
  local copies, waits for them, and re-layouts  12.6 us (4%)
  other arithmetic  9.51 us (3%)
    pallas_call x7, Pallas kernels, call(): pl.pallas_call(kernel, out_shape=tuple(out_shape), in_specs=list(in_specs...  92.2 us
    ppermute x13, waiting for transfers between devices, permuted(): return lax.ppermute(x, GROUP, [(at(*a), at(*b)) for a, b in pairs])  62.7 us
    psum x1, waiting for transfers between devices, on_device(): grads_sum = lax.psum(grads, ('z', 'c'))  42.2 us
    ppermute x13, starting transfers between devices, permuted(): return lax.ppermute(x, GROUP, [(at(*a), at(*b)) for a, b in pairs])  30.4 us
    ppermute x6, starting transfers between devices, passed_along(): return lax.ppermute(x, ('z', 'c'), pairs)  14.8 us
    unnamed x28, local copies, waits for them, and re-layouts  6.84 us
  transfers between devices with their start and end apart: 23, of which 8 were waited for; matrix products, arithmetic and copies ran while one was open for 4% of the time, Pallas kernels for 31%

profile of v11, /device:TPU:0, one launch (start us, length us, event | category | flops | bytes accessed | tf_op | source)
XLA Modules:
  0.0 280.5 jit_solution(8464919183869769830)
XLA Ops:
  7.2 1.6 copy_multiply_fusion
  8.9 1.5 pad_maximum_fusion.refs_4_
  10.8 2.6 shard_map.120
  13.4 2.5 collective-permute-start
  16.0 23.3 %collective-permute-done.refs_0_.refs_8_ = bf16[512,1024]{1,0:T(8,128)(2,1)} collective-permute-done((bf16[512,1024]{1,0:T(8,128)(2,1)}, bf16[512,1024]{1,0:T(8,128)(2,1)}, u32[]{:S(2)}, u32[]{:S(2)}) %collective-permute-start) | collective-permute-done | bytes 1048608 | tf_op jit(solution)/shard_map/ppermute | solution.py:487
  39.3 0.9 collective-permute-done.1.refs_1_.refs_9_
  40.1 1.7 broadcast_select_fusion.4
  41.9 1.5 collective-permute-start.2
  44.1 1.0 broadcast_select_fusion
  45.1 0.8 slice.9.weight
  46.1 9.6 %collective-permute-done.2.refs_2_.refs_10_ = bf16[512,1024]{1,0:T(8,128)(2,1)S(1)} collective-permute-done((bf16[512,1024]{1,0:T(8,128)(2,1)S(1)}, bf16[512,1024]{1,0:T(8,128)(2,1)S(1)}, u32[]{:S(2)}, u32[]{:S(2)}) %collective-permute-start.2) | collective-permute-done | bytes 1048608 | tf_op jit(solution)/shard_map/ppermute | solution.py:487
  55.7 1.2 broadcast_select_fusion.3.refs_3_.refs_11_
  57.0 1.5 collective-permute-start.7
  58.5 3.8 %collective-permute-start.8 = (bf16[512,1024]{1,0:T(8,128)(2,1)S(1)}, bf16[512,1024]{1,0:T(8,128)(2,1)}, u32[]{:S(2)}, u32[]{:S(2)}) collective-permute-start(bf16[512,1024]{1,0:T(8,128)(2,1)S(1)} %copy-done.1), channel_id=1, source_target_pairs={{3,0},{5,1},{1,2},{7,3},{0,4},{6,5},{2,6},{4,7},{11,8},{13,9},{9,1... | collective-permute-start | bytes 3145736 | tf_op jit(solution)/shard_map/ppermute | solution.py:487
  62.3 1.3 dynamic-slice_bitcast_fusion.order
  63.6 1.6 copy.14.weight
  65.2 9.8 %shard_map.121 = (bf16[2048,768]{1,0:T(8,128)(2,1)}, bf16[1536,512]{1,0:T(8,128)(2,1)}, bf16[1536,512]{1,0:T(8,128)(2,1)}, bf16[1536,1024]{1,0:T(8,128)(2,1)}, bf16[1536,1024]{1,0:T(8,128)(2,1)}) custom-call(s32[4]{0:T(128)} %dynamic-slice_bitcast_fusion.order, bf16[1024,768]{1,0:T(8,128)(2,1)} %copy.14.weight, ...), custom_call_target="tpu_custom_call" | custom-call | flops 3221225472 | bytes 18350096 | tf_op jit(solution)/shard_map/pallas_call | solution.py:200
  75.0 2.1 collective-permute-start.5
  77.0 1.3 collective-permute-start.6
  78.3 0.8 collective-permute-done.7.refs_0_.refs_4_
  79.2 6.1 %collective-permute-done.8.refs_1_.refs_5_ = bf16[512,1024]{1,0:T(8,128)(2,1)} collective-permute-done((bf16[512,1024]{1,0:T(8,128)(2,1)S(1)}, bf16[512,1024]{1,0:T(8,128)(2,1)}, u32[]{:S(2)}, u32[]{:S(2)}) %collective-permute-start.8) | collective-permute-done | bytes 1048608 | tf_op jit(solution)/shard_map/ppermute | solution.py:487
  85.2 1.3 broadcast_select_fusion.2
  86.6 1.4 collective-permute-start.9
  88.7 11.6 %collective-permute-done.9.refs_2_.refs_6_ = bf16[512,1024]{1,0:T(8,128)(2,1)S(1)} collective-permute-done((bf16[512,1024]{1,0:T(8,128)(2,1)S(1)}, bf16[512,1024]{1,0:T(8,128)(2,1)S(1)}, u32[]{:S(2)}, u32[]{:S(2)}) %collective-permute-start.9) | collective-permute-done | bytes 1048608 | tf_op jit(solution)/shard_map/ppermute | solution.py:487
  100.3 1.0 copy-done.9
  101.3 1.1 broadcast_select_fusion.1.refs_3_.refs_7_
  102.4 5.2 %collective-permute-start.11 = (bf16[1536,1024]{1,0:T(8,128)(2,1)}, bf16[1536,1024]{1,0:T(8,128)(2,1)}, u32[]{:S(2)}, u32[]{:S(2)}) collective-permute-start(bf16[1536,1024]{1,0:T(8,128)(2,1)} %get-tuple-element.92), channel_id=1, source_target_pairs={{0,1},{1,8},{8,9},{9,16},{16,17},{17,24},{24,25},{2,3},{3,10},{10,... | collective-permute-start | bytes 9437192 | tf_op jit(solution)/shard_map/ppermute | solution.py:456
  107.6 1.3 collective-permute-start.12
  109.6 1.2 collective-permute-start.15
  110.8 42.1 %shard_map.122 = (bf16[512,512]{1,0:T(8,128)(2,1)}, bf16[512,512]{1,0:T(8,128)(2,1)}, bf16[512,512]{1,0:T(8,128)(2,1)}, bf16[512,512]{1,0:T(8,128)(2,1)}, f32[20...) custom-call(s32[20]{0:T(128)} %pad_dynamic-slice_fusion.cells, ...), custom_call_target="tpu_custom_call" | custom-call | flops 13958643712 | bytes 20447328 | tf_op jit(solution)/shard_map/pallas_call | solution.py:200
  152.9 1.3 collective-permute-start.13
  154.2 3.7 %collective-permute-start.14 = (bf16[1536,512]{1,0:T(8,128)(2,1)}, bf16[1536,512]{1,0:T(8,128)(2,1)S(1)}, u32[]{:S(2)}, u32[]{:S(2)}) collective-permute-start(bf16[1536,512]{1,0:T(8,128)(2,1)} %get-tuple-element.91.refs_14_), channel_id=1, source_target_pairs={{0,1},{1,8},{8,9},{9,16},{16,17},{17,24},{24,25},{2,3},{3,10},{10,... | collective-permute-start | bytes 4718600 | tf_op jit(solution)/shard_map/ppermute | solution.py:456
  157.9 14.5 %shard_map.123 = bf16[1024,1024]{1,0:T(8,128)(2,1)} custom-call(s32[4]{0:T(128)} %dynamic-slice_bitcast_fusion.order, bf16[512,512]{1,0:T(8,128)(2,1)} %get-tuple-element.85.refs_0_, bf16[512,512]{1,0:T(8,128)(2,1)} %get-tuple-element.86.refs_1_, bf16[512,512]{1,0:T(8,128)(2,1)} %get-tuple-element.87.refs_2_, bf16[512,512]{1,0:T(8,128)(2,1)} %get-tuple-element.88.refs_3_, ...), custom_call_target="tpu_custom_call" | custom-call | flops 7516192768 | bytes 26214416 | tf_op jit(solution)/shard_map/pallas_call | solution.py:200
  172.5 1.2 copy-done.4
  173.6 1.2 copy-done.5
  174.8 6.8 %shard_map.124 = (bf16[512,1024]{1,0:T(8,128)(2,1)}, bf16[512,1024]{1,0:T(8,128)(2,1)}, bf16[512,1024]{1,0:T(8,128)(2,1)}, bf16[512,1024]{1,0:T(8,128)(2,1)}) custom-call(s32[4]{0:T(128)} %dynamic-slice_bitcast_fusion.order, f32[2048,512]{1,0:T(8,128)} %get-tuple-element.89.refs_12_.own, bf16[1536,512]{1,0:T(8,128)(2,1)} %copy-done.4, ...), custom_call_target="tpu_custom_call" | custom-call | tf_op jit(solution)/shard_map/pallas_call | solution.py:200
  182.4 3.2 %collective-permute-start.17 = (bf16[512,1024]{1,0:T(8,128)(2,1)}, bf16[512,1024]{1,0:T(8,128)(2,1)S(1)}, u32[]{:S(2)}, u32[]{:S(2)}) collective-permute-start(bf16[512,1024]{1,0:T(8,128)(2,1)} %get-tuple-element.101), channel_id=1, source_target_pairs={{0,3},{1,5},{2,1},{3,7},{4,0},{5,6},{6,2},{7,4},{8,11},{9,13},{10,... | collective-permute-start | bytes 3145736 | tf_op jit(solution)/shard_map/ppermute | solution.py:487
  185.6 1.2 collective-permute-start.18
  186.8 9.5 %collective-permute-start.19 = (bf16[512,1024]{1,0:T(8,128)(2,1)}, bf16[512,1024]{1,0:T(8,128)(2,1)}, u32[]{:S(2)}, u32[]{:S(2)}) collective-permute-start(bf16[512,1024]{1,0:T(8,128)(2,1)} %get-tuple-element.103), channel_id=1, source_target_pairs={{0,0},{1,6},{2,2},{3,4},{4,3},{5,5},{6,1},{7,7},{8,8},{9,14},{10,1... | collective-permute-start | bytes 3145736 | tf_op jit(solution)/shard_map/ppermute | solution.py:487
  196.3 42.2 %all-reduce.3.cloned.1.call-done.mine = bf16[1024,1024]{1,0:T(8,128)(2,1)} async-done(((bf16[1024,1024]{1,0:T(8,128)(2,1)}), bf16[1024,1024]{1,0:T(8,128)(2,1)}) %all-reduce.3.cloned.1.call-update) | async-done | bytes 2097168 | tf_op jit(solution)/shard_map/psum | solution.py:543
  238.5 1.0 copy-done.11
  239.5 1.0 copy-done.12
  240.5 3.6 %collective-permute-start.21 = (bf16[1024,1024]{1,0:T(8,128)(2,1)}, bf16[1024,1024]{1,0:T(8,128)(2,1)S(1)}, u32[]{:S(2)}, u32[]{:S(2)}) collective-permute-start(bf16[1024,1024]{1,0:T(8,128)(2,1)} %all-reduce.3.cloned.1.call-done.mine), channel_id=1, source_target_pairs={{5,1},{7,3},{0,4},{2,6},{13,9},{15,11},{8,12},{10,14},{21,17},{23,... | collective-permute-start | bytes 6291464 | tf_op jit(solution)/shard_map/ppermute | solution.py:487
  244.1 1.3 dynamic-slice_bitcast_fusion.1.leads
  245.4 12.0 %shard_map.125 = (bf16[512,1024]{1,0:T(8,128)(2,1)}, bf16[512,1024]{1,0:T(8,128)(2,1)}) custom-call(s32[4]{0:T(128)} %dynamic-slice_bitcast_fusion.1.leads, bf16[512,1024]{1,0:T(8,128)(2,1)} %tokens.3, f32[1,1024]{1,0:T(1,128)} %bitcast.19, bf16[512,1024]{1,0:T(8,128)(2,1)} %copy-done.10, bf16[512,1024]{1,0:T(8,128)(2,1)} %copy-done.11, ...), custom_call_target="tpu_custom_call" | custom-call | flops 4294967296 | bytes 15732752 | tf_op jit(solution)/shard_map/pallas_call | solution.py:200
  257.4 10.4 %collective-permute-done.21.other = bf16[1024,1024]{1,0:T(8,128)(2,1)S(1)} collective-permute-done((bf16[1024,1024]{1,0:T(8,128)(2,1)}, bf16[1024,1024]{1,0:T(8,128)(2,1)S(1)}, u32[]{:S(2)}, u32[]{:S(2)}) %collective-permute-start.21) | collective-permute-done | bytes 2097184 | tf_op jit(solution)/shard_map/ppermute | solution.py:487
  267.8 1.4 copy-done.2
  269.2 4.5 %shard_map.126 = (f32[4,192,1024]{2,1,0:T(8,128)}, f32[4,64,1024]{2,1,0:T(8,128)}) custom-call(s32[1]{0:T(128)} %bitcast.8.flag, bf16[1024,1024]{1,0:T(8,128)(2,1)} %all-reduce.3.cloned.1.call-done.mine, bf16[1024,1024]{1,0:T(8,128)(2,1)} %copy-done.2), custom_call_target="tpu_custom_call" | custom-call | flops 1048576 | bytes 8388612 | tf_op jit(solution)/shard_map/pallas_call | solution.py:200
  (47 shorter events, 3.8 us)
Async XLA Ops:
  7.2 1.7 copy-start.3
  7.2 231.3 %all-reduce.3.cloned.1.call-start = ((), (), s32[]{:S(2)}) async-start(), calls=%async_computation | async-start | bytes 4194304 | tf_op jit(solution)/shard_map/psum | solution.py:543
  10.4 33.7 %collective-permute-start.4 = (bf16[1024,1024]{1,0:T(8,128)(2,1)}, bf16[1024,1024]{1,0:T(8,128)(2,1)}, u32[]{:S(2)}, u32[]{:S(2)}) collective-permute-start(bf16[1024,1024]{1,0:T(8,128)(2,1)} %pad_maximum_fusion.refs_4_), channel_id=1, source_target_pairs={{0,1},{1,0},{2,3},{3,2},{4,5},{5,4},{6,7},{7,6},{8,9},{9,8},{10,11... | collective-permute-start | bytes 6291464 | tf_op jit(solution)/shard_map/ppermute | solution.py:514
  13.4 25.8 %collective-permute-start = (bf16[512,1024]{1,0:T(8,128)(2,1)}, bf16[512,1024]{1,0:T(8,128)(2,1)}, u32[]{:S(2)}, u32[]{:S(2)}) collective-permute-start(bf16[512,1024]{1,0:T(8,128)(2,1)} %shard_map.120), channel_id=1, source_target_pairs={{2,0},{4,1},{0,2},{6,3},{1,4},{7,5},{3,6},{5,7},{10,8},{12,9},{8,1... | collective-permute-start | bytes 3145736 | tf_op jit(solution)/shard_map/ppermute | solution.py:487
  15.9 24.2 %collective-permute-start.1 = (bf16[512,1024]{1,0:T(8,128)(2,1)}, bf16[512,1024]{1,0:T(8,128)(2,1)S(1)}, u32[]{:S(2)}, u32[]{:S(2)}) collective-permute-start(bf16[512,1024]{1,0:T(8,128)(2,1)} %shard_map.120), channel_id=1, source_target_pairs={{3,0},{5,1},{1,2},{7,3},{0,4},{6,5},{2,6},{4,7},{11,8},{13,9},{9,1... | collective-permute-start | bytes 3145736 | tf_op jit(solution)/shard_map/ppermute | solution.py:487
  40.1 5.0 %copy-start.7 = (bf16[512,1024]{1,0:T(8,128)(2,1)}, bf16[512,1024]{1,0:T(8,128)(2,1)S(1)}, u32[]{:S(2)}) copy-start(bf16[512,1024]{1,0:T(8,128)(2,1)S(1)} %collective-permute-done.1.refs_1_.refs_9_) | copy-start | bytes 3145732
  41.9 13.8 %collective-permute-start.2 = (bf16[512,1024]{1,0:T(8,128)(2,1)S(1)}, bf16[512,1024]{1,0:T(8,128)(2,1)S(1)}, u32[]{:S(2)}, u32[]{:S(2)}) collective-permute-start(bf16[512,1024]{1,0:T(8,128)(2,1)S(1)} %broadcast_select_fusion.4), channel_id=1, source_target_pairs={{0,4},{1,0},{2,6},{3,2},{4,5},{5,1},{6,7},{7,3},{8,12},{9,8},{10,1... | collective-permute-start | bytes 3145736 | tf_op jit(solution)/shard_map/ppermute | solution.py:487
  43.4 12.3 %collective-permute-start.3 = (bf16[512,1024]{1,0:T(8,128)(2,1)}, bf16[512,1024]{1,0:T(8,128)(2,1)S(1)}, u32[]{:S(2)}, u32[]{:S(2)}) collective-permute-start(bf16[512,1024]{1,0:T(8,128)(2,1)} %collective-permute-done.refs_0_.refs_8_), channel_id=1, source_target_pairs={{1,3},{3,1},{4,6},{6,4},{9,11},{11,9},{12,14},{14,12},{17,19},{19,... | collective-permute-start | bytes 3145736 | tf_op jit(solution)/shard_map/ppermute | solution.py:487
  45.1 10.6 %copy-start = (bf16[512,1024]{1,0:T(8,128)(2,1)S(1)}, bf16[512,1024]{1,0:T(8,128)(2,1)}, u32[]{:S(2)}) copy-start(bf16[512,1024]{1,0:T(8,128)(2,1)} %shard_map.120) | copy-start | bytes 3145732
  46.1 10.9 %copy-start.1 = (bf16[512,1024]{1,0:T(8,128)(2,1)S(1)}, bf16[512,1024]{1,0:T(8,128)(2,1)}, u32[]{:S(2)}) copy-start(bf16[512,1024]{1,0:T(8,128)(2,1)} %param.14) | copy-start | bytes 3145732
  55.7 1.3 copy-start.8
  57.0 22.2 %collective-permute-start.7 = (bf16[512,1024]{1,0:T(8,128)(2,1)S(1)}, bf16[512,1024]{1,0:T(8,128)(2,1)}, u32[]{:S(2)}, u32[]{:S(2)}) collective-permute-start(bf16[512,1024]{1,0:T(8,128)(2,1)S(1)} %copy-done.1), channel_id=1, source_target_pairs={{2,0},{4,1},{0,2},{6,3},{1,4},{7,5},{3,6},{5,7},{10,8},{12,9},{8,1... | collective-permute-start | bytes 3145736 | tf_op jit(solution)/shard_map/ppermute | solution.py:487
  58.5 26.8 %collective-permute-start.8 = (bf16[512,1024]{1,0:T(8,128)(2,1)S(1)}, bf16[512,1024]{1,0:T(8,128)(2,1)}, u32[]{:S(2)}, u32[]{:S(2)}) collective-permute-start(bf16[512,1024]{1,0:T(8,128)(2,1)S(1)} %copy-done.1), channel_id=1, source_target_pairs={{3,0},{5,1},{1,2},{7,3},{0,4},{6,5},{2,6},{4,7},{11,8},{13,9},{9,1... | collective-permute-start | bytes 3145736 | tf_op jit(solution)/shard_map/ppermute | solution.py:487
  75.0 27.4 %collective-permute-start.5 = (bf16[1536,512]{1,0:T(8,128)(2,1)}, bf16[1536,512]{1,0:T(8,128)(2,1)S(1)}, u32[]{:S(2)}, u32[]{:S(2)}) collective-permute-start(bf16[1536,512]{1,0:T(8,128)(2,1)} %get-tuple-element.68), channel_id=1, source_target_pairs={{0,1},{1,8},{8,9},{9,16},{16,17},{17,24},{24,25},{2,3},{3,10},{10,... | collective-permute-start | bytes 4718600 | tf_op jit(solution)/shard_map/ppermute | solution.py:456
  77.0 25.4 %collective-permute-start.6 = (bf16[1536,512]{1,0:T(8,128)(2,1)}, bf16[1536,512]{1,0:T(8,128)(2,1)}, u32[]{:S(2)}, u32[]{:S(2)}) collective-permute-start(bf16[1536,512]{1,0:T(8,128)(2,1)} %get-tuple-element.69), channel_id=1, source_target_pairs={{1,0},{8,1},{9,8},{16,9},{17,16},{24,17},{25,24},{3,2},{10,3},{11,... | collective-permute-start | bytes 4718600 | tf_op jit(solution)/shard_map/ppermute | solution.py:456
  86.6 22.3 %copy-start.13 = (s32[64]{0:T(128)S(1)}, s32[64]{0:T(128)}, u32[]{:S(2)}) copy-start(s32[64]{0:T(128)} %param.13) | copy-start | bytes 772
  86.6 13.7 %collective-permute-start.9 = (bf16[512,1024]{1,0:T(8,128)(2,1)S(1)}, bf16[512,1024]{1,0:T(8,128)(2,1)S(1)}, u32[]{:S(2)}, u32[]{:S(2)}) collective-permute-start(bf16[512,1024]{1,0:T(8,128)(2,1)S(1)} %broadcast_select_fusion.2), channel_id=1, source_target_pairs={{0,4},{1,0},{2,6},{3,2},{4,5},{5,1},{6,7},{7,3},{8,12},{9,8},{10,1... | collective-permute-start | bytes 3145736 | tf_op jit(solution)/shard_map/ppermute | solution.py:487
  88.0 13.3 %collective-permute-start.10 = (bf16[512,1024]{1,0:T(8,128)(2,1)}, bf16[512,1024]{1,0:T(8,128)(2,1)S(1)}, u32[]{:S(2)}, u32[]{:S(2)}) collective-permute-start(bf16[512,1024]{1,0:T(8,128)(2,1)} %collective-permute-done.7.refs_0_.refs_4_), channel_id=1, source_target_pairs={{1,3},{3,1},{4,6},{6,4},{9,11},{11,9},{12,14},{14,12},{17,19},{19,... | collective-permute-start | bytes 3145736 | tf_op jit(solution)/shard_map/ppermute | solution.py:487
  100.3 1.0 copy-start.9
  102.4 8.4 %copy-start.6 = (bf16[1536,512]{1,0:T(8,128)(2,1)}, bf16[1536,512]{1,0:T(8,128)(2,1)S(1)}, u32[]{:S(2)}) copy-start(bf16[1536,512]{1,0:T(8,128)(2,1)S(1)} %collective-permute-done.5.kv_top) | copy-start | bytes 4718596
  102.4 55.5 %collective-permute-start.11 = (bf16[1536,1024]{1,0:T(8,128)(2,1)}, bf16[1536,1024]{1,0:T(8,128)(2,1)}, u32[]{:S(2)}, u32[]{:S(2)}) collective-permute-start(bf16[1536,1024]{1,0:T(8,128)(2,1)} %get-tuple-element.92), channel_id=1, source_target_pairs={{0,1},{1,8},{8,9},{9,16},{16,17},{17,24},{24,25},{2,3},{3,10},{10,... | collective-permute-start | bytes 9437192 | tf_op jit(solution)/shard_map/ppermute | solution.py:456
  107.6 50.3 %collective-permute-start.12 = (bf16[1536,1024]{1,0:T(8,128)(2,1)}, bf16[1536,1024]{1,0:T(8,128)(2,1)}, u32[]{:S(2)}, u32[]{:S(2)}) collective-permute-start(bf16[1536,1024]{1,0:T(8,128)(2,1)} %get-tuple-element.93), channel_id=1, source_target_pairs={{1,0},{8,1},{9,8},{16,9},{17,16},{24,17},{25,24},{3,2},{10,3},{11,... | collective-permute-start | bytes 9437192 | tf_op jit(solution)/shard_map/ppermute | solution.py:456
  109.6 72.0 %collective-permute-start.15 = (bf16[1024,1024]{1,0:T(8,128)(2,1)}, bf16[1024,1024]{1,0:T(8,128)(2,1)}, u32[]{:S(2)}, u32[]{:S(2)}) collective-permute-start(bf16[1024,1024]{1,0:T(8,128)(2,1)} %pad_maximum_fusion.refs_4_), channel_id=1, source_target_pairs={{2,0},{0,2},{3,1},{1,3},{6,4},{4,6},{7,5},{5,7},{10,8},{8,10},{11,... | collective-permute-start | bytes 6291464 | tf_op jit(solution)/shard_map/ppermute | solution.py:511
  152.9 19.5 %collective-permute-start.13 = (bf16[1536,512]{1,0:T(8,128)(2,1)}, bf16[1536,512]{1,0:T(8,128)(2,1)S(1)}, u32[]{:S(2)}, u32[]{:S(2)}) collective-permute-start(bf16[1536,512]{1,0:T(8,128)(2,1)} %get-tuple-element.90.refs_13_), channel_id=1, source_target_pairs={{1,0},{8,1},{9,8},{16,9},{17,16},{24,17},{25,24},{3,2},{10,3},{11,... | collective-permute-start | bytes 4718600 | tf_op jit(solution)/shard_map/ppermute | solution.py:456
  154.2 18.2 %collective-permute-start.14 = (bf16[1536,512]{1,0:T(8,128)(2,1)}, bf16[1536,512]{1,0:T(8,128)(2,1)S(1)}, u32[]{:S(2)}, u32[]{:S(2)}) collective-permute-start(bf16[1536,512]{1,0:T(8,128)(2,1)} %get-tuple-element.91.refs_14_), channel_id=1, source_target_pairs={{0,1},{1,8},{8,9},{9,16},{16,17},{17,24},{24,25},{2,3},{3,10},{10,... | collective-permute-start | bytes 4718600 | tf_op jit(solution)/shard_map/ppermute | solution.py:456
  172.4 1.2 copy-start.4
  173.6 1.2 copy-start.5
  181.6 56.9 %collective-permute-start.16 = (bf16[512,1024]{1,0:T(8,128)(2,1)}, bf16[512,1024]{1,0:T(8,128)(2,1)S(1)}, u32[]{:S(2)}, u32[]{:S(2)}) collective-permute-start(bf16[512,1024]{1,0:T(8,128)(2,1)} %get-tuple-element.100), channel_id=1, source_target_pairs={{0,2},{1,4},{2,0},{3,6},{4,1},{5,7},{6,3},{7,5},{8,10},{9,12},{10,... | collective-permute-start | bytes 3145736 | tf_op jit(solution)/shard_map/ppermute | solution.py:487
  182.4 56.1 %collective-permute-start.17 = (bf16[512,1024]{1,0:T(8,128)(2,1)}, bf16[512,1024]{1,0:T(8,128)(2,1)S(1)}, u32[]{:S(2)}, u32[]{:S(2)}) collective-permute-start(bf16[512,1024]{1,0:T(8,128)(2,1)} %get-tuple-element.101), channel_id=1, source_target_pairs={{0,3},{1,5},{2,1},{3,7},{4,0},{5,6},{6,2},{7,4},{8,11},{9,13},{10,... | collective-permute-start | bytes 3145736 | tf_op jit(solution)/shard_map/ppermute | solution.py:487
  185.6 52.9 %collective-permute-start.18 = (bf16[512,1024]{1,0:T(8,128)(2,1)}, bf16[512,1024]{1,0:T(8,128)(2,1)S(1)}, u32[]{:S(2)}, u32[]{:S(2)}) collective-permute-start(bf16[512,1024]{1,0:T(8,128)(2,1)} %get-tuple-element.102), channel_id=1, source_target_pairs={{0,1},{1,7},{2,3},{3,5},{4,2},{5,4},{6,0},{7,6},{8,9},{9,15},{10,1... | collective-permute-start | bytes 3145736 | tf_op jit(solution)/shard_map/ppermute | solution.py:487
  186.8 53.7 %collective-permute-start.19 = (bf16[512,1024]{1,0:T(8,128)(2,1)}, bf16[512,1024]{1,0:T(8,128)(2,1)}, u32[]{:S(2)}, u32[]{:S(2)}) collective-permute-start(bf16[512,1024]{1,0:T(8,128)(2,1)} %get-tuple-element.103), channel_id=1, source_target_pairs={{0,0},{1,6},{2,2},{3,4},{4,3},{5,5},{6,1},{7,7},{8,8},{9,14},{10,1... | collective-permute-start | bytes 3145736 | tf_op jit(solution)/shard_map/ppermute | solution.py:487
  238.5 6.9 %collective-permute-start.20 = (bf16[1024,1024]{1,0:T(8,128)(2,1)}, bf16[1024,1024]{1,0:T(8,128)(2,1)}, u32[]{:S(2)}, u32[]{:S(2)}) collective-permute-start(bf16[1024,1024]{1,0:T(8,128)(2,1)} %collective-permute-done.15.refs_5_), channel_id=1, source_target_pairs={{0,1},{1,0},{2,3},{3,2},{4,5},{5,4},{6,7},{7,6},{8,9},{9,8},{10,11... | collective-permute-start | bytes 6291464 | tf_op jit(solution)/shard_map/ppermute | solution.py:514
  238.5 6.9 %copy-start.10 = (bf16[512,1024]{1,0:T(8,128)(2,1)}, bf16[512,1024]{1,0:T(8,128)(2,1)S(1)}, u32[]{:S(2)}) copy-start(bf16[512,1024]{1,0:T(8,128)(2,1)S(1)} %collective-permute-done.16.refs_0_) | copy-start | bytes 3145732
  238.5 1.0 copy-start.11
  239.5 1.0 copy-start.12
  240.5 27.3 %collective-permute-start.21 = (bf16[1024,1024]{1,0:T(8,128)(2,1)}, bf16[1024,1024]{1,0:T(8,128)(2,1)S(1)}, u32[]{:S(2)}, u32[]{:S(2)}) collective-permute-start(bf16[1024,1024]{1,0:T(8,128)(2,1)} %all-reduce.3.cloned.1.call-done.mine), channel_id=1, source_target_pairs={{5,1},{7,3},{0,4},{2,6},{13,9},{15,11},{8,12},{10,14},{21,17},{23,... | collective-permute-start | bytes 6291464 | tf_op jit(solution)/shard_map/ppermute | solution.py:487
  267.8 1.4 copy-start.2
Sparse Core Ops, SparseCore 0:
  172.5 65.9 all-reduce.2

commit v12 on v11

--- a/solution.py
+++ b/solution.py
@@ -330,44 +330,49 @@
 
 def weight_grad_kernel(steps, order, *refs):
     (outq_parts, upstream, normed), refs = [refs[i * steps:(i + 1) * steps] for i in range(3)], refs[3 * steps:]
-    dkv, dkv_top, dkv_bot, normed_top, normed_bot, grad, outq, up, own, sems = refs
-    feats, chunk = outq.shape[1] // 2, outq_parts[0].shape[0]
+    wide, (grad, outq, up, own, sums, dkv_halos, normed_halos, sems, wide_sems) = refs[:5], refs[5:]
+    feats, chunk, halo = outq.shape[1] // 2, outq_parts[0].shape[0], HALO * LONGITUDES
     groups = [
         [
             pltpu.make_async_copy(part, held.at[pl.ds(pl.multiple_of(order[i], 16), chunk)], sems.at[group, i])
             for i, part in enumerate(parts)
         ]
-        for group, (parts, held) in enumerate(((outq_parts, outq), (normed, own), (upstream, up)))
-    ]
-    for moves in groups:
-        for move in moves:
-            move.start()
+        for group, (parts, held) in enumerate(((outq_parts, outq), (upstream, up), (normed, own)))
+    ]
+    places = [sums] + [held.at[pl.ds(at, halo)] for held in (dkv_halos, normed_halos) for at in (0, halo)]
+    wide_moves = [
+        pltpu.make_async_copy(part, held, wide_sems.at[i]) for i, (part, held) in enumerate(zip(wide, places))
+    ]
+    for move in groups[0] + groups[1] + groups[2] + wide_moves:
+        move.start()
 
     def product(left, right):
         return lax.dot_general(left, right, (((0,), (0,)), ((), ())), preferred_element_type=F32)
 
-    keyval = product(dkv_top[...], normed_top[...]) + product(dkv_bot[...], normed_bot[...])
-    for moves in groups[:2]:
-        for move in moves:
-            move.wait()
-    grad[2 * feats:, :] = (keyval + product(dkv[...].astype(BF16), own[...])).astype(BF16)
+    for move in groups[0] + groups[1]:
+        move.wait()
+    grad[:feats, :] = product(outq[:, :feats], up[...]).astype(BF16)
+    for move in groups[2]:
+        move.wait()
     grad[feats:2 * feats, :] = product(outq[:, feats:], own[...]).astype(BF16)
-    for move in groups[2]:
-        move.wait()
-    grad[:feats, :] = product(outq[:, :feats], up[...]).astype(BF16)
+    for move in wide_moves:
+        move.wait()
+    keyval = product(sums[...].astype(BF16), own[...])
+    grad[2 * feats:, :] = (keyval + product(dkv_halos[...], normed_halos[...])).astype(BF16)
 
 
 def weight_grads(order, outq_parts, upstream, normed, dkv, dkv_halos, normed_halos):
     steps, (chunk, rows), width = len(normed), outq_parts[0].shape, normed[0].shape[1]
-    band = steps * chunk
+    band, halos = steps * chunk, 2 * HALO * LONGITUDES
     return call(
         functools.partial(weight_grad_kernel, steps),
-        [shape(2 * rows, width)], [SMEM] + [HBM] * (3 * steps) + [VMEM] * 5, [VMEM],
+        [shape(2 * rows, width)], [SMEM] + [HBM] * (3 * steps + 5), [VMEM],
         (order, *outq_parts, *upstream, *normed, dkv, *dkv_halos, *normed_halos),
-        flops=2 * width * rows * (2 * band + 2 * HALO * LONGITUDES),
+        flops=2 * width * rows * (2 * band + halos),
         scratch=[
             pltpu.VMEM((band, rows), BF16), pltpu.VMEM((band, width), BF16), pltpu.VMEM((band, width), BF16),
-            pltpu.SemaphoreType.DMA((3, steps)),
+            pltpu.VMEM((band, rows), F32), pltpu.VMEM((halos, rows), BF16), pltpu.VMEM((halos, width), BF16),
+            pltpu.SemaphoreType.DMA((3, steps)), pltpu.SemaphoreType.DMA((5,)),
         ],
     )[0]
 
@@ -410,25 +415,32 @@
 
 
 def finish_kernel(scale, flag, mine, other, grad_qkv, grad_out):
-    heads = grad_out.shape[0]
-    for h in range(heads):
-        for i in range(4):
-            at = pl.ds((i * heads + h) * HEAD_WIDTH, HEAD_WIDTH)
-            part = jnp.where(flag[0] == 1, mine[at, :], other[at, :]).astype(F32)
-            if i == 0:
-                grad_out[h] = part * scale
-            else:
-                factor = scale * HEAD_WIDTH ** -0.5 if i == 1 else scale
-                grad_qkv[h, (i - 1) * HEAD_WIDTH:i * HEAD_WIDTH, :] = part * factor
+    for i in range(4):
+        part = jnp.where(flag[0] == 1, mine[i, 0], other[i, 0]).astype(F32)
+        if i == 0:
+            grad_out[0] = part * scale
+        else:
+            factor = scale * HEAD_WIDTH ** -0.5 if i == 1 else scale
+            grad_qkv[0, (i - 1) * HEAD_WIDTH:i * HEAD_WIDTH, :] = part * factor
 
 
 def finished(scale, flag, mine, other):
     heads, width = mine.shape[0] // (4 * HEAD_WIDTH), mine.shape[1]
-    return call(
+    by_head = lambda x: x.reshape(4, heads, HEAD_WIDTH, width)
+    sums = pl.BlockSpec((4, 1, HEAD_WIDTH, width), lambda h: (0, h, 0, 0))
+    result = lambda rows: pl.BlockSpec((1, rows, width), lambda h: (h, 0, 0))
+    return pl.pallas_call(
         functools.partial(finish_kernel, scale),
-        [jax.ShapeDtypeStruct((heads, 3 * HEAD_WIDTH, width), F32), jax.ShapeDtypeStruct((heads, HEAD_WIDTH, width), F32)],
-        [SMEM, VMEM, VMEM], [VMEM] * 2, (flag, mine, other), flops=mine.size,
-    )
+        grid=(heads,),
+        out_shape=(
+            jax.ShapeDtypeStruct((heads, 3 * HEAD_WIDTH, width), F32),
+            jax.ShapeDtypeStruct((heads, HEAD_WIDTH, width), F32),
+        ),
+        in_specs=[SMEM, sums, sums],
+        out_specs=(result(3 * HEAD_WIDTH), result(HEAD_WIDTH)),
+        compiler_params=pltpu.CompilerParams(vmem_limit_bytes=32 * 2**20),
+        cost_estimate=pl.CostEstimate(flops=mine.size, transcendentals=0, bytes_accessed=8 * mine.size),
+    )(flag, by_head(mine), by_head(other))
 
 
 from jax.sharding import Mesh, PartitionSpec as P
@@ -513,17 +525,20 @@
     def from_sibling(x):
         return lax.ppermute(x, "c", [(0, 1), (1, 0)])
 
+    normed = norm(tokens, gain)
+    normed, qkv_weight, out_weight = lax.optimization_barrier((normed, qkv_weight, out_weight))
+
     def split(qkv, out):
         eighth = jnp.asarray([HEAD_WIDTH ** -0.5, 1.0, 1.0], BF16)[None, :, None, None]
         qkv = (qkv.reshape(heads, 3, HEAD_WIDTH, WIDTH) * eighth).transpose(1, 0, 2, 3)
         return jnp.concatenate([qkv.reshape(3 * feats, WIDTH), out.reshape(feats, WIDTH)], axis=0)
 
     blocks = [split(qkv_weight, out_weight)]
-    sibling = from_sibling(blocks[0])
+    normed_parts, hop = gathered(normed)
+    sibling = from_sibling(after(blocks[0], *hop))
     group = jnp.where(c == y, blocks[0], sibling)
     group_qkv, group_out = group[:3 * feats].T, group[3 * feats:]
 
-    normed_parts, hop = gathered(norm(tokens, gain))
     *normed_parts, group_qkv, group_out = lax.optimization_barrier((*normed_parts, group_qkv, group_out))
     qkv, kv_up, kv_down, normed_up, normed_down = projections(order, group_qkv, normed_parts)
     kv_top, kv_bot = passed_along(kv_up, 1), passed_along(kv_down, -1)

time: 282 us -> 280 us (level)
    pallas_call x0 -> x1, Pallas kernels: none -> 4.23 us  [finished(): pl.pallas_call(functools.partial(finish_kernel, scale), grid=(heads,), ou...]
    pallas_call x7 -> x6, Pallas kernels: 92.2 us -> 89.5 us  [call(): pl.pallas_call(kernel, out_shape=tuple(out_shape), in_specs=list(in_specs...]
    unnamed x28 -> x26, local copies, waits for them, and re-layouts: 6.84 us -> 4.77 us
  transfers between devices with their start and end apart: 23 -> 23, of which waited for: 8 -> 7; matrix products, arithmetic and copies ran while one was open for 4% -> 5% of each run, Pallas kernels for 31% -> 31%
where the time goes in v12:
time: 280 us; the launch traced here: 279 us
  waiting for transfers between devices  104 us (37%)
  Pallas kernels  93.8 us (34%)
  starting transfers between devices  47.3 us (17%)
  between operations  14.3 us (5%)
  local copies, waits for them, and re-layouts  10.4 us (4%)
  other arithmetic  8.93 us (3%)
    pallas_call x6, Pallas kernels, call(): pl.pallas_call(kernel, out_shape=tuple(out_shape), in_specs=list(in_specs...  89.5 us
    ppermute x13, waiting for transfers between devices, permuted(): return lax.ppermute(x, GROUP, [(at(*a), at(*b)) for a, b in pairs])  60.4 us
    psum x1, waiting for transfers between devices, on_device(): grads_sum = lax.psum(grads, ('z', 'c'))  44.1 us
    ppermute x13, starting transfers between devices, permuted(): return lax.ppermute(x, GROUP, [(at(*a), at(*b)) for a, b in pairs])  30.8 us
    ppermute x6, starting transfers between devices, passed_along(): return lax.ppermute(x, ('z', 'c'), pairs)  14.9 us
  transfers between devices with their start and end apart: 23, of which 7 were waited for; matrix products, arithmetic and copies ran while one was open for 5% of the time, Pallas kernels for 31%

profile of v12, /device:TPU:0, one launch (start us, length us, event | category | flops | bytes accessed | tf_op | source)
XLA Modules:
  0.0 279.2 jit_solution(8357762637051545798)
XLA Ops:
  7.2 2.6 shard_map.120
  9.8 2.9 %collective-permute-start = (bf16[512,1024]{1,0:T(8,128)(2,1)}, bf16[512,1024]{1,0:T(8,128)(2,1)}, u32[]{:S(2)}, u32[]{:S(2)}) collective-permute-start(bf16[512,1024]{1,0:T(8,128)(2,1)} %shard_map.120), channel_id=1, source_target_pairs={{2,0},{4,1},{0,2},{6,3},{1,4},{7,5},{3,6},{5,7},{10,8},{12,9},{8,1... | collective-permute-start | bytes 3145736 | tf_op jit(solution)/shard_map/ppermute | solution.py:499
  12.8 1.6 copy_multiply_fusion
  14.4 1.5 pad_maximum_fusion.refs_4_
  16.0 20.2 %collective-permute-done.refs_0_.refs_8_ = bf16[512,1024]{1,0:T(8,128)(2,1)} collective-permute-done((bf16[512,1024]{1,0:T(8,128)(2,1)}, bf16[512,1024]{1,0:T(8,128)(2,1)}, u32[]{:S(2)}, u32[]{:S(2)}) %collective-permute-start) | collective-permute-done | bytes 1048608 | tf_op jit(solution)/shard_map/ppermute | solution.py:499
  36.1 1.0 collective-permute-done.1.refs_1_.refs_9_
  37.2 1.3 broadcast_select_fusion.4
  38.7 0.7 collective-permute-start.3
  39.4 11.6 %collective-permute-done.2.refs_2_.refs_10_ = bf16[512,1024]{1,0:T(8,128)(2,1)S(1)} collective-permute-done((bf16[512,1024]{1,0:T(8,128)(2,1)S(1)}, bf16[512,1024]{1,0:T(8,128)(2,1)S(1)}, u32[]{:S(2)}, u32[]{:S(2)}) %collective-permute-start.2) | collective-permute-done | bytes 1048608 | tf_op jit(solution)/shard_map/ppermute | solution.py:499
  51.0 1.0 copy-done.8
  52.0 1.1 broadcast_select_fusion.3.refs_3_.refs_11_
  53.1 1.0 broadcast_select_fusion
  54.2 0.8 slice.9.weight
  55.5 1.5 collective-permute-start.7
  57.0 5.5 %collective-permute-start.8 = (bf16[512,1024]{1,0:T(8,128)(2,1)S(1)}, bf16[512,1024]{1,0:T(8,128)(2,1)}, u32[]{:S(2)}, u32[]{:S(2)}) collective-permute-start(bf16[512,1024]{1,0:T(8,128)(2,1)S(1)} %copy-done.2), channel_id=1, source_target_pairs={{3,0},{5,1},{1,2},{7,3},{0,4},{6,5},{2,6},{4,7},{11,8},{13,9},{9,1... | collective-permute-start | bytes 3145736 | tf_op jit(solution)/shard_map/ppermute | solution.py:499
  62.4 1.3 dynamic-slice_bitcast_fusion.order
  63.7 1.6 copy.14.weight
  65.3 9.8 %shard_map.121 = (bf16[2048,768]{1,0:T(8,128)(2,1)}, bf16[1536,512]{1,0:T(8,128)(2,1)}, bf16[1536,512]{1,0:T(8,128)(2,1)}, bf16[1536,1024]{1,0:T(8,128)(2,1)}, bf16[1536,1024]{1,0:T(8,128)(2,1)}) custom-call(s32[4]{0:T(128)} %dynamic-slice_bitcast_fusion.order, bf16[1024,768]{1,0:T(8,128)(2,1)} %copy.14.weight, ...), custom_call_target="tpu_custom_call" | custom-call | flops 3221225472 | bytes 18350096 | tf_op jit(solution)/shard_map/pallas_call | solution.py:200
  75.1 2.1 collective-permute-start.5
  77.2 1.3 collective-permute-start.6
  78.5 6.9 %collective-permute-done.8.refs_1_.refs_5_ = bf16[512,1024]{1,0:T(8,128)(2,1)} collective-permute-done((bf16[512,1024]{1,0:T(8,128)(2,1)S(1)}, bf16[512,1024]{1,0:T(8,128)(2,1)}, u32[]{:S(2)}, u32[]{:S(2)}) %collective-permute-start.8) | collective-permute-done | bytes 1048608 | tf_op jit(solution)/shard_map/ppermute | solution.py:499
  85.4 1.3 broadcast_select_fusion.2
  86.7 1.4 collective-permute-start.9
  88.1 0.7 collective-permute-start.10
  88.8 11.6 %collective-permute-done.9.refs_2_.refs_6_ = bf16[512,1024]{1,0:T(8,128)(2,1)S(1)} collective-permute-done((bf16[512,1024]{1,0:T(8,128)(2,1)S(1)}, bf16[512,1024]{1,0:T(8,128)(2,1)S(1)}, u32[]{:S(2)}, u32[]{:S(2)}) %collective-permute-start.9) | collective-permute-done | bytes 1048608 | tf_op jit(solution)/shard_map/ppermute | solution.py:499
  100.4 1.0 copy-done.9
  101.4 1.1 broadcast_select_fusion.1.refs_3_.refs_7_
  102.5 5.3 %collective-permute-start.11 = (bf16[1536,1024]{1,0:T(8,128)(2,1)}, bf16[1536,1024]{1,0:T(8,128)(2,1)}, u32[]{:S(2)}, u32[]{:S(2)}) collective-permute-start(bf16[1536,1024]{1,0:T(8,128)(2,1)} %get-tuple-element.100), channel_id=1, source_target_pairs={{0,1},{1,8},{8,9},{9,16},{16,17},{17,24},{24,25},{2,3},{3,10},{10,... | collective-permute-start | bytes 9437192 | tf_op jit(solution)/shard_map/ppermute | solution.py:468
  107.8 1.3 collective-permute-start.12
  109.1 0.6 pad_dynamic-slice_fusion.cells
  109.7 1.5 collective-permute-start.15
  111.2 42.1 %shard_map.122 = (bf16[512,512]{1,0:T(8,128)(2,1)}, bf16[512,512]{1,0:T(8,128)(2,1)}, bf16[512,512]{1,0:T(8,128)(2,1)}, bf16[512,512]{1,0:T(8,128)(2,1)}, f32[20...) custom-call(s32[20]{0:T(128)} %pad_dynamic-slice_fusion.cells, ...), custom_call_target="tpu_custom_call" | custom-call | flops 13958643712 | bytes 20447328 | tf_op jit(solution)/shard_map/pallas_call | solution.py:200
  153.3 1.3 collective-permute-start.13
  154.6 3.7 %collective-permute-start.14 = (bf16[1536,512]{1,0:T(8,128)(2,1)}, bf16[1536,512]{1,0:T(8,128)(2,1)S(1)}, u32[]{:S(2)}, u32[]{:S(2)}) collective-permute-start(bf16[1536,512]{1,0:T(8,128)(2,1)} %get-tuple-element.99.refs_14_), channel_id=1, source_target_pairs={{0,1},{1,8},{8,9},{9,16},{16,17},{17,24},{24,25},{2,3},{3,10},{10,... | collective-permute-start | bytes 4718600 | tf_op jit(solution)/shard_map/ppermute | solution.py:468
  158.3 16.1 %shard_map.123 = bf16[1024,1024]{1,0:T(8,128)(2,1)} custom-call(s32[4]{0:T(128)} %dynamic-slice_bitcast_fusion.order, bf16[512,512]{1,0:T(8,128)(2,1)} %get-tuple-element.93.refs_0_, bf16[512,512]{1,0:T(8,128)(2,1)} %get-tuple-element.94.refs_1_, bf16[512,512]{1,0:T(8,128)(2,1)} %get-tuple-element.95.refs_2_, bf16[512,512]{1,0:T(8,128)(2,1)} %get-tuple-element.96.refs_3_, ...), custom_call_target="tpu_custom_call" | custom-call | flops 7516192768 | bytes 26214416 | tf_op jit(solution)/shard_map/pallas_call | solution.py:200
  174.5 1.1 copy-done.4
  175.6 1.2 copy-done.5
  176.8 6.8 %shard_map.124 = (bf16[512,1024]{1,0:T(8,128)(2,1)}, bf16[512,1024]{1,0:T(8,128)(2,1)}, bf16[512,1024]{1,0:T(8,128)(2,1)}, bf16[512,1024]{1,0:T(8,128)(2,1)}) custom-call(s32[4]{0:T(128)} %dynamic-slice_bitcast_fusion.order, f32[2048,512]{1,0:T(8,128)} %get-tuple-element.97.refs_12_.own, bf16[1536,512]{1,0:T(8,128)(2,1)} %copy-done.4, ...), custom_call_target="tpu_custom_call" | custom-call | tf_op jit(solution)/shard_map/pallas_call | solution.py:200
  183.6 0.5 collective-permute-start.16
  184.1 1.5 collective-permute-start.17
  185.6 1.5 collective-permute-start.18
  187.1 9.5 %collective-permute-start.19 = (bf16[512,1024]{1,0:T(8,128)(2,1)}, bf16[512,1024]{1,0:T(8,128)(2,1)}, u32[]{:S(2)}, u32[]{:S(2)}) collective-permute-start(bf16[512,1024]{1,0:T(8,128)(2,1)} %get-tuple-element.111), channel_id=1, source_target_pairs={{0,0},{1,6},{2,2},{3,4},{4,3},{5,5},{6,1},{7,7},{8,8},{9,14},{10,1... | collective-permute-start | bytes 3145736 | tf_op jit(solution)/shard_map/ppermute | solution.py:499
  196.7 44.1 %all-reduce.3.cloned.1.call-done = bf16[1024,1024]{1,0:T(8,128)(2,1)} async-done(((bf16[1024,1024]{1,0:T(8,128)(2,1)}), bf16[1024,1024]{1,0:T(8,128)(2,1)}) %all-reduce.3.cloned.1.call-update) | async-done | bytes 2097168 | tf_op jit(solution)/shard_map/psum | solution.py:558
  240.8 4.8 %collective-permute-start.21 = (bf16[1024,1024]{1,0:T(8,128)(2,1)}, bf16[1024,1024]{1,0:T(8,128)(2,1)}, u32[]{:S(2)}, u32[]{:S(2)}) collective-permute-start(bf16[1024,1024]{1,0:T(8,128)(2,1)} %all-reduce.3.cloned.1.call-done), channel_id=1, source_target_pairs={{5,1},{7,3},{0,4},{2,6},{13,9},{15,11},{8,12},{10,14},{21,17},{23,... | collective-permute-start | bytes 6291464 | tf_op jit(solution)/shard_map/ppermute | solution.py:499
  245.6 1.2 dynamic-slice_bitcast_fusion.1.leads
  246.8 12.1 %shard_map.125 = (bf16[512,1024]{1,0:T(8,128)(2,1)}, bf16[512,1024]{1,0:T(8,128)(2,1)}) custom-call(s32[4]{0:T(128)} %dynamic-slice_bitcast_fusion.1.leads, bf16[512,1024]{1,0:T(8,128)(2,1)} %tokens.3, f32[1,1024]{1,0:T(1,128)} %bitcast.22, bf16[512,1024]{1,0:T(8,128)(2,1)} %copy-done.10, bf16[512,1024]{1,0:T(8,128)(2,1)} %copy-done.11, ...), custom_call_target="tpu_custom_call" | custom-call | flops 4294967296 | bytes 15732752 | tf_op jit(solution)/shard_map/pallas_call | solution.py:200
  258.9 9.2 %collective-permute-done.21 = bf16[1024,1024]{1,0:T(8,128)(2,1)} collective-permute-done((bf16[1024,1024]{1,0:T(8,128)(2,1)}, bf16[1024,1024]{1,0:T(8,128)(2,1)}, u32[]{:S(2)}, u32[]{:S(2)}) %collective-permute-start.21) | collective-permute-done | bytes 2097184 | tf_op jit(solution)/shard_map/ppermute | solution.py:499
  268.1 4.2 %shard_map.126 = (f32[4,192,1024]{2,1,0:T(8,128)}, f32[4,64,1024]{2,1,0:T(8,128)}) custom-call(s32[1]{0:T(128)} %bitcast.8.flag, bf16[4,4,64,1024]{3,2,1,0:T(8,128)(2,1)S(1)} %bitcast.15, bf16[4,4,64,1024]{3,2,1,0:T(8,128)(2,1)} %bitcast.10.other), custom_call_target="tpu_custom_call" | custom-call | flops 1048576 | bytes 8388608 | tf_op jit(solution)/shard_map/pallas_call | solution.py:432
  (45 shorter events, 1.0 us)
Async XLA Ops:
  7.2 5.7 %copy-start.6 = (bf16[3]{0:T(256)(128)(2,1)S(1)}, bf16[3]{0:T(256)(128)(2,1)}, u32[]{:S(2)}) copy-start(bf16[3]{0:T(256)(128)(2,1)} %constant.30.clone) | copy-start | bytes 22
  7.2 233.5 %all-reduce.3.cloned.1.call-start = ((), (), s32[]{:S(2)}) async-start(), calls=%async_computation | async-start | bytes 4194304 | tf_op jit(solution)/shard_map/psum | solution.py:558
  9.8 4.6 %copy-start.3 = (bf16[4,64,1024]{2,1,0:T(8,128)(2,1)S(1)}, bf16[4,64,1024]{2,1,0:T(8,128)(2,1)}, u32[]{:S(2)}) copy-start(bf16[4,64,1024]{2,1,0:T(8,128)(2,1)} %param.12) | copy-start | bytes 1572868
  9.8 26.3 %collective-permute-start = (bf16[512,1024]{1,0:T(8,128)(2,1)}, bf16[512,1024]{1,0:T(8,128)(2,1)}, u32[]{:S(2)}, u32[]{:S(2)}) collective-permute-start(bf16[512,1024]{1,0:T(8,128)(2,1)} %shard_map.120), channel_id=1, source_target_pairs={{2,0},{4,1},{0,2},{6,3},{1,4},{7,5},{3,6},{5,7},{10,8},{12,9},{8,1... | collective-permute-start | bytes 3145736 | tf_op jit(solution)/shard_map/ppermute | solution.py:499
  12.8 24.3 %collective-permute-start.1 = (bf16[512,1024]{1,0:T(8,128)(2,1)}, bf16[512,1024]{1,0:T(8,128)(2,1)}, u32[]{:S(2)}, u32[]{:S(2)}) collective-permute-start(bf16[512,1024]{1,0:T(8,128)(2,1)} %shard_map.120), channel_id=1, source_target_pairs={{3,0},{5,1},{1,2},{7,3},{0,4},{6,5},{2,6},{4,7},{11,8},{13,9},{9,1... | collective-permute-start | bytes 3145736 | tf_op jit(solution)/shard_map/ppermute | solution.py:499
  14.4 22.8 %copy-start.1 = (bf16[512,1024]{1,0:T(8,128)(2,1)S(1)}, bf16[512,1024]{1,0:T(8,128)(2,1)}, u32[]{:S(2)}) copy-start(bf16[512,1024]{1,0:T(8,128)(2,1)} %shard_map.120) | copy-start | bytes 3145732
  37.1 16.0 %collective-permute-start.4 = (bf16[1024,1024]{1,0:T(8,128)(2,1)}, bf16[1024,1024]{1,0:T(8,128)(2,1)}, u32[]{:S(2)}, u32[]{:S(2)}) collective-permute-start(bf16[1024,1024]{1,0:T(8,128)(2,1)} %pad_maximum_fusion.refs_4_), channel_id=1, source_target_pairs={{0,1},{1,0},{2,3},{3,2},{4,5},{5,4},{6,7},{7,6},{8,9},{9,8},{10,11... | collective-permute-start | bytes 6291464 | tf_op jit(solution)/shard_map/ppermute | solution.py:526
  38.5 12.5 %collective-permute-start.2 = (bf16[512,1024]{1,0:T(8,128)(2,1)S(1)}, bf16[512,1024]{1,0:T(8,128)(2,1)S(1)}, u32[]{:S(2)}, u32[]{:S(2)}) collective-permute-start(bf16[512,1024]{1,0:T(8,128)(2,1)S(1)} %broadcast_select_fusion.4), channel_id=1, source_target_pairs={{0,4},{1,0},{2,6},{3,2},{4,5},{5,1},{6,7},{7,3},{8,12},{9,8},{10,1... | collective-permute-start | bytes 3145736 | tf_op jit(solution)/shard_map/ppermute | solution.py:499
  38.7 13.3 %collective-permute-start.3 = (bf16[512,1024]{1,0:T(8,128)(2,1)}, bf16[512,1024]{1,0:T(8,128)(2,1)S(1)}, u32[]{:S(2)}, u32[]{:S(2)}) collective-permute-start(bf16[512,1024]{1,0:T(8,128)(2,1)} %collective-permute-done.refs_0_.refs_8_), channel_id=1, source_target_pairs={{1,3},{3,1},{4,6},{6,4},{9,11},{11,9},{12,14},{14,12},{17,19},{19,... | collective-permute-start | bytes 3145736 | tf_op jit(solution)/shard_map/ppermute | solution.py:499
  51.0 1.0 copy-start.8
  54.1 1.4 copy-start.2
  55.5 23.0 %collective-permute-start.7 = (bf16[512,1024]{1,0:T(8,128)(2,1)S(1)}, bf16[512,1024]{1,0:T(8,128)(2,1)}, u32[]{:S(2)}, u32[]{:S(2)}) collective-permute-start(bf16[512,1024]{1,0:T(8,128)(2,1)S(1)} %copy-done.2), channel_id=1, source_target_pairs={{2,0},{4,1},{0,2},{6,3},{1,4},{7,5},{3,6},{5,7},{10,8},{12,9},{8,1... | collective-permute-start | bytes 3145736 | tf_op jit(solution)/shard_map/ppermute | solution.py:499
  57.0 28.4 %collective-permute-start.8 = (bf16[512,1024]{1,0:T(8,128)(2,1)S(1)}, bf16[512,1024]{1,0:T(8,128)(2,1)}, u32[]{:S(2)}, u32[]{:S(2)}) collective-permute-start(bf16[512,1024]{1,0:T(8,128)(2,1)S(1)} %copy-done.2), channel_id=1, source_target_pairs={{3,0},{5,1},{1,2},{7,3},{0,4},{6,5},{2,6},{4,7},{11,8},{13,9},{9,1... | collective-permute-start | bytes 3145736 | tf_op jit(solution)/shard_map/ppermute | solution.py:499
  75.1 27.4 %collective-permute-start.5 = (bf16[1536,512]{1,0:T(8,128)(2,1)}, bf16[1536,512]{1,0:T(8,128)(2,1)S(1)}, u32[]{:S(2)}, u32[]{:S(2)}) collective-permute-start(bf16[1536,512]{1,0:T(8,128)(2,1)} %get-tuple-element.76), channel_id=1, source_target_pairs={{0,1},{1,8},{8,9},{9,16},{16,17},{17,24},{24,25},{2,3},{3,10},{10,... | collective-permute-start | bytes 4718600 | tf_op jit(solution)/shard_map/ppermute | solution.py:468
  77.2 25.3 %collective-permute-start.6 = (bf16[1536,512]{1,0:T(8,128)(2,1)}, bf16[1536,512]{1,0:T(8,128)(2,1)}, u32[]{:S(2)}, u32[]{:S(2)}) collective-permute-start(bf16[1536,512]{1,0:T(8,128)(2,1)} %get-tuple-element.77), channel_id=1, source_target_pairs={{1,0},{8,1},{9,8},{16,9},{17,16},{24,17},{25,24},{3,2},{10,3},{11,... | collective-permute-start | bytes 4718600 | tf_op jit(solution)/shard_map/ppermute | solution.py:468
  86.7 22.3 %copy-start.12 = (s32[64]{0:T(128)S(1)}, s32[64]{0:T(128)}, u32[]{:S(2)}) copy-start(s32[64]{0:T(128)} %param.13) | copy-start | bytes 772
  86.7 13.7 %collective-permute-start.9 = (bf16[512,1024]{1,0:T(8,128)(2,1)S(1)}, bf16[512,1024]{1,0:T(8,128)(2,1)S(1)}, u32[]{:S(2)}, u32[]{:S(2)}) collective-permute-start(bf16[512,1024]{1,0:T(8,128)(2,1)S(1)} %broadcast_select_fusion.2), channel_id=1, source_target_pairs={{0,4},{1,0},{2,6},{3,2},{4,5},{5,1},{6,7},{7,3},{8,12},{9,8},{10,1... | collective-permute-start | bytes 3145736 | tf_op jit(solution)/shard_map/ppermute | solution.py:499
  88.1 13.3 %collective-permute-start.10 = (bf16[512,1024]{1,0:T(8,128)(2,1)}, bf16[512,1024]{1,0:T(8,128)(2,1)S(1)}, u32[]{:S(2)}, u32[]{:S(2)}) collective-permute-start(bf16[512,1024]{1,0:T(8,128)(2,1)} %collective-permute-done.7.refs_0_.refs_4_), channel_id=1, source_target_pairs={{1,3},{3,1},{4,6},{6,4},{9,11},{11,9},{12,14},{14,12},{17,19},{19,... | collective-permute-start | bytes 3145736 | tf_op jit(solution)/shard_map/ppermute | solution.py:499
  100.4 1.0 copy-start.9
  102.5 8.7 %copy-start.7 = (bf16[1536,512]{1,0:T(8,128)(2,1)}, bf16[1536,512]{1,0:T(8,128)(2,1)S(1)}, u32[]{:S(2)}) copy-start(bf16[1536,512]{1,0:T(8,128)(2,1)S(1)} %collective-permute-done.5.kv_top) | copy-start | bytes 4718596
  102.5 55.8 %collective-permute-start.11 = (bf16[1536,1024]{1,0:T(8,128)(2,1)}, bf16[1536,1024]{1,0:T(8,128)(2,1)}, u32[]{:S(2)}, u32[]{:S(2)}) collective-permute-start(bf16[1536,1024]{1,0:T(8,128)(2,1)} %get-tuple-element.100), channel_id=1, source_target_pairs={{0,1},{1,8},{8,9},{9,16},{16,17},{17,24},{24,25},{2,3},{3,10},{10,... | collective-permute-start | bytes 9437192 | tf_op jit(solution)/shard_map/ppermute | solution.py:468
  107.8 50.5 %collective-permute-start.12 = (bf16[1536,1024]{1,0:T(8,128)(2,1)}, bf16[1536,1024]{1,0:T(8,128)(2,1)}, u32[]{:S(2)}, u32[]{:S(2)}) collective-permute-start(bf16[1536,1024]{1,0:T(8,128)(2,1)} %get-tuple-element.101), channel_id=1, source_target_pairs={{1,0},{8,1},{9,8},{16,9},{17,16},{24,17},{25,24},{3,2},{10,3},{11,... | collective-permute-start | bytes 9437192 | tf_op jit(solution)/shard_map/ppermute | solution.py:468
  109.7 73.9 %collective-permute-start.15 = (bf16[1024,1024]{1,0:T(8,128)(2,1)}, bf16[1024,1024]{1,0:T(8,128)(2,1)}, u32[]{:S(2)}, u32[]{:S(2)}) collective-permute-start(bf16[1024,1024]{1,0:T(8,128)(2,1)} %pad_maximum_fusion.refs_4_), channel_id=1, source_target_pairs={{2,0},{0,2},{3,1},{1,3},{6,4},{4,6},{7,5},{5,7},{10,8},{8,10},{11,... | collective-permute-start | bytes 6291464 | tf_op jit(solution)/shard_map/ppermute | solution.py:523
  153.3 21.1 %collective-permute-start.13 = (bf16[1536,512]{1,0:T(8,128)(2,1)}, bf16[1536,512]{1,0:T(8,128)(2,1)S(1)}, u32[]{:S(2)}, u32[]{:S(2)}) collective-permute-start(bf16[1536,512]{1,0:T(8,128)(2,1)} %get-tuple-element.98.refs_13_), channel_id=1, source_target_pairs={{1,0},{8,1},{9,8},{16,9},{17,16},{24,17},{25,24},{3,2},{10,3},{11,... | collective-permute-start | bytes 4718600 | tf_op jit(solution)/shard_map/ppermute | solution.py:468
  154.6 19.8 %collective-permute-start.14 = (bf16[1536,512]{1,0:T(8,128)(2,1)}, bf16[1536,512]{1,0:T(8,128)(2,1)S(1)}, u32[]{:S(2)}, u32[]{:S(2)}) collective-permute-start(bf16[1536,512]{1,0:T(8,128)(2,1)} %get-tuple-element.99.refs_14_), channel_id=1, source_target_pairs={{0,1},{1,8},{8,9},{9,16},{16,17},{17,24},{24,25},{2,3},{3,10},{10,... | collective-permute-start | bytes 4718600 | tf_op jit(solution)/shard_map/ppermute | solution.py:468
  174.4 1.2 copy-start.4
  175.6 1.2 copy-start.5
  183.6 57.1 %collective-permute-start.16 = (bf16[512,1024]{1,0:T(8,128)(2,1)}, bf16[512,1024]{1,0:T(8,128)(2,1)S(1)}, u32[]{:S(2)}, u32[]{:S(2)}) collective-permute-start(bf16[512,1024]{1,0:T(8,128)(2,1)} %get-tuple-element.108), channel_id=1, source_target_pairs={{0,2},{1,4},{2,0},{3,6},{4,1},{5,7},{6,3},{7,5},{8,10},{9,12},{10,... | collective-permute-start | bytes 3145736 | tf_op jit(solution)/shard_map/ppermute | solution.py:499
  184.1 56.6 %collective-permute-start.17 = (bf16[512,1024]{1,0:T(8,128)(2,1)}, bf16[512,1024]{1,0:T(8,128)(2,1)S(1)}, u32[]{:S(2)}, u32[]{:S(2)}) collective-permute-start(bf16[512,1024]{1,0:T(8,128)(2,1)} %get-tuple-element.109), channel_id=1, source_target_pairs={{0,3},{1,5},{2,1},{3,7},{4,0},{5,6},{6,2},{7,4},{8,11},{9,13},{10,... | collective-permute-start | bytes 3145736 | tf_op jit(solution)/shard_map/ppermute | solution.py:499
  185.6 55.1 %collective-permute-start.18 = (bf16[512,1024]{1,0:T(8,128)(2,1)}, bf16[512,1024]{1,0:T(8,128)(2,1)}, u32[]{:S(2)}, u32[]{:S(2)}) collective-permute-start(bf16[512,1024]{1,0:T(8,128)(2,1)} %get-tuple-element.110), channel_id=1, source_target_pairs={{0,1},{1,7},{2,3},{3,5},{4,2},{5,4},{6,0},{7,6},{8,9},{9,15},{10,1... | collective-permute-start | bytes 3145736 | tf_op jit(solution)/shard_map/ppermute | solution.py:499
  187.1 53.6 %collective-permute-start.19 = (bf16[512,1024]{1,0:T(8,128)(2,1)}, bf16[512,1024]{1,0:T(8,128)(2,1)}, u32[]{:S(2)}, u32[]{:S(2)}) collective-permute-start(bf16[512,1024]{1,0:T(8,128)(2,1)} %get-tuple-element.111), channel_id=1, source_target_pairs={{0,0},{1,6},{2,2},{3,4},{4,3},{5,5},{6,1},{7,7},{8,8},{9,14},{10,1... | collective-permute-start | bytes 3145736 | tf_op jit(solution)/shard_map/ppermute | solution.py:499
  240.7 6.0 %collective-permute-start.20 = (bf16[1024,1024]{1,0:T(8,128)(2,1)}, bf16[1024,1024]{1,0:T(8,128)(2,1)}, u32[]{:S(2)}, u32[]{:S(2)}) collective-permute-start(bf16[1024,1024]{1,0:T(8,128)(2,1)} %collective-permute-done.15.refs_5_), channel_id=1, source_target_pairs={{0,1},{1,0},{2,3},{3,2},{4,5},{5,4},{6,7},{7,6},{8,9},{9,8},{10,11... | collective-permute-start | bytes 6291464 | tf_op jit(solution)/shard_map/ppermute | solution.py:526
  240.7 6.0 %copy-start.10 = (bf16[512,1024]{1,0:T(8,128)(2,1)}, bf16[512,1024]{1,0:T(8,128)(2,1)S(1)}, u32[]{:S(2)}) copy-start(bf16[512,1024]{1,0:T(8,128)(2,1)S(1)} %collective-permute-done.16.refs_0_) | copy-start | bytes 3145732
  240.7 4.9 %copy-start.11 = (bf16[512,1024]{1,0:T(8,128)(2,1)}, bf16[512,1024]{1,0:T(8,128)(2,1)S(1)}, u32[]{:S(2)}) copy-start(bf16[512,1024]{1,0:T(8,128)(2,1)S(1)} %collective-permute-done.17.refs_1_) | copy-start | bytes 3145732
  240.8 27.3 %collective-permute-start.21 = (bf16[1024,1024]{1,0:T(8,128)(2,1)}, bf16[1024,1024]{1,0:T(8,128)(2,1)}, u32[]{:S(2)}, u32[]{:S(2)}) collective-permute-start(bf16[1024,1024]{1,0:T(8,128)(2,1)} %all-reduce.3.cloned.1.call-done), channel_id=1, source_target_pairs={{5,1},{7,3},{0,4},{2,6},{13,9},{15,11},{8,12},{10,14},{21,17},{23,... | collective-permute-start | bytes 6291464 | tf_op jit(solution)/shard_map/ppermute | solution.py:499
  246.8 21.3 %copy-start = (bf16[1024,1024]{1,0:T(8,128)(2,1)S(1)}, bf16[1024,1024]{1,0:T(8,128)(2,1)}, u32[]{:S(2)}) copy-start(bf16[1024,1024]{1,0:T(8,128)(2,1)} %all-reduce.3.cloned.1.call-done) | copy-start | bytes 6291460
Sparse Core Ops, SparseCore 0:
  174.6 66.1 all-reduce.2

commit v13 on v12

--- a/solution.py
+++ b/solution.py
@@ -122,6 +122,8 @@
             + jnp.concatenate([live_s[index[j], keys, :]] * (LANES // 128), axis=1)
             for j in range(window)
         ]
+        grad_probs = [nt(v_s[index[j], keys, :], grads) for j in range(window)]
+        yield
         highest = jnp.max(functools.reduce(jnp.maximum, scores), axis=0, keepdims=True)
         terms = [jnp.exp(score - highest) for score in scores]
         total = jnp.sum(sum(terms), axis=0, keepdims=True)
@@ -132,10 +134,10 @@
         live = start + query_lane % tile_cols < query_cells
         inverse = jnp.where(live, 1.0 / total, 0.0)
         probs = [term * inverse for term in terms]
-        grad_probs = [nt(v_s[index[j], keys, :], grads) for j in range(window)]
         delta = jnp.sum(sum(p * g for p, g in zip(probs, grad_probs)), axis=0, keepdims=True)
         weights = [p.astype(jnp.bfloat16) for p in probs]
         grad_scores = [(p * (g - delta)).astype(jnp.bfloat16) for p, g in zip(probs, grad_probs)]
+        yield
         for j in range(window):
             dv_s[index[j], keys, :] += nn(weights[j], grads)
             dk_s[index[j], keys, :] += nn(grad_scores[j], queries)
@@ -149,8 +151,9 @@
             outq[at, feats:] = grad_query[row * tile_cols:(row + 1) * tile_cols]
 
     def tile_pair(tile, carry):
-        for upper in range(2):
-            one_tile(upper, tile)
+        low, high = one_tile(0, tile), one_tile(1, tile)
+        for stage in (low, high, low, low, high, high):
+            next(stage, None)
         return carry
 
     for move in moves:
@@ -330,49 +333,44 @@
 
 def weight_grad_kernel(steps, order, *refs):
     (outq_parts, upstream, normed), refs = [refs[i * steps:(i + 1) * steps] for i in range(3)], refs[3 * steps:]
-    wide, (grad, outq, up, own, sums, dkv_halos, normed_halos, sems, wide_sems) = refs[:5], refs[5:]
-    feats, chunk, halo = outq.shape[1] // 2, outq_parts[0].shape[0], HALO * LONGITUDES
+    dkv, dkv_top, dkv_bot, normed_top, normed_bot, grad, outq, up, own, sems = refs
+    feats, chunk = outq.shape[1] // 2, outq_parts[0].shape[0]
     groups = [
         [
             pltpu.make_async_copy(part, held.at[pl.ds(pl.multiple_of(order[i], 16), chunk)], sems.at[group, i])
             for i, part in enumerate(parts)
         ]
-        for group, (parts, held) in enumerate(((outq_parts, outq), (upstream, up), (normed, own)))
+        for group, (parts, held) in enumerate(((outq_parts, outq), (normed, own), (upstream, up)))
     ]
-    places = [sums] + [held.at[pl.ds(at, halo)] for held in (dkv_halos, normed_halos) for at in (0, halo)]
-    wide_moves = [
-        pltpu.make_async_copy(part, held, wide_sems.at[i]) for i, (part, held) in enumerate(zip(wide, places))
-    ]
-    for move in groups[0] + groups[1] + groups[2] + wide_moves:
-        move.start()
+    for moves in groups:
+        for move in moves:
+            move.start()
 
     def product(left, right):
         return lax.dot_general(left, right, (((0,), (0,)), ((), ())), preferred_element_type=F32)
 
-    for move in groups[0] + groups[1]:
+    keyval = product(dkv_top[...], normed_top[...]) + product(dkv_bot[...], normed_bot[...])
+    for moves in groups[:2]:
+        for move in moves:
+            move.wait()
+    grad[2 * feats:, :] = (keyval + product(dkv[...].astype(BF16), own[...])).astype(BF16)
+    grad[feats:2 * feats, :] = product(outq[:, feats:], own[...]).astype(BF16)
+    for move in groups[2]:
         move.wait()
     grad[:feats, :] = product(outq[:, :feats], up[...]).astype(BF16)
-    for move in groups[2]:
-        move.wait()
-    grad[feats:2 * feats, :] = product(outq[:, feats:], own[...]).astype(BF16)
-    for move in wide_moves:
-        move.wait()
-    keyval = product(sums[...].astype(BF16), own[...])
-    grad[2 * feats:, :] = (keyval + product(dkv_halos[...], normed_halos[...])).astype(BF16)
 
 
 def weight_grads(order, outq_parts, upstream, normed, dkv, dkv_halos, normed_halos):
     steps, (chunk, rows), width = len(normed), outq_parts[0].shape, normed[0].shape[1]
-    band, halos = steps * chunk, 2 * HALO * LONGITUDES
+    band = steps * chunk
     return call(
         functools.partial(weight_grad_kernel, steps),
-        [shape(2 * rows, width)], [SMEM] + [HBM] * (3 * steps + 5), [VMEM],
+        [shape(2 * rows, width)], [SMEM] + [HBM] * (3 * steps) + [VMEM] * 5, [VMEM],
         (order, *outq_parts, *upstream, *normed, dkv, *dkv_halos, *normed_halos),
-        flops=2 * width * rows * (2 * band + halos),
+        flops=2 * width * rows * (2 * band + 2 * HALO * LONGITUDES),
         scratch=[
             pltpu.VMEM((band, rows), BF16), pltpu.VMEM((band, width), BF16), pltpu.VMEM((band, width), BF16),
-            pltpu.VMEM((band, rows), F32), pltpu.VMEM((halos, rows), BF16), pltpu.VMEM((halos, width), BF16),
-            pltpu.SemaphoreType.DMA((3, steps)), pltpu.SemaphoreType.DMA((5,)),
+            pltpu.SemaphoreType.DMA((3, steps)),
         ],
     )[0]
 

time: 280 us -> 278 us (level)
  transfers between devices with their start and end apart: 23 -> 23, of which waited for: 7 -> 7; matrix products, arithmetic and copies ran while one was open for 5% -> 5% of each run, Pallas kernels for 31% -> 30%
where the time goes in v13:
time: 278 us; the launch traced here: 276 us
  waiting for transfers between devices  103 us (37%)
  Pallas kernels  91 us (33%)
  starting transfers between devices  49.1 us (18%)
  between operations  14.3 us (5%)
  local copies, waits for them, and re-layouts  10.4 us (4%)
  other arithmetic  8.93 us (3%)
    pallas_call x6, Pallas kernels, call(): pl.pallas_call(kernel, out_shape=tuple(out_shape), in_specs=list(in_specs...  86.7 us
    ppermute x13, waiting for transfers between devices, permuted(): return lax.ppermute(x, GROUP, [(at(*a), at(*b)) for a, b in pairs])  60.4 us
    psum x1, waiting for transfers between devices, on_device(): grads_sum = lax.psum(grads, ('z', 'c'))  42.3 us
    ppermute x13, starting transfers between devices, permuted(): return lax.ppermute(x, GROUP, [(at(*a), at(*b)) for a, b in pairs])  32.6 us
    ppermute x6, starting transfers between devices, passed_along(): return lax.ppermute(x, ('z', 'c'), pairs)  14.9 us
  transfers between devices with their start and end apart: 23, of which 7 were waited for; matrix products, arithmetic and copies ran while one was open for 5% of the time, Pallas kernels for 30%

profile of v13, /device:TPU:0, one launch (start us, length us, event | category | flops | bytes accessed | tf_op | source)
XLA Modules:
  0.0 276.4 jit_solution(14442510301824198806)
XLA Ops:
  7.2 2.6 shard_map.120
  9.8 2.9 %collective-permute-start = (bf16[512,1024]{1,0:T(8,128)(2,1)}, bf16[512,1024]{1,0:T(8,128)(2,1)}, u32[]{:S(2)}, u32[]{:S(2)}) collective-permute-start(bf16[512,1024]{1,0:T(8,128)(2,1)} %shard_map.120), channel_id=1, source_target_pairs={{2,0},{4,1},{0,2},{6,3},{1,4},{7,5},{3,6},{5,7},{10,8},{12,9},{8,1... | collective-permute-start | bytes 3145736 | tf_op jit(solution)/shard_map/ppermute | solution.py:497
  12.8 1.6 copy_multiply_fusion
  14.4 1.5 pad_maximum_fusion.refs_4_
  16.0 20.2 %collective-permute-done.refs_0_.refs_8_ = bf16[512,1024]{1,0:T(8,128)(2,1)} collective-permute-done((bf16[512,1024]{1,0:T(8,128)(2,1)}, bf16[512,1024]{1,0:T(8,128)(2,1)}, u32[]{:S(2)}, u32[]{:S(2)}) %collective-permute-start) | collective-permute-done | bytes 1048608 | tf_op jit(solution)/shard_map/ppermute | solution.py:497
  36.1 1.0 collective-permute-done.1.refs_1_.refs_9_
  37.2 1.3 broadcast_select_fusion.4
  38.7 0.7 collective-permute-start.3
  39.4 11.6 %collective-permute-done.2.refs_2_.refs_10_ = bf16[512,1024]{1,0:T(8,128)(2,1)S(1)} collective-permute-done((bf16[512,1024]{1,0:T(8,128)(2,1)S(1)}, bf16[512,1024]{1,0:T(8,128)(2,1)S(1)}, u32[]{:S(2)}, u32[]{:S(2)}) %collective-permute-start.2) | collective-permute-done | bytes 1048608 | tf_op jit(solution)/shard_map/ppermute | solution.py:497
  51.0 1.0 copy-done.8
  52.0 1.1 broadcast_select_fusion.3.refs_3_.refs_11_
  53.1 1.0 broadcast_select_fusion
  54.2 0.8 slice.9.weight
  55.5 1.5 collective-permute-start.7
  57.0 5.5 %collective-permute-start.8 = (bf16[512,1024]{1,0:T(8,128)(2,1)S(1)}, bf16[512,1024]{1,0:T(8,128)(2,1)}, u32[]{:S(2)}, u32[]{:S(2)}) collective-permute-start(bf16[512,1024]{1,0:T(8,128)(2,1)S(1)} %copy-done.2), channel_id=1, source_target_pairs={{3,0},{5,1},{1,2},{7,3},{0,4},{6,5},{2,6},{4,7},{11,8},{13,9},{9,1... | collective-permute-start | bytes 3145736 | tf_op jit(solution)/shard_map/ppermute | solution.py:497
  62.4 1.3 dynamic-slice_bitcast_fusion.order
  63.7 1.6 copy.14.weight
  65.3 9.8 %shard_map.121 = (bf16[2048,768]{1,0:T(8,128)(2,1)}, bf16[1536,512]{1,0:T(8,128)(2,1)}, bf16[1536,512]{1,0:T(8,128)(2,1)}, bf16[1536,1024]{1,0:T(8,128)(2,1)}, bf16[1536,1024]{1,0:T(8,128)(2,1)}) custom-call(s32[4]{0:T(128)} %dynamic-slice_bitcast_fusion.order, bf16[1024,768]{1,0:T(8,128)(2,1)} %copy.14.weight, ...), custom_call_target="tpu_custom_call" | custom-call | flops 3221225472 | bytes 18350096 | tf_op jit(solution)/shard_map/pallas_call | solution.py:203
  75.1 2.1 collective-permute-start.5
  77.2 1.3 collective-permute-start.6
  78.5 6.9 %collective-permute-done.8.refs_1_.refs_5_ = bf16[512,1024]{1,0:T(8,128)(2,1)} collective-permute-done((bf16[512,1024]{1,0:T(8,128)(2,1)S(1)}, bf16[512,1024]{1,0:T(8,128)(2,1)}, u32[]{:S(2)}, u32[]{:S(2)}) %collective-permute-start.8) | collective-permute-done | bytes 1048608 | tf_op jit(solution)/shard_map/ppermute | solution.py:497
  85.4 1.3 broadcast_select_fusion.2
  86.7 1.4 collective-permute-start.9
  88.1 0.7 collective-permute-start.10
  88.8 11.6 %collective-permute-done.9.refs_2_.refs_6_ = bf16[512,1024]{1,0:T(8,128)(2,1)S(1)} collective-permute-done((bf16[512,1024]{1,0:T(8,128)(2,1)S(1)}, bf16[512,1024]{1,0:T(8,128)(2,1)S(1)}, u32[]{:S(2)}, u32[]{:S(2)}) %collective-permute-start.9) | collective-permute-done | bytes 1048608 | tf_op jit(solution)/shard_map/ppermute | solution.py:497
  100.4 1.0 copy-done.9
  101.4 1.1 broadcast_select_fusion.1.refs_3_.refs_7_
  102.5 5.3 %collective-permute-start.11 = (bf16[1536,1024]{1,0:T(8,128)(2,1)}, bf16[1536,1024]{1,0:T(8,128)(2,1)}, u32[]{:S(2)}, u32[]{:S(2)}) collective-permute-start(bf16[1536,1024]{1,0:T(8,128)(2,1)} %get-tuple-element.100), channel_id=1, source_target_pairs={{0,1},{1,8},{8,9},{9,16},{16,17},{17,24},{24,25},{2,3},{3,10},{10,... | collective-permute-start | bytes 9437192 | tf_op jit(solution)/shard_map/ppermute | solution.py:466
  107.8 1.3 collective-permute-start.12
  109.1 0.6 pad_dynamic-slice_fusion.cells
  109.7 1.5 collective-permute-start.15
  111.2 41.0 %shard_map.122 = (bf16[512,512]{1,0:T(8,128)(2,1)}, bf16[512,512]{1,0:T(8,128)(2,1)}, bf16[512,512]{1,0:T(8,128)(2,1)}, bf16[512,512]{1,0:T(8,128)(2,1)}, f32[20...) custom-call(s32[20]{0:T(128)} %pad_dynamic-slice_fusion.cells, ...), custom_call_target="tpu_custom_call" | custom-call | flops 13958643712 | bytes 20447328 | tf_op jit(solution)/shard_map/pallas_call | solution.py:203
  152.2 1.3 collective-permute-start.13
  153.5 3.7 %collective-permute-start.14 = (bf16[1536,512]{1,0:T(8,128)(2,1)}, bf16[1536,512]{1,0:T(8,128)(2,1)S(1)}, u32[]{:S(2)}, u32[]{:S(2)}) collective-permute-start(bf16[1536,512]{1,0:T(8,128)(2,1)} %get-tuple-element.99.refs_14_), channel_id=1, source_target_pairs={{0,1},{1,8},{8,9},{9,16},{16,17},{17,24},{24,25},{2,3},{3,10},{10,... | collective-permute-start | bytes 4718600 | tf_op jit(solution)/shard_map/ppermute | solution.py:466
  157.1 14.5 %shard_map.123 = bf16[1024,1024]{1,0:T(8,128)(2,1)} custom-call(s32[4]{0:T(128)} %dynamic-slice_bitcast_fusion.order, bf16[512,512]{1,0:T(8,128)(2,1)} %get-tuple-element.93.refs_0_, bf16[512,512]{1,0:T(8,128)(2,1)} %get-tuple-element.94.refs_1_, bf16[512,512]{1,0:T(8,128)(2,1)} %get-tuple-element.95.refs_2_, bf16[512,512]{1,0:T(8,128)(2,1)} %get-tuple-element.96.refs_3_, ...), custom_call_target="tpu_custom_call" | custom-call | flops 7516192768 | bytes 26214416 | tf_op jit(solution)/shard_map/pallas_call | solution.py:203
  171.7 1.1 copy-done.4
  172.8 1.2 copy-done.5
  174.0 6.8 %shard_map.124 = (bf16[512,1024]{1,0:T(8,128)(2,1)}, bf16[512,1024]{1,0:T(8,128)(2,1)}, bf16[512,1024]{1,0:T(8,128)(2,1)}, bf16[512,1024]{1,0:T(8,128)(2,1)}) custom-call(s32[4]{0:T(128)} %dynamic-slice_bitcast_fusion.order, f32[2048,512]{1,0:T(8,128)} %get-tuple-element.97.refs_12_.own, bf16[1536,512]{1,0:T(8,128)(2,1)} %copy-done.4, ...), custom_call_target="tpu_custom_call" | custom-call | tf_op jit(solution)/shard_map/pallas_call | solution.py:203
  180.8 0.5 collective-permute-start.16
  181.4 3.2 %collective-permute-start.17 = (bf16[512,1024]{1,0:T(8,128)(2,1)}, bf16[512,1024]{1,0:T(8,128)(2,1)S(1)}, u32[]{:S(2)}, u32[]{:S(2)}) collective-permute-start(bf16[512,1024]{1,0:T(8,128)(2,1)} %get-tuple-element.109), channel_id=1, source_target_pairs={{0,3},{1,5},{2,1},{3,7},{4,0},{5,6},{6,2},{7,4},{8,11},{9,13},{10,... | collective-permute-start | bytes 3145736 | tf_op jit(solution)/shard_map/ppermute | solution.py:497
  184.6 1.6 collective-permute-start.18
  186.2 9.5 %collective-permute-start.19 = (bf16[512,1024]{1,0:T(8,128)(2,1)}, bf16[512,1024]{1,0:T(8,128)(2,1)}, u32[]{:S(2)}, u32[]{:S(2)}) collective-permute-start(bf16[512,1024]{1,0:T(8,128)(2,1)} %get-tuple-element.111), channel_id=1, source_target_pairs={{0,0},{1,6},{2,2},{3,4},{4,3},{5,5},{6,1},{7,7},{8,8},{9,14},{10,1... | collective-permute-start | bytes 3145736 | tf_op jit(solution)/shard_map/ppermute | solution.py:497
  195.7 42.3 %all-reduce.3.cloned.1.call-done = bf16[1024,1024]{1,0:T(8,128)(2,1)} async-done(((bf16[1024,1024]{1,0:T(8,128)(2,1)}), bf16[1024,1024]{1,0:T(8,128)(2,1)}) %all-reduce.3.cloned.1.call-update) | async-done | bytes 2097168 | tf_op jit(solution)/shard_map/psum | solution.py:556
  238.0 4.8 %collective-permute-start.21 = (bf16[1024,1024]{1,0:T(8,128)(2,1)}, bf16[1024,1024]{1,0:T(8,128)(2,1)}, u32[]{:S(2)}, u32[]{:S(2)}) collective-permute-start(bf16[1024,1024]{1,0:T(8,128)(2,1)} %all-reduce.3.cloned.1.call-done), channel_id=1, source_target_pairs={{5,1},{7,3},{0,4},{2,6},{13,9},{15,11},{8,12},{10,14},{21,17},{23,... | collective-permute-start | bytes 6291464 | tf_op jit(solution)/shard_map/ppermute | solution.py:497
  242.9 1.2 dynamic-slice_bitcast_fusion.1.leads
  244.0 12.1 %shard_map.125 = (bf16[512,1024]{1,0:T(8,128)(2,1)}, bf16[512,1024]{1,0:T(8,128)(2,1)}) custom-call(s32[4]{0:T(128)} %dynamic-slice_bitcast_fusion.1.leads, bf16[512,1024]{1,0:T(8,128)(2,1)} %tokens.3, f32[1,1024]{1,0:T(1,128)} %bitcast.22, bf16[512,1024]{1,0:T(8,128)(2,1)} %copy-done.10, bf16[512,1024]{1,0:T(8,128)(2,1)} %copy-done.11, ...), custom_call_target="tpu_custom_call" | custom-call | flops 4294967296 | bytes 15732752 | tf_op jit(solution)/shard_map/pallas_call | solution.py:203
  256.2 9.2 %collective-permute-done.21 = bf16[1024,1024]{1,0:T(8,128)(2,1)} collective-permute-done((bf16[1024,1024]{1,0:T(8,128)(2,1)}, bf16[1024,1024]{1,0:T(8,128)(2,1)}, u32[]{:S(2)}, u32[]{:S(2)}) %collective-permute-start.21) | collective-permute-done | bytes 2097184 | tf_op jit(solution)/shard_map/ppermute | solution.py:497
  265.3 4.2 %shard_map.126 = (f32[4,192,1024]{2,1,0:T(8,128)}, f32[4,64,1024]{2,1,0:T(8,128)}) custom-call(s32[1]{0:T(128)} %bitcast.8.flag, bf16[4,4,64,1024]{3,2,1,0:T(8,128)(2,1)S(1)} %bitcast.15, bf16[4,4,64,1024]{3,2,1,0:T(8,128)(2,1)} %bitcast.10.other), custom_call_target="tpu_custom_call" | custom-call | flops 1048576 | bytes 8388608 | tf_op jit(solution)/shard_map/pallas_call | solution.py:430
  (45 shorter events, 1.0 us)
Async XLA Ops:
  7.2 5.7 %copy-start.6 = (bf16[3]{0:T(256)(128)(2,1)S(1)}, bf16[3]{0:T(256)(128)(2,1)}, u32[]{:S(2)}) copy-start(bf16[3]{0:T(256)(128)(2,1)} %constant.30.clone) | copy-start | bytes 22
  7.2 230.8 %all-reduce.3.cloned.1.call-start = ((), (), s32[]{:S(2)}) async-start(), calls=%async_computation | async-start | bytes 4194304 | tf_op jit(solution)/shard_map/psum | solution.py:556
  9.8 4.6 %copy-start.3 = (bf16[4,64,1024]{2,1,0:T(8,128)(2,1)S(1)}, bf16[4,64,1024]{2,1,0:T(8,128)(2,1)}, u32[]{:S(2)}) copy-start(bf16[4,64,1024]{2,1,0:T(8,128)(2,1)} %param.12) | copy-start | bytes 1572868
  9.8 26.3 %collective-permute-start = (bf16[512,1024]{1,0:T(8,128)(2,1)}, bf16[512,1024]{1,0:T(8,128)(2,1)}, u32[]{:S(2)}, u32[]{:S(2)}) collective-permute-start(bf16[512,1024]{1,0:T(8,128)(2,1)} %shard_map.120), channel_id=1, source_target_pairs={{2,0},{4,1},{0,2},{6,3},{1,4},{7,5},{3,6},{5,7},{10,8},{12,9},{8,1... | collective-permute-start | bytes 3145736 | tf_op jit(solution)/shard_map/ppermute | solution.py:497
  12.8 24.3 %collective-permute-start.1 = (bf16[512,1024]{1,0:T(8,128)(2,1)}, bf16[512,1024]{1,0:T(8,128)(2,1)}, u32[]{:S(2)}, u32[]{:S(2)}) collective-permute-start(bf16[512,1024]{1,0:T(8,128)(2,1)} %shard_map.120), channel_id=1, source_target_pairs={{3,0},{5,1},{1,2},{7,3},{0,4},{6,5},{2,6},{4,7},{11,8},{13,9},{9,1... | collective-permute-start | bytes 3145736 | tf_op jit(solution)/shard_map/ppermute | solution.py:497
  14.4 22.8 %copy-start.1 = (bf16[512,1024]{1,0:T(8,128)(2,1)S(1)}, bf16[512,1024]{1,0:T(8,128)(2,1)}, u32[]{:S(2)}) copy-start(bf16[512,1024]{1,0:T(8,128)(2,1)} %shard_map.120) | copy-start | bytes 3145732
  37.1 16.0 %collective-permute-start.4 = (bf16[1024,1024]{1,0:T(8,128)(2,1)}, bf16[1024,1024]{1,0:T(8,128)(2,1)}, u32[]{:S(2)}, u32[]{:S(2)}) collective-permute-start(bf16[1024,1024]{1,0:T(8,128)(2,1)} %pad_maximum_fusion.refs_4_), channel_id=1, source_target_pairs={{0,1},{1,0},{2,3},{3,2},{4,5},{5,4},{6,7},{7,6},{8,9},{9,8},{10,11... | collective-permute-start | bytes 6291464 | tf_op jit(solution)/shard_map/ppermute | solution.py:524
  38.5 12.5 %collective-permute-start.2 = (bf16[512,1024]{1,0:T(8,128)(2,1)S(1)}, bf16[512,1024]{1,0:T(8,128)(2,1)S(1)}, u32[]{:S(2)}, u32[]{:S(2)}) collective-permute-start(bf16[512,1024]{1,0:T(8,128)(2,1)S(1)} %broadcast_select_fusion.4), channel_id=1, source_target_pairs={{0,4},{1,0},{2,6},{3,2},{4,5},{5,1},{6,7},{7,3},{8,12},{9,8},{10,1... | collective-permute-start | bytes 3145736 | tf_op jit(solution)/shard_map/ppermute | solution.py:497
  38.7 13.3 %collective-permute-start.3 = (bf16[512,1024]{1,0:T(8,128)(2,1)}, bf16[512,1024]{1,0:T(8,128)(2,1)S(1)}, u32[]{:S(2)}, u32[]{:S(2)}) collective-permute-start(bf16[512,1024]{1,0:T(8,128)(2,1)} %collective-permute-done.refs_0_.refs_8_), channel_id=1, source_target_pairs={{1,3},{3,1},{4,6},{6,4},{9,11},{11,9},{12,14},{14,12},{17,19},{19,... | collective-permute-start | bytes 3145736 | tf_op jit(solution)/shard_map/ppermute | solution.py:497
  51.0 1.0 copy-start.8
  54.1 1.4 copy-start.2
  55.5 23.0 %collective-permute-start.7 = (bf16[512,1024]{1,0:T(8,128)(2,1)S(1)}, bf16[512,1024]{1,0:T(8,128)(2,1)}, u32[]{:S(2)}, u32[]{:S(2)}) collective-permute-start(bf16[512,1024]{1,0:T(8,128)(2,1)S(1)} %copy-done.2), channel_id=1, source_target_pairs={{2,0},{4,1},{0,2},{6,3},{1,4},{7,5},{3,6},{5,7},{10,8},{12,9},{8,1... | collective-permute-start | bytes 3145736 | tf_op jit(solution)/shard_map/ppermute | solution.py:497
  57.0 28.4 %collective-permute-start.8 = (bf16[512,1024]{1,0:T(8,128)(2,1)S(1)}, bf16[512,1024]{1,0:T(8,128)(2,1)}, u32[]{:S(2)}, u32[]{:S(2)}) collective-permute-start(bf16[512,1024]{1,0:T(8,128)(2,1)S(1)} %copy-done.2), channel_id=1, source_target_pairs={{3,0},{5,1},{1,2},{7,3},{0,4},{6,5},{2,6},{4,7},{11,8},{13,9},{9,1... | collective-permute-start | bytes 3145736 | tf_op jit(solution)/shard_map/ppermute | solution.py:497
  75.1 27.4 %collective-permute-start.5 = (bf16[1536,512]{1,0:T(8,128)(2,1)}, bf16[1536,512]{1,0:T(8,128)(2,1)S(1)}, u32[]{:S(2)}, u32[]{:S(2)}) collective-permute-start(bf16[1536,512]{1,0:T(8,128)(2,1)} %get-tuple-element.76), channel_id=1, source_target_pairs={{0,1},{1,8},{8,9},{9,16},{16,17},{17,24},{24,25},{2,3},{3,10},{10,... | collective-permute-start | bytes 4718600 | tf_op jit(solution)/shard_map/ppermute | solution.py:466
  77.2 25.3 %collective-permute-start.6 = (bf16[1536,512]{1,0:T(8,128)(2,1)}, bf16[1536,512]{1,0:T(8,128)(2,1)}, u32[]{:S(2)}, u32[]{:S(2)}) collective-permute-start(bf16[1536,512]{1,0:T(8,128)(2,1)} %get-tuple-element.77), channel_id=1, source_target_pairs={{1,0},{8,1},{9,8},{16,9},{17,16},{24,17},{25,24},{3,2},{10,3},{11,... | collective-permute-start | bytes 4718600 | tf_op jit(solution)/shard_map/ppermute | solution.py:466
  86.7 22.3 %copy-start.12 = (s32[64]{0:T(128)S(1)}, s32[64]{0:T(128)}, u32[]{:S(2)}) copy-start(s32[64]{0:T(128)} %param.13) | copy-start | bytes 772
  86.7 13.7 %collective-permute-start.9 = (bf16[512,1024]{1,0:T(8,128)(2,1)S(1)}, bf16[512,1024]{1,0:T(8,128)(2,1)S(1)}, u32[]{:S(2)}, u32[]{:S(2)}) collective-permute-start(bf16[512,1024]{1,0:T(8,128)(2,1)S(1)} %broadcast_select_fusion.2), channel_id=1, source_target_pairs={{0,4},{1,0},{2,6},{3,2},{4,5},{5,1},{6,7},{7,3},{8,12},{9,8},{10,1... | collective-permute-start | bytes 3145736 | tf_op jit(solution)/shard_map/ppermute | solution.py:497
  88.1 13.3 %collective-permute-start.10 = (bf16[512,1024]{1,0:T(8,128)(2,1)}, bf16[512,1024]{1,0:T(8,128)(2,1)S(1)}, u32[]{:S(2)}, u32[]{:S(2)}) collective-permute-start(bf16[512,1024]{1,0:T(8,128)(2,1)} %collective-permute-done.7.refs_0_.refs_4_), channel_id=1, source_target_pairs={{1,3},{3,1},{4,6},{6,4},{9,11},{11,9},{12,14},{14,12},{17,19},{19,... | collective-permute-start | bytes 3145736 | tf_op jit(solution)/shard_map/ppermute | solution.py:497
  100.4 1.0 copy-start.9
  102.5 8.7 %copy-start.7 = (bf16[1536,512]{1,0:T(8,128)(2,1)}, bf16[1536,512]{1,0:T(8,128)(2,1)S(1)}, u32[]{:S(2)}) copy-start(bf16[1536,512]{1,0:T(8,128)(2,1)S(1)} %collective-permute-done.5.kv_top) | copy-start | bytes 4718596
  102.5 54.6 %collective-permute-start.11 = (bf16[1536,1024]{1,0:T(8,128)(2,1)}, bf16[1536,1024]{1,0:T(8,128)(2,1)}, u32[]{:S(2)}, u32[]{:S(2)}) collective-permute-start(bf16[1536,1024]{1,0:T(8,128)(2,1)} %get-tuple-element.100), channel_id=1, source_target_pairs={{0,1},{1,8},{8,9},{9,16},{16,17},{17,24},{24,25},{2,3},{3,10},{10,... | collective-permute-start | bytes 9437192 | tf_op jit(solution)/shard_map/ppermute | solution.py:466
  107.8 49.4 %collective-permute-start.12 = (bf16[1536,1024]{1,0:T(8,128)(2,1)}, bf16[1536,1024]{1,0:T(8,128)(2,1)}, u32[]{:S(2)}, u32[]{:S(2)}) collective-permute-start(bf16[1536,1024]{1,0:T(8,128)(2,1)} %get-tuple-element.101), channel_id=1, source_target_pairs={{1,0},{8,1},{9,8},{16,9},{17,16},{24,17},{25,24},{3,2},{10,3},{11,... | collective-permute-start | bytes 9437192 | tf_op jit(solution)/shard_map/ppermute | solution.py:466
  109.7 71.1 %collective-permute-start.15 = (bf16[1024,1024]{1,0:T(8,128)(2,1)}, bf16[1024,1024]{1,0:T(8,128)(2,1)}, u32[]{:S(2)}, u32[]{:S(2)}) collective-permute-start(bf16[1024,1024]{1,0:T(8,128)(2,1)} %pad_maximum_fusion.refs_4_), channel_id=1, source_target_pairs={{2,0},{0,2},{3,1},{1,3},{6,4},{4,6},{7,5},{5,7},{10,8},{8,10},{11,... | collective-permute-start | bytes 6291464 | tf_op jit(solution)/shard_map/ppermute | solution.py:521
  152.2 19.5 %collective-permute-start.13 = (bf16[1536,512]{1,0:T(8,128)(2,1)}, bf16[1536,512]{1,0:T(8,128)(2,1)S(1)}, u32[]{:S(2)}, u32[]{:S(2)}) collective-permute-start(bf16[1536,512]{1,0:T(8,128)(2,1)} %get-tuple-element.98.refs_13_), channel_id=1, source_target_pairs={{1,0},{8,1},{9,8},{16,9},{17,16},{24,17},{25,24},{3,2},{10,3},{11,... | collective-permute-start | bytes 4718600 | tf_op jit(solution)/shard_map/ppermute | solution.py:466
  153.5 18.2 %collective-permute-start.14 = (bf16[1536,512]{1,0:T(8,128)(2,1)}, bf16[1536,512]{1,0:T(8,128)(2,1)S(1)}, u32[]{:S(2)}, u32[]{:S(2)}) collective-permute-start(bf16[1536,512]{1,0:T(8,128)(2,1)} %get-tuple-element.99.refs_14_), channel_id=1, source_target_pairs={{0,1},{1,8},{8,9},{9,16},{16,17},{17,24},{24,25},{2,3},{3,10},{10,... | collective-permute-start | bytes 4718600 | tf_op jit(solution)/shard_map/ppermute | solution.py:466
  171.7 1.2 copy-start.4
  172.8 1.2 copy-start.5
  180.8 57.2 %collective-permute-start.16 = (bf16[512,1024]{1,0:T(8,128)(2,1)}, bf16[512,1024]{1,0:T(8,128)(2,1)S(1)}, u32[]{:S(2)}, u32[]{:S(2)}) collective-permute-start(bf16[512,1024]{1,0:T(8,128)(2,1)} %get-tuple-element.108), channel_id=1, source_target_pairs={{0,2},{1,4},{2,0},{3,6},{4,1},{5,7},{6,3},{7,5},{8,10},{9,12},{10,... | collective-permute-start | bytes 3145736 | tf_op jit(solution)/shard_map/ppermute | solution.py:497
  181.4 56.6 %collective-permute-start.17 = (bf16[512,1024]{1,0:T(8,128)(2,1)}, bf16[512,1024]{1,0:T(8,128)(2,1)S(1)}, u32[]{:S(2)}, u32[]{:S(2)}) collective-permute-start(bf16[512,1024]{1,0:T(8,128)(2,1)} %get-tuple-element.109), channel_id=1, source_target_pairs={{0,3},{1,5},{2,1},{3,7},{4,0},{5,6},{6,2},{7,4},{8,11},{9,13},{10,... | collective-permute-start | bytes 3145736 | tf_op jit(solution)/shard_map/ppermute | solution.py:497
  184.6 53.4 %collective-permute-start.18 = (bf16[512,1024]{1,0:T(8,128)(2,1)}, bf16[512,1024]{1,0:T(8,128)(2,1)}, u32[]{:S(2)}, u32[]{:S(2)}) collective-permute-start(bf16[512,1024]{1,0:T(8,128)(2,1)} %get-tuple-element.110), channel_id=1, source_target_pairs={{0,1},{1,7},{2,3},{3,5},{4,2},{5,4},{6,0},{7,6},{8,9},{9,15},{10,1... | collective-permute-start | bytes 3145736 | tf_op jit(solution)/shard_map/ppermute | solution.py:497
  186.2 51.9 %collective-permute-start.19 = (bf16[512,1024]{1,0:T(8,128)(2,1)}, bf16[512,1024]{1,0:T(8,128)(2,1)}, u32[]{:S(2)}, u32[]{:S(2)}) collective-permute-start(bf16[512,1024]{1,0:T(8,128)(2,1)} %get-tuple-element.111), channel_id=1, source_target_pairs={{0,0},{1,6},{2,2},{3,4},{4,3},{5,5},{6,1},{7,7},{8,8},{9,14},{10,1... | collective-permute-start | bytes 3145736 | tf_op jit(solution)/shard_map/ppermute | solution.py:497
  238.0 6.0 %collective-permute-start.20 = (bf16[1024,1024]{1,0:T(8,128)(2,1)}, bf16[1024,1024]{1,0:T(8,128)(2,1)}, u32[]{:S(2)}, u32[]{:S(2)}) collective-permute-start(bf16[1024,1024]{1,0:T(8,128)(2,1)} %collective-permute-done.15.refs_5_), channel_id=1, source_target_pairs={{0,1},{1,0},{2,3},{3,2},{4,5},{5,4},{6,7},{7,6},{8,9},{9,8},{10,11... | collective-permute-start | bytes 6291464 | tf_op jit(solution)/shard_map/ppermute | solution.py:524
  238.0 6.0 %copy-start.10 = (bf16[512,1024]{1,0:T(8,128)(2,1)}, bf16[512,1024]{1,0:T(8,128)(2,1)S(1)}, u32[]{:S(2)}) copy-start(bf16[512,1024]{1,0:T(8,128)(2,1)S(1)} %collective-permute-done.16.refs_0_) | copy-start | bytes 3145732
  238.0 4.9 %copy-start.11 = (bf16[512,1024]{1,0:T(8,128)(2,1)}, bf16[512,1024]{1,0:T(8,128)(2,1)S(1)}, u32[]{:S(2)}) copy-start(bf16[512,1024]{1,0:T(8,128)(2,1)S(1)} %collective-permute-done.17.refs_1_) | copy-start | bytes 3145732
  238.0 27.3 %collective-permute-start.21 = (bf16[1024,1024]{1,0:T(8,128)(2,1)}, bf16[1024,1024]{1,0:T(8,128)(2,1)}, u32[]{:S(2)}, u32[]{:S(2)}) collective-permute-start(bf16[1024,1024]{1,0:T(8,128)(2,1)} %all-reduce.3.cloned.1.call-done), channel_id=1, source_target_pairs={{5,1},{7,3},{0,4},{2,6},{13,9},{15,11},{8,12},{10,14},{21,17},{23,... | collective-permute-start | bytes 6291464 | tf_op jit(solution)/shard_map/ppermute | solution.py:497
  244.0 21.3 %copy-start = (bf16[1024,1024]{1,0:T(8,128)(2,1)S(1)}, bf16[1024,1024]{1,0:T(8,128)(2,1)}, u32[]{:S(2)}) copy-start(bf16[1024,1024]{1,0:T(8,128)(2,1)} %all-reduce.3.cloned.1.call-done) | copy-start | bytes 6291460
Sparse Core Ops, SparseCore 0:
  171.8 66.1 all-reduce.2

commit v14 on v13

--- a/solution.py
+++ b/solution.py
@@ -272,7 +272,7 @@
         move.wait()
 
 
-def projection_kernel(steps, feats, order, weight, *refs):
+def projection_kernel(steps, feats, order, flag, mine, sibling, *refs):
     parts, (qkv, kv_up, kv_down, normed_up, normed_down, held, sems) = refs[:steps], refs[steps:]
     chunk = parts[0].shape[0]
     halo, rest = HALO * LONGITUDES, (BAND_ROWS - HALO) * LONGITUDES
@@ -287,7 +287,8 @@
     for move in moves:
         move.start()
     for i in range(3):
-        product = nn(held[...], weight[:, i * feats:(i + 1) * feats]).astype(BF16)
+        at = slice(i * feats, (i + 1) * feats)
+        product = nt(held[...], jnp.where(flag[0] == 1, mine[at, :], sibling[at, :])).astype(BF16)
         qkv[:, i * feats:(i + 1) * feats] = product
         if i:
             kv_up[:, (i - 1) * feats:i * feats] = product[rest:]
@@ -296,14 +297,14 @@
         move.wait()
 
 
-def projections(order, weight, parts):
-    steps, feats, width = len(parts), weight.shape[1] // 3, parts[0].shape[1]
+def projections(order, flag, mine, sibling, parts):
+    steps, feats, width = len(parts), mine.shape[0] // 4, parts[0].shape[1]
     band, halo = BAND_ROWS * LONGITUDES, HALO * LONGITUDES
     return call(
         functools.partial(projection_kernel, steps, feats),
         [shape(band, 3 * feats)] + [shape(halo, 2 * feats)] * 2 + [shape(halo, width)] * 2,
-        [SMEM, VMEM] + [HBM] * steps, [VMEM] * 3 + [HBM] * 2, (order, weight, *parts),
-        flops=2 * band * weight.size,
+        [SMEM, SMEM, VMEM, VMEM] + [HBM] * steps, [VMEM] * 3 + [HBM] * 2, (order, flag, mine, sibling, *parts),
+        flops=6 * band * feats * width,
         scratch=[pltpu.VMEM((band, width), BF16), pltpu.SemaphoreType.DMA((steps,))],
     )
 
@@ -499,13 +500,13 @@
     def send_back(parts):
         return [permuted(x, list(zip(spots, slot))) for x, slot in zip(parts, slots)]
 
-    def gathered(x, *others):
+    def gathered(x, *others, extra=()):
         sent = lambda slot: permuted(x, list(zip(slot, spots)))
         if halves != 2:
             parts = [sent(slot) for slot in slots]
-            return parts, parts
-        first, second = lax.optimization_barrier((sent(slots[0]), sent(slots[1])))
-        hop = first, second
+            return parts, (*parts, *extra)
+        hop = lax.optimization_barrier((sent(slots[0]), sent(slots[1]), *extra))
+        first, second = hop[:2]
         first = after(first, *others)
         third = permuted(
             jnp.where(c == y, first, x),
@@ -532,13 +533,12 @@
         return jnp.concatenate([qkv.reshape(3 * feats, WIDTH), out.reshape(feats, WIDTH)], axis=0)
 
     blocks = [split(qkv_weight, out_weight)]
-    normed_parts, hop = gathered(normed)
+    flag = jnp.reshape(c == y, (1,)).astype(jnp.int32)
+    normed_parts, (*hop, order, leads, flag) = gathered(normed, extra=(order, leads, flag))
     sibling = from_sibling(after(blocks[0], *hop))
-    group = jnp.where(c == y, blocks[0], sibling)
-    group_qkv, group_out = group[:3 * feats].T, group[3 * feats:]
-
-    *normed_parts, group_qkv, group_out = lax.optimization_barrier((*normed_parts, group_qkv, group_out))
-    qkv, kv_up, kv_down, normed_up, normed_down = projections(order, group_qkv, normed_parts)
+    group_out = jnp.where(c == y, blocks[0][3 * feats:], sibling[3 * feats:])
+    *normed_parts, sibling = lax.optimization_barrier((*normed_parts, sibling))
+    qkv, kv_up, kv_down, normed_up, normed_down = projections(order, flag, blocks[0], sibling, normed_parts)
     kv_top, kv_bot = passed_along(kv_up, 1), passed_along(kv_down, -1)
     upstream_parts, _ = gathered(after(upstream, *normed_parts), qkv)
 
@@ -562,7 +562,7 @@
     update, grad_input = token_outputs(leads, tokens, gain, parts_own, blocks)
     grads = after(grads_sum, *parts_own)
     pairs = [((1 - y, m, 1 - y), (y, m, 1 - y)) for y in range(2) for m in range(halves)]
-    flag = after(jnp.reshape(c == y, (1,)).astype(jnp.int32), grad_input, update)
+    flag = after(flag, grad_input, update)
     grad_qkv, grad_out = finished(grad_scale, flag, grads, permuted(grads, pairs))
     return update, grad_input, grad_qkv, grad_out
 

time: 278 us -> 279 us (level)
  local copies, waits for them, and re-layouts: 10.4 us -> 4.03 us
  waiting for transfers between devices: 103 us -> 109 us
    ppermute x13, waiting for transfers between devices: 60.4 us -> 64 us  [permuted(): return lax.ppermute(x, GROUP, [(at(*a), at(*b)) for a, b in pairs])]
  transfers between devices with their start and end apart: 23 -> 23, of which waited for: 7 -> 7; matrix products, arithmetic and copies ran while one was open for 5% -> 3% of each run, Pallas kernels for 30% -> 30%
where the time goes in v14:
time: 279 us; the launch traced here: 278 us
  waiting for transfers between devices  109 us (39%)
  Pallas kernels  91.7 us (33%)
  starting transfers between devices  51.8 us (19%)
  between operations  14.3 us (5%)
  other arithmetic  7.32 us (3%)
  local copies, waits for them, and re-layouts  4.03 us (1%)
    pallas_call x6, Pallas kernels, call(): pl.pallas_call(kernel, out_shape=tuple(out_shape), in_specs=list(in_specs...  87.5 us
    ppermute x13, waiting for transfers between devices, permuted(): return lax.ppermute(x, GROUP, [(at(*a), at(*b)) for a, b in pairs])  64 us
    psum x1, waiting for transfers between devices, on_device(): grads_sum = lax.psum(grads, ('z', 'c'))  44.9 us
    ppermute x13, starting transfers between devices, permuted(): return lax.ppermute(x, GROUP, [(at(*a), at(*b)) for a, b in pairs])  33.3 us
    ppermute x6, starting transfers between devices, passed_along(): return lax.ppermute(x, ('z', 'c'), pairs)  16.8 us
  transfers between devices with their start and end apart: 23, of which 7 were waited for; matrix products, arithmetic and copies ran while one was open for 3% of the time, Pallas kernels for 30%

profile of v14, /device:TPU:0, one launch (start us, length us, event | category | flops | bytes accessed | tf_op | source)
XLA Modules:
  0.0 278.1 jit_solution(17249244820412151870)
XLA Ops:
  7.2 0.0 all-reduce.3.cloned.1.call-start
  7.2 2.7 shard_map.120
  9.9 2.9 %collective-permute-start = (bf16[512,1024]{1,0:T(8,128)(2,1)}, bf16[512,1024]{1,0:T(8,128)(2,1)}, u32[]{:S(2)}, u32[]{:S(2)}) collective-permute-start(bf16[512,1024]{1,0:T(8,128)(2,1)} %shard_map.120), channel_id=1, source_target_pairs={{2,0},{4,1},{0,2},{6,3},{1,4},{7,5},{3,6},{5,7},{10,8},{12,9},{8,1... | collective-permute-start | bytes 3145736 | tf_op jit(solution)/shard_map/ppermute | solution.py:498
  12.9 0.1 collective-permute-start.1
  12.9 1.3 dynamic-slice_bitcast_fusion
  14.2 0.2 copy_multiply_fusion
  14.4 0.2 pad_maximum_fusion.mine.refs_4_
  14.6 21.6 %collective-permute-done.refs_0_.refs_8_ = bf16[512,1024]{1,0:T(8,128)(2,1)} collective-permute-done((bf16[512,1024]{1,0:T(8,128)(2,1)}, bf16[512,1024]{1,0:T(8,128)(2,1)}, u32[]{:S(2)}, u32[]{:S(2)}) %collective-permute-start) | collective-permute-done | bytes 1048608 | tf_op jit(solution)/shard_map/ppermute | solution.py:498
  36.2 1.0 collective-permute-done.1.refs_1_.refs_9_
  37.2 0.1 collective-permute-start.4
  37.3 1.4 broadcast_select_fusion.3
  38.7 0.2 collective-permute-start.2
  38.9 0.8 collective-permute-start.3
  39.7 11.5 %collective-permute-done.2.refs_2_.refs_10_ = bf16[512,1024]{1,0:T(8,128)(2,1)S(1)} collective-permute-done((bf16[512,1024]{1,0:T(8,128)(2,1)S(1)}, bf16[512,1024]{1,0:T(8,128)(2,1)S(1)}, u32[]{:S(2)}, u32[]{:S(2)}) %collective-permute-start.2) | collective-permute-done | bytes 1048608 | tf_op jit(solution)/shard_map/ppermute | solution.py:498
  51.2 1.3 broadcast_select_fusion.2.refs_3_.refs_11_
  52.5 0.0 copy-done.8
  52.5 1.5 collective-permute-start.7
  54.0 5.8 %collective-permute-start.8 = (bf16[512,1024]{1,0:T(8,128)(2,1)S(1)}, bf16[512,1024]{1,0:T(8,128)(2,1)S(1)}, u32[]{:S(2)}, u32[]{:S(2)}) collective-permute-start(bf16[512,1024]{1,0:T(8,128)(2,1)S(1)} %copy-done.2), channel_id=1, source_target_pairs={{3,0},{5,1},{1,2},{7,3},{0,4},{6,5},{2,6},{4,7},{11,8},{13,9},{9,1... | collective-permute-start | bytes 3145736 | tf_op jit(solution)/shard_map/ppermute | solution.py:498
  59.9 10.6 %shard_map.121 = (bf16[2048,768]{1,0:T(8,128)(2,1)}, bf16[1536,512]{1,0:T(8,128)(2,1)}, bf16[1536,512]{1,0:T(8,128)(2,1)}, bf16[1536,1024]{1,0:T(8,128)(2,1)}, bf16[1536,1024]{1,0:T(8,128)(2,1)}) custom-call(s32[4]{0:T(128)} %get-tuple-element.106.order, s32[1]{0:T(128)} %bitcast.3.flag, bf16[1024,1024]{1,0:T(8,128)(2,1)} %copy-done.3, ...), custom_call_target="tpu_custom_call" | custom-call | flops 3221225472 | bytes 20971540 | tf_op jit(solution)/shard_map/pallas_call | solution.py:203
  70.5 3.1 %collective-permute-start.5 = (bf16[1536,512]{1,0:T(8,128)(2,1)}, bf16[1536,512]{1,0:T(8,128)(2,1)}, u32[]{:S(2)}, u32[]{:S(2)}) collective-permute-start(bf16[1536,512]{1,0:T(8,128)(2,1)} %get-tuple-element.81), channel_id=1, source_target_pairs={{0,1},{1,8},{8,9},{9,16},{16,17},{17,24},{24,25},{2,3},{3,10},{10,... | collective-permute-start | bytes 4718600 | tf_op jit(solution)/shard_map/ppermute | solution.py:467
  73.6 1.3 collective-permute-start.6
  74.9 7.9 %collective-permute-done.8.refs_1_.refs_5_ = bf16[512,1024]{1,0:T(8,128)(2,1)S(1)} collective-permute-done((bf16[512,1024]{1,0:T(8,128)(2,1)S(1)}, bf16[512,1024]{1,0:T(8,128)(2,1)S(1)}, u32[]{:S(2)}, u32[]{:S(2)}) %collective-permute-start.8) | collective-permute-done | bytes 1048608 | tf_op jit(solution)/shard_map/ppermute | solution.py:498
  82.8 1.0 copy-done.9
  83.7 1.3 broadcast_select_fusion.1
  85.1 1.3 collective-permute-start.9
  86.4 0.7 collective-permute-start.10
  87.1 11.6 %collective-permute-done.9.refs_2_.refs_6_ = bf16[512,1024]{1,0:T(8,128)(2,1)S(1)} collective-permute-done((bf16[512,1024]{1,0:T(8,128)(2,1)S(1)}, bf16[512,1024]{1,0:T(8,128)(2,1)S(1)}, u32[]{:S(2)}, u32[]{:S(2)}) %collective-permute-start.9) | collective-permute-done | bytes 1048608 | tf_op jit(solution)/shard_map/ppermute | solution.py:498
  98.7 1.0 copy-done.10
  99.7 1.1 broadcast_select_fusion.refs_3_.refs_7_
  100.8 5.3 %collective-permute-start.11 = (bf16[1536,1024]{1,0:T(8,128)(2,1)}, bf16[1536,1024]{1,0:T(8,128)(2,1)}, u32[]{:S(2)}, u32[]{:S(2)}) collective-permute-start(bf16[1536,1024]{1,0:T(8,128)(2,1)} %get-tuple-element.104), channel_id=1, source_target_pairs={{0,1},{1,8},{8,9},{9,16},{16,17},{17,24},{24,25},{2,3},{3,10},{10,... | collective-permute-start | bytes 9437192 | tf_op jit(solution)/shard_map/ppermute | solution.py:467
  106.1 1.3 collective-permute-start.12
  107.4 0.7 pad_dynamic-slice_fusion.cells
  108.1 1.9 slice_select_fusion.weight
  110.0 1.5 collective-permute-start.15
  111.5 41.0 %shard_map.122 = (bf16[512,512]{1,0:T(8,128)(2,1)}, bf16[512,512]{1,0:T(8,128)(2,1)}, bf16[512,512]{1,0:T(8,128)(2,1)}, bf16[512,512]{1,0:T(8,128)(2,1)}, f32[20...) custom-call(s32[20]{0:T(128)} %pad_dynamic-slice_fusion.cells, s32[4]{0:T(128)} %get-tuple-element.106.order, ...), custom_call_target="tpu_custom_call" | custom-call | flops 13958643712 | bytes 20447328 | tf_op jit(solution)/shard_map/pallas_call | solution.py:203
  152.5 1.3 collective-permute-start.13
  153.8 4.6 %collective-permute-start.14 = (bf16[1536,512]{1,0:T(8,128)(2,1)}, bf16[1536,512]{1,0:T(8,128)(2,1)}, u32[]{:S(2)}, u32[]{:S(2)}) collective-permute-start(bf16[1536,512]{1,0:T(8,128)(2,1)} %get-tuple-element.103.refs_14_), channel_id=1, source_target_pairs={{0,1},{1,8},{8,9},{9,16},{16,17},{17,24},{24,25},{2,3},{3,10},{10,... | collective-permute-start | bytes 4718600 | tf_op jit(solution)/shard_map/ppermute | solution.py:467
  158.4 14.5 %shard_map.123 = bf16[1024,1024]{1,0:T(8,128)(2,1)} custom-call(s32[4]{0:T(128)} %get-tuple-element.106.order, bf16[512,512]{1,0:T(8,128)(2,1)} %get-tuple-element.97.refs_0_, bf16[512,512]{1,0:T(8,128)(2,1)} %get-tuple-element.98.refs_1_, bf16[512,512]{1,0:T(8,128)(2,1)} %get-tuple-element.99.refs_2_, bf16[512,512]{1,0:T(8,128)(2,1)} %get-tuple-element.100.refs_3_, ...), custom_call_target="tpu_custom_call" | custom-call | flops 7516192768 | bytes 26214416 | tf_op jit(solution)/shard_map/pallas_call | solution.py:203
  172.9 6.7 %shard_map.124 = (bf16[512,1024]{1,0:T(8,128)(2,1)}, bf16[512,1024]{1,0:T(8,128)(2,1)}, bf16[512,1024]{1,0:T(8,128)(2,1)}, bf16[512,1024]{1,0:T(8,128)(2,1)}) custom-call(s32[4]{0:T(128)} %get-tuple-element.106.order, f32[2048,512]{1,0:T(8,128)} %get-tuple-element.101.refs_12_.own, bf16[1536,512]{1,0:T(8,128)(2,1)} %collective-permute-done.13.above, ...), custom_call_target="tpu_custom_call" | custom-call | tf_op jit(solution)/shard_map/pallas_call | solution.py:203
  179.6 0.5 collective-permute-start.16
  180.1 3.3 %collective-permute-start.17 = (bf16[512,1024]{1,0:T(8,128)(2,1)}, bf16[512,1024]{1,0:T(8,128)(2,1)}, u32[]{:S(2)}, u32[]{:S(2)}) collective-permute-start(bf16[512,1024]{1,0:T(8,128)(2,1)} %get-tuple-element.113), channel_id=1, source_target_pairs={{0,3},{1,5},{2,1},{3,7},{4,0},{5,6},{6,2},{7,4},{8,11},{9,13},{10,... | collective-permute-start | bytes 3145736 | tf_op jit(solution)/shard_map/ppermute | solution.py:498
  183.5 1.6 collective-permute-start.18
  185.1 9.4 %collective-permute-start.19 = (bf16[512,1024]{1,0:T(8,128)(2,1)}, bf16[512,1024]{1,0:T(8,128)(2,1)}, u32[]{:S(2)}, u32[]{:S(2)}) collective-permute-start(bf16[512,1024]{1,0:T(8,128)(2,1)} %get-tuple-element.115), channel_id=1, source_target_pairs={{0,0},{1,6},{2,2},{3,4},{4,3},{5,5},{6,1},{7,7},{8,8},{9,14},{10,1... | collective-permute-start | bytes 3145736 | tf_op jit(solution)/shard_map/ppermute | solution.py:498
  194.5 44.9 %all-reduce.3.cloned.1.call-done = bf16[1024,1024]{1,0:T(8,128)(2,1)} async-done(((bf16[1024,1024]{1,0:T(8,128)(2,1)}), bf16[1024,1024]{1,0:T(8,128)(2,1)}) %all-reduce.3.cloned.1.call-update) | async-done | bytes 2097168 | tf_op jit(solution)/shard_map/psum | solution.py:556
  239.5 5.0 %collective-permute-start.21 = (bf16[1024,1024]{1,0:T(8,128)(2,1)}, bf16[1024,1024]{1,0:T(8,128)(2,1)}, u32[]{:S(2)}, u32[]{:S(2)}) collective-permute-start(bf16[1024,1024]{1,0:T(8,128)(2,1)} %all-reduce.3.cloned.1.call-done), channel_id=1, source_target_pairs={{5,1},{7,3},{0,4},{2,6},{13,9},{15,11},{8,12},{10,14},{21,17},{23,... | collective-permute-start | bytes 6291464 | tf_op jit(solution)/shard_map/ppermute | solution.py:498
  244.5 12.0 %shard_map.125 = (bf16[512,1024]{1,0:T(8,128)(2,1)}, bf16[512,1024]{1,0:T(8,128)(2,1)}) custom-call(s32[4]{0:T(128)} %get-tuple-element.65.leads, bf16[512,1024]{1,0:T(8,128)(2,1)} %tokens.3, f32[1,1024]{1,0:T(1,128)} %bitcast.19, bf16[512,1024]{1,0:T(8,128)(2,1)} %copy-done.11, bf16[512,1024]{1,0:T(8,128)(2,1)} %collective-permute-done.17.refs_1_, ...), custom_call_target="tpu_custom_call" | custom-call | flops 4294967296 | bytes 15732752 | tf_op jit(solution)/shard_map/pallas_call | solution.py:203
  256.5 10.5 %collective-permute-done.21 = bf16[1024,1024]{1,0:T(8,128)(2,1)} collective-permute-done((bf16[1024,1024]{1,0:T(8,128)(2,1)}, bf16[1024,1024]{1,0:T(8,128)(2,1)}, u32[]{:S(2)}, u32[]{:S(2)}) %collective-permute-start.21) | collective-permute-done | bytes 2097184 | tf_op jit(solution)/shard_map/ppermute | solution.py:498
  267.0 4.2 %shard_map.126 = (f32[4,192,1024]{2,1,0:T(8,128)}, f32[4,64,1024]{2,1,0:T(8,128)}) custom-call(s32[1]{0:T(128)} %bitcast.3.flag, bf16[4,4,64,1024]{3,2,1,0:T(8,128)(2,1)S(1)} %bitcast.14, bf16[4,4,64,1024]{3,2,1,0:T(8,128)(2,1)} %bitcast.9.other), custom_call_target="tpu_custom_call" | custom-call | flops 1048576 | bytes 8388608 | tf_op jit(solution)/shard_map/pallas_call | solution.py:431
  (41 shorter events, 0.1 us)
Async XLA Ops:
  7.2 7.1 %copy-start.7 = (bf16[3]{0:T(256)(128)(2,1)S(1)}, bf16[3]{0:T(256)(128)(2,1)}, u32[]{:S(2)}) copy-start(bf16[3]{0:T(256)(128)(2,1)} %constant.30.clone) | copy-start | bytes 22
  7.2 7.1 %copy-start.6 = (bf16[4,192,1024]{2,1,0:T(8,128)(2,1)S(1)}, bf16[4,192,1024]{2,1,0:T(8,128)(2,1)}, u32[]{:S(2)}) copy-start(bf16[4,192,1024]{2,1,0:T(8,128)(2,1)} %param.11) | copy-start | bytes 4718596
  7.2 232.3 %all-reduce.3.cloned.1.call-start = ((), (), s32[]{:S(2)}) async-start(), calls=%async_computation | async-start | bytes 4194304 | tf_op jit(solution)/shard_map/psum | solution.py:556
  9.9 4.5 %copy-start.5 = (bf16[4,64,1024]{2,1,0:T(8,128)(2,1)S(1)}, bf16[4,64,1024]{2,1,0:T(8,128)(2,1)}, u32[]{:S(2)}) copy-start(bf16[4,64,1024]{2,1,0:T(8,128)(2,1)} %param.12) | copy-start | bytes 1572868
  9.9 26.3 %collective-permute-start = (bf16[512,1024]{1,0:T(8,128)(2,1)}, bf16[512,1024]{1,0:T(8,128)(2,1)}, u32[]{:S(2)}, u32[]{:S(2)}) collective-permute-start(bf16[512,1024]{1,0:T(8,128)(2,1)} %shard_map.120), channel_id=1, source_target_pairs={{2,0},{4,1},{0,2},{6,3},{1,4},{7,5},{3,6},{5,7},{10,8},{12,9},{8,1... | collective-permute-start | bytes 3145736 | tf_op jit(solution)/shard_map/ppermute | solution.py:498
  12.9 24.3 %collective-permute-start.1 = (bf16[512,1024]{1,0:T(8,128)(2,1)}, bf16[512,1024]{1,0:T(8,128)(2,1)}, u32[]{:S(2)}, u32[]{:S(2)}) collective-permute-start(bf16[512,1024]{1,0:T(8,128)(2,1)} %shard_map.120), channel_id=1, source_target_pairs={{3,0},{5,1},{1,2},{7,3},{0,4},{6,5},{2,6},{4,7},{11,8},{13,9},{9,1... | collective-permute-start | bytes 3145736 | tf_op jit(solution)/shard_map/ppermute | solution.py:498
  14.4 22.9 %copy-start.1 = (bf16[512,1024]{1,0:T(8,128)(2,1)S(1)}, bf16[512,1024]{1,0:T(8,128)(2,1)}, u32[]{:S(2)}) copy-start(bf16[512,1024]{1,0:T(8,128)(2,1)} %shard_map.120) | copy-start | bytes 3145732
  14.6 37.8 %copy-start.3 = (bf16[1024,1024]{1,0:T(8,128)(2,1)}, bf16[1024,1024]{1,0:T(8,128)(2,1)S(1)}, u32[]{:S(2)}) copy-start(bf16[1024,1024]{1,0:T(8,128)(2,1)S(1)} %pad_maximum_fusion.mine.refs_4_) | copy-start | bytes 6291460
  37.2 15.3 %collective-permute-start.4 = (bf16[1024,1024]{1,0:T(8,128)(2,1)S(1)}, bf16[1024,1024]{1,0:T(8,128)(2,1)}, u32[]{:S(2)}, u32[]{:S(2)}) collective-permute-start(bf16[1024,1024]{1,0:T(8,128)(2,1)S(1)} %pad_maximum_fusion.mine.refs_4_), channel_id=1, source_target_pairs={{0,1},{1,0},{2,3},{3,2},{4,5},{5,4},{6,7},{7,6},{8,9},{9,8},{10,11... | collective-permute-start | bytes 6291464 | tf_op jit(solution)/shard_map/ppermute | solution.py:525
  38.7 13.8 %copy-start.2 = (bf16[512,1024]{1,0:T(8,128)(2,1)S(1)}, bf16[512,1024]{1,0:T(8,128)(2,1)}, u32[]{:S(2)}) copy-start(bf16[512,1024]{1,0:T(8,128)(2,1)} %param.14) | copy-start | bytes 3145732
  38.7 12.5 %collective-permute-start.2 = (bf16[512,1024]{1,0:T(8,128)(2,1)S(1)}, bf16[512,1024]{1,0:T(8,128)(2,1)S(1)}, u32[]{:S(2)}, u32[]{:S(2)}) collective-permute-start(bf16[512,1024]{1,0:T(8,128)(2,1)S(1)} %broadcast_select_fusion.3), channel_id=1, source_target_pairs={{0,4},{1,0},{2,6},{3,2},{4,5},{5,1},{6,7},{7,3},{8,12},{9,8},{10,1... | collective-permute-start | bytes 3145736 | tf_op jit(solution)/shard_map/ppermute | solution.py:498
  38.9 12.3 %collective-permute-start.3 = (bf16[512,1024]{1,0:T(8,128)(2,1)}, bf16[512,1024]{1,0:T(8,128)(2,1)S(1)}, u32[]{:S(2)}, u32[]{:S(2)}) collective-permute-start(bf16[512,1024]{1,0:T(8,128)(2,1)} %collective-permute-done.refs_0_.refs_8_), channel_id=1, source_target_pairs={{1,3},{3,1},{4,6},{6,4},{9,11},{11,9},{12,14},{14,12},{17,19},{19,... | collective-permute-start | bytes 3145736 | tf_op jit(solution)/shard_map/ppermute | solution.py:498
  51.2 1.3 copy-start.8
  52.5 22.4 %collective-permute-start.7 = (bf16[512,1024]{1,0:T(8,128)(2,1)S(1)}, bf16[512,1024]{1,0:T(8,128)(2,1)}, u32[]{:S(2)}, u32[]{:S(2)}) collective-permute-start(bf16[512,1024]{1,0:T(8,128)(2,1)S(1)} %copy-done.2), channel_id=1, source_target_pairs={{2,0},{4,1},{0,2},{6,3},{1,4},{7,5},{3,6},{5,7},{10,8},{12,9},{8,1... | collective-permute-start | bytes 3145736 | tf_op jit(solution)/shard_map/ppermute | solution.py:498
  54.0 28.7 %collective-permute-start.8 = (bf16[512,1024]{1,0:T(8,128)(2,1)S(1)}, bf16[512,1024]{1,0:T(8,128)(2,1)S(1)}, u32[]{:S(2)}, u32[]{:S(2)}) collective-permute-start(bf16[512,1024]{1,0:T(8,128)(2,1)S(1)} %copy-done.2), channel_id=1, source_target_pairs={{3,0},{5,1},{1,2},{7,3},{0,4},{6,5},{2,6},{4,7},{11,8},{13,9},{9,1... | collective-permute-start | bytes 3145736 | tf_op jit(solution)/shard_map/ppermute | solution.py:498
  70.5 30.3 %collective-permute-start.5 = (bf16[1536,512]{1,0:T(8,128)(2,1)}, bf16[1536,512]{1,0:T(8,128)(2,1)}, u32[]{:S(2)}, u32[]{:S(2)}) collective-permute-start(bf16[1536,512]{1,0:T(8,128)(2,1)} %get-tuple-element.81), channel_id=1, source_target_pairs={{0,1},{1,8},{8,9},{9,16},{16,17},{17,24},{24,25},{2,3},{3,10},{10,... | collective-permute-start | bytes 4718600 | tf_op jit(solution)/shard_map/ppermute | solution.py:467
  73.6 27.2 %collective-permute-start.6 = (bf16[1536,512]{1,0:T(8,128)(2,1)}, bf16[1536,512]{1,0:T(8,128)(2,1)}, u32[]{:S(2)}, u32[]{:S(2)}) collective-permute-start(bf16[1536,512]{1,0:T(8,128)(2,1)} %get-tuple-element.82), channel_id=1, source_target_pairs={{1,0},{8,1},{9,8},{16,9},{17,16},{24,17},{25,24},{3,2},{10,3},{11,... | collective-permute-start | bytes 4718600 | tf_op jit(solution)/shard_map/ppermute | solution.py:467
  82.8 1.0 copy-start.9
  85.1 22.3 %copy-start.12 = (s32[64]{0:T(128)S(1)}, s32[64]{0:T(128)}, u32[]{:S(2)}) copy-start(s32[64]{0:T(128)} %param.13) | copy-start | bytes 772
  85.1 24.9 %copy-start.4 = (bf16[1024,1024]{1,0:T(8,128)(2,1)S(1)}, bf16[1024,1024]{1,0:T(8,128)(2,1)}, u32[]{:S(2)}) copy-start(bf16[1024,1024]{1,0:T(8,128)(2,1)} %copy-done.3) | copy-start | bytes 6291460
  85.1 13.6 %collective-permute-start.9 = (bf16[512,1024]{1,0:T(8,128)(2,1)S(1)}, bf16[512,1024]{1,0:T(8,128)(2,1)S(1)}, u32[]{:S(2)}, u32[]{:S(2)}) collective-permute-start(bf16[512,1024]{1,0:T(8,128)(2,1)S(1)} %broadcast_select_fusion.1), channel_id=1, source_target_pairs={{0,4},{1,0},{2,6},{3,2},{4,5},{5,1},{6,7},{7,3},{8,12},{9,8},{10,1... | collective-permute-start | bytes 3145736 | tf_op jit(solution)/shard_map/ppermute | solution.py:498
  86.4 13.3 %collective-permute-start.10 = (bf16[512,1024]{1,0:T(8,128)(2,1)}, bf16[512,1024]{1,0:T(8,128)(2,1)S(1)}, u32[]{:S(2)}, u32[]{:S(2)}) collective-permute-start(bf16[512,1024]{1,0:T(8,128)(2,1)} %collective-permute-done.7.refs_0_.refs_4_), channel_id=1, source_target_pairs={{1,3},{3,1},{4,6},{6,4},{9,11},{11,9},{12,14},{14,12},{17,19},{19,... | collective-permute-start | bytes 3145736 | tf_op jit(solution)/shard_map/ppermute | solution.py:498
  98.7 1.0 copy-start.10
  100.8 57.5 %collective-permute-start.11 = (bf16[1536,1024]{1,0:T(8,128)(2,1)}, bf16[1536,1024]{1,0:T(8,128)(2,1)}, u32[]{:S(2)}, u32[]{:S(2)}) collective-permute-start(bf16[1536,1024]{1,0:T(8,128)(2,1)} %get-tuple-element.104), channel_id=1, source_target_pairs={{0,1},{1,8},{8,9},{9,16},{16,17},{17,24},{24,25},{2,3},{3,10},{10,... | collective-permute-start | bytes 9437192 | tf_op jit(solution)/shard_map/ppermute | solution.py:467
  106.1 52.2 %collective-permute-start.12 = (bf16[1536,1024]{1,0:T(8,128)(2,1)}, bf16[1536,1024]{1,0:T(8,128)(2,1)}, u32[]{:S(2)}, u32[]{:S(2)}) collective-permute-start(bf16[1536,1024]{1,0:T(8,128)(2,1)} %get-tuple-element.105), channel_id=1, source_target_pairs={{1,0},{8,1},{9,8},{16,9},{17,16},{24,17},{25,24},{3,2},{10,3},{11,... | collective-permute-start | bytes 9437192 | tf_op jit(solution)/shard_map/ppermute | solution.py:467
  110.0 69.6 %collective-permute-start.15 = (bf16[1024,1024]{1,0:T(8,128)(2,1)S(1)}, bf16[1024,1024]{1,0:T(8,128)(2,1)}, u32[]{:S(2)}, u32[]{:S(2)}) collective-permute-start(bf16[1024,1024]{1,0:T(8,128)(2,1)S(1)} %copy-done.4), channel_id=1, source_target_pairs={{2,0},{0,2},{3,1},{1,3},{6,4},{4,6},{7,5},{5,7},{10,8},{8,10},{11,... | collective-permute-start | bytes 6291464 | tf_op jit(solution)/shard_map/ppermute | solution.py:522
  152.5 20.4 %collective-permute-start.13 = (bf16[1536,512]{1,0:T(8,128)(2,1)}, bf16[1536,512]{1,0:T(8,128)(2,1)}, u32[]{:S(2)}, u32[]{:S(2)}) collective-permute-start(bf16[1536,512]{1,0:T(8,128)(2,1)} %get-tuple-element.102.refs_13_), channel_id=1, source_target_pairs={{1,0},{8,1},{9,8},{16,9},{17,16},{24,17},{25,24},{3,2},{10,3},{11,... | collective-permute-start | bytes 4718600 | tf_op jit(solution)/shard_map/ppermute | solution.py:467
  153.8 19.1 %collective-permute-start.14 = (bf16[1536,512]{1,0:T(8,128)(2,1)}, bf16[1536,512]{1,0:T(8,128)(2,1)}, u32[]{:S(2)}, u32[]{:S(2)}) collective-permute-start(bf16[1536,512]{1,0:T(8,128)(2,1)} %get-tuple-element.103.refs_14_), channel_id=1, source_target_pairs={{0,1},{1,8},{8,9},{9,16},{16,17},{17,24},{24,25},{2,3},{3,10},{10,... | collective-permute-start | bytes 4718600 | tf_op jit(solution)/shard_map/ppermute | solution.py:467
  179.6 59.8 %collective-permute-start.16 = (bf16[512,1024]{1,0:T(8,128)(2,1)}, bf16[512,1024]{1,0:T(8,128)(2,1)S(1)}, u32[]{:S(2)}, u32[]{:S(2)}) collective-permute-start(bf16[512,1024]{1,0:T(8,128)(2,1)} %get-tuple-element.112), channel_id=1, source_target_pairs={{0,2},{1,4},{2,0},{3,6},{4,1},{5,7},{6,3},{7,5},{8,10},{9,12},{10,... | collective-permute-start | bytes 3145736 | tf_op jit(solution)/shard_map/ppermute | solution.py:498
  180.1 59.3 %collective-permute-start.17 = (bf16[512,1024]{1,0:T(8,128)(2,1)}, bf16[512,1024]{1,0:T(8,128)(2,1)}, u32[]{:S(2)}, u32[]{:S(2)}) collective-permute-start(bf16[512,1024]{1,0:T(8,128)(2,1)} %get-tuple-element.113), channel_id=1, source_target_pairs={{0,3},{1,5},{2,1},{3,7},{4,0},{5,6},{6,2},{7,4},{8,11},{9,13},{10,... | collective-permute-start | bytes 3145736 | tf_op jit(solution)/shard_map/ppermute | solution.py:498
  183.5 56.0 %collective-permute-start.18 = (bf16[512,1024]{1,0:T(8,128)(2,1)}, bf16[512,1024]{1,0:T(8,128)(2,1)}, u32[]{:S(2)}, u32[]{:S(2)}) collective-permute-start(bf16[512,1024]{1,0:T(8,128)(2,1)} %get-tuple-element.114), channel_id=1, source_target_pairs={{0,1},{1,7},{2,3},{3,5},{4,2},{5,4},{6,0},{7,6},{8,9},{9,15},{10,1... | collective-permute-start | bytes 3145736 | tf_op jit(solution)/shard_map/ppermute | solution.py:498
  185.1 54.4 %collective-permute-start.19 = (bf16[512,1024]{1,0:T(8,128)(2,1)}, bf16[512,1024]{1,0:T(8,128)(2,1)}, u32[]{:S(2)}, u32[]{:S(2)}) collective-permute-start(bf16[512,1024]{1,0:T(8,128)(2,1)} %get-tuple-element.115), channel_id=1, source_target_pairs={{0,0},{1,6},{2,2},{3,4},{4,3},{5,5},{6,1},{7,7},{8,8},{9,14},{10,1... | collective-permute-start | bytes 3145736 | tf_op jit(solution)/shard_map/ppermute | solution.py:498
  239.4 27.6 %copy-start = (bf16[1024,1024]{1,0:T(8,128)(2,1)S(1)}, bf16[1024,1024]{1,0:T(8,128)(2,1)}, u32[]{:S(2)}) copy-start(bf16[1024,1024]{1,0:T(8,128)(2,1)} %all-reduce.3.cloned.1.call-done) | copy-start | bytes 6291460
  239.4 5.1 %collective-permute-start.20 = (bf16[1024,1024]{1,0:T(8,128)(2,1)}, bf16[1024,1024]{1,0:T(8,128)(2,1)}, u32[]{:S(2)}, u32[]{:S(2)}) collective-permute-start(bf16[1024,1024]{1,0:T(8,128)(2,1)} %collective-permute-done.15.refs_5_), channel_id=1, source_target_pairs={{0,1},{1,0},{2,3},{3,2},{4,5},{5,4},{6,7},{7,6},{8,9},{9,8},{10,11... | collective-permute-start | bytes 6291464 | tf_op jit(solution)/shard_map/ppermute | solution.py:525
  239.4 5.0 %copy-start.11 = (bf16[512,1024]{1,0:T(8,128)(2,1)}, bf16[512,1024]{1,0:T(8,128)(2,1)S(1)}, u32[]{:S(2)}) copy-start(bf16[512,1024]{1,0:T(8,128)(2,1)S(1)} %collective-permute-done.16.refs_0_) | copy-start | bytes 3145732
  239.5 27.5 %collective-permute-start.21 = (bf16[1024,1024]{1,0:T(8,128)(2,1)}, bf16[1024,1024]{1,0:T(8,128)(2,1)}, u32[]{:S(2)}, u32[]{:S(2)}) collective-permute-start(bf16[1024,1024]{1,0:T(8,128)(2,1)} %all-reduce.3.cloned.1.call-done), channel_id=1, source_target_pairs={{5,1},{7,3},{0,4},{2,6},{13,9},{15,11},{8,12},{10,14},{21,17},{23,... | collective-permute-start | bytes 6291464 | tf_op jit(solution)/shard_map/ppermute | solution.py:498
Sparse Core Ops, SparseCore 0:
  173.0 66.4 all-reduce.2
